TPU v7x, 32 devices: a whole 2x2x4 slice. The times are simulated.
32 devices in a mesh: grp: 2 (over y), wide: 4 (over z), sec: 2 (over x), sub: 2 (over core).
Axes of the slice: x: 2, y: 2, z: 4, core: 2. Of those that a mesh axis runs over, the one named last changes fastest.
Arguments:
- tokens: bfloat16 [128, 4096], P(('grp', 'wide', 'sec', 'sub')), parts along dimension 0, may hold values from -6 to 6
- expert_ids: int32 [128, 8], P(('grp', 'wide', 'sec', 'sub')), parts along dimension 0, may hold values from 0 to 31, all different within a row; in each aligned block of 4 rows (0 to 3, 4 to 7, ...) at most 2 rows name the same one
- gate_numer: int32 [128, 8], P(('grp', 'wide', 'sec', 'sub')), parts along dimension 0, may hold values from 1 to 1024
- w_gate: bfloat16 [32, 1536, 4096], P('wide', ('sec', 'sub')), may hold values from -0.09375 to 0.09375
- w_up: bfloat16 [32, 1536, 4096], P('wide', ('sec', 'sub')), may hold values from -0.09375 to 0.09375
- w_down: bfloat16 [32, 1536, 4096], P('wide', ('sec', 'sub')), may hold values from -0.15625 to 0.15625
Outputs:
- mixed: bfloat16 [128, 4096], P(('grp', 'wide', 'sec', 'sub')), parts along dimension 0
There are 2 independent parts, one for each index of `grp`. A program takes and returns all parts, laid end to end along the dimension named above; an argument that names none is the same for every part. Nothing has to cross between parts.
Inputs may be any that keep to these rules, and one draw needn't show every extreme that they name: `expert_ids`: each row names 8 different experts. In the 4 rows of one device no expert is named by more than 2 rows, a bound that some block reaches.
All inputs are finite; a program needn't handle non-finite values.
Results may differ from a plain program's by a relative error of at most 0.012.
Values may be sent and summed in bfloat16 or wider, within the bound.
No kernel may reach another device: no remote copies, remote signals or barrier semaphores. Data moves between devices by JAX's collectives and lax.ppermute only.
A program may use at most 192 MiB of HBM per device.

v0:
```python
import jax
import jax.numpy as jnp
from jax import lax
from jax.sharding import PartitionSpec as P

D = 4096
EXPERTS = 32
CAP = 2


def block_dispatch(block_ids, wide_count, local_count):
    onehot = (block_ids[:, :, None] == jnp.arange(EXPERTS, dtype=jnp.int32)).astype(jnp.int32)
    per_row = jnp.sum(onehot, axis=1)
    before = jnp.cumsum(per_row, axis=0) - per_row
    slot_of = jnp.sum(onehot * before[:, None, :], axis=-1)
    slot_hit = (slot_of[:, :, None] == jnp.arange(CAP, dtype=jnp.int32)).astype(jnp.int32)
    select = jnp.einsum("rke,rkc->ecr", onehot, slot_hit)
    select = select.reshape(wide_count, local_count, CAP, block_ids.shape[0]).transpose(0, 2, 1, 3)
    return (select.astype(jnp.bfloat16), slot_of)


def local(tokens, expert_ids, gate_numer, w_gate, w_up, w_down):
    local_count = w_gate.shape[0]
    wide_count = EXPERTS // local_count
    select, slot_of = block_dispatch(expert_ids, wide_count, local_count)
    outgoing = jnp.einsum(
        "wcjr,rd->wcjd", select, tokens, preferred_element_type=jnp.float32
    ).astype(jnp.bfloat16)
    arrived = lax.all_to_all(outgoing, "wide", split_axis=0, concat_axis=0, tiled=True)
    arrived = arrived.reshape(wide_count * CAP, local_count, D)
    block_rows = lax.all_gather(arrived, ("sec", "sub"), axis=0, tiled=True)
    gate_out = jnp.einsum("njd,jfd->njf", block_rows, w_gate, preferred_element_type=jnp.float32)
    up_out = jnp.einsum("njd,jfd->njf", block_rows, w_up, preferred_element_type=jnp.float32)
    hidden = (jax.nn.silu(gate_out) * up_out).astype(jnp.bfloat16)
    own_share = lax.psum_scatter(
        jnp.einsum("njf,jfd->njd", hidden, w_down, preferred_element_type=jnp.float32).astype(
            jnp.bfloat16
        ),
        ("sec", "sub"),
        scatter_dimension=0,
        tiled=True,
    )
    expert_out = own_share.reshape(wide_count, CAP, local_count, D)
    returned = lax.all_to_all(expert_out, "wide", split_axis=0, concat_axis=0, tiled=True)
    flat_rows = returned.reshape(wide_count * CAP * local_count, D)
    flat_index = (
        expert_ids // local_count * CAP + slot_of
    ) * local_count + expert_ids % local_count
    picked = flat_rows[flat_index]
    numer = gate_numer.astype(jnp.float32)
    weight = numer / jnp.sum(numer, axis=-1, keepdims=True)
    mixed = jnp.sum(weight[..., None] * picked.astype(jnp.float32), axis=1)
    return mixed.astype(jnp.bfloat16)


def solution(mesh):
    return jax.shard_map(
        local,
        mesh=mesh,
        in_specs=(
            P(("grp", "wide", "sec", "sub"), None),
            P(("grp", "wide", "sec", "sub"), None),
            P(("grp", "wide", "sec", "sub"), None),
            P("wide", ("sec", "sub"), None),
            P("wide", ("sec", "sub"), None),
            P("wide", ("sec", "sub"), None),
        ),
        out_specs=P(("grp", "wide", "sec", "sub"), None),
        check_vma=False,
    )
```

profile of v0, /device:TPU:0, one launch (start us, length us, event | category | flops | bytes accessed | tf_op | source)
XLA Modules:
  0.0 152.5 jit_solution(14900996409318525977)
XLA Ops:
  6.5 0.0 copy-start
  6.5 0.0 all-gather.2.cloned.1.call-start
  6.5 0.8 convert_reduce_fusion
  7.4 0.9 select_reduce_fusion
  8.3 0.9 convolution_bitcast_fusion.2
  9.1 0.1 convert_element_type.38
  9.2 0.0 copy-done
  9.2 0.3 convolution_convert_fusion.1
  9.6 20.6 %all_to_all.10 = bf16[4,2,8,4096]{3,2,1,0:T(8,128)(2,1)S(1)} all-to-all(bf16[4,2,8,4096]{3,2,1,0:T(8,128)(2,1)S(1)} %convolution_convert_fusion.1), channel_id=1, replica_groups=mesh['grp'=2,'wide'=4,'sec'=2,'sub'=2] {'wide'}, dimensions={0} | all-to-all | bytes 1048576 | tf_op jit(solution)/shard_map/all_to_all | solution.py:29
  30.2 1.1 copy.11
  31.3 0.0 all-gather.2.cloned.1.call-update
  31.3 0.0 reduce-scatter.4.cloned.1.call-start
  31.3 21.8 %all-gather.2.cloned.1.call-done = bf16[32,8,4096]{2,0,1:T(8,128)(2,1)} async-done(((bf16[8,8,4096]{2,0,1:T(8,128)(2,1)}), bf16[32,8,4096]{2,0,1:T(8,128)(2,1)}) %all-gather.2.cloned.1.call-update) | async-done | bytes 2097168 | tf_op jit(solution)/shard_map/all_gather | solution.py:31
  53.1 0.0 copy-start.1
  53.1 12.7 %convolution_bitcast_fusion.1 = f32[32,8,384]{2,0,1:T(8,128)S(1)} fusion(bf16[32,8,4096]{2,0,1:T(8,128)(2,1)} %all-gather.2.cloned.1.call-done, bf16[8,384,4096]{2,1,0:T(8,128)(2,1)} %param.9), kind=kOutput, calls=%fused_computation.5 | convolution fusion | flops 805306368 | bytes 27656192 | tf_op jit(solution)/shard_map/njd,jfd->njf/dot_general | solution.py:32
  65.9 0.0 copy-done.1
  65.9 0.0 copy-start.2
  65.9 0.0 copy-start.3
  65.9 21.3 %fusion = bf16[8,4,8,4096]{3,2,1,0:T(8,128)(2,1)} fusion(bf16[8,384,4096]{2,1,0:T(8,128)(2,1)} %param.11, bf16[32,8,4096]{2,0,1:T(8,128)(2,1)S(1)} %copy-done.1, bf16[8,384,4096]{2,1,0:T(8,128)(2,1)} %param.10, f32[32,8,384]{2,0,1:T(8,128)S(1)} %convolution_bitcast_fusion.1), kind=kOutput, calls=%fused_computation.2 | convolution fusion | flops 1612251136 | bytes 54919168 | tf_op jit(solution)/shard_map/njf,jfd->njd/dot_general | solution.py:36
  87.3 3.2 %copy.17 = bf16[8,4,8,4096]{3,2,0,1:T(8,128)(2,1)} copy(bf16[8,4,8,4096]{3,2,1,0:T(8,128)(2,1)} %fusion) | data formatting | bytes 4194304
  90.4 0.0 reduce-scatter.4.cloned.1.call-update
  90.5 31.6 %reduce-scatter.4.cloned.1.call-done = bf16[8,32768]{1,0:T(8,128)(2,1)} async-done(((bf16[32,32768]{1,0:T(8,128)(2,1)}), bf16[8,32768]{1,0:T(8,128)(2,1)}) %reduce-scatter.4.cloned.1.call-update) | async-done | bytes 524304
  122.0 1.4 reshape.25
  123.4 1.3 copy.12
  124.7 4.6 %all-to-all-start.1 = ((bf16[4,2,8,4096]{3,1,2,0:T(2,128)(2,1)}), bf16[4,2,8,4096]{3,1,2,0:T(2,128)(2,1)S(1)}, u32[]{:S(2)}, u32[]{:S(2)}) async-start(bf16[4,2,8,4096]{3,1,2,0:T(2,128)(2,1)} %copy.12), calls=%async_computation.1 | async-start | bytes 1048576 | tf_op jit(solution)/shard_map/all_to_all | solution.py:44
  129.3 0.0 copy-done.2
  129.3 0.1 reshape.29
  129.4 0.0 copy-done.3
  129.4 0.1 convert_reduce_fusion.1
  129.5 0.1 convert_divide_fusion
  129.6 14.2 %all-to-all-done.1 = bf16[4,2,8,4096]{3,1,2,0:T(2,128)(2,1)S(1)} async-done(((bf16[4,2,8,4096]{3,1,2,0:T(2,128)(2,1)}), bf16[4,2,8,4096]{3,1,2,0:T(2,128)(2,1)S(1)}, u32[]{:S(2)}, u32[]{:S(2)}) %all-to-all-start.1) | async-done | bytes 524320 | tf_op jit(solution)/shard_map/all_to_all | solution.py:44
  143.8 0.3 copy.13
  144.1 0.7 gather_fusion
  144.8 0.9 fusion.3
  (4 shorter events, 0.1 us)
Async XLA Ops:
  6.5 2.7 %copy-start = (bf16[4,4096]{1,0:T(4,128)(2,1)S(1)}, bf16[4,4096]{1,0:T(4,128)(2,1)}, u32[]{:S(2)}) copy-start(bf16[4,4096]{1,0:T(4,128)(2,1)} %param.6) | copy-start | bytes 98308
  6.5 46.6 %all-gather.2.cloned.1.call-start = ((), (), s32[]{:S(2)}) async-start(), calls=%async_computation.3 | async-start | bytes 2621440 | tf_op jit(solution)/shard_map/all_gather | solution.py:31
  31.3 90.7 %reduce-scatter.4.cloned.1.call-start = ((), (), s32[]{:S(2)}) async-start(), calls=%async_computation.4 | async-start | bytes 2621440
  53.1 12.8 %copy-start.1 = (bf16[32,8,4096]{2,0,1:T(8,128)(2,1)S(1)}, bf16[32,8,4096]{2,0,1:T(8,128)(2,1)}, u32[]{:S(2)}) copy-start(bf16[32,8,4096]{2,0,1:T(8,128)(2,1)} %all-gather.2.cloned.1.call-done) | copy-start | bytes 6291460
  65.9 63.4 %copy-start.2 = (s32[4,8]{1,0:T(4,128)S(1)}, s32[4,8]{1,0:T(4,128)}, u32[]{:S(2)}) copy-start(s32[4,8]{1,0:T(4,128)} %param.7) | copy-start | bytes 388
  65.9 63.5 %copy-start.3 = (s32[4,8]{1,0:T(4,128)S(1)}, s32[4,8]{1,0:T(4,128)}, u32[]{:S(2)}) copy-start(s32[4,8]{1,0:T(4,128)} %param.8) | copy-start | bytes 388
  124.7 19.1 %all-to-all-start.1 = ((bf16[4,2,8,4096]{3,1,2,0:T(2,128)(2,1)}), bf16[4,2,8,4096]{3,1,2,0:T(2,128)(2,1)S(1)}, u32[]{:S(2)}, u32[]{:S(2)}) async-start(bf16[4,2,8,4096]{3,1,2,0:T(2,128)(2,1)} %copy.12), calls=%async_computation.1 | async-start | bytes 1048576 | tf_op jit(solution)/shard_map/all_to_all | solution.py:44
Sparse Core Ops, SparseCore 0:
  31.4 21.6 all-gather.1
  90.6 31.4 reduce-scatter.3
where the time goes:
time: 153 us
  waiting for transfers between devices  67.6 us (44%)
  matrix products  35.3 us (23%)
  blocking collectives  20.6 us (13%)
  between operations  13.5 us (9%)
  local copies, waits for them, and re-layouts  8.09 us (5%)
  starting transfers between devices  4.64 us (3%)
  other arithmetic  2.8 us (2%)
    unnamed x3, waiting for transfers between devices  31.6 us
    all_gather x1, waiting for transfers between devices, local(): block_rows = lax.all_gather(arrived, ('sec', 'sub'), axis=0, tiled=True)  21.8 us
    dot_general x1, matrix products, local(): jnp.einsum('njf,jfd->njd', hidden, w_down, preferred_element_type=jnp.flo...  21.3 us
    all_to_all x1, blocking collectives, local(): lax.all_to_all(outgoing, 'wide', split_axis=0, concat_axis=0, tiled=True)  20.6 us
    all_to_all x1, waiting for transfers between devices, local(): lax.all_to_all(expert_out, 'wide', split_axis=0, concat_axis=0, tiled=True)  14.2 us
    dot_general x1, matrix products, local(): jnp.einsum('njd,jfd->njf', block_rows, w_gate, preferred_element_type=jnp...  12.7 us
    all_to_all x1, starting transfers between devices, local(): lax.all_to_all(expert_out, 'wide', split_axis=0, concat_axis=0, tiled=True)  4.6 us
    unnamed x9, local copies, waits for them, and re-layouts  3.18 us
  transfers between devices with their start and end apart: 3, of which 3 were waited for; matrix products, arithmetic and copies ran while one was open for 0% of the time, Pallas kernels for 0%

commit v1 on v0

v1 whole, which is shorter than its diff:
```python
import jax
import jax.numpy as jnp
from jax import lax
from jax.sharding import PartitionSpec as P

EXPERTS = 32
PART = ("wide", "sec", "sub")


def row_weights(expert_ids, gate_numer):
    numer = gate_numer.astype(jnp.float32)
    weight = numer / jnp.sum(numer, axis=-1, keepdims=True)
    chosen = expert_ids[:, :, None] == jnp.arange(EXPERTS, dtype=jnp.int32)
    return jnp.sum(jnp.where(chosen, weight[:, :, None], 0.0), axis=1)


def local(tokens, expert_ids, gate_numer, w_gate, w_up, w_down):
    local_count, ff_dev, depth = w_gate.shape
    weight = row_weights(expert_ids, gate_numer)
    high = weight.astype(jnp.bfloat16)
    low = (weight - high.astype(jnp.float32)).astype(jnp.bfloat16)
    pad = jnp.zeros((tokens.shape[0], 128 - 2 * EXPERTS), jnp.bfloat16)
    row = jnp.concatenate([tokens, high, low, pad], axis=1)
    rows = lax.all_gather(row, PART, axis=0, tiled=True)
    x = rows[:, :depth]
    both = rows[:, depth:depth + EXPERTS].astype(jnp.float32) + rows[
        :, depth + EXPERTS:depth + 2 * EXPERTS
    ].astype(jnp.float32)
    first = lax.axis_index("wide") * local_count
    mine = lax.dynamic_slice_in_dim(both, first, local_count, axis=1)
    gate_out = jnp.einsum("nd,jfd->njf", x, w_gate, preferred_element_type=jnp.float32)
    up_out = jnp.einsum("nd,jfd->njf", x, w_up, preferred_element_type=jnp.float32)
    hidden = (jax.nn.silu(gate_out) * up_out * mine[:, :, None]).astype(jnp.bfloat16)
    share = jnp.einsum("njf,jfd->nd", hidden, w_down, preferred_element_type=jnp.float32)
    return lax.psum_scatter(
        share.astype(jnp.bfloat16), PART, scatter_dimension=0, tiled=True
    )


def solution(mesh):
    rows = P(("grp", "wide", "sec", "sub"), None)
    weights = P("wide", ("sec", "sub"), None)
    return jax.shard_map(
        local,
        mesh=mesh,
        in_specs=(rows, rows, rows, weights, weights, weights),
        out_specs=rows,
        check_vma=False,
    )
```

time: 153 us -> 166 us (1.085)
  waiting for transfers between devices: 67.6 us -> 86.3 us
  local copies, waits for them, and re-layouts: 8.09 us -> 3.18 us
  starting transfers between devices: 4.64 us -> 0.01 us
  blocking collectives: 20.6 us -> 24.6 us
    unnamed x3 -> x2, waiting for transfers between devices: 31.6 us -> 86.3 us
    all_gather x0 -> x1, blocking collectives: none -> 24.6 us  [local(): rows = lax.all_gather(row, PART, axis=0, tiled=True)]
    all_gather x1 -> x0, waiting for transfers between devices: 21.8 us -> none  [local(): block_rows = lax.all_gather(arrived, ('sec', 'sub'), axis=0, tiled=True)]
    all_to_all x1 -> x0, blocking collectives: 20.6 us -> none  [local(): lax.all_to_all(outgoing, 'wide', split_axis=0, concat_axis=0, tiled=True)]
    all_to_all x1 -> x0, waiting for transfers between devices: 14.2 us -> none  [local(): lax.all_to_all(expert_out, 'wide', split_axis=0, concat_axis=0, tiled=True)]
    all_to_all x1 -> x0, starting transfers between devices: 4.6 us -> none  [local(): lax.all_to_all(expert_out, 'wide', split_axis=0, concat_axis=0, tiled=True)]
    reshape x3 -> x0, local copies, waits for them, and re-layouts: 3.74 us -> none  [the longest x2 2.65 us: local(): expert_out = own_share.reshape(wide_count, CAP, local_count, D)]
    dot_general x4 -> x2, matrix products: 35.3 us -> 34.8 us  [the longest x1 22.3 us: local(): jnp.einsum('njf,jfd->nd', hidden, w_down, preferred_element_type=jnp.floa...]
  transfers between devices with their start and end apart: 3 -> 1, of which waited for: 3 -> 1; matrix products, arithmetic and copies ran while one was open for 0% -> 0% of each run, Pallas kernels for 0% -> 0%
where the time goes in v1:
time: 166 us; the launch traced here: 165 us
  waiting for transfers between devices  86.3 us (52%)
  matrix products  34.8 us (21%)
  blocking collectives  24.6 us (15%)
  between operations  14.1 us (8%)
  local copies, waits for them, and re-layouts  3.18 us (2%)
  other arithmetic  2.41 us (1%)
    unnamed x2, waiting for transfers between devices  86.3 us
    all_gather x1, blocking collectives, local(): rows = lax.all_gather(row, PART, axis=0, tiled=True)  24.6 us
    dot_general x1, matrix products, local(): jnp.einsum('njf,jfd->nd', hidden, w_down, preferred_element_type=jnp.floa...  22.3 us
    dot_general x1, matrix products, local(): jnp.einsum('nd,jfd->njf', x, w_gate, preferred_element_type=jnp.float32)  12.4 us
  transfers between devices with their start and end apart: 1, of which 1 were waited for; matrix products, arithmetic and copies ran while one was open for 0% of the time, Pallas kernels for 0%

profile of v1, /device:TPU:0, one launch (start us, length us, event | category | flops | bytes accessed | tf_op | source)
XLA Modules:
  0.0 165.4 jit_solution(3073006547123136049)
XLA Ops:
  6.5 0.0 all-reduce.3.cloned.1.call-start
  6.5 0.8 convert_reduce_fusion
  7.3 0.8 convert_divide_fusion
  8.1 0.8 select_reduce_fusion
  8.9 0.9 concatenate.3
  9.7 24.6 %all-gather = bf16[16,4,4224]{2,1,0:T(4,128)(2,1)S(1)} all-gather(bf16[1,4,4224]{2,1,0:T(4,128)(2,1)S(1)} %bitcast.14), channel_id=1, replica_groups=mesh['grp'=2,'wide'=4,'sec'=2,'sub'=2] {'wide','sec','sub'}, dimensions={0}, use_global_device_ids=true | all-gather | bytes 574464 | tf_op jit(solution)/shard_map/all_gather | solution.py:24
  34.4 0.1 reshape.5
  34.5 0.1 fusion.12
  34.6 0.1 convert_add_fusion
  34.7 0.1 copy.9
  34.7 12.4 %fusion.8 = f32[64,8,384]{2,0,1:T(8,128)S(1)} fusion(bf16[8,384,4096]{2,1,0:T(8,128)(2,1)} %param.9, bf16[64,4224]{1,0:T(8,128)(2,1)S(1)} %reshape.5), kind=kOutput, calls=%fused_computation.11 | convolution fusion | flops 1610612736 | bytes 26476544 | tf_op jit(solution)/shard_map/nd,jfd->njf/dot_general | solution.py:31
  47.2 0.0 copy-start
  47.2 22.3 %fusion = bf16[64,4096]{1,0:T(8,128)(2,1)} fusion(bf16[8,384,4096]{2,1,0:T(8,128)(2,1)} %param.11, bf16[8,384,4096]{2,1,0:T(8,128)(2,1)} %param.10, f32[64,8,384]{2,0,1:T(8,128)S(1)} %fusion.8, bf16[64,4224]{1,0:T(8,128)(2,1)S(1)} %reshape.5, f32[64,8]{0,1:T(8,128)S(1)} %copy.9), kind=kOutput, calls=%fused_computation.1 | convolution fusion | flops 3222863872 | bytes 52170752 | tf_op jit(solution)/shard_map/njf,jfd->nd/dot_general | solution.py:34
  69.5 0.0 all-reduce.3.cloned.1.call-update
  69.6 0.0 copy-done
  69.6 0.6 dynamic-slice
  70.8 86.3 %all-reduce.3.cloned.1.call-done = bf16[64,4096]{1,0:T(8,128)(2,1)} async-done(((bf16[64,4096]{1,0:T(8,128)(2,1)}), bf16[64,4096]{1,0:T(8,128)(2,1)}) %all-reduce.3.cloned.1.call-update) | async-done | bytes 524304
  157.1 1.5 constant_dynamic-slice_fusion
  (2 shorter events, 0.0 us)
Async XLA Ops:
  6.5 150.5 %all-reduce.3.cloned.1.call-start = ((), (), s32[]{:S(2)}) async-start(), calls=%async_computation | async-start | bytes 1048576
  47.2 22.4 %copy-start = (u32[32]{0:T(128)S(1)}, u32[32]{0:T(128)}, u32[]{:S(2)}) copy-start(u32[32]{0:T(128)} %constant.23) | copy-start | bytes 388
Sparse Core Ops, SparseCore 0:
  69.7 87.3 all-reduce.2

commit v2 on v1

v2 whole, which is shorter than its diff:
```python
import jax
import jax.numpy as jnp
from jax import lax
from jax.sharding import PartitionSpec as P

EXPERTS = 32


def row_weights(expert_ids, gate_numer):
    numer = gate_numer.astype(jnp.float32)
    weight = numer / jnp.sum(numer, axis=-1, keepdims=True)
    chosen = expert_ids[:, :, None] == jnp.arange(EXPERTS, dtype=jnp.int32)
    return jnp.sum(jnp.where(chosen, weight[:, :, None], 0.0), axis=1)


def shift(x, axis, size, by):
    return lax.ppermute(x, axis, [(i, (i + by) % size) for i in range(size)])


def gather(x, axis, size):
    return jnp.concatenate([x] + [shift(x, axis, size, -s) for s in range(1, size)], axis=0)


def scatter(total, axis, size):
    blocks = total.reshape(size, total.shape[0] // size, total.shape[1])
    arrived = [
        shift(blocks[s].astype(jnp.bfloat16), axis, size, s).astype(jnp.float32)
        for s in range(1, size)
    ]
    return sum(arrived, blocks[0])


def build(axes):
    def local(tokens, expert_ids, gate_numer, w_gate, w_up, w_down):
        local_count, ff_dev, depth = w_gate.shape
        weight = row_weights(expert_ids, gate_numer)
        high = weight.astype(jnp.bfloat16)
        low = (weight - high.astype(jnp.float32)).astype(jnp.bfloat16)
        pad = jnp.zeros((tokens.shape[0], 128 - 2 * EXPERTS), jnp.bfloat16)
        rows = jnp.concatenate([tokens, high, low, pad], axis=1)
        for axis in axes:
            rows = gather(rows, *axis)
        x = rows[:, :depth]
        both = rows[:, depth:depth + EXPERTS].astype(jnp.float32) + rows[
            :, depth + EXPERTS:depth + 2 * EXPERTS
        ].astype(jnp.float32)
        first = lax.axis_index("wide") * local_count
        mine = lax.dynamic_slice_in_dim(both, first, local_count, axis=1)
        gate_out = jnp.einsum("nd,jfd->njf", x, w_gate, preferred_element_type=jnp.float32)
        up_out = jnp.einsum("nd,jfd->njf", x, w_up, preferred_element_type=jnp.float32)
        hidden = (jax.nn.silu(gate_out) * up_out * mine[:, :, None]).astype(jnp.bfloat16)
        total = jnp.einsum("njf,jfd->nd", hidden, w_down, preferred_element_type=jnp.float32)
        for axis in reversed(axes):
            total = scatter(total, *axis)
        return total.astype(jnp.bfloat16)

    return local


def solution(mesh):
    rows = P(("grp", "wide", "sec", "sub"), None)
    weights = P("wide", ("sec", "sub"), None)
    axes = [(name, mesh.shape[name]) for name in ("wide", "sec", "sub")]
    return jax.shard_map(
        build(axes),
        mesh=mesh,
        in_specs=(rows, rows, rows, weights, weights, weights),
        out_specs=rows,
        check_vma=False,
    )
```

time: 166 us -> 71.2 us (0.43)
  waiting for transfers between devices: 86.3 us -> 17.9 us
  blocking collectives: 24.6 us -> 0 us
  starting transfers between devices: 0.01 us -> 14.2 us
  between operations: 14.1 us -> 0.11 us
    unnamed x2 -> x0, waiting for transfers between devices: 86.3 us -> none
    all_gather x1 -> x0, blocking collectives: 24.6 us -> none  [local(): rows = lax.all_gather(row, PART, axis=0, tiled=True)]
    ppermute x0 -> x10, waiting for transfers between devices: none -> 17.9 us  [shift(): return lax.ppermute(x, axis, [(i, (i + by) % size) for i in range(size)])]
    ppermute x0 -> x10, starting transfers between devices: none -> 14.2 us  [shift(): return lax.ppermute(x, axis, [(i, (i + by) % size) for i in range(size)])]
    unnamed x5 -> x0, local copies, waits for them, and re-layouts: 2.19 us -> none
  transfers between devices with their start and end apart: 1 -> 10, of which waited for: 1 -> 8; matrix products, arithmetic and copies ran while one was open for 0% -> 0% of each run, Pallas kernels for 0% -> 0%
where the time goes in v2:
time: 71.2 us; the launch traced here: 71 us
  matrix products  34 us (48%)
  waiting for transfers between devices  17.9 us (25%)
  starting transfers between devices  14.2 us (20%)
  other arithmetic  3.23 us (5%)
  local copies, waits for them, and re-layouts  1.59 us (2%)
    dot_general x1, matrix products, local(): jnp.einsum('njf,jfd->nd', hidden, w_down, preferred_element_type=jnp.floa...  21.5 us
    ppermute x10, waiting for transfers between devices, shift(): return lax.ppermute(x, axis, [(i, (i + by) % size) for i in range(size)])  17.9 us
    ppermute x10, starting transfers between devices, shift(): return lax.ppermute(x, axis, [(i, (i + by) % size) for i in range(size)])  14.2 us
    dot_general x1, matrix products, local(): jnp.einsum('nd,jfd->njf', x, w_gate, preferred_element_type=jnp.float32)  12.4 us
  transfers between devices with their start and end apart: 10, of which 8 were waited for; matrix products, arithmetic and copies ran while one was open for 0% of the time, Pallas kernels for 0%

profile of v2, /device:TPU:0, one launch (start us, length us, event | category | flops | bytes accessed | tf_op | source)
XLA Modules:
  0.0 71.0 jit_solution(8247094174178700139)
XLA Ops:
  0.0 0.8 %convert_reduce_fusion = f32[4]{0:T(128)S(1)} fusion(s32[4,8]{1,0:T(4,128)} %param.8), kind=kLoop, calls=%fused_computation.21 | loop fusion | flops 60 | bytes 144 | tf_op jit(solution)/shard_map/reduce_sum | solution.py:11
  0.8 0.8 %convert_divide_fusion = f32[4,8]{1,0:T(4,128)S(1)} fusion(s32[4,8]{1,0:T(4,128)} %param.8, f32[4]{0:T(128)S(1)} %convert_reduce_fusion), kind=kLoop, calls=%fused_computation.20 | loop fusion | flops 64 | bytes 272 | tf_op jit(solution)/shard_map/div | solution.py:11
  1.6 0.8 %select_reduce_fusion = f32[4,32]{1,0:T(4,128)S(1)} fusion(f32[4,8]{1,0:T(4,128)S(1)} %convert_divide_fusion, s32[4,8]{1,0:T(4,128)} %param.7), kind=kLoop, calls=%fused_computation.17 | loop fusion | flops 2944 | bytes 768 | tf_op jit(solution)/shard_map/reduce_sum | solution.py:13
  2.3 0.9 %concatenate.14 = bf16[4,4224]{1,0:T(4,128)(2,1)S(1)} concatenate(bf16[4,4096]{1,0:T(4,128)(2,1)} %param.6, bf16[4,32]{1,0:T(4,128)(2,1)S(1)} %get-tuple-element.8, bf16[4,32]{1,0:T(4,128)(2,1)S(1)} %get-tuple-element.7, bf16[4,64]{1,0:T(4,128)(2,1)S(1)} %broadcast_in_dim.22), dimensions={1} | concatenate | bytes 67584 | tf_op jit(solution)/shard_map/concatenate | solution.py:40
  3.2 3.0 %collective-permute-start.2 = (bf16[4,4224]{1,0:T(4,128)(2,1)S(1)}, bf16[4,4224]{1,0:T(4,128)(2,1)S(1)}, u32[]{:S(2)}, u32[]{:S(2)}) collective-permute-start(bf16[4,4224]{1,0:T(4,128)(2,1)S(1)} %concatenate.14), channel_id=1, source_target_pairs={{0,4},{4,8},{8,12},{12,0},{1,5},{5,9},{9,13},{13,1},{2,6},{6,10},{... | collective-permute-start | bytes 101384 | tf_op jit(solution)/shard_map/ppermute | solution.py:17
  6.2 2.6 %collective-permute-start.1 = (bf16[4,4224]{1,0:T(4,128)(2,1)S(1)}, bf16[4,4224]{1,0:T(4,128)(2,1)S(1)}, u32[]{:S(2)}, u32[]{:S(2)}) collective-permute-start(bf16[4,4224]{1,0:T(4,128)(2,1)S(1)} %concatenate.14), channel_id=1, source_target_pairs={{0,8},{4,12},{8,0},{12,4},{1,9},{5,13},{9,1},{13,5},{2,10},{6,14},... | collective-permute-start | bytes 101384 | tf_op jit(solution)/shard_map/ppermute | solution.py:17
  8.8 1.3 %collective-permute-start = (bf16[4,4224]{1,0:T(4,128)(2,1)S(1)}, bf16[4,4224]{1,0:T(4,128)(2,1)S(1)}, u32[]{:S(2)}, u32[]{:S(2)}) collective-permute-start(bf16[4,4224]{1,0:T(4,128)(2,1)S(1)} %concatenate.14), channel_id=1, source_target_pairs={{0,12},{4,0},{8,4},{12,8},{1,13},{5,1},{9,5},{13,9},{2,14},{6,2},{... | collective-permute-start | bytes 101384 | tf_op jit(solution)/shard_map/ppermute | solution.py:17
  10.2 0.0 collective-permute-done.2
  10.2 1.2 %collective-permute-done.1 = bf16[4,4224]{1,0:T(4,128)(2,1)S(1)} collective-permute-done((bf16[4,4224]{1,0:T(4,128)(2,1)S(1)}, bf16[4,4224]{1,0:T(4,128)(2,1)S(1)}, u32[]{:S(2)}, u32[]{:S(2)}) %collective-permute-start.1) | collective-permute-done | bytes 33824 | tf_op jit(solution)/shard_map/ppermute | solution.py:17
  11.4 1.3 %collective-permute-done = bf16[4,4224]{1,0:T(4,128)(2,1)S(1)} collective-permute-done((bf16[4,4224]{1,0:T(4,128)(2,1)S(1)}, bf16[4,4224]{1,0:T(4,128)(2,1)S(1)}, u32[]{:S(2)}, u32[]{:S(2)}) %collective-permute-start) | collective-permute-done | bytes 33824 | tf_op jit(solution)/shard_map/ppermute | solution.py:17
  12.7 0.1 pad_maximum_fusion
  12.8 1.6 %collective-permute-start.3 = (bf16[16,4224]{1,0:T(8,128)(2,1)S(1)}, bf16[16,4224]{1,0:T(8,128)(2,1)S(1)}, u32[]{:S(2)}, u32[]{:S(2)}) collective-permute-start(bf16[16,4224]{1,0:T(8,128)(2,1)S(1)} %pad_maximum_fusion), channel_id=1, source_target_pairs={{0,2},{2,0},{1,3},{3,1},{4,6},{6,4},{5,7},{7,5},{8,10},{10,8},{9,1... | collective-permute-start | bytes 405512 | tf_op jit(solution)/shard_map/ppermute | solution.py:17
  14.4 3.5 %collective-permute-done.3 = bf16[16,4224]{1,0:T(8,128)(2,1)S(1)} collective-permute-done((bf16[16,4224]{1,0:T(8,128)(2,1)S(1)}, bf16[16,4224]{1,0:T(8,128)(2,1)S(1)}, u32[]{:S(2)}, u32[]{:S(2)}) %collective-permute-start.3) | collective-permute-done | bytes 135200 | tf_op jit(solution)/shard_map/ppermute | solution.py:17
  17.9 0.2 concatenate.16
  18.1 0.1 collective-permute-start.4
  18.2 1.5 %collective-permute-done.4 = bf16[32,4224]{1,0:T(8,128)(2,1)S(1)} collective-permute-done((bf16[32,4224]{1,0:T(8,128)(2,1)S(1)}, bf16[32,4224]{1,0:T(8,128)(2,1)S(1)}, u32[]{:S(2)}, u32[]{:S(2)}) %collective-permute-start.4) | collective-permute-done | bytes 270368 | tf_op jit(solution)/shard_map/ppermute | solution.py:17
  19.7 0.3 concatenate.17
  20.0 0.1 fusion.9
  20.1 0.1 convert_add_fusion
  20.2 0.1 copy.8
  20.3 12.4 %fusion.1 = f32[64,8,384]{2,0,1:T(8,128)S(1)} fusion(bf16[8,384,4096]{2,1,0:T(8,128)(2,1)} %param.9, bf16[64,4224]{1,0:T(8,128)(2,1)S(1)} %concatenate.17), kind=kOutput, calls=%fused_computation.6 | convolution fusion | flops 1610612736 | bytes 26476544 | tf_op jit(solution)/shard_map/nd,jfd->njf/dot_general | solution.py:49
  32.7 21.5 %convolution_bitcast_fusion = f32[64,4096]{1,0:T(8,128)S(1)} fusion(bf16[8,384,4096]{2,1,0:T(8,128)(2,1)} %param.11, f32[64,8,384]{2,0,1:T(8,128)S(1)} %fusion.1, bf16[8,384,4096]{2,1,0:T(8,128)(2,1)} %param.10, bf16[64,4224]{1,0:T(8,128)(2,1)S(1)} %concatenate.17, f32[64,8]{0,1:T(8,128)S(1)} %copy.8), kind=kOutput, calls=%fused_computation | convolution fusion | flops 3222601728 | bytes 52695040 | tf_op jit(solution)/shard_map/njf,jfd->nd/dot_general | solution.py:52
  54.3 0.2 collective-permute-start.5
  54.5 1.4 %collective-permute-done.5 = bf16[32,4096]{1,0:T(8,128)(2,1)S(1)} collective-permute-done((bf16[32,4096]{1,0:T(8,128)(2,1)S(1)}, bf16[32,4096]{1,0:T(8,128)(2,1)S(1)}, u32[]{:S(2)}, u32[]{:S(2)}) %collective-permute-start.5) | collective-permute-done | bytes 262176 | tf_op jit(solution)/shard_map/ppermute | solution.py:17
  55.9 0.1 slice_add_fusion
  56.0 1.6 %collective-permute-start.6 = (bf16[16,4096]{1,0:T(8,128)(2,1)S(1)}, bf16[16,4096]{1,0:T(8,128)(2,1)S(1)}, u32[]{:S(2)}, u32[]{:S(2)}) collective-permute-start(bf16[16,4096]{1,0:T(8,128)(2,1)S(1)} %slice.87), channel_id=1, source_target_pairs={{0,2},{2,0},{1,3},{3,1},{4,6},{6,4},{5,7},{7,5},{8,10},{10,8},{9,1... | collective-permute-start | bytes 393224 | tf_op jit(solution)/shard_map/ppermute | solution.py:17
  57.5 4.0 %collective-permute-done.6 = bf16[16,4096]{1,0:T(8,128)(2,1)S(1)} collective-permute-done((bf16[16,4096]{1,0:T(8,128)(2,1)S(1)}, bf16[16,4096]{1,0:T(8,128)(2,1)S(1)}, u32[]{:S(2)}, u32[]{:S(2)}) %collective-permute-start.6) | collective-permute-done | bytes 131104 | tf_op jit(solution)/shard_map/ppermute | solution.py:17
  61.7 0.3 collective-permute-start.7
  62.0 3.6 %collective-permute-start.9 = (bf16[4,4096]{1,0:T(4,128)(2,1)S(1)}, bf16[4,4096]{1,0:T(4,128)(2,1)S(1)}, u32[]{:S(2)}, u32[]{:S(2)}) collective-permute-start(bf16[4,4096]{1,0:T(4,128)(2,1)S(1)} %get-tuple-element.12), channel_id=1, source_target_pairs={{0,12},{4,0},{8,4},{12,8},{1,13},{5,1},{9,5},{13,9},{2,14},{6,2},{... | collective-permute-start | bytes 98312 | tf_op jit(solution)/shard_map/ppermute | solution.py:17
  65.5 0.0 collective-permute-start.8
  65.5 2.1 %collective-permute-done.7 = bf16[4,4096]{1,0:T(4,128)(2,1)S(1)} collective-permute-done((bf16[4,4096]{1,0:T(4,128)(2,1)S(1)}, bf16[4,4096]{1,0:T(4,128)(2,1)S(1)}, u32[]{:S(2)}, u32[]{:S(2)}) %collective-permute-start.7) | collective-permute-done | bytes 32800 | tf_op jit(solution)/shard_map/ppermute | solution.py:17
  67.6 0.0 collective-permute-done.9
  67.6 2.8 %collective-permute-done.8 = bf16[4,4096]{1,0:T(4,128)(2,1)S(1)} collective-permute-done((bf16[4,4096]{1,0:T(4,128)(2,1)S(1)}, bf16[4,4096]{1,0:T(4,128)(2,1)S(1)}, u32[]{:S(2)}, u32[]{:S(2)}) %collective-permute-start.8) | collective-permute-done | bytes 32800 | tf_op jit(solution)/shard_map/ppermute | solution.py:17
  70.4 0.6 fusion.6
  (6 shorter events, 0.1 us)
Async XLA Ops:
  3.2 7.0 %collective-permute-start.2 = (bf16[4,4224]{1,0:T(4,128)(2,1)S(1)}, bf16[4,4224]{1,0:T(4,128)(2,1)S(1)}, u32[]{:S(2)}, u32[]{:S(2)}) collective-permute-start(bf16[4,4224]{1,0:T(4,128)(2,1)S(1)} %concatenate.14), channel_id=1, source_target_pairs={{0,4},{4,8},{8,12},{12,0},{1,5},{5,9},{9,13},{13,1},{2,6},{6,10},{... | collective-permute-start | bytes 101384 | tf_op jit(solution)/shard_map/ppermute | solution.py:17
  6.2 5.2 %collective-permute-start.1 = (bf16[4,4224]{1,0:T(4,128)(2,1)S(1)}, bf16[4,4224]{1,0:T(4,128)(2,1)S(1)}, u32[]{:S(2)}, u32[]{:S(2)}) collective-permute-start(bf16[4,4224]{1,0:T(4,128)(2,1)S(1)} %concatenate.14), channel_id=1, source_target_pairs={{0,8},{4,12},{8,0},{12,4},{1,9},{5,13},{9,1},{13,5},{2,10},{6,14},... | collective-permute-start | bytes 101384 | tf_op jit(solution)/shard_map/ppermute | solution.py:17
  8.8 3.9 %collective-permute-start = (bf16[4,4224]{1,0:T(4,128)(2,1)S(1)}, bf16[4,4224]{1,0:T(4,128)(2,1)S(1)}, u32[]{:S(2)}, u32[]{:S(2)}) collective-permute-start(bf16[4,4224]{1,0:T(4,128)(2,1)S(1)} %concatenate.14), channel_id=1, source_target_pairs={{0,12},{4,0},{8,4},{12,8},{1,13},{5,1},{9,5},{13,9},{2,14},{6,2},{... | collective-permute-start | bytes 101384 | tf_op jit(solution)/shard_map/ppermute | solution.py:17
  12.8 5.1 %collective-permute-start.3 = (bf16[16,4224]{1,0:T(8,128)(2,1)S(1)}, bf16[16,4224]{1,0:T(8,128)(2,1)S(1)}, u32[]{:S(2)}, u32[]{:S(2)}) collective-permute-start(bf16[16,4224]{1,0:T(8,128)(2,1)S(1)} %pad_maximum_fusion), channel_id=1, source_target_pairs={{0,2},{2,0},{1,3},{3,1},{4,6},{6,4},{5,7},{7,5},{8,10},{10,8},{9,1... | collective-permute-start | bytes 405512 | tf_op jit(solution)/shard_map/ppermute | solution.py:17
  18.1 1.6 %collective-permute-start.4 = (bf16[32,4224]{1,0:T(8,128)(2,1)S(1)}, bf16[32,4224]{1,0:T(8,128)(2,1)S(1)}, u32[]{:S(2)}, u32[]{:S(2)}) collective-permute-start(bf16[32,4224]{1,0:T(8,128)(2,1)S(1)} %concatenate.16), channel_id=1, source_target_pairs={{0,1},{1,0},{2,3},{3,2},{4,5},{5,4},{6,7},{7,6},{8,9},{9,8},{10,11... | collective-permute-start | bytes 811016 | tf_op jit(solution)/shard_map/ppermute | solution.py:17
  54.3 1.6 %collective-permute-start.5 = (bf16[32,4096]{1,0:T(8,128)(2,1)S(1)}, bf16[32,4096]{1,0:T(8,128)(2,1)S(1)}, u32[]{:S(2)}, u32[]{:S(2)}) collective-permute-start(bf16[32,4096]{1,0:T(8,128)(2,1)S(1)} %slice.86), channel_id=1, source_target_pairs={{0,1},{1,0},{2,3},{3,2},{4,5},{5,4},{6,7},{7,6},{8,9},{9,8},{10,11... | collective-permute-start | bytes 786440 | tf_op jit(solution)/shard_map/ppermute | solution.py:17
  56.0 5.6 %collective-permute-start.6 = (bf16[16,4096]{1,0:T(8,128)(2,1)S(1)}, bf16[16,4096]{1,0:T(8,128)(2,1)S(1)}, u32[]{:S(2)}, u32[]{:S(2)}) collective-permute-start(bf16[16,4096]{1,0:T(8,128)(2,1)S(1)} %slice.87), channel_id=1, source_target_pairs={{0,2},{2,0},{1,3},{3,1},{4,6},{6,4},{5,7},{7,5},{8,10},{10,8},{9,1... | collective-permute-start | bytes 393224 | tf_op jit(solution)/shard_map/ppermute | solution.py:17
  61.7 5.9 %collective-permute-start.7 = (bf16[4,4096]{1,0:T(4,128)(2,1)S(1)}, bf16[4,4096]{1,0:T(4,128)(2,1)S(1)}, u32[]{:S(2)}, u32[]{:S(2)}) collective-permute-start(bf16[4,4096]{1,0:T(4,128)(2,1)S(1)} %get-tuple-element.11), channel_id=1, source_target_pairs={{0,4},{4,8},{8,12},{12,0},{1,5},{5,9},{9,13},{13,1},{2,6},{6,10},{... | collective-permute-start | bytes 98312 | tf_op jit(solution)/shard_map/ppermute | solution.py:17
  62.0 5.6 %collective-permute-start.9 = (bf16[4,4096]{1,0:T(4,128)(2,1)S(1)}, bf16[4,4096]{1,0:T(4,128)(2,1)S(1)}, u32[]{:S(2)}, u32[]{:S(2)}) collective-permute-start(bf16[4,4096]{1,0:T(4,128)(2,1)S(1)} %get-tuple-element.12), channel_id=1, source_target_pairs={{0,12},{4,0},{8,4},{12,8},{1,13},{5,1},{9,5},{13,9},{2,14},{6,2},{... | collective-permute-start | bytes 98312 | tf_op jit(solution)/shard_map/ppermute | solution.py:17
  65.5 4.8 %collective-permute-start.8 = (bf16[4,4096]{1,0:T(4,128)(2,1)S(1)}, bf16[4,4096]{1,0:T(4,128)(2,1)S(1)}, u32[]{:S(2)}, u32[]{:S(2)}) collective-permute-start(bf16[4,4096]{1,0:T(4,128)(2,1)S(1)} %get-tuple-element.13), channel_id=1, source_target_pairs={{0,8},{4,12},{8,0},{12,4},{1,9},{5,13},{9,1},{13,5},{2,10},{6,14},... | collective-permute-start | bytes 98312 | tf_op jit(solution)/shard_map/ppermute | solution.py:17

commit v3 on v2

v3 whole, which is shorter than its diff:
```python
import functools

import jax
import jax.numpy as jnp
from jax import lax
from jax.experimental import pallas as pl
from jax.experimental.pallas import tpu as pltpu
from jax.sharding import PartitionSpec as P

EXPERTS = 32
SIDE = 128
SLOTS = 4


def shift(x, axis, size, by):
    return lax.ppermute(x, axis, [(i, (i + by) % size) for i in range(size)])


def gather(x, axis, size):
    return jnp.concatenate([x] + [shift(x, axis, size, -s) for s in range(1, size)], axis=0)


def scatter(total, axis, size):
    blocks = total.reshape(size, total.shape[0] // size, total.shape[1])
    arrived = [
        shift(blocks[s].astype(jnp.bfloat16), axis, size, s).astype(jnp.float32)
        for s in range(1, size)
    ]
    return sum(arrived, blocks[0])


def with_routing(tokens, expert_ids, gate_numer):
    side = jnp.concatenate([expert_ids, gate_numer >> 5, gate_numer & 31], axis=1)
    pad = jnp.zeros((tokens.shape[0], SIDE - side.shape[1]), jnp.bfloat16)
    return jnp.concatenate([tokens, side.astype(jnp.bfloat16), pad], axis=1)


def dense_weights(side, top):
    ids = side[:, :top]
    numer = side[:, top:2 * top] * 32.0 + side[:, 2 * top:3 * top]
    weight = numer / jnp.sum(numer, axis=-1, keepdims=True)
    lane = lax.broadcasted_iota(jnp.int32, (side.shape[0], SIDE), 1)
    expert = jnp.where(lane < EXPERTS, lane, lane - EXPERTS).astype(jnp.float32)
    full = jnp.zeros((side.shape[0], SIDE), jnp.float32)
    for k in range(top):
        full = full + jnp.where(expert == ids[:, k:k + 1], weight[:, k:k + 1], 0.0)
    high = full.astype(jnp.bfloat16).astype(jnp.float32)
    return jnp.where(lane < EXPERTS, high, full - high).astype(jnp.bfloat16)


def layer(top, ff_dev, row_block, rows_ref, gate_ref, up_ref, down_ref, out_ref,
          gates, ups, downs, weights, hidden, sem):
    units, depth = down_ref.shape
    step_units = gates.shape[1]
    steps = units // step_units
    count = rows_ref.shape[0]

    def copies(step, slot):
        span = pl.ds(pl.multiple_of(step * step_units, step_units), step_units)
        return [
            pltpu.make_async_copy(src.at[span], dst.at[slot], sem.at[i, slot])
            for i, (src, dst) in enumerate(
                [(gate_ref, gates), (up_ref, ups), (down_ref, downs)]
            )
        ]

    for step in range(min(SLOTS - 1, steps)):
        for copy in copies(step, step):
            copy.start()

    first = lax.axis_index("wide") * (units // ff_dev)

    def each_block(body):
        if count == row_block:
            body(pl.ds(0, row_block))
        else:
            @pl.loop(0, count // row_block)
            def _(b):
                body(pl.ds(pl.multiple_of(b * row_block, row_block), row_block))

    def prepare(block):
        side = rows_ref[block, depth:depth + SIDE].astype(jnp.float32)
        weights[block, :] = dense_weights(side, top)
        out_ref[block, :] = jnp.zeros((row_block, depth), jnp.float32)

    each_block(prepare)

    @pl.loop(0, steps)
    def _(step):
        slot = lax.rem(step, SLOTS)

        @pl.when(step + SLOTS - 1 < steps)
        def _():
            for copy in copies(step + SLOTS - 1, lax.rem(step + SLOTS - 1, SLOTS)):
                copy.start()

        expert = lax.broadcasted_iota(jnp.int32, (SIDE, step_units), 0)
        place = jnp.where(expert < EXPERTS, expert, expert - EXPERTS) - first
        unit = step * step_units + lax.broadcasted_iota(jnp.int32, (SIDE, step_units), 1)
        low = place * ff_dev
        pick = ((unit >= low) & (unit < low + ff_dev) & (expert < 2 * EXPERTS))
        pick = jnp.where(pick, 1.0, 0.0).astype(jnp.bfloat16)
        now = copies(step, slot)
        now[0].wait()
        now[1].wait()

        def first_half(block):
            x = rows_ref[block, :depth]
            last = (((1,), (1,)), ((), ()))
            g = lax.dot_general(x, gates[slot], last, preferred_element_type=jnp.float32)
            u = lax.dot_general(x, ups[slot], last, preferred_element_type=jnp.float32)
            scale = jnp.dot(weights[block, :], pick, preferred_element_type=jnp.float32)
            hidden[block, :] = (g / (1.0 + jnp.exp(-g)) * u * scale).astype(jnp.bfloat16)

        each_block(first_half)
        now[2].wait()

        def second_half(block):
            out_ref[block, :] += jnp.dot(
                hidden[block, :], downs[slot], preferred_element_type=jnp.float32
            )

        each_block(second_half)


def build(axes):
    def local(tokens, expert_ids, gate_numer, w_gate, w_up, w_down):
        local_count, ff_dev, depth = w_gate.shape
        units = local_count * ff_dev
        step_units = next(n for n in range(256, 0, -16) if units % n == 0)
        rows = with_routing(tokens, expert_ids, gate_numer)
        for axis in axes:
            rows = gather(rows, *axis)
        count = rows.shape[0]
        total = pl.pallas_call(
            functools.partial(layer, expert_ids.shape[1], ff_dev, min(count, 64)),
            out_shape=jax.ShapeDtypeStruct((count, depth), jnp.float32),
            in_specs=[pl.BlockSpec(memory_space=pltpu.VMEM)]
            + [pl.BlockSpec(memory_space=pl.ANY)] * 3,
            out_specs=pl.BlockSpec(memory_space=pltpu.VMEM),
            scratch_shapes=[pltpu.VMEM((SLOTS, step_units, depth), jnp.bfloat16)] * 3
            + [
                pltpu.VMEM((count, SIDE), jnp.bfloat16),
                pltpu.VMEM((count, step_units), jnp.bfloat16),
                pltpu.SemaphoreType.DMA((3, SLOTS)),
            ],
            compiler_params=pltpu.CompilerParams(vmem_limit_bytes=56 << 20),
            cost_estimate=pl.CostEstimate(
                flops=6 * count * units * depth,
                bytes_accessed=6 * units * depth,
                transcendentals=count * units,
            ),
            name="expert_layer",
        )(
            rows,
            w_gate.reshape(units, depth),
            w_up.reshape(units, depth),
            w_down.reshape(units, depth),
        )
        for axis in reversed(axes):
            total = scatter(total, *axis)
        return total.astype(jnp.bfloat16)

    return local


def solution(mesh):
    rows = P(("grp", "wide", "sec", "sub"), None)
    weights = P("wide", ("sec", "sub"), None)
    axes = [(name, mesh.shape[name]) for name in ("wide", "sec", "sub")]
    return jax.shard_map(
        build(axes),
        mesh=mesh,
        in_specs=(rows, rows, rows, weights, weights, weights),
        out_specs=rows,
        check_vma=False,
    )
```

time: 71.2 us -> 68.5 us (0.962)
  matrix products: 34 us -> 0 us
  Pallas kernels: 0 us -> 27.2 us
  local copies, waits for them, and re-layouts: 1.59 us -> 5.5 us
    dot_general x2 -> x0, matrix products: 34 us -> none  [the longest x1 21.5 us: local(): jnp.einsum('njf,jfd->nd', hidden, w_down, preferred_element_type=jnp.floa...]
    pallas_call x0 -> x1, Pallas kernels: none -> 27.2 us  [local(): pl.pallas_call(functools.partial(layer, expert_ids.shape[1], ff_dev, min(...]
    concatenate x2, local copies, waits for them, and re-layouts: 0.51 us -> 3.52 us  [gather(): jnp.concatenate([x] + [shift(x, axis, size, -s) for s in range(1, size)],...]
    reduce_sum x2 -> x0, other arithmetic: 1.57 us -> none  [the longest x1 0.8 us: row_weights(): weight = numer / jnp.sum(numer, axis=-1, keepdims=True)]
    another operation x1 -> x3, other arithmetic: 0.03 us -> 1.4 us
    slice x3, local copies, waits for them, and re-layouts: 0.09 us -> 1.13 us  [scatter(): blocks[s].astype(jnp.bfloat16)]
    add x1, other arithmetic: 0.06 us -> 1.1 us  [scatter(): return sum(arrived, blocks[0])]
    div x1 -> x0, other arithmetic: 0.75 us -> none  [row_weights(): weight = numer / jnp.sum(numer, axis=-1, keepdims=True)]
where the time goes in v3:
time: 68.5 us; the launch traced here: 68.1 us
  Pallas kernels  27.2 us (40%)
  waiting for transfers between devices  17.9 us (26%)
  starting transfers between devices  14.2 us (21%)
  local copies, waits for them, and re-layouts  5.5 us (8%)
  other arithmetic  3.23 us (5%)
    pallas_call x1, Pallas kernels, local(): pl.pallas_call(functools.partial(layer, expert_ids.shape[1], ff_dev, min(...  27.2 us
    ppermute x10, waiting for transfers between devices, shift(): return lax.ppermute(x, axis, [(i, (i + by) % size) for i in range(size)])  17.9 us
    ppermute x10, starting transfers between devices, shift(): return lax.ppermute(x, axis, [(i, (i + by) % size) for i in range(size)])  14.2 us
    concatenate x2, local copies, waits for them, and re-layouts, gather(): jnp.concatenate([x] + [shift(x, axis, size, -s) for s in range(1, size)],...  3.52 us
    another operation x3, other arithmetic  1.4 us
  transfers between devices with their start and end apart: 10, of which 8 were waited for; matrix products, arithmetic and copies ran while one was open for 0% of the time, Pallas kernels for 0%

profile of v3, /device:TPU:0, one launch (start us, length us, event | category | flops | bytes accessed | tf_op | source)
XLA Modules:
  0.0 68.1 jit_solution(16477480173235184861)
XLA Ops:
  0.0 0.7 %convert.20 = bf16[4,8]{1,0:T(4,128)(2,1)S(1)} convert(s32[4,8]{1,0:T(4,128)} %param.7) | non-fusion elementwise | flops 32 | bytes 192 | tf_op jit(solution)/shard_map/convert.5
  0.7 0.7 %and_convert_fusion = (bf16[4,8]{1,0:T(4,128)(2,1)S(1)}, bf16[4,8]{1,0:T(4,128)(2,1)S(1)}) fusion(s32[4,8]{1,0:T(4,128)} %param.8), kind=kLoop, calls=%fused_computation.9 | loop fusion | flops 128 | bytes 256 | tf_op jit(solution)/shard_map/convert.7
  1.4 0.9 %concatenate.17 = bf16[4,4224]{1,0:T(4,128)(2,1)S(1)} concatenate(bf16[4,4096]{1,0:T(4,128)(2,1)} %param.6, bf16[4,8]{1,0:T(4,128)(2,1)S(1)} %convert.20, bf16[4,8]{1,0:T(4,128)(2,1)S(1)} %get-tuple-element.11, bf16[4,8]{1,0:T(4,128)(2,1)S(1)} %get-tuple-element.10, bf16[4,104]{1,0:T(4,128)(2,1)S(1)} %broadcast_in_dim.3), dimensions={1} | concatenate | bytes 67584 | tf_op jit(solution)/shard_map/concatenate | solution.py:35
  2.2 3.0 %collective-permute-start.2 = (bf16[4,4224]{1,0:T(4,128)(2,1)S(1)}, bf16[4,4224]{1,0:T(4,128)(2,1)S(1)}, u32[]{:S(2)}, u32[]{:S(2)}) collective-permute-start(bf16[4,4224]{1,0:T(4,128)(2,1)S(1)} %concatenate.17), channel_id=1, source_target_pairs={{0,4},{4,8},{8,12},{12,0},{1,5},{5,9},{9,13},{13,1},{2,6},{6,10},{... | collective-permute-start | bytes 101384 | tf_op jit(solution)/shard_map/ppermute | solution.py:16
  5.3 2.6 %collective-permute-start.1 = (bf16[4,4224]{1,0:T(4,128)(2,1)S(1)}, bf16[4,4224]{1,0:T(4,128)(2,1)S(1)}, u32[]{:S(2)}, u32[]{:S(2)}) collective-permute-start(bf16[4,4224]{1,0:T(4,128)(2,1)S(1)} %concatenate.17), channel_id=1, source_target_pairs={{0,8},{4,12},{8,0},{12,4},{1,9},{5,13},{9,1},{13,5},{2,10},{6,14},... | collective-permute-start | bytes 101384 | tf_op jit(solution)/shard_map/ppermute | solution.py:16
  7.8 1.3 %collective-permute-start = (bf16[4,4224]{1,0:T(4,128)(2,1)S(1)}, bf16[4,4224]{1,0:T(4,128)(2,1)S(1)}, u32[]{:S(2)}, u32[]{:S(2)}) collective-permute-start(bf16[4,4224]{1,0:T(4,128)(2,1)S(1)} %concatenate.17), channel_id=1, source_target_pairs={{0,12},{4,0},{8,4},{12,8},{1,13},{5,1},{9,5},{13,9},{2,14},{6,2},{... | collective-permute-start | bytes 101384 | tf_op jit(solution)/shard_map/ppermute | solution.py:16
  9.2 0.0 collective-permute-done.2
  9.2 1.2 %collective-permute-done.1 = bf16[4,4224]{1,0:T(4,128)(2,1)S(1)} collective-permute-done((bf16[4,4224]{1,0:T(4,128)(2,1)S(1)}, bf16[4,4224]{1,0:T(4,128)(2,1)S(1)}, u32[]{:S(2)}, u32[]{:S(2)}) %collective-permute-start.1) | collective-permute-done | bytes 33824 | tf_op jit(solution)/shard_map/ppermute | solution.py:16
  10.4 1.3 %collective-permute-done = bf16[4,4224]{1,0:T(4,128)(2,1)S(1)} collective-permute-done((bf16[4,4224]{1,0:T(4,128)(2,1)S(1)}, bf16[4,4224]{1,0:T(4,128)(2,1)S(1)}, u32[]{:S(2)}, u32[]{:S(2)}) %collective-permute-start) | collective-permute-done | bytes 33824 | tf_op jit(solution)/shard_map/ppermute | solution.py:16
  11.8 0.1 pad_maximum_fusion
  11.9 1.6 %collective-permute-start.3 = (bf16[16,4224]{1,0:T(8,128)(2,1)S(1)}, bf16[16,4224]{1,0:T(8,128)(2,1)S(1)}, u32[]{:S(2)}, u32[]{:S(2)}) collective-permute-start(bf16[16,4224]{1,0:T(8,128)(2,1)S(1)} %pad_maximum_fusion), channel_id=1, source_target_pairs={{0,2},{2,0},{1,3},{3,1},{4,6},{6,4},{5,7},{7,5},{8,10},{10,8},{9,1... | collective-permute-start | bytes 405512 | tf_op jit(solution)/shard_map/ppermute | solution.py:16
  13.4 3.5 %collective-permute-done.3 = bf16[16,4224]{1,0:T(8,128)(2,1)S(1)} collective-permute-done((bf16[16,4224]{1,0:T(8,128)(2,1)S(1)}, bf16[16,4224]{1,0:T(8,128)(2,1)S(1)}, u32[]{:S(2)}, u32[]{:S(2)}) %collective-permute-start.3) | collective-permute-done | bytes 135200 | tf_op jit(solution)/shard_map/ppermute | solution.py:16
  16.9 0.2 concatenate.19
  17.1 0.1 collective-permute-start.4
  17.2 1.5 %collective-permute-done.4 = bf16[32,4224]{1,0:T(8,128)(2,1)S(1)} collective-permute-done((bf16[32,4224]{1,0:T(8,128)(2,1)S(1)}, bf16[32,4224]{1,0:T(8,128)(2,1)S(1)}, u32[]{:S(2)}, u32[]{:S(2)}) %collective-permute-start.4) | collective-permute-done | bytes 270368 | tf_op jit(solution)/shard_map/ppermute | solution.py:16
  18.7 3.3 %concatenate.20.rows_ref = bf16[64,4224]{1,0:T(8,128)(2,1)} concatenate(bf16[4,4224]{1,0:T(4,128)(2,1)S(1)} %concatenate.17, bf16[4,4224]{1,0:T(4,128)(2,1)S(1)} %collective-permute-done, bf16[4,4224]{1,0:T(4,128)(2,1)S(1)} %collective-permute-done.1, bf16[4,4224]{1,0:T(4,128)(2,1)S(1)} %collective-permute-done.2, bf16[16,4224]{1,0:T(8,128)(2,1)S(1)} %collective-permute-done.3, ...), dimensions={0} | concatenate | bytes 1081344 | tf_op jit(solution)/shard_map/concatenate | solution.py:20
  22.1 27.2 %expert_layer.1 = f32[64,4096]{1,0:T(8,128)} custom-call(bf16[64,4224]{1,0:T(8,128)(2,1)} %concatenate.20.rows_ref, bf16[3072,4096]{1,0:T(8,128)(2,1)} %bitcast.3, bf16[3072,4096]{1,0:T(8,128)(2,1)} %bitcast.4, bf16[3072,4096]{1,0:T(8,128)(2,1)} %bitcast.5), custom_call_target="tpu_custom_call" | custom-call | flops 4831838208 | bytes 75497472 | tf_op jit(solution)/shard_map/expert_layer/pallas_call | solution.py:135
  49.3 1.1 %slice.64 = bf16[32,4096]{1,0:T(8,128)(2,1)S(1)} slice(f32[64,4096]{1,0:T(8,128)} %expert_layer.1), slice={[32:64], [0:4096]} | slice | bytes 524288 | tf_op jit(solution)/shard_map/slice | solution.py:26
  50.3 0.2 collective-permute-start.5
  50.5 1.4 %collective-permute-done.5 = bf16[32,4096]{1,0:T(8,128)(2,1)S(1)} collective-permute-done((bf16[32,4096]{1,0:T(8,128)(2,1)S(1)}, bf16[32,4096]{1,0:T(8,128)(2,1)S(1)}, u32[]{:S(2)}, u32[]{:S(2)}) %collective-permute-start.5) | collective-permute-done | bytes 262176 | tf_op jit(solution)/shard_map/ppermute | solution.py:16
  51.9 1.1 %slice_add_fusion = f32[32,4096]{1,0:T(8,128)S(1)} fusion(f32[64,4096]{1,0:T(8,128)} %expert_layer.1, bf16[32,4096]{1,0:T(8,128)(2,1)S(1)} %collective-permute-done.5), kind=kLoop, calls=%fused_computation.1 | loop fusion | flops 262144 | bytes 1310720 | tf_op jit(solution)/shard_map/add | solution.py:29
  53.1 1.6 %collective-permute-start.6 = (bf16[16,4096]{1,0:T(8,128)(2,1)S(1)}, bf16[16,4096]{1,0:T(8,128)(2,1)S(1)}, u32[]{:S(2)}, u32[]{:S(2)}) collective-permute-start(bf16[16,4096]{1,0:T(8,128)(2,1)S(1)} %slice.65), channel_id=1, source_target_pairs={{0,2},{2,0},{1,3},{3,1},{4,6},{6,4},{5,7},{7,5},{8,10},{10,8},{9,1... | collective-permute-start | bytes 393224 | tf_op jit(solution)/shard_map/ppermute | solution.py:16
  54.6 4.1 %collective-permute-done.6 = bf16[16,4096]{1,0:T(8,128)(2,1)S(1)} collective-permute-done((bf16[16,4096]{1,0:T(8,128)(2,1)S(1)}, bf16[16,4096]{1,0:T(8,128)(2,1)S(1)}, u32[]{:S(2)}, u32[]{:S(2)}) %collective-permute-start.6) | collective-permute-done | bytes 131104 | tf_op jit(solution)/shard_map/ppermute | solution.py:16
  58.8 0.3 collective-permute-start.7
  59.1 3.6 %collective-permute-start.9 = (bf16[4,4096]{1,0:T(4,128)(2,1)S(1)}, bf16[4,4096]{1,0:T(4,128)(2,1)S(1)}, u32[]{:S(2)}, u32[]{:S(2)}) collective-permute-start(bf16[4,4096]{1,0:T(4,128)(2,1)S(1)} %get-tuple-element.8), channel_id=1, source_target_pairs={{0,12},{4,0},{8,4},{12,8},{1,13},{5,1},{9,5},{13,9},{2,14},{6,2},{... | collective-permute-start | bytes 98312 | tf_op jit(solution)/shard_map/ppermute | solution.py:16
  62.6 0.0 collective-permute-start.8
  62.6 2.1 %collective-permute-done.7 = bf16[4,4096]{1,0:T(4,128)(2,1)S(1)} collective-permute-done((bf16[4,4096]{1,0:T(4,128)(2,1)S(1)}, bf16[4,4096]{1,0:T(4,128)(2,1)S(1)}, u32[]{:S(2)}, u32[]{:S(2)}) %collective-permute-start.7) | collective-permute-done | bytes 32800 | tf_op jit(solution)/shard_map/ppermute | solution.py:16
  64.7 0.0 collective-permute-done.9
  64.7 2.8 %collective-permute-done.8 = bf16[4,4096]{1,0:T(4,128)(2,1)S(1)} collective-permute-done((bf16[4,4096]{1,0:T(4,128)(2,1)S(1)}, bf16[4,4096]{1,0:T(4,128)(2,1)S(1)}, u32[]{:S(2)}, u32[]{:S(2)}) %collective-permute-start.8) | collective-permute-done | bytes 32800 | tf_op jit(solution)/shard_map/ppermute | solution.py:16
  67.4 0.6 fusion.2
  (4 shorter events, 0.1 us)
Async XLA Ops:
  2.2 7.0 %collective-permute-start.2 = (bf16[4,4224]{1,0:T(4,128)(2,1)S(1)}, bf16[4,4224]{1,0:T(4,128)(2,1)S(1)}, u32[]{:S(2)}, u32[]{:S(2)}) collective-permute-start(bf16[4,4224]{1,0:T(4,128)(2,1)S(1)} %concatenate.17), channel_id=1, source_target_pairs={{0,4},{4,8},{8,12},{12,0},{1,5},{5,9},{9,13},{13,1},{2,6},{6,10},{... | collective-permute-start | bytes 101384 | tf_op jit(solution)/shard_map/ppermute | solution.py:16
  5.3 5.2 %collective-permute-start.1 = (bf16[4,4224]{1,0:T(4,128)(2,1)S(1)}, bf16[4,4224]{1,0:T(4,128)(2,1)S(1)}, u32[]{:S(2)}, u32[]{:S(2)}) collective-permute-start(bf16[4,4224]{1,0:T(4,128)(2,1)S(1)} %concatenate.17), channel_id=1, source_target_pairs={{0,8},{4,12},{8,0},{12,4},{1,9},{5,13},{9,1},{13,5},{2,10},{6,14},... | collective-permute-start | bytes 101384 | tf_op jit(solution)/shard_map/ppermute | solution.py:16
  7.8 3.9 %collective-permute-start = (bf16[4,4224]{1,0:T(4,128)(2,1)S(1)}, bf16[4,4224]{1,0:T(4,128)(2,1)S(1)}, u32[]{:S(2)}, u32[]{:S(2)}) collective-permute-start(bf16[4,4224]{1,0:T(4,128)(2,1)S(1)} %concatenate.17), channel_id=1, source_target_pairs={{0,12},{4,0},{8,4},{12,8},{1,13},{5,1},{9,5},{13,9},{2,14},{6,2},{... | collective-permute-start | bytes 101384 | tf_op jit(solution)/shard_map/ppermute | solution.py:16
  11.9 5.1 %collective-permute-start.3 = (bf16[16,4224]{1,0:T(8,128)(2,1)S(1)}, bf16[16,4224]{1,0:T(8,128)(2,1)S(1)}, u32[]{:S(2)}, u32[]{:S(2)}) collective-permute-start(bf16[16,4224]{1,0:T(8,128)(2,1)S(1)} %pad_maximum_fusion), channel_id=1, source_target_pairs={{0,2},{2,0},{1,3},{3,1},{4,6},{6,4},{5,7},{7,5},{8,10},{10,8},{9,1... | collective-permute-start | bytes 405512 | tf_op jit(solution)/shard_map/ppermute | solution.py:16
  17.1 1.6 %collective-permute-start.4 = (bf16[32,4224]{1,0:T(8,128)(2,1)S(1)}, bf16[32,4224]{1,0:T(8,128)(2,1)S(1)}, u32[]{:S(2)}, u32[]{:S(2)}) collective-permute-start(bf16[32,4224]{1,0:T(8,128)(2,1)S(1)} %concatenate.19), channel_id=1, source_target_pairs={{0,1},{1,0},{2,3},{3,2},{4,5},{5,4},{6,7},{7,6},{8,9},{9,8},{10,11... | collective-permute-start | bytes 811016 | tf_op jit(solution)/shard_map/ppermute | solution.py:16
  50.3 1.6 %collective-permute-start.5 = (bf16[32,4096]{1,0:T(8,128)(2,1)S(1)}, bf16[32,4096]{1,0:T(8,128)(2,1)S(1)}, u32[]{:S(2)}, u32[]{:S(2)}) collective-permute-start(bf16[32,4096]{1,0:T(8,128)(2,1)S(1)} %slice.64), channel_id=1, source_target_pairs={{0,1},{1,0},{2,3},{3,2},{4,5},{5,4},{6,7},{7,6},{8,9},{9,8},{10,11... | collective-permute-start | bytes 786440 | tf_op jit(solution)/shard_map/ppermute | solution.py:16
  53.1 5.6 %collective-permute-start.6 = (bf16[16,4096]{1,0:T(8,128)(2,1)S(1)}, bf16[16,4096]{1,0:T(8,128)(2,1)S(1)}, u32[]{:S(2)}, u32[]{:S(2)}) collective-permute-start(bf16[16,4096]{1,0:T(8,128)(2,1)S(1)} %slice.65), channel_id=1, source_target_pairs={{0,2},{2,0},{1,3},{3,1},{4,6},{6,4},{5,7},{7,5},{8,10},{10,8},{9,1... | collective-permute-start | bytes 393224 | tf_op jit(solution)/shard_map/ppermute | solution.py:16
  58.8 5.9 %collective-permute-start.7 = (bf16[4,4096]{1,0:T(4,128)(2,1)S(1)}, bf16[4,4096]{1,0:T(4,128)(2,1)S(1)}, u32[]{:S(2)}, u32[]{:S(2)}) collective-permute-start(bf16[4,4096]{1,0:T(4,128)(2,1)S(1)} %get-tuple-element.7), channel_id=1, source_target_pairs={{0,4},{4,8},{8,12},{12,0},{1,5},{5,9},{9,13},{13,1},{2,6},{6,10},{... | collective-permute-start | bytes 98312 | tf_op jit(solution)/shard_map/ppermute | solution.py:16
  59.1 5.6 %collective-permute-start.9 = (bf16[4,4096]{1,0:T(4,128)(2,1)S(1)}, bf16[4,4096]{1,0:T(4,128)(2,1)S(1)}, u32[]{:S(2)}, u32[]{:S(2)}) collective-permute-start(bf16[4,4096]{1,0:T(4,128)(2,1)S(1)} %get-tuple-element.8), channel_id=1, source_target_pairs={{0,12},{4,0},{8,4},{12,8},{1,13},{5,1},{9,5},{13,9},{2,14},{6,2},{... | collective-permute-start | bytes 98312 | tf_op jit(solution)/shard_map/ppermute | solution.py:16
  62.6 4.8 %collective-permute-start.8 = (bf16[4,4096]{1,0:T(4,128)(2,1)S(1)}, bf16[4,4096]{1,0:T(4,128)(2,1)S(1)}, u32[]{:S(2)}, u32[]{:S(2)}) collective-permute-start(bf16[4,4096]{1,0:T(4,128)(2,1)S(1)} %get-tuple-element.9), channel_id=1, source_target_pairs={{0,8},{4,12},{8,0},{12,4},{1,9},{5,13},{9,1},{13,5},{2,10},{6,14},... | collective-permute-start | bytes 98312 | tf_op jit(solution)/shard_map/ppermute | solution.py:16

commit v4 on v3

v4 whole, which is shorter than its diff:
```python
import functools

import jax
import jax.numpy as jnp
from jax import lax
from jax.experimental import pallas as pl
from jax.experimental.pallas import tpu as pltpu
from jax.sharding import PartitionSpec as P

EXPERTS = 32
SIDE = 128
SLOTS = 3
TILE = 1024
EARLY = (2, 1, 1)
GRANT = 22 << 20


def swap(x, axis, size, by):
    return lax.ppermute(x, axis, [(i, i ^ by) for i in range(size)])


def with_routing(tokens_ref, ids_ref, numer_ref, out_ref):
    rows, depth = tokens_ref.shape
    top = ids_ref.shape[1]
    out_ref[:, :depth] = tokens_ref[...]
    ids, numer = ids_ref[...], numer_ref[...]
    pad = jnp.zeros((rows, SIDE - 3 * top), jnp.int32)
    side = jnp.concatenate([ids, numer >> 5, numer & 31, pad], axis=1)
    out_ref[:, depth:] = side.astype(jnp.float32).astype(jnp.bfloat16)


def dense_weights(side, top):
    ids = side[:, :top]
    numer = side[:, top:2 * top] * 32.0 + side[:, 2 * top:3 * top]
    weight = numer / jnp.sum(numer, axis=-1, keepdims=True)
    lane = lax.broadcasted_iota(jnp.int32, (side.shape[0], SIDE), 1)
    expert = jnp.where(lane < EXPERTS, lane, lane - EXPERTS).astype(jnp.float32)
    full = jnp.zeros((side.shape[0], SIDE), jnp.float32)
    for k in range(top):
        full = full + jnp.where(expert == ids[:, k:k + 1], weight[:, k:k + 1], 0.0)
    high = full.astype(jnp.bfloat16).astype(jnp.float32)
    return jnp.where(lane < EXPERTS, high, full - high).astype(jnp.bfloat16)


def bring(at, gate_ref, up_ref, down_ref, after_ref, gates, ups, downs, end_ref, sem):
    pieces = sem.shape[1]
    size = gates.shape[0] // pieces
    started = []
    for p in range(pieces):
        for i, (ref, held) in enumerate([(gate_ref, gates), (up_ref, ups), (down_ref, downs)]):
            started.append(
                pltpu.make_async_copy(
                    ref.at[pl.ds(at + p * size, size)], held.at[pl.ds(p * size, size)], sem.at[i, p]
                )
            )
    for copy in started:
        copy.start()
    end_ref[...] = jnp.zeros_like(end_ref)
    for copy in started:
        copy.wait()


def layer(top, ff_dev, row_block, step_units, parts, rows_ref, *refs):
    held, refs = refs[:3 * parts], refs[3 * parts:]
    (gate_ref, up_ref, down_ref, out_ref, gates, ups, downs, weights, hidden, sem) = refs
    units, depth = down_ref.shape
    steps = units // step_units
    count = rows_ref.shape[0]
    early = sum(held[3 * p].shape[0] for p in range(parts)) // step_units

    def copies(step, slot):
        span = pl.ds(pl.multiple_of(step * step_units, step_units), step_units)
        return [
            pltpu.make_async_copy(src.at[span], dst.at[slot], sem.at[i, slot])
            for i, (src, dst) in enumerate(
                [(gate_ref, gates), (up_ref, ups), (down_ref, downs)]
            )
        ]

    for step in range(early, min(early + SLOTS - 1, steps)):
        for copy in copies(step, step - early):
            copy.start()

    first = lax.axis_index("wide") * (units // ff_dev)

    def each_block(body):
        if count == row_block:
            body(pl.ds(0, row_block))
        else:
            @pl.loop(0, count // row_block)
            def _(b):
                body(pl.ds(pl.multiple_of(b * row_block, row_block), row_block))

    def prepare(block):
        side = rows_ref[block, depth:depth + SIDE].astype(jnp.float32)
        weights[block, :] = dense_weights(side, top)
        out_ref[block, :] = jnp.zeros((row_block, depth), jnp.float32)

    each_block(prepare)

    def work(step, gate, up, down, ready=None):
        expert = lax.broadcasted_iota(jnp.int32, (SIDE, step_units), 0)
        place = jnp.where(expert < EXPERTS, expert, expert - EXPERTS) - first
        unit = step * step_units + lax.broadcasted_iota(jnp.int32, (SIDE, step_units), 1)
        low = place * ff_dev
        pick = (unit >= low) & (unit < low + ff_dev) & (expert < 2 * EXPERTS)
        pick = jnp.where(pick, 1.0, 0.0).astype(jnp.bfloat16)
        if ready is not None:
            ready[0].wait()
            ready[1].wait()

        def first_half(block):
            def add(c, sums):
                cols = pl.ds(pl.multiple_of(c * TILE, TILE), TILE)
                x = rows_ref[block, cols]
                last = (((1,), (1,)), ((), ()))
                return tuple(
                    total + lax.dot_general(x, w[:, cols], last, preferred_element_type=jnp.float32)
                    for total, w in zip(sums, (gate, up))
                )

            zero = jnp.zeros((row_block, step_units), jnp.float32)
            g, u = lax.fori_loop(0, depth // TILE, add, (zero, zero))
            scale = jnp.dot(weights[block, :], pick, preferred_element_type=jnp.float32)
            hidden[block, :] = (g / (1.0 + jnp.exp(-g)) * u * scale).astype(jnp.bfloat16)

        each_block(first_half)
        if ready is not None:
            ready[2].wait()

        def second_half(block):
            h = hidden[block, :]

            @pl.loop(0, depth // TILE)
            def _(c):
                cols = pl.ds(pl.multiple_of(c * TILE, TILE), TILE)
                out_ref[block, cols] += jnp.dot(h, down[:, cols], preferred_element_type=jnp.float32)

        each_block(second_half)

    done = 0
    for p in range(parts):
        inside = held[3 * p].shape[0] // step_units

        @pl.loop(0, inside)
        def _(s):
            span = pl.ds(pl.multiple_of(s * step_units, step_units), step_units)
            work(done + s, *[ref.at[span] for ref in held[3 * p:3 * p + 3]])

        done += inside

    @pl.loop(early, steps)
    def _(step):
        slot = lax.rem(step - early, SLOTS)

        @pl.when(step + SLOTS - 1 < steps)
        def _():
            for copy in copies(step + SLOTS - 1, lax.rem(step - early + SLOTS - 1, SLOTS)):
                copy.start()

        work(step, gates.at[slot], ups.at[slot], downs.at[slot], copies(step, slot))


def build(axes):
    def local(tokens, expert_ids, gate_numer, w_gate, w_up, w_down):
        local_count, ff_dev, depth = w_gate.shape
        units = local_count * ff_dev
        step_units = next(n for n in range(256, 0, -16) if units % n == 0)
        weights = [w.reshape(units, depth) for w in (w_gate, w_up, w_down)]
        weights = [pltpu.with_memory_space_constraint(w, pltpu.HBM) for w in weights]
        rows = pl.pallas_call(
            with_routing,
            out_shape=jax.ShapeDtypeStruct((tokens.shape[0], depth + SIDE), jnp.bfloat16),
            in_specs=[pl.BlockSpec(memory_space=pltpu.VMEM)] * 3,
            out_specs=pl.BlockSpec(memory_space=pltpu.VMEM),
            compiler_params=pltpu.CompilerParams(vmem_limit_bytes=2 << 20),
            name="with_routing",
        )(tokens, expert_ids, gate_numer)
        hops = []
        for axis, size in axes:
            by = size // 2
            while by:
                hops.append((axis, size, by))
                by //= 2
        held = []
        at = 0
        for number, hop in enumerate(hops):
            theirs = swap(rows, *hop)
            steps = EARLY[number] if number < len(EARLY) and units >= 8 * step_units else 0
            if steps:
                span = steps * step_units
                *brought, end = pl.pallas_call(
                    functools.partial(bring, at),
                    out_shape=[pltpu.VMEM((span, depth), jnp.bfloat16)] * 3
                    + [jax.ShapeDtypeStruct((8, 128), jnp.float32)],
                    in_specs=[pl.BlockSpec(memory_space=pltpu.HBM)] * 3
                    + [pl.BlockSpec(memory_space=pl.ANY)],
                    out_specs=[pl.BlockSpec(memory_space=pltpu.VMEM)] * 4,
                    scratch_shapes=[pltpu.SemaphoreType.DMA((3, 2 * steps))],
                    compiler_params=pltpu.CompilerParams(vmem_limit_bytes=1 << 20),
                    cost_estimate=pl.CostEstimate(
                        flops=0, bytes_accessed=6 * span * depth, transcendentals=0
                    ),
                    name="bring_weights",
                )(*weights, rows)
                held += brought
                at += span
                theirs = theirs + end[0, 0].astype(jnp.bfloat16)
            rows = jnp.concatenate([rows, theirs], axis=0)
        count = rows.shape[0]
        total = pl.pallas_call(
            functools.partial(
                layer, expert_ids.shape[1], ff_dev, min(count, 64), step_units, len(held) // 3
            ),
            out_shape=jax.ShapeDtypeStruct((count, depth), jnp.float32),
            in_specs=[pl.BlockSpec(memory_space=pltpu.VMEM)] * (1 + len(held))
            + [pl.BlockSpec(memory_space=pltpu.HBM)] * 3,
            out_specs=pl.BlockSpec(memory_space=pltpu.VMEM),
            scratch_shapes=[pltpu.VMEM((SLOTS, step_units, depth), jnp.bfloat16)] * 3
            + [
                pltpu.VMEM((count, SIDE), jnp.bfloat16),
                pltpu.VMEM((count, step_units), jnp.bfloat16),
                pltpu.SemaphoreType.DMA((3, SLOTS)),
            ],
            compiler_params=pltpu.CompilerParams(vmem_limit_bytes=GRANT),
            cost_estimate=pl.CostEstimate(
                flops=6 * count * units * depth,
                bytes_accessed=6 * units * depth,
                transcendentals=count * units,
            ),
            name="expert_layer",
        )(rows, *held, *weights)
        for hop in reversed(hops):
            half = total.shape[0] // 2
            theirs = swap(total[half:].astype(jnp.bfloat16), *hop)
            total = total[:half] + theirs.astype(jnp.float32)
        return total.astype(jnp.bfloat16)

    return local


def solution(mesh):
    rows = P(("grp", "wide", "sec", "sub"), None)
    weights = P("wide", ("sec", "sub"), None)
    axes = [(name, mesh.shape[name]) for name in ("wide", "sec", "sub")]
    return jax.shard_map(
        build(axes),
        mesh=mesh,
        in_specs=(rows, rows, rows, weights, weights, weights),
        out_specs=rows,
        check_vma=False,
    )
```

time: 68.5 us -> 104 us (1.52)
  local copies, waits for them, and re-layouts: 5.5 us -> 31.1 us
  Pallas kernels: 27.2 us -> 44.3 us
  starting transfers between devices: 14.2 us -> 9.03 us
  waiting for transfers between devices: 17.9 us -> 16.5 us
    unnamed x0 -> x38, local copies, waits for them, and re-layouts: none -> 29.2 us
    pallas_call x0 -> x4, Pallas kernels: none -> 10.5 us  [the longest x3 10.4 us: local(): pl.pallas_call(functools.partial(bring, at), out_shape=[pltpu.VMEM((span,...]
    pallas_call x1, Pallas kernels: 27.2 us -> 33.9 us  [local(): pl.pallas_call(functools.partial(layer, expert_ids.shape[1], ff_dev, min(...]
    ppermute x10 -> x8, starting transfers between devices: 14.2 us -> 9.03 us  [swap(): return lax.ppermute(x, axis, [(i, i ^ by) for i in range(size)])]
    concatenate x3 -> x1, local copies, waits for them, and re-layouts: 4.37 us -> 0.27 us  [local(): rows = jnp.concatenate([rows, theirs], axis=0)]
    ppermute x10 -> x8, waiting for transfers between devices: 17.9 us -> 16.5 us  [swap(): return lax.ppermute(x, axis, [(i, i ^ by) for i in range(size)])]
    another operation x3, other arithmetic: 1.4 us -> 0.01 us
  transfers between devices with their start and end apart: 10 -> 8, of which waited for: 8 -> 5; matrix products, arithmetic and copies ran while one was open for 0% -> 1% of each run, Pallas kernels for 0% -> 10%
where the time goes in v4:
time: 104 us
  Pallas kernels  44.3 us (43%)
  local copies, waits for them, and re-layouts  31.1 us (30%)
  waiting for transfers between devices  16.5 us (16%)
  starting transfers between devices  9.03 us (9%)
  other arithmetic  2.88 us (3%)
    pallas_call x1, Pallas kernels, local(): pl.pallas_call(functools.partial(layer, expert_ids.shape[1], ff_dev, min(...  33.9 us
    unnamed x38, local copies, waits for them, and re-layouts  29.2 us
    ppermute x8, waiting for transfers between devices, swap(): return lax.ppermute(x, axis, [(i, i ^ by) for i in range(size)])  16.5 us
    pallas_call x3, Pallas kernels, local(): pl.pallas_call(functools.partial(bring, at), out_shape=[pltpu.VMEM((span,...  10.4 us
    ppermute x8, starting transfers between devices, swap(): return lax.ppermute(x, axis, [(i, i ^ by) for i in range(size)])  9.03 us
  transfers between devices with their start and end apart: 8, of which 5 were waited for; matrix products, arithmetic and copies ran while one was open for 1% of the time, Pallas kernels for 10%

profile of v4, /device:TPU:0, one launch (start us, length us, event | category | flops | bytes accessed | tf_op | source)
XLA Modules:
  0.0 104.0 jit_solution(9168542725142641522)
XLA Ops:
  0.0 0.8 copy-done.16
  0.8 0.7 copy-done.17
  1.4 0.7 copy-done.18
  2.1 0.1 with_routing.1.after_ref
  2.2 4.0 %collective-permute-start = (bf16[4,4224]{1,0:T(4,128)(2,1)S(1)}, bf16[4,4224]{1,0:T(4,128)(2,1)S(1)}, u32[]{:S(2)}, u32[]{:S(2)}) collective-permute-start(bf16[4,4224]{1,0:T(4,128)(2,1)S(1)} %with_routing.1.after_ref), channel_id=1, source_target_pairs={{0,8},{4,12},{8,0},{12,4},{1,9},{5,13},{9,1},{13,5},{2,10},{6,14},... | collective-permute-start | bytes 101384 | tf_op jit(solution)/shard_map/ppermute | solution.py:19
  6.2 4.7 %bring_weights.3 = (bf16[512,4096]{1,0:T(8,128)(2,1)S(1)}, bf16[512,4096]{1,0:T(8,128)(2,1)S(1)}, bf16[512,4096]{1,0:T(8,128)(2,1)S(1)}, f32[8,128]{1,0:T(8,128)S(1)}) custom-call(bf16[3072,4096]{1,0:T(8,128)(2,1)} %bitcast.6, bf16[3072,4096]{1,0:T(8,128)(2,1)} %bitcast.10, bf16[3072,4096]{1,0:T(8,128)(2,1)} %bitcast.14, ...), custom_call_target="tpu_custom_call" | custom-call | bytes 12582912 | tf_op jit(solution)/shard_map/bring_weights/pallas_call | solution.py:192
  11.0 1.9 %copy-done = bf16[512,4096]{1,0:T(8,128)(2,1)} copy-done((bf16[512,4096]{1,0:T(8,128)(2,1)}, bf16[512,4096]{1,0:T(8,128)(2,1)S(1)}, u32[]{:S(2)}) %copy-start) | copy-done | bytes 4194328
  12.9 2.0 %copy-done.2 = bf16[512,4096]{1,0:T(8,128)(2,1)} copy-done((bf16[512,4096]{1,0:T(8,128)(2,1)}, bf16[512,4096]{1,0:T(8,128)(2,1)S(1)}, u32[]{:S(2)}) %copy-start.2) | copy-done | bytes 4194328
  14.9 2.0 %copy-done.4 = bf16[512,4096]{1,0:T(8,128)(2,1)} copy-done((bf16[512,4096]{1,0:T(8,128)(2,1)}, bf16[512,4096]{1,0:T(8,128)(2,1)S(1)}, u32[]{:S(2)}) %copy-start.4) | copy-done | bytes 4194328
  16.9 0.5 slice.40
  17.4 0.7 broadcast_add_fusion.2
  18.2 1.6 %collective-permute-start.1 = (bf16[8,4224]{1,0:T(8,128)(2,1)S(1)}, bf16[8,4224]{1,0:T(8,128)(2,1)S(1)}, u32[]{:S(2)}, u32[]{:S(2)}) collective-permute-start(bf16[8,4224]{1,0:T(8,128)(2,1)S(1)} %pad_maximum_fusion.2.after_ref), channel_id=1, source_target_pairs={{0,4},{4,0},{8,12},{12,8},{1,5},{5,1},{9,13},{13,9},{2,6},{6,2},{1... | collective-permute-start | bytes 202760 | tf_op jit(solution)/shard_map/ppermute | solution.py:19
  19.8 2.9 %bring_weights.4 = (bf16[256,4096]{1,0:T(8,128)(2,1)S(1)}, bf16[256,4096]{1,0:T(8,128)(2,1)S(1)}, bf16[256,4096]{1,0:T(8,128)(2,1)S(1)}, f32[8,128]{1,0:T(8,128)S(1)}) custom-call(bf16[3072,4096]{1,0:T(8,128)(2,1)} %bitcast.7, bf16[3072,4096]{1,0:T(8,128)(2,1)} %bitcast.11, bf16[3072,4096]{1,0:T(8,128)(2,1)} %bitcast.15, ...), custom_call_target="tpu_custom_call" | custom-call | bytes 6291456 | tf_op jit(solution)/shard_map/bring_weights/pallas_call | solution.py:192
  22.7 1.3 %copy-done.6 = bf16[256,4096]{1,0:T(8,128)(2,1)} copy-done((bf16[256,4096]{1,0:T(8,128)(2,1)}, bf16[256,4096]{1,0:T(8,128)(2,1)S(1)}, u32[]{:S(2)}) %copy-start.6) | copy-done | bytes 2097176
  24.0 1.3 %copy-done.8 = bf16[256,4096]{1,0:T(8,128)(2,1)} copy-done((bf16[256,4096]{1,0:T(8,128)(2,1)}, bf16[256,4096]{1,0:T(8,128)(2,1)S(1)}, u32[]{:S(2)}) %copy-start.8) | copy-done | bytes 2097176
  25.3 0.5 slice.41
  25.8 0.7 broadcast_add_fusion.1
  26.5 0.1 pad_maximum_fusion.1.after_ref
  26.5 1.6 %collective-permute-start.2 = (bf16[16,4224]{1,0:T(8,128)(2,1)S(1)}, bf16[16,4224]{1,0:T(8,128)(2,1)S(1)}, u32[]{:S(2)}, u32[]{:S(2)}) collective-permute-start(bf16[16,4224]{1,0:T(8,128)(2,1)S(1)} %pad_maximum_fusion.1.after_ref), channel_id=1, source_target_pairs={{0,2},{2,0},{1,3},{3,1},{4,6},{6,4},{5,7},{7,5},{8,10},{10,8},{9,1... | collective-permute-start | bytes 405512 | tf_op jit(solution)/shard_map/ppermute | solution.py:19
  28.1 2.9 %bring_weights.5 = (bf16[256,4096]{1,0:T(8,128)(2,1)S(1)}, bf16[256,4096]{1,0:T(8,128)(2,1)S(1)}, bf16[256,4096]{1,0:T(8,128)(2,1)S(1)}, f32[8,128]{1,0:T(8,128)S(1)}) custom-call(bf16[3072,4096]{1,0:T(8,128)(2,1)} %bitcast.8, bf16[3072,4096]{1,0:T(8,128)(2,1)} %bitcast.12, bf16[3072,4096]{1,0:T(8,128)(2,1)} %bitcast.16, ...), custom_call_target="tpu_custom_call" | custom-call | bytes 6291456 | tf_op jit(solution)/shard_map/bring_weights/pallas_call | solution.py:192
  30.9 1.3 %copy-done.10 = bf16[256,4096]{1,0:T(8,128)(2,1)} copy-done((bf16[256,4096]{1,0:T(8,128)(2,1)}, bf16[256,4096]{1,0:T(8,128)(2,1)S(1)}, u32[]{:S(2)}) %copy-start.10) | copy-done | bytes 2097176
  32.3 1.3 %copy-done.12 = bf16[256,4096]{1,0:T(8,128)(2,1)} copy-done((bf16[256,4096]{1,0:T(8,128)(2,1)}, bf16[256,4096]{1,0:T(8,128)(2,1)S(1)}, u32[]{:S(2)}) %copy-start.12) | copy-done | bytes 2097176
  33.6 1.4 %copy-done.14 = bf16[256,4096]{1,0:T(8,128)(2,1)} copy-done((bf16[256,4096]{1,0:T(8,128)(2,1)}, bf16[256,4096]{1,0:T(8,128)(2,1)S(1)}, u32[]{:S(2)}) %copy-start.14) | copy-done | bytes 2097176
  34.9 0.5 slice.42
  35.5 0.7 broadcast_add_fusion
  36.1 0.1 pad_maximum_fusion
  36.2 0.1 collective-permute-start.3
  36.3 1.5 %collective-permute-done.3 = bf16[32,4224]{1,0:T(8,128)(2,1)S(1)} collective-permute-done((bf16[32,4224]{1,0:T(8,128)(2,1)S(1)}, bf16[32,4224]{1,0:T(8,128)(2,1)S(1)}, u32[]{:S(2)}, u32[]{:S(2)}) %collective-permute-start.3) | collective-permute-done | bytes 270368 | tf_op jit(solution)/shard_map/ppermute | solution.py:19
  37.8 0.3 concatenate.18.rows_ref
  38.1 2.2 %copy-done.1 = bf16[512,4096]{1,0:T(8,128)(2,1)S(1)} copy-done((bf16[512,4096]{1,0:T(8,128)(2,1)S(1)}, bf16[512,4096]{1,0:T(8,128)(2,1)}, u32[]{:S(2)}) %copy-start.1) | copy-done | bytes 4194328
  40.3 2.2 %copy-done.3 = bf16[512,4096]{1,0:T(8,128)(2,1)S(1)} copy-done((bf16[512,4096]{1,0:T(8,128)(2,1)S(1)}, bf16[512,4096]{1,0:T(8,128)(2,1)}, u32[]{:S(2)}) %copy-start.3) | copy-done | bytes 4194328
  42.5 2.2 %copy-done.5 = bf16[512,4096]{1,0:T(8,128)(2,1)S(1)} copy-done((bf16[512,4096]{1,0:T(8,128)(2,1)S(1)}, bf16[512,4096]{1,0:T(8,128)(2,1)}, u32[]{:S(2)}) %copy-start.5) | copy-done | bytes 4194328
  44.7 1.6 %copy-done.7 = bf16[256,4096]{1,0:T(8,128)(2,1)S(1)} copy-done((bf16[256,4096]{1,0:T(8,128)(2,1)S(1)}, bf16[256,4096]{1,0:T(8,128)(2,1)}, u32[]{:S(2)}) %copy-start.7) | copy-done | bytes 2097176
  46.3 1.6 %copy-done.9 = bf16[256,4096]{1,0:T(8,128)(2,1)S(1)} copy-done((bf16[256,4096]{1,0:T(8,128)(2,1)S(1)}, bf16[256,4096]{1,0:T(8,128)(2,1)}, u32[]{:S(2)}) %copy-start.9) | copy-done | bytes 2097176
  47.8 1.6 %copy-done.11 = bf16[256,4096]{1,0:T(8,128)(2,1)S(1)} copy-done((bf16[256,4096]{1,0:T(8,128)(2,1)S(1)}, bf16[256,4096]{1,0:T(8,128)(2,1)}, u32[]{:S(2)}) %copy-start.11) | copy-done | bytes 2097176
  49.4 1.6 %copy-done.13 = bf16[256,4096]{1,0:T(8,128)(2,1)S(1)} copy-done((bf16[256,4096]{1,0:T(8,128)(2,1)S(1)}, bf16[256,4096]{1,0:T(8,128)(2,1)}, u32[]{:S(2)}) %copy-start.13) | copy-done | bytes 2097176
  51.0 1.6 %copy-done.15 = bf16[256,4096]{1,0:T(8,128)(2,1)S(1)} copy-done((bf16[256,4096]{1,0:T(8,128)(2,1)S(1)}, bf16[256,4096]{1,0:T(8,128)(2,1)}, u32[]{:S(2)}) %copy-start.15) | copy-done | bytes 2097176
  52.6 33.9 %expert_layer.1 = f32[64,4096]{1,0:T(8,128)S(1)} custom-call(bf16[64,4224]{1,0:T(8,128)(2,1)S(1)} %concatenate.18.rows_ref, bf16[512,4096]{1,0:T(8,128)(2,1)S(1)} %copy-done.1, bf16[512,4096]{1,0:T(8,128)(2,1)S(1)} %copy-done.3, bf16[512,4096]{1,0:T(8,128)(2,1)S(1)} %copy-done.5, bf16[256,4096]{1,0:T(8,128)(2,1)S(1)} %get-tuple-element.23.refs_3_, ...), custom_call_target="tpu_custom_call" | custom-call | flops 4831838208 | bytes 75497472 | tf_op jit(solution)/shard_map/expert_layer/pallas_call | solution.py:211
  86.5 0.2 collective-permute-start.4
  86.7 1.4 %collective-permute-done.4 = bf16[32,4096]{1,0:T(8,128)(2,1)S(1)} collective-permute-done((bf16[32,4096]{1,0:T(8,128)(2,1)S(1)}, bf16[32,4096]{1,0:T(8,128)(2,1)S(1)}, u32[]{:S(2)}, u32[]{:S(2)}) %collective-permute-start.4) | collective-permute-done | bytes 262176 | tf_op jit(solution)/shard_map/ppermute | solution.py:19
  88.1 0.1 slice_add_fusion
  88.2 0.6 collective-permute-start.5
  88.8 5.0 %collective-permute-done.5 = bf16[16,4096]{1,0:T(8,128)(2,1)S(1)} collective-permute-done((bf16[16,4096]{1,0:T(8,128)(2,1)S(1)}, bf16[16,4096]{1,0:T(8,128)(2,1)S(1)}, u32[]{:S(2)}, u32[]{:S(2)}) %collective-permute-start.5) | collective-permute-done | bytes 131104 | tf_op jit(solution)/shard_map/ppermute | solution.py:19
  93.9 0.5 collective-permute-start.6
  94.4 3.8 %collective-permute-done.6 = bf16[8,4096]{1,0:T(8,128)(2,1)S(1)} collective-permute-done((bf16[8,4096]{1,0:T(8,128)(2,1)S(1)}, bf16[8,4096]{1,0:T(8,128)(2,1)S(1)}, u32[]{:S(2)}, u32[]{:S(2)}) %collective-permute-start.6) | collective-permute-done | bytes 65568 | tf_op jit(solution)/shard_map/ppermute | solution.py:19
  98.2 0.4 collective-permute-start.7
  98.6 4.7 %collective-permute-done.7 = bf16[4,4096]{1,0:T(4,128)(2,1)S(1)} collective-permute-done((bf16[4,4096]{1,0:T(4,128)(2,1)S(1)}, bf16[4,4096]{1,0:T(4,128)(2,1)S(1)}, u32[]{:S(2)}, u32[]{:S(2)}) %collective-permute-start.7) | collective-permute-done | bytes 32800 | tf_op jit(solution)/shard_map/ppermute | solution.py:19
  103.3 0.6 fusion
  (32 shorter events, 0.2 us)
Async XLA Ops:
  0.0 0.8 copy-start.16
  0.8 0.7 copy-start.17
  1.4 0.7 copy-start.18
  2.2 15.2 %collective-permute-start = (bf16[4,4224]{1,0:T(4,128)(2,1)S(1)}, bf16[4,4224]{1,0:T(4,128)(2,1)S(1)}, u32[]{:S(2)}, u32[]{:S(2)}) collective-permute-start(bf16[4,4224]{1,0:T(4,128)(2,1)S(1)} %with_routing.1.after_ref), channel_id=1, source_target_pairs={{0,8},{4,12},{8,0},{12,4},{1,9},{5,13},{9,1},{13,5},{2,10},{6,14},... | collective-permute-start | bytes 101384 | tf_op jit(solution)/shard_map/ppermute | solution.py:19
  10.9 2.0 %copy-start = (bf16[512,4096]{1,0:T(8,128)(2,1)}, bf16[512,4096]{1,0:T(8,128)(2,1)S(1)}, u32[]{:S(2)}) copy-start(bf16[512,4096]{1,0:T(8,128)(2,1)S(1)} %get-tuple-element.20.refs_0_) | copy-start | bytes 12582916
  12.9 2.0 %copy-start.2 = (bf16[512,4096]{1,0:T(8,128)(2,1)}, bf16[512,4096]{1,0:T(8,128)(2,1)S(1)}, u32[]{:S(2)}) copy-start(bf16[512,4096]{1,0:T(8,128)(2,1)S(1)} %get-tuple-element.21.refs_1_) | copy-start | bytes 12582916
  14.9 2.0 %copy-start.4 = (bf16[512,4096]{1,0:T(8,128)(2,1)}, bf16[512,4096]{1,0:T(8,128)(2,1)S(1)}, u32[]{:S(2)}) copy-start(bf16[512,4096]{1,0:T(8,128)(2,1)S(1)} %get-tuple-element.22.refs_2_) | copy-start | bytes 12582916
  18.2 7.6 %collective-permute-start.1 = (bf16[8,4224]{1,0:T(8,128)(2,1)S(1)}, bf16[8,4224]{1,0:T(8,128)(2,1)S(1)}, u32[]{:S(2)}, u32[]{:S(2)}) collective-permute-start(bf16[8,4224]{1,0:T(8,128)(2,1)S(1)} %pad_maximum_fusion.2.after_ref), channel_id=1, source_target_pairs={{0,4},{4,0},{8,12},{12,8},{1,5},{5,1},{9,13},{13,9},{2,6},{6,2},{1... | collective-permute-start | bytes 202760 | tf_op jit(solution)/shard_map/ppermute | solution.py:19
  22.7 1.3 %copy-start.6 = (bf16[256,4096]{1,0:T(8,128)(2,1)}, bf16[256,4096]{1,0:T(8,128)(2,1)S(1)}, u32[]{:S(2)}) copy-start(bf16[256,4096]{1,0:T(8,128)(2,1)S(1)} %get-tuple-element.24.refs_4_) | copy-start | bytes 6291460
  24.0 1.3 %copy-start.8 = (bf16[256,4096]{1,0:T(8,128)(2,1)}, bf16[256,4096]{1,0:T(8,128)(2,1)S(1)}, u32[]{:S(2)}) copy-start(bf16[256,4096]{1,0:T(8,128)(2,1)S(1)} %get-tuple-element.25.refs_5_) | copy-start | bytes 6291460
  26.5 8.9 %collective-permute-start.2 = (bf16[16,4224]{1,0:T(8,128)(2,1)S(1)}, bf16[16,4224]{1,0:T(8,128)(2,1)S(1)}, u32[]{:S(2)}, u32[]{:S(2)}) collective-permute-start(bf16[16,4224]{1,0:T(8,128)(2,1)S(1)} %pad_maximum_fusion.1.after_ref), channel_id=1, source_target_pairs={{0,2},{2,0},{1,3},{3,1},{4,6},{6,4},{5,7},{7,5},{8,10},{10,8},{9,1... | collective-permute-start | bytes 405512 | tf_op jit(solution)/shard_map/ppermute | solution.py:19
  30.9 1.3 %copy-start.10 = (bf16[256,4096]{1,0:T(8,128)(2,1)}, bf16[256,4096]{1,0:T(8,128)(2,1)S(1)}, u32[]{:S(2)}) copy-start(bf16[256,4096]{1,0:T(8,128)(2,1)S(1)} %get-tuple-element.26.refs_6_) | copy-start | bytes 6291460
  32.3 1.3 %copy-start.12 = (bf16[256,4096]{1,0:T(8,128)(2,1)}, bf16[256,4096]{1,0:T(8,128)(2,1)S(1)}, u32[]{:S(2)}) copy-start(bf16[256,4096]{1,0:T(8,128)(2,1)S(1)} %get-tuple-element.27.refs_7_) | copy-start | bytes 6291460
  33.6 1.4 %copy-start.14 = (bf16[256,4096]{1,0:T(8,128)(2,1)}, bf16[256,4096]{1,0:T(8,128)(2,1)S(1)}, u32[]{:S(2)}) copy-start(bf16[256,4096]{1,0:T(8,128)(2,1)S(1)} %get-tuple-element.28.refs_8_) | copy-start | bytes 6291460
  36.2 1.6 %collective-permute-start.3 = (bf16[32,4224]{1,0:T(8,128)(2,1)S(1)}, bf16[32,4224]{1,0:T(8,128)(2,1)S(1)}, u32[]{:S(2)}, u32[]{:S(2)}) collective-permute-start(bf16[32,4224]{1,0:T(8,128)(2,1)S(1)} %pad_maximum_fusion), channel_id=1, source_target_pairs={{0,1},{1,0},{2,3},{3,2},{4,5},{5,4},{6,7},{7,6},{8,9},{9,8},{10,11... | collective-permute-start | bytes 811016 | tf_op jit(solution)/shard_map/ppermute | solution.py:19
  38.1 2.2 %copy-start.1 = (bf16[512,4096]{1,0:T(8,128)(2,1)S(1)}, bf16[512,4096]{1,0:T(8,128)(2,1)}, u32[]{:S(2)}) copy-start(bf16[512,4096]{1,0:T(8,128)(2,1)} %copy-done) | copy-start | bytes 12582916
  40.3 2.2 %copy-start.3 = (bf16[512,4096]{1,0:T(8,128)(2,1)S(1)}, bf16[512,4096]{1,0:T(8,128)(2,1)}, u32[]{:S(2)}) copy-start(bf16[512,4096]{1,0:T(8,128)(2,1)} %copy-done.2) | copy-start | bytes 12582916
  42.5 2.2 %copy-start.5 = (bf16[512,4096]{1,0:T(8,128)(2,1)S(1)}, bf16[512,4096]{1,0:T(8,128)(2,1)}, u32[]{:S(2)}) copy-start(bf16[512,4096]{1,0:T(8,128)(2,1)} %copy-done.4) | copy-start | bytes 12582916
  44.7 1.6 %copy-start.7 = (bf16[256,4096]{1,0:T(8,128)(2,1)S(1)}, bf16[256,4096]{1,0:T(8,128)(2,1)}, u32[]{:S(2)}) copy-start(bf16[256,4096]{1,0:T(8,128)(2,1)} %copy-done.6) | copy-start | bytes 6291460
  46.3 1.6 %copy-start.9 = (bf16[256,4096]{1,0:T(8,128)(2,1)S(1)}, bf16[256,4096]{1,0:T(8,128)(2,1)}, u32[]{:S(2)}) copy-start(bf16[256,4096]{1,0:T(8,128)(2,1)} %copy-done.8) | copy-start | bytes 6291460
  47.8 1.6 %copy-start.11 = (bf16[256,4096]{1,0:T(8,128)(2,1)S(1)}, bf16[256,4096]{1,0:T(8,128)(2,1)}, u32[]{:S(2)}) copy-start(bf16[256,4096]{1,0:T(8,128)(2,1)} %copy-done.10) | copy-start | bytes 6291460
  49.4 1.6 %copy-start.13 = (bf16[256,4096]{1,0:T(8,128)(2,1)S(1)}, bf16[256,4096]{1,0:T(8,128)(2,1)}, u32[]{:S(2)}) copy-start(bf16[256,4096]{1,0:T(8,128)(2,1)} %copy-done.12) | copy-start | bytes 6291460
  51.0 1.6 %copy-start.15 = (bf16[256,4096]{1,0:T(8,128)(2,1)S(1)}, bf16[256,4096]{1,0:T(8,128)(2,1)}, u32[]{:S(2)}) copy-start(bf16[256,4096]{1,0:T(8,128)(2,1)} %copy-done.14) | copy-start | bytes 6291460
  86.5 1.6 %collective-permute-start.4 = (bf16[32,4096]{1,0:T(8,128)(2,1)S(1)}, bf16[32,4096]{1,0:T(8,128)(2,1)S(1)}, u32[]{:S(2)}, u32[]{:S(2)}) collective-permute-start(bf16[32,4096]{1,0:T(8,128)(2,1)S(1)} %slice.69), channel_id=1, source_target_pairs={{0,1},{1,0},{2,3},{3,2},{4,5},{5,4},{6,7},{7,6},{8,9},{9,8},{10,11... | collective-permute-start | bytes 786440 | tf_op jit(solution)/shard_map/ppermute | solution.py:19
  88.2 5.6 %collective-permute-start.5 = (bf16[16,4096]{1,0:T(8,128)(2,1)S(1)}, bf16[16,4096]{1,0:T(8,128)(2,1)S(1)}, u32[]{:S(2)}, u32[]{:S(2)}) collective-permute-start(bf16[16,4096]{1,0:T(8,128)(2,1)S(1)} %slice.70), channel_id=1, source_target_pairs={{0,2},{2,0},{1,3},{3,1},{4,6},{6,4},{5,7},{7,5},{8,10},{10,8},{9,1... | collective-permute-start | bytes 393224 | tf_op jit(solution)/shard_map/ppermute | solution.py:19
  93.9 4.3 %collective-permute-start.6 = (bf16[8,4096]{1,0:T(8,128)(2,1)S(1)}, bf16[8,4096]{1,0:T(8,128)(2,1)S(1)}, u32[]{:S(2)}, u32[]{:S(2)}) collective-permute-start(bf16[8,4096]{1,0:T(8,128)(2,1)S(1)} %slice.71), channel_id=1, source_target_pairs={{0,4},{4,0},{8,12},{12,8},{1,5},{5,1},{9,13},{13,9},{2,6},{6,2},{1... | collective-permute-start | bytes 196616 | tf_op jit(solution)/shard_map/ppermute | solution.py:19
  98.2 5.1 %collective-permute-start.7 = (bf16[4,4096]{1,0:T(4,128)(2,1)S(1)}, bf16[4,4096]{1,0:T(4,128)(2,1)S(1)}, u32[]{:S(2)}, u32[]{:S(2)}) collective-permute-start(bf16[4,4096]{1,0:T(4,128)(2,1)S(1)} %slice.72), channel_id=1, source_target_pairs={{0,8},{4,12},{8,0},{12,4},{1,9},{5,13},{9,1},{13,5},{2,10},{6,14},... | collective-permute-start | bytes 98312 | tf_op jit(solution)/shard_map/ppermute | solution.py:19

commit v5 on v4

v5 whole, which is shorter than its diff:
```python
import functools

import jax
import jax.numpy as jnp
from jax import lax
from jax.experimental import pallas as pl
from jax.experimental.pallas import tpu as pltpu
from jax.sharding import PartitionSpec as P

EXPERTS = 32
SIDE = 128
SLOTS = 2
EARLY = (2, 2, 1)
GRANT = 19 << 20

VMEM = pl.BlockSpec(memory_space=pltpu.VMEM)
HBM = pl.BlockSpec(memory_space=pltpu.HBM)
LAST = (((1,), (1,)), ((), ()))


def swap(x, axis, size, by):
    return lax.ppermute(x, axis, [(i, i ^ by) for i in range(size)])


def with_routing(tokens_ref, ids_ref, numer_ref, out_ref, ids, numer, sem):
    rows, depth = tokens_ref.shape
    top = ids_ref.shape[1]
    pairs = [(tokens_ref, out_ref.at[:, pl.ds(0, depth)]), (ids_ref, ids), (numer_ref, numer)]
    started = [pltpu.make_async_copy(a, b, sem.at[i]) for i, (a, b) in enumerate(pairs)]
    for copy in started:
        copy.start()
    for copy in started:
        copy.wait()
    pad = jnp.zeros((rows, SIDE - 3 * top), jnp.int32)
    side = jnp.concatenate([ids[...], numer[...] >> 5, numer[...] & 31, pad], axis=1)
    out_ref[:, depth:] = side.astype(jnp.float32).astype(jnp.bfloat16)


def join(mine_ref, theirs_ref, *refs):
    out_ref = refs[-1]
    count = mine_ref.shape[0]
    out_ref[:count, :] = mine_ref[...]
    out_ref[count:, :] = theirs_ref[...]


def bring(at, gate_ref, up_ref, down_ref, after_ref, gates, ups, downs, end_ref, sem):
    pieces = sem.shape[1]
    size = gates.shape[0] // pieces
    started = []
    for p in range(pieces):
        for i, (ref, held) in enumerate([(gate_ref, gates), (up_ref, ups), (down_ref, downs)]):
            started.append(
                pltpu.make_async_copy(
                    ref.at[pl.ds(at + p * size, size)], held.at[pl.ds(p * size, size)], sem.at[i, p]
                )
            )
    for copy in started:
        copy.start()
    end_ref[...] = jnp.zeros_like(end_ref)
    for copy in started:
        copy.wait()


def dense_weights(side, top):
    ids = side[:, :top]
    numer = side[:, top:2 * top] * 32.0 + side[:, 2 * top:3 * top]
    weight = numer / jnp.sum(numer, axis=-1, keepdims=True)
    lane = lax.broadcasted_iota(jnp.int32, (side.shape[0], SIDE), 1)
    expert = jnp.where(lane < EXPERTS, lane, lane - EXPERTS).astype(jnp.float32)
    full = jnp.zeros((side.shape[0], SIDE), jnp.float32)
    for k in range(top):
        full = full + jnp.where(expert == ids[:, k:k + 1], weight[:, k:k + 1], 0.0)
    high = full.astype(jnp.bfloat16).astype(jnp.float32)
    return jnp.where(lane < EXPERTS, high, full - high).astype(jnp.bfloat16)


def layer(top, ff_dev, row_block, step_units, parts, mine_ref, theirs_ref, *refs):
    held, refs = refs[:3 * parts], refs[3 * parts:]
    (gate_ref, up_ref, down_ref, keep_ref, send_ref,
     rows_ref, total, gates, ups, downs, weights, hidden, sem) = refs
    units, depth = down_ref.shape
    steps = units // step_units
    count = rows_ref.shape[0]
    half = count // 2
    early = sum(held[3 * p].shape[0] for p in range(parts)) // step_units

    def copies(step, slot):
        span = pl.ds(pl.multiple_of(step * step_units, step_units), step_units)
        return [
            pltpu.make_async_copy(src.at[span], dst.at[slot], sem.at[i, slot])
            for i, (src, dst) in enumerate(
                [(gate_ref, gates), (up_ref, ups), (down_ref, downs)]
            )
        ]

    for step in range(early, min(early + SLOTS - 1, steps)):
        for copy in copies(step, step - early):
            copy.start()

    first = lax.axis_index("wide") * (units // ff_dev)

    def each_block(body):
        if count == row_block:
            body(pl.ds(0, row_block))
        else:
            @pl.loop(0, count // row_block)
            def _(b):
                body(pl.ds(pl.multiple_of(b * row_block, row_block), row_block))

    rows_ref[:half, :] = mine_ref[...]
    rows_ref[half:, :] = theirs_ref[...]

    def prepare(block):
        side = rows_ref[block, depth:depth + SIDE].astype(jnp.float32)
        weights[block, :] = dense_weights(side, top)
        total[block, :] = jnp.zeros((row_block, depth), jnp.float32)

    each_block(prepare)

    def work(step, gate, up, down, ready=None):
        expert = lax.broadcasted_iota(jnp.int32, (SIDE, step_units), 0)
        place = jnp.where(expert < EXPERTS, expert, expert - EXPERTS) - first
        unit = step * step_units + lax.broadcasted_iota(jnp.int32, (SIDE, step_units), 1)
        low = place * ff_dev
        pick = (unit >= low) & (unit < low + ff_dev) & (expert < 2 * EXPERTS)
        pick = jnp.where(pick, 1.0, 0.0).astype(jnp.bfloat16)
        if ready is not None:
            ready[0].wait()
            ready[1].wait()

        def first_half(block):
            x = rows_ref[block, :depth]
            g = lax.dot_general(x, gate[...], LAST, preferred_element_type=jnp.float32)
            u = lax.dot_general(x, up[...], LAST, preferred_element_type=jnp.float32)
            scale = jnp.dot(weights[block, :], pick, preferred_element_type=jnp.float32)
            hidden[block, :] = (g / (1.0 + jnp.exp(-g)) * u * scale).astype(jnp.bfloat16)

        each_block(first_half)
        if ready is not None:
            ready[2].wait()

        def second_half(block):
            total[block, :] += jnp.dot(
                hidden[block, :], down[...], preferred_element_type=jnp.float32
            )

        each_block(second_half)

    done = 0
    for p in range(parts):
        inside = held[3 * p].shape[0] // step_units

        @pl.loop(0, inside)
        def _(s):
            span = pl.ds(pl.multiple_of(s * step_units, step_units), step_units)
            work(done + s, *[ref.at[span] for ref in held[3 * p:3 * p + 3]])

        done += inside

    @pl.loop(early, steps)
    def _(step):
        slot = lax.rem(step - early, SLOTS)

        @pl.when(step + SLOTS - 1 < steps)
        def _():
            for copy in copies(step + SLOTS - 1, lax.rem(step - early + SLOTS - 1, SLOTS)):
                copy.start()

        work(step, gates.at[slot], ups.at[slot], downs.at[slot], copies(step, slot))

    keep_ref[...] = total[:half, :]
    send_ref[...] = total[half:, :].astype(jnp.bfloat16)


def build(axes):
    def local(tokens, expert_ids, gate_numer, w_gate, w_up, w_down):
        local_count, ff_dev, depth = w_gate.shape
        units = local_count * ff_dev
        top = expert_ids.shape[1]
        step_units = next(n for n in range(256, 0, -16) if units % n == 0)
        weights = [w.reshape(units, depth) for w in (w_gate, w_up, w_down)]
        weights = [pltpu.with_memory_space_constraint(w, pltpu.HBM) for w in weights]
        small = pltpu.CompilerParams(vmem_limit_bytes=2 << 20)
        own = (tokens, expert_ids, gate_numer)
        own = [pltpu.with_memory_space_constraint(a, pltpu.HBM) for a in own]
        rows = pl.pallas_call(
            with_routing,
            out_shape=jax.ShapeDtypeStruct((tokens.shape[0], depth + SIDE), jnp.bfloat16),
            in_specs=[HBM] * 3,
            out_specs=VMEM,
            scratch_shapes=[
                pltpu.VMEM(expert_ids.shape, jnp.int32),
                pltpu.VMEM(gate_numer.shape, jnp.int32),
                pltpu.SemaphoreType.DMA((3,)),
            ],
            compiler_params=small,
            name="with_routing",
        )(*own)
        hops = []
        for axis, size in axes:
            by = size // 2
            while by:
                hops.append((axis, size, by))
                by //= 2
        held = []
        at = 0
        for number, hop in enumerate(hops):
            theirs = swap(rows, *hop)
            steps = EARLY[number] if number < len(EARLY) and units >= 8 * step_units else 0
            ends = []
            if steps:
                span = steps * step_units
                *brought, end = pl.pallas_call(
                    functools.partial(bring, at),
                    out_shape=[pltpu.VMEM((span, depth), jnp.bfloat16)] * 3
                    + [jax.ShapeDtypeStruct((8, 128), jnp.float32)],
                    in_specs=[HBM] * 3 + [pl.BlockSpec(memory_space=pl.ANY)],
                    out_specs=[VMEM] * 4,
                    scratch_shapes=[pltpu.SemaphoreType.DMA((3, 2 * steps))],
                    compiler_params=small,
                    cost_estimate=pl.CostEstimate(
                        flops=0, bytes_accessed=6 * span * depth, transcendentals=0
                    ),
                    name="bring_weights",
                )(*weights, rows)
                held += brought
                at += span
                ends = [end]
            if hop is hops[-1]:
                break
            count = rows.shape[0]
            if count <= 64:
                rows = pl.pallas_call(
                    join,
                    out_shape=jax.ShapeDtypeStruct((2 * count, depth + SIDE), jnp.bfloat16),
                    in_specs=[VMEM] * 2 + [pl.BlockSpec(memory_space=pl.ANY)] * len(ends),
                    out_specs=VMEM,
                    compiler_params=small,
                    name="join",
                )(rows, theirs, *ends)
            else:
                rows = jnp.concatenate([rows, theirs], axis=0)
        half = rows.shape[0]
        count = 2 * half
        keep, send = pl.pallas_call(
            functools.partial(layer, top, ff_dev, min(count, 64), step_units, len(held) // 3),
            out_shape=[
                jax.ShapeDtypeStruct((half, depth), jnp.float32),
                jax.ShapeDtypeStruct((half, depth), jnp.bfloat16),
            ],
            in_specs=[VMEM] * (2 + len(held)) + [HBM] * 3,
            out_specs=[VMEM] * 2,
            scratch_shapes=[
                pltpu.VMEM((count, depth + SIDE), jnp.bfloat16),
                pltpu.VMEM((count, depth), jnp.float32),
            ]
            + [pltpu.VMEM((SLOTS, step_units, depth), jnp.bfloat16)] * 3
            + [
                pltpu.VMEM((count, SIDE), jnp.bfloat16),
                pltpu.VMEM((count, step_units), jnp.bfloat16),
                pltpu.SemaphoreType.DMA((3, SLOTS)),
            ],
            compiler_params=pltpu.CompilerParams(
                vmem_limit_bytes=GRANT if count == 64 else 60 << 20
            ),
            cost_estimate=pl.CostEstimate(
                flops=6 * count * units * depth,
                bytes_accessed=6 * (units - at) * depth,
                transcendentals=count * units,
            ),
            name="expert_layer",
        )(rows, theirs, *held, *weights)
        total = keep + swap(send, *hops[-1]).astype(jnp.float32)
        for hop in reversed(hops[:-1]):
            half = total.shape[0] // 2
            theirs = swap(total[half:].astype(jnp.bfloat16), *hop)
            total = total[:half] + theirs.astype(jnp.float32)
        return total.astype(jnp.bfloat16)

    return local


def solution(mesh):
    rows = P(("grp", "wide", "sec", "sub"), None)
    weights = P("wide", ("sec", "sub"), None)
    axes = [(name, mesh.shape[name]) for name in ("wide", "sec", "sub")]
    return jax.shard_map(
        build(axes),
        mesh=mesh,
        in_specs=(rows, rows, rows, weights, weights, weights),
        out_specs=rows,
        check_vma=False,
    )
```

time: 104 us -> 65.1 us (0.63)
  local copies, waits for them, and re-layouts: 31.1 us -> 0.04 us
  Pallas kernels: 44.3 us -> 37.8 us
  other arithmetic: 2.88 us -> 0.73 us
  starting transfers between devices: 9.03 us -> 10.1 us
    unnamed x38 -> x0, local copies, waits for them, and re-layouts: 29.2 us -> none
    pallas_call x1 -> x4, Pallas kernels: 33.9 us -> 24.7 us  [the longest x1 24.6 us: local(): pl.pallas_call(functools.partial(layer, top, ff_dev, min(count, 64), step...]
    add x3 -> x1, other arithmetic: 1.98 us -> 0.06 us  [local(): total = keep + swap(send, *hops[-1]).astype(jnp.float32)]
    pallas_call x3, Pallas kernels: 10.4 us -> 12.3 us  [local(): pl.pallas_call(functools.partial(bring, at), out_shape=[pltpu.VMEM((span,...]
    slice x3 -> x0, local copies, waits for them, and re-layouts: 1.54 us -> none  [local(): theirs = theirs + end[0, 0].astype(jnp.bfloat16)]
  transfers between devices with their start and end apart: 8 -> 8, of which waited for: 5 -> 6; matrix products, arithmetic and copies ran while one was open for 1% -> 0% of each run, Pallas kernels for 10% -> 19%
where the time goes in v5:
time: 65.1 us; the launch traced here: 64.9 us
  Pallas kernels  37.8 us (58%)
  waiting for transfers between devices  16.2 us (25%)
  starting transfers between devices  10.1 us (16%)
  other arithmetic  0.73 us (1%)
    pallas_call x1, Pallas kernels, local(): pl.pallas_call(functools.partial(layer, top, ff_dev, min(count, 64), step...  24.6 us
    ppermute x8, waiting for transfers between devices, swap(): return lax.ppermute(x, axis, [(i, i ^ by) for i in range(size)])  16.2 us
    pallas_call x3, Pallas kernels, local(): pl.pallas_call(functools.partial(bring, at), out_shape=[pltpu.VMEM((span,...  12.3 us
    ppermute x8, starting transfers between devices, swap(): return lax.ppermute(x, axis, [(i, i ^ by) for i in range(size)])  10.1 us
  transfers between devices with their start and end apart: 8, of which 6 were waited for; matrix products, arithmetic and copies ran while one was open for 0% of the time, Pallas kernels for 19%

profile of v5, /device:TPU:0, one launch (start us, length us, event | category | flops | bytes accessed | tf_op | source)
XLA Modules:
  0.0 64.9 jit_solution(6407095514771958259)
XLA Ops:
  0.0 0.9 %with_routing.1.after_ref.mine_ref = bf16[4,4224]{1,0:T(4,128)(2,1)S(1)} custom-call(bf16[4,4096]{1,0:T(4,128)(2,1)} %tokens_ref.1, s32[4,8]{1,0:T(4,128)} %ids_ref.1, s32[4,8]{1,0:T(4,128)} %numer_ref.1), custom_call_target="tpu_custom_call" | custom-call | tf_op jit(solution)/shard_map/with_routing/pallas_call | solution.py:186
  0.9 4.1 %collective-permute-start = (bf16[4,4224]{1,0:T(4,128)(2,1)S(1)}, bf16[4,4224]{1,0:T(4,128)(2,1)S(1)}, u32[]{:S(2)}, u32[]{:S(2)}) collective-permute-start(bf16[4,4224]{1,0:T(4,128)(2,1)S(1)} %with_routing.1.after_ref.mine_ref), channel_id=1, source_target_pairs={{0,8},{4,12},{8,0},{12,4},{1,9},{5,13},{9,1},{13,5},{2,10},{6,14},... | collective-permute-start | bytes 101384 | tf_op jit(solution)/shard_map/ppermute | solution.py:22
  5.0 4.7 %bring_weights.3 = (bf16[512,4096]{1,0:T(8,128)(2,1)S(1)}, bf16[512,4096]{1,0:T(8,128)(2,1)S(1)}, bf16[512,4096]{1,0:T(8,128)(2,1)S(1)}, f32[8,128]{1,0:T(8,128)S(1)}) custom-call(bf16[3072,4096]{1,0:T(8,128)(2,1)} %bitcast.3, bf16[3072,4096]{1,0:T(8,128)(2,1)} %bitcast.7, bf16[3072,4096]{1,0:T(8,128)(2,1)} %bitcast.11, ...), custom_call_target="tpu_custom_call" | custom-call | bytes 12582912 | tf_op jit(solution)/shard_map/bring_weights/pallas_call | solution.py:213
  9.7 0.0 collective-permute-done.theirs_ref
  9.7 1.6 %collective-permute-start.1 = (bf16[8,4224]{1,0:T(8,128)(2,1)S(1)}, bf16[8,4224]{1,0:T(8,128)(2,1)S(1)}, u32[]{:S(2)}, u32[]{:S(2)}) collective-permute-start(bf16[8,4224]{1,0:T(8,128)(2,1)S(1)} %join.3.after_ref.mine_ref), channel_id=1, source_target_pairs={{0,4},{4,0},{8,12},{12,8},{1,5},{5,1},{9,13},{13,9},{2,6},{6,2},{1... | collective-permute-start | bytes 202760 | tf_op jit(solution)/shard_map/ppermute | solution.py:22
  11.4 4.7 %bring_weights.4 = (bf16[512,4096]{1,0:T(8,128)(2,1)S(1)}, bf16[512,4096]{1,0:T(8,128)(2,1)S(1)}, bf16[512,4096]{1,0:T(8,128)(2,1)S(1)}, f32[8,128]{1,0:T(8,128)S(1)}) custom-call(bf16[3072,4096]{1,0:T(8,128)(2,1)} %bitcast.4, bf16[3072,4096]{1,0:T(8,128)(2,1)} %bitcast.8, bf16[3072,4096]{1,0:T(8,128)(2,1)} %bitcast.12, ...), custom_call_target="tpu_custom_call" | custom-call | bytes 12582912 | tf_op jit(solution)/shard_map/bring_weights/pallas_call | solution.py:213
  16.1 0.0 collective-permute-done.1.theirs_ref
  16.1 1.6 %collective-permute-start.2 = (bf16[16,4224]{1,0:T(8,128)(2,1)S(1)}, bf16[16,4224]{1,0:T(8,128)(2,1)S(1)}, u32[]{:S(2)}, u32[]{:S(2)}) collective-permute-start(bf16[16,4224]{1,0:T(8,128)(2,1)S(1)} %join.4.after_ref.mine_ref), channel_id=1, source_target_pairs={{0,2},{2,0},{1,3},{3,1},{4,6},{6,4},{5,7},{7,5},{8,10},{10,8},{9,1... | collective-permute-start | bytes 405512 | tf_op jit(solution)/shard_map/ppermute | solution.py:22
  17.7 2.9 %bring_weights.5 = (bf16[256,4096]{1,0:T(8,128)(2,1)S(1)}, bf16[256,4096]{1,0:T(8,128)(2,1)S(1)}, bf16[256,4096]{1,0:T(8,128)(2,1)S(1)}, f32[8,128]{1,0:T(8,128)S(1)}) custom-call(bf16[3072,4096]{1,0:T(8,128)(2,1)} %bitcast.5, bf16[3072,4096]{1,0:T(8,128)(2,1)} %bitcast.9, bf16[3072,4096]{1,0:T(8,128)(2,1)} %bitcast.13, ...), custom_call_target="tpu_custom_call" | custom-call | bytes 6291456 | tf_op jit(solution)/shard_map/bring_weights/pallas_call | solution.py:213
  20.5 0.7 %collective-permute-done.2.theirs_ref = bf16[16,4224]{1,0:T(8,128)(2,1)S(1)} collective-permute-done((bf16[16,4224]{1,0:T(8,128)(2,1)S(1)}, bf16[16,4224]{1,0:T(8,128)(2,1)S(1)}, u32[]{:S(2)}, u32[]{:S(2)}) %collective-permute-start.2) | collective-permute-done | bytes 135200 | tf_op jit(solution)/shard_map/ppermute | solution.py:22
  21.2 0.1 collective-permute-start.3
  21.3 1.5 %collective-permute-done.3.theirs_ref = bf16[32,4224]{1,0:T(8,128)(2,1)S(1)} collective-permute-done((bf16[32,4224]{1,0:T(8,128)(2,1)S(1)}, bf16[32,4224]{1,0:T(8,128)(2,1)S(1)}, u32[]{:S(2)}, u32[]{:S(2)}) %collective-permute-start.3) | collective-permute-done | bytes 270368 | tf_op jit(solution)/shard_map/ppermute | solution.py:22
  22.8 24.6 %expert_layer.1 = (f32[32,4096]{1,0:T(8,128)S(1)}, bf16[32,4096]{1,0:T(8,128)(2,1)S(1)}) custom-call(bf16[32,4224]{1,0:T(8,128)(2,1)S(1)} %join.5.mine_ref, bf16[32,4224]{1,0:T(8,128)(2,1)S(1)} %collective-permute-done.3.theirs_ref, bf16[512,4096]{1,0:T(8,128)(2,1)S(1)} %get-tuple-element.22.refs_0_, bf16[512,4096]{1,0:T(8,128)(2,1)S(1)} %get-tuple-element.23.refs_1_, ...), custom_call_target="tpu_custom_call" | custom-call | flops 4831838208 | bytes 44040192 | tf_op jit(solution)/shard_map/expert_layer/pallas_call | solution.py:245
  47.4 0.2 collective-permute-start.4
  47.6 1.4 %collective-permute-done.4 = bf16[32,4096]{1,0:T(8,128)(2,1)S(1)} collective-permute-done((bf16[32,4096]{1,0:T(8,128)(2,1)S(1)}, bf16[32,4096]{1,0:T(8,128)(2,1)S(1)}, u32[]{:S(2)}, u32[]{:S(2)}) %collective-permute-start.4) | collective-permute-done | bytes 262176 | tf_op jit(solution)/shard_map/ppermute | solution.py:22
  49.0 0.1 convert_add_fusion
  49.1 1.6 %collective-permute-start.5 = (bf16[16,4096]{1,0:T(8,128)(2,1)S(1)}, bf16[16,4096]{1,0:T(8,128)(2,1)S(1)}, u32[]{:S(2)}, u32[]{:S(2)}) collective-permute-start(bf16[16,4096]{1,0:T(8,128)(2,1)S(1)} %slice.41), channel_id=1, source_target_pairs={{0,2},{2,0},{1,3},{3,1},{4,6},{6,4},{5,7},{7,5},{8,10},{10,8},{9,1... | collective-permute-start | bytes 393224 | tf_op jit(solution)/shard_map/ppermute | solution.py:22
  50.7 4.0 %collective-permute-done.5 = bf16[16,4096]{1,0:T(8,128)(2,1)S(1)} collective-permute-done((bf16[16,4096]{1,0:T(8,128)(2,1)S(1)}, bf16[16,4096]{1,0:T(8,128)(2,1)S(1)}, u32[]{:S(2)}, u32[]{:S(2)}) %collective-permute-start.5) | collective-permute-done | bytes 131104 | tf_op jit(solution)/shard_map/ppermute | solution.py:22
  54.8 0.5 collective-permute-start.6
  55.3 3.8 %collective-permute-done.6 = bf16[8,4096]{1,0:T(8,128)(2,1)S(1)} collective-permute-done((bf16[8,4096]{1,0:T(8,128)(2,1)S(1)}, bf16[8,4096]{1,0:T(8,128)(2,1)S(1)}, u32[]{:S(2)}, u32[]{:S(2)}) %collective-permute-start.6) | collective-permute-done | bytes 65568 | tf_op jit(solution)/shard_map/ppermute | solution.py:22
  59.1 0.4 collective-permute-start.7
  59.5 4.7 %collective-permute-done.7 = bf16[4,4096]{1,0:T(4,128)(2,1)S(1)} collective-permute-done((bf16[4,4096]{1,0:T(4,128)(2,1)S(1)}, bf16[4,4096]{1,0:T(4,128)(2,1)S(1)}, u32[]{:S(2)}, u32[]{:S(2)}) %collective-permute-start.7) | collective-permute-done | bytes 32800 | tf_op jit(solution)/shard_map/ppermute | solution.py:22
  64.3 0.6 fusion
  (8 shorter events, 0.1 us)
Async XLA Ops:
  0.9 8.8 %collective-permute-start = (bf16[4,4224]{1,0:T(4,128)(2,1)S(1)}, bf16[4,4224]{1,0:T(4,128)(2,1)S(1)}, u32[]{:S(2)}, u32[]{:S(2)}) collective-permute-start(bf16[4,4224]{1,0:T(4,128)(2,1)S(1)} %with_routing.1.after_ref.mine_ref), channel_id=1, source_target_pairs={{0,8},{4,12},{8,0},{12,4},{1,9},{5,13},{9,1},{13,5},{2,10},{6,14},... | collective-permute-start | bytes 101384 | tf_op jit(solution)/shard_map/ppermute | solution.py:22
  9.7 6.4 %collective-permute-start.1 = (bf16[8,4224]{1,0:T(8,128)(2,1)S(1)}, bf16[8,4224]{1,0:T(8,128)(2,1)S(1)}, u32[]{:S(2)}, u32[]{:S(2)}) collective-permute-start(bf16[8,4224]{1,0:T(8,128)(2,1)S(1)} %join.3.after_ref.mine_ref), channel_id=1, source_target_pairs={{0,4},{4,0},{8,12},{12,8},{1,5},{5,1},{9,13},{13,9},{2,6},{6,2},{1... | collective-permute-start | bytes 202760 | tf_op jit(solution)/shard_map/ppermute | solution.py:22
  16.1 5.1 %collective-permute-start.2 = (bf16[16,4224]{1,0:T(8,128)(2,1)S(1)}, bf16[16,4224]{1,0:T(8,128)(2,1)S(1)}, u32[]{:S(2)}, u32[]{:S(2)}) collective-permute-start(bf16[16,4224]{1,0:T(8,128)(2,1)S(1)} %join.4.after_ref.mine_ref), channel_id=1, source_target_pairs={{0,2},{2,0},{1,3},{3,1},{4,6},{6,4},{5,7},{7,5},{8,10},{10,8},{9,1... | collective-permute-start | bytes 405512 | tf_op jit(solution)/shard_map/ppermute | solution.py:22
  21.2 1.6 %collective-permute-start.3 = (bf16[32,4224]{1,0:T(8,128)(2,1)S(1)}, bf16[32,4224]{1,0:T(8,128)(2,1)S(1)}, u32[]{:S(2)}, u32[]{:S(2)}) collective-permute-start(bf16[32,4224]{1,0:T(8,128)(2,1)S(1)} %join.5.mine_ref), channel_id=1, source_target_pairs={{0,1},{1,0},{2,3},{3,2},{4,5},{5,4},{6,7},{7,6},{8,9},{9,8},{10,11... | collective-permute-start | bytes 811016 | tf_op jit(solution)/shard_map/ppermute | solution.py:22
  47.4 1.6 %collective-permute-start.4 = (bf16[32,4096]{1,0:T(8,128)(2,1)S(1)}, bf16[32,4096]{1,0:T(8,128)(2,1)S(1)}, u32[]{:S(2)}, u32[]{:S(2)}) collective-permute-start(bf16[32,4096]{1,0:T(8,128)(2,1)S(1)} %get-tuple-element.32), channel_id=1, source_target_pairs={{0,1},{1,0},{2,3},{3,2},{4,5},{5,4},{6,7},{7,6},{8,9},{9,8},{10,11... | collective-permute-start | bytes 786440 | tf_op jit(solution)/shard_map/ppermute | solution.py:22
  49.1 5.6 %collective-permute-start.5 = (bf16[16,4096]{1,0:T(8,128)(2,1)S(1)}, bf16[16,4096]{1,0:T(8,128)(2,1)S(1)}, u32[]{:S(2)}, u32[]{:S(2)}) collective-permute-start(bf16[16,4096]{1,0:T(8,128)(2,1)S(1)} %slice.41), channel_id=1, source_target_pairs={{0,2},{2,0},{1,3},{3,1},{4,6},{6,4},{5,7},{7,5},{8,10},{10,8},{9,1... | collective-permute-start | bytes 393224 | tf_op jit(solution)/shard_map/ppermute | solution.py:22
  54.8 4.3 %collective-permute-start.6 = (bf16[8,4096]{1,0:T(8,128)(2,1)S(1)}, bf16[8,4096]{1,0:T(8,128)(2,1)S(1)}, u32[]{:S(2)}, u32[]{:S(2)}) collective-permute-start(bf16[8,4096]{1,0:T(8,128)(2,1)S(1)} %slice.42), channel_id=1, source_target_pairs={{0,4},{4,0},{8,12},{12,8},{1,5},{5,1},{9,13},{13,9},{2,6},{6,2},{1... | collective-permute-start | bytes 196616 | tf_op jit(solution)/shard_map/ppermute | solution.py:22
  59.1 5.1 %collective-permute-start.7 = (bf16[4,4096]{1,0:T(4,128)(2,1)S(1)}, bf16[4,4096]{1,0:T(4,128)(2,1)S(1)}, u32[]{:S(2)}, u32[]{:S(2)}) collective-permute-start(bf16[4,4096]{1,0:T(4,128)(2,1)S(1)} %slice.43), channel_id=1, source_target_pairs={{0,8},{4,12},{8,0},{12,4},{1,9},{5,13},{9,1},{13,5},{2,10},{6,14},... | collective-permute-start | bytes 98312 | tf_op jit(solution)/shard_map/ppermute | solution.py:22

commit v6 on v5

--- a/solution.py
+++ b/solution.py
@@ -118,9 +118,9 @@
     each_block(prepare)
 
     def work(step, gate, up, down, ready=None):
-        expert = lax.broadcasted_iota(jnp.int32, (SIDE, step_units), 0)
+        expert = lax.broadcasted_iota(jnp.int32, (step_units, SIDE), 1)
         place = jnp.where(expert < EXPERTS, expert, expert - EXPERTS) - first
-        unit = step * step_units + lax.broadcasted_iota(jnp.int32, (SIDE, step_units), 1)
+        unit = step * step_units + lax.broadcasted_iota(jnp.int32, (step_units, SIDE), 0)
         low = place * ff_dev
         pick = (unit >= low) & (unit < low + ff_dev) & (expert < 2 * EXPERTS)
         pick = jnp.where(pick, 1.0, 0.0).astype(jnp.bfloat16)
@@ -130,10 +130,13 @@
 
         def first_half(block):
             x = rows_ref[block, :depth]
-            g = lax.dot_general(x, gate[...], LAST, preferred_element_type=jnp.float32)
-            u = lax.dot_general(x, up[...], LAST, preferred_element_type=jnp.float32)
-            scale = jnp.dot(weights[block, :], pick, preferred_element_type=jnp.float32)
-            hidden[block, :] = (g / (1.0 + jnp.exp(-g)) * u * scale).astype(jnp.bfloat16)
+            g = lax.dot_general(gate[...], x, LAST, preferred_element_type=jnp.float32)
+            u = lax.dot_general(up[...], x, LAST, preferred_element_type=jnp.float32)
+            scale = lax.dot_general(
+                pick, weights[block, :], LAST, preferred_element_type=jnp.float32
+            )
+            h = g / (1.0 + jnp.exp(-g)) * u * scale
+            hidden[block, :] = jnp.transpose(h).astype(jnp.bfloat16)
 
         each_block(first_half)
         if ready is not None:

time: 65.1 us -> 64.3 us (0.988)
  Pallas kernels: 37.8 us -> 37 us
    pallas_call x1, Pallas kernels: 24.6 us -> 23.8 us  [local(): pl.pallas_call(functools.partial(layer, top, ff_dev, min(count, 64), step...]
where the time goes in v6:
time: 64.3 us; the launch traced here: 64.1 us
  Pallas kernels  37 us (58%)
  waiting for transfers between devices  16.1 us (25%)
  starting transfers between devices  10.1 us (16%)
  other arithmetic  0.73 us (1%)
    pallas_call x1, Pallas kernels, local(): pl.pallas_call(functools.partial(layer, top, ff_dev, min(count, 64), step...  23.8 us
    ppermute x8, waiting for transfers between devices, swap(): return lax.ppermute(x, axis, [(i, i ^ by) for i in range(size)])  16.1 us
    pallas_call x3, Pallas kernels, local(): pl.pallas_call(functools.partial(bring, at), out_shape=[pltpu.VMEM((span,...  12.3 us
    ppermute x8, starting transfers between devices, swap(): return lax.ppermute(x, axis, [(i, i ^ by) for i in range(size)])  10.1 us
  transfers between devices with their start and end apart: 8, of which 6 were waited for; matrix products, arithmetic and copies ran while one was open for 0% of the time, Pallas kernels for 19%

profile of v6, /device:TPU:0, one launch (start us, length us, event | category | flops | bytes accessed | tf_op | source)
XLA Modules:
  0.0 64.1 jit_solution(17923304682011707891)
XLA Ops:
  0.0 0.9 %with_routing.1.after_ref.mine_ref = bf16[4,4224]{1,0:T(4,128)(2,1)S(1)} custom-call(bf16[4,4096]{1,0:T(4,128)(2,1)} %tokens_ref.1, s32[4,8]{1,0:T(4,128)} %ids_ref.1, s32[4,8]{1,0:T(4,128)} %numer_ref.1), custom_call_target="tpu_custom_call" | custom-call | tf_op jit(solution)/shard_map/with_routing/pallas_call | solution.py:189
  0.9 4.1 %collective-permute-start = (bf16[4,4224]{1,0:T(4,128)(2,1)S(1)}, bf16[4,4224]{1,0:T(4,128)(2,1)S(1)}, u32[]{:S(2)}, u32[]{:S(2)}) collective-permute-start(bf16[4,4224]{1,0:T(4,128)(2,1)S(1)} %with_routing.1.after_ref.mine_ref), channel_id=1, source_target_pairs={{0,8},{4,12},{8,0},{12,4},{1,9},{5,13},{9,1},{13,5},{2,10},{6,14},... | collective-permute-start | bytes 101384 | tf_op jit(solution)/shard_map/ppermute | solution.py:22
  5.0 4.7 %bring_weights.3 = (bf16[512,4096]{1,0:T(8,128)(2,1)S(1)}, bf16[512,4096]{1,0:T(8,128)(2,1)S(1)}, bf16[512,4096]{1,0:T(8,128)(2,1)S(1)}, f32[8,128]{1,0:T(8,128)S(1)}) custom-call(bf16[3072,4096]{1,0:T(8,128)(2,1)} %bitcast.3, bf16[3072,4096]{1,0:T(8,128)(2,1)} %bitcast.7, bf16[3072,4096]{1,0:T(8,128)(2,1)} %bitcast.11, ...), custom_call_target="tpu_custom_call" | custom-call | bytes 12582912 | tf_op jit(solution)/shard_map/bring_weights/pallas_call | solution.py:216
  9.7 0.0 collective-permute-done.theirs_ref
  9.7 1.6 %collective-permute-start.1 = (bf16[8,4224]{1,0:T(8,128)(2,1)S(1)}, bf16[8,4224]{1,0:T(8,128)(2,1)S(1)}, u32[]{:S(2)}, u32[]{:S(2)}) collective-permute-start(bf16[8,4224]{1,0:T(8,128)(2,1)S(1)} %join.3.after_ref.mine_ref), channel_id=1, source_target_pairs={{0,4},{4,0},{8,12},{12,8},{1,5},{5,1},{9,13},{13,9},{2,6},{6,2},{1... | collective-permute-start | bytes 202760 | tf_op jit(solution)/shard_map/ppermute | solution.py:22
  11.4 4.7 %bring_weights.4 = (bf16[512,4096]{1,0:T(8,128)(2,1)S(1)}, bf16[512,4096]{1,0:T(8,128)(2,1)S(1)}, bf16[512,4096]{1,0:T(8,128)(2,1)S(1)}, f32[8,128]{1,0:T(8,128)S(1)}) custom-call(bf16[3072,4096]{1,0:T(8,128)(2,1)} %bitcast.4, bf16[3072,4096]{1,0:T(8,128)(2,1)} %bitcast.8, bf16[3072,4096]{1,0:T(8,128)(2,1)} %bitcast.12, ...), custom_call_target="tpu_custom_call" | custom-call | bytes 12582912 | tf_op jit(solution)/shard_map/bring_weights/pallas_call | solution.py:216
  16.1 0.0 collective-permute-done.1.theirs_ref
  16.1 1.6 %collective-permute-start.2 = (bf16[16,4224]{1,0:T(8,128)(2,1)S(1)}, bf16[16,4224]{1,0:T(8,128)(2,1)S(1)}, u32[]{:S(2)}, u32[]{:S(2)}) collective-permute-start(bf16[16,4224]{1,0:T(8,128)(2,1)S(1)} %join.4.after_ref.mine_ref), channel_id=1, source_target_pairs={{0,2},{2,0},{1,3},{3,1},{4,6},{6,4},{5,7},{7,5},{8,10},{10,8},{9,1... | collective-permute-start | bytes 405512 | tf_op jit(solution)/shard_map/ppermute | solution.py:22
  17.7 2.9 %bring_weights.5 = (bf16[256,4096]{1,0:T(8,128)(2,1)S(1)}, bf16[256,4096]{1,0:T(8,128)(2,1)S(1)}, bf16[256,4096]{1,0:T(8,128)(2,1)S(1)}, f32[8,128]{1,0:T(8,128)S(1)}) custom-call(bf16[3072,4096]{1,0:T(8,128)(2,1)} %bitcast.5, bf16[3072,4096]{1,0:T(8,128)(2,1)} %bitcast.9, bf16[3072,4096]{1,0:T(8,128)(2,1)} %bitcast.13, ...), custom_call_target="tpu_custom_call" | custom-call | bytes 6291456 | tf_op jit(solution)/shard_map/bring_weights/pallas_call | solution.py:216
  20.5 0.7 %collective-permute-done.2.theirs_ref = bf16[16,4224]{1,0:T(8,128)(2,1)S(1)} collective-permute-done((bf16[16,4224]{1,0:T(8,128)(2,1)S(1)}, bf16[16,4224]{1,0:T(8,128)(2,1)S(1)}, u32[]{:S(2)}, u32[]{:S(2)}) %collective-permute-start.2) | collective-permute-done | bytes 135200 | tf_op jit(solution)/shard_map/ppermute | solution.py:22
  21.2 0.1 collective-permute-start.3
  21.3 1.5 %collective-permute-done.3.theirs_ref = bf16[32,4224]{1,0:T(8,128)(2,1)S(1)} collective-permute-done((bf16[32,4224]{1,0:T(8,128)(2,1)S(1)}, bf16[32,4224]{1,0:T(8,128)(2,1)S(1)}, u32[]{:S(2)}, u32[]{:S(2)}) %collective-permute-start.3) | collective-permute-done | bytes 270368 | tf_op jit(solution)/shard_map/ppermute | solution.py:22
  22.8 23.8 %expert_layer.1 = (f32[32,4096]{1,0:T(8,128)S(1)}, bf16[32,4096]{1,0:T(8,128)(2,1)S(1)}) custom-call(bf16[32,4224]{1,0:T(8,128)(2,1)S(1)} %join.5.mine_ref, bf16[32,4224]{1,0:T(8,128)(2,1)S(1)} %collective-permute-done.3.theirs_ref, bf16[512,4096]{1,0:T(8,128)(2,1)S(1)} %get-tuple-element.22.refs_0_, bf16[512,4096]{1,0:T(8,128)(2,1)S(1)} %get-tuple-element.23.refs_1_, ...), custom_call_target="tpu_custom_call" | custom-call | flops 4831838208 | bytes 44040192 | tf_op jit(solution)/shard_map/expert_layer/pallas_call | solution.py:248
  46.6 0.2 collective-permute-start.4
  46.8 1.4 %collective-permute-done.4 = bf16[32,4096]{1,0:T(8,128)(2,1)S(1)} collective-permute-done((bf16[32,4096]{1,0:T(8,128)(2,1)S(1)}, bf16[32,4096]{1,0:T(8,128)(2,1)S(1)}, u32[]{:S(2)}, u32[]{:S(2)}) %collective-permute-start.4) | collective-permute-done | bytes 262176 | tf_op jit(solution)/shard_map/ppermute | solution.py:22
  48.2 0.1 convert_add_fusion
  48.3 1.6 %collective-permute-start.5 = (bf16[16,4096]{1,0:T(8,128)(2,1)S(1)}, bf16[16,4096]{1,0:T(8,128)(2,1)S(1)}, u32[]{:S(2)}, u32[]{:S(2)}) collective-permute-start(bf16[16,4096]{1,0:T(8,128)(2,1)S(1)} %slice.41), channel_id=1, source_target_pairs={{0,2},{2,0},{1,3},{3,1},{4,6},{6,4},{5,7},{7,5},{8,10},{10,8},{9,1... | collective-permute-start | bytes 393224 | tf_op jit(solution)/shard_map/ppermute | solution.py:22
  49.9 4.0 %collective-permute-done.5 = bf16[16,4096]{1,0:T(8,128)(2,1)S(1)} collective-permute-done((bf16[16,4096]{1,0:T(8,128)(2,1)S(1)}, bf16[16,4096]{1,0:T(8,128)(2,1)S(1)}, u32[]{:S(2)}, u32[]{:S(2)}) %collective-permute-start.5) | collective-permute-done | bytes 131104 | tf_op jit(solution)/shard_map/ppermute | solution.py:22
  54.0 0.5 collective-permute-start.6
  54.5 3.8 %collective-permute-done.6 = bf16[8,4096]{1,0:T(8,128)(2,1)S(1)} collective-permute-done((bf16[8,4096]{1,0:T(8,128)(2,1)S(1)}, bf16[8,4096]{1,0:T(8,128)(2,1)S(1)}, u32[]{:S(2)}, u32[]{:S(2)}) %collective-permute-start.6) | collective-permute-done | bytes 65568 | tf_op jit(solution)/shard_map/ppermute | solution.py:22
  58.3 0.4 collective-permute-start.7
  58.8 4.7 %collective-permute-done.7 = bf16[4,4096]{1,0:T(4,128)(2,1)S(1)} collective-permute-done((bf16[4,4096]{1,0:T(4,128)(2,1)S(1)}, bf16[4,4096]{1,0:T(4,128)(2,1)S(1)}, u32[]{:S(2)}, u32[]{:S(2)}) %collective-permute-start.7) | collective-permute-done | bytes 32800 | tf_op jit(solution)/shard_map/ppermute | solution.py:22
  63.5 0.6 fusion
  (8 shorter events, 0.1 us)
Async XLA Ops:
  0.9 8.8 %collective-permute-start = (bf16[4,4224]{1,0:T(4,128)(2,1)S(1)}, bf16[4,4224]{1,0:T(4,128)(2,1)S(1)}, u32[]{:S(2)}, u32[]{:S(2)}) collective-permute-start(bf16[4,4224]{1,0:T(4,128)(2,1)S(1)} %with_routing.1.after_ref.mine_ref), channel_id=1, source_target_pairs={{0,8},{4,12},{8,0},{12,4},{1,9},{5,13},{9,1},{13,5},{2,10},{6,14},... | collective-permute-start | bytes 101384 | tf_op jit(solution)/shard_map/ppermute | solution.py:22
  9.7 6.4 %collective-permute-start.1 = (bf16[8,4224]{1,0:T(8,128)(2,1)S(1)}, bf16[8,4224]{1,0:T(8,128)(2,1)S(1)}, u32[]{:S(2)}, u32[]{:S(2)}) collective-permute-start(bf16[8,4224]{1,0:T(8,128)(2,1)S(1)} %join.3.after_ref.mine_ref), channel_id=1, source_target_pairs={{0,4},{4,0},{8,12},{12,8},{1,5},{5,1},{9,13},{13,9},{2,6},{6,2},{1... | collective-permute-start | bytes 202760 | tf_op jit(solution)/shard_map/ppermute | solution.py:22
  16.1 5.1 %collective-permute-start.2 = (bf16[16,4224]{1,0:T(8,128)(2,1)S(1)}, bf16[16,4224]{1,0:T(8,128)(2,1)S(1)}, u32[]{:S(2)}, u32[]{:S(2)}) collective-permute-start(bf16[16,4224]{1,0:T(8,128)(2,1)S(1)} %join.4.after_ref.mine_ref), channel_id=1, source_target_pairs={{0,2},{2,0},{1,3},{3,1},{4,6},{6,4},{5,7},{7,5},{8,10},{10,8},{9,1... | collective-permute-start | bytes 405512 | tf_op jit(solution)/shard_map/ppermute | solution.py:22
  21.2 1.6 %collective-permute-start.3 = (bf16[32,4224]{1,0:T(8,128)(2,1)S(1)}, bf16[32,4224]{1,0:T(8,128)(2,1)S(1)}, u32[]{:S(2)}, u32[]{:S(2)}) collective-permute-start(bf16[32,4224]{1,0:T(8,128)(2,1)S(1)} %join.5.mine_ref), channel_id=1, source_target_pairs={{0,1},{1,0},{2,3},{3,2},{4,5},{5,4},{6,7},{7,6},{8,9},{9,8},{10,11... | collective-permute-start | bytes 811016 | tf_op jit(solution)/shard_map/ppermute | solution.py:22
  46.6 1.6 %collective-permute-start.4 = (bf16[32,4096]{1,0:T(8,128)(2,1)S(1)}, bf16[32,4096]{1,0:T(8,128)(2,1)S(1)}, u32[]{:S(2)}, u32[]{:S(2)}) collective-permute-start(bf16[32,4096]{1,0:T(8,128)(2,1)S(1)} %get-tuple-element.32), channel_id=1, source_target_pairs={{0,1},{1,0},{2,3},{3,2},{4,5},{5,4},{6,7},{7,6},{8,9},{9,8},{10,11... | collective-permute-start | bytes 786440 | tf_op jit(solution)/shard_map/ppermute | solution.py:22
  48.3 5.6 %collective-permute-start.5 = (bf16[16,4096]{1,0:T(8,128)(2,1)S(1)}, bf16[16,4096]{1,0:T(8,128)(2,1)S(1)}, u32[]{:S(2)}, u32[]{:S(2)}) collective-permute-start(bf16[16,4096]{1,0:T(8,128)(2,1)S(1)} %slice.41), channel_id=1, source_target_pairs={{0,2},{2,0},{1,3},{3,1},{4,6},{6,4},{5,7},{7,5},{8,10},{10,8},{9,1... | collective-permute-start | bytes 393224 | tf_op jit(solution)/shard_map/ppermute | solution.py:22
  54.0 4.3 %collective-permute-start.6 = (bf16[8,4096]{1,0:T(8,128)(2,1)S(1)}, bf16[8,4096]{1,0:T(8,128)(2,1)S(1)}, u32[]{:S(2)}, u32[]{:S(2)}) collective-permute-start(bf16[8,4096]{1,0:T(8,128)(2,1)S(1)} %slice.42), channel_id=1, source_target_pairs={{0,4},{4,0},{8,12},{12,8},{1,5},{5,1},{9,13},{13,9},{2,6},{6,2},{1... | collective-permute-start | bytes 196616 | tf_op jit(solution)/shard_map/ppermute | solution.py:22
  58.3 5.1 %collective-permute-start.7 = (bf16[4,4096]{1,0:T(4,128)(2,1)S(1)}, bf16[4,4096]{1,0:T(4,128)(2,1)S(1)}, u32[]{:S(2)}, u32[]{:S(2)}) collective-permute-start(bf16[4,4096]{1,0:T(4,128)(2,1)S(1)} %slice.43), channel_id=1, source_target_pairs={{0,8},{4,12},{8,0},{12,4},{1,9},{5,13},{9,1},{13,5},{2,10},{6,14},... | collective-permute-start | bytes 98312 | tf_op jit(solution)/shard_map/ppermute | solution.py:22

commit v7 on v6

v7 whole, which is shorter than its diff:
```python
import functools

import jax
import jax.numpy as jnp
from jax import lax
from jax.experimental import pallas as pl
from jax.experimental.pallas import tpu as pltpu
from jax.sharding import PartitionSpec as P

EXPERTS = 32
SIDE = 128
SLOTS = 3
EARLY = (0, 1, 1)
GRANT = 8 << 20

VMEM = pl.BlockSpec(memory_space=pltpu.VMEM)
HBM = pl.BlockSpec(memory_space=pltpu.HBM)
LAST = (((1,), (1,)), ((), ()))


def swap(x, axis, size, by):
    return lax.ppermute(x, axis, [(i, i ^ by) for i in range(size)])


def with_routing(tokens_ref, ids_ref, numer_ref, out_ref, ids, numer, sem):
    rows, depth = tokens_ref.shape
    top = ids_ref.shape[1]
    pairs = [(tokens_ref, out_ref.at[:, pl.ds(0, depth)]), (ids_ref, ids), (numer_ref, numer)]
    started = [pltpu.make_async_copy(a, b, sem.at[i]) for i, (a, b) in enumerate(pairs)]
    for copy in started:
        copy.start()
    for copy in started:
        copy.wait()
    pad = jnp.zeros((rows, SIDE - 3 * top), jnp.int32)
    side = jnp.concatenate([ids[...], numer[...] >> 5, numer[...] & 31, pad], axis=1)
    out_ref[:, depth:] = side.astype(jnp.float32).astype(jnp.bfloat16)


def join(mine_ref, theirs_ref, *refs):
    out_ref = refs[-1]
    count = mine_ref.shape[0]
    out_ref[:count, :] = mine_ref[...]
    out_ref[count:, :] = theirs_ref[...]


def bring(first, count, gate_ref, up_ref, down_ref, after_ref, *refs):
    gates, ups, downs, end_ref, sem = refs[-5:]
    size = gates.shape[1]
    started = []
    for step in range(first, first + count):
        for i, (ref, ring) in enumerate([(gate_ref, gates), (up_ref, ups), (down_ref, downs)]):
            for part in range(2):
                half = size // 2
                started.append(
                    pltpu.make_async_copy(
                        ref.at[pl.ds(step * size + part * half, half)],
                        ring.at[step, pl.ds(part * half, half)],
                        sem.at[i, step - first, part],
                    )
                )
    for copy in started:
        copy.start()
    end_ref[...] = jnp.zeros_like(end_ref)
    for copy in started:
        copy.wait()


def dense_weights(side, top):
    ids = side[:, :top]
    numer = side[:, top:2 * top] * 32.0 + side[:, 2 * top:3 * top]
    weight = numer / jnp.sum(numer, axis=-1, keepdims=True)
    lane = lax.broadcasted_iota(jnp.int32, (side.shape[0], SIDE), 1)
    expert = jnp.where(lane < EXPERTS, lane, lane - EXPERTS).astype(jnp.float32)
    full = jnp.zeros((side.shape[0], SIDE), jnp.float32)
    for k in range(top):
        full = full + jnp.where(expert == ids[:, k:k + 1], weight[:, k:k + 1], 0.0)
    high = full.astype(jnp.bfloat16).astype(jnp.float32)
    return jnp.where(lane < EXPERTS, high, full - high).astype(jnp.bfloat16)


def layer(top, ff_dev, row_block, step_units, early, mine_ref, theirs_ref, gate_ref, up_ref,
          down_ref, *refs):
    if early:
        refs = refs[3:]
    keep_ref, send_ref, gates, ups, downs, rows_ref, total, weights, hidden, sem = refs
    units, depth = down_ref.shape
    steps = units // step_units
    count = rows_ref.shape[0]
    half = count // 2
    slots = gates.shape[0]

    def copy_of(i, step):
        src, ring = [(gate_ref, gates), (up_ref, ups), (down_ref, downs)][i]
        slot = lax.rem(step, ring.shape[0])
        span = pl.ds(pl.multiple_of(step * step_units, step_units), step_units)
        return pltpu.make_async_copy(src.at[span], ring.at[slot], sem.at[i, slot])

    def start(step):
        for i in range(3):
            copy_of(i, step).start()

    def wait(i, step):
        if isinstance(step, int):
            if step >= early:
                copy_of(i, jnp.int32(step)).wait()
        else:
            @pl.when(step >= early)
            def _():
                copy_of(i, step).wait()

    for step in range(early, min(slots, steps)):
        start(jnp.int32(step))

    first = lax.axis_index("wide") * (units // ff_dev)

    def each_block(body):
        if count == row_block:
            body(pl.ds(0, row_block))
        else:
            @pl.loop(0, count // row_block)
            def _(b):
                body(pl.ds(pl.multiple_of(b * row_block, row_block), row_block))

    rows_ref[:half, :] = mine_ref[...]
    rows_ref[half:, :] = theirs_ref[...]

    def prepare(block):
        side = rows_ref[block, depth:depth + SIDE].astype(jnp.float32)
        weights[block, :] = dense_weights(side, top)
        total[block, :] = jnp.zeros((row_block, depth), jnp.float32)

    each_block(prepare)

    def products(step, block):
        x = rows_ref[block, :depth]
        gate, up = [ring.at[lax.rem(step, ring.shape[0])] for ring in (gates, ups)]
        g = lax.dot_general(gate[...], x, LAST, preferred_element_type=jnp.float32)
        u = lax.dot_general(up[...], x, LAST, preferred_element_type=jnp.float32)
        return g, u

    def activate(step, block, g, u):
        expert = lax.broadcasted_iota(jnp.int32, (step_units, SIDE), 1)
        place = jnp.where(expert < EXPERTS, expert, expert - EXPERTS) - first
        unit = step * step_units + lax.broadcasted_iota(jnp.int32, (step_units, SIDE), 0)
        low = place * ff_dev
        pick = (unit >= low) & (unit < low + ff_dev) & (expert < 2 * EXPERTS)
        pick = jnp.where(pick, 1.0, 0.0).astype(jnp.bfloat16)
        scale = lax.dot_general(pick, weights[block, :], LAST, preferred_element_type=jnp.float32)
        h = g / (1.0 + jnp.exp(-g)) * u * scale
        hidden[lax.rem(step, 2), block, :] = jnp.transpose(h).astype(jnp.bfloat16)

    def down_product(step, block):
        down = downs.at[lax.rem(step, downs.shape[0])]
        total[block, :] += jnp.dot(
            hidden[lax.rem(step, 2), block, :], down[...], preferred_element_type=jnp.float32
        )

    wait(0, 0)
    wait(1, 0)
    each_block(lambda block: activate(0, block, *products(jnp.int32(0), block)))

    @pl.loop(1, steps)
    def _(step):
        @pl.when(step - 1 + slots < steps)
        def _():
            start(step - 1 + slots)

        wait(0, step)
        wait(1, step)
        wait(2, step - 1)

        def both(block):
            g, u = products(step, block)
            down_product(step - 1, block)
            activate(step, block, g, u)

        each_block(both)

    wait(2, steps - 1)
    each_block(lambda block: down_product(jnp.int32(steps - 1), block))
    keep_ref[...] = total[:half, :]
    send_ref[...] = total[half:, :].astype(jnp.bfloat16)


def build(axes):
    def local(tokens, expert_ids, gate_numer, w_gate, w_up, w_down):
        local_count, ff_dev, depth = w_gate.shape
        units = local_count * ff_dev
        top = expert_ids.shape[1]
        step_units = next(n for n in range(256, 0, -16) if units % n == 0)
        weights = [w.reshape(units, depth) for w in (w_gate, w_up, w_down)]
        weights = [pltpu.with_memory_space_constraint(w, pltpu.HBM) for w in weights]
        small = pltpu.CompilerParams(vmem_limit_bytes=2 << 20)
        own = (tokens, expert_ids, gate_numer)
        own = [pltpu.with_memory_space_constraint(a, pltpu.HBM) for a in own]
        rows = pl.pallas_call(
            with_routing,
            out_shape=jax.ShapeDtypeStruct((tokens.shape[0], depth + SIDE), jnp.bfloat16),
            in_specs=[HBM] * 3,
            out_specs=VMEM,
            scratch_shapes=[
                pltpu.VMEM(expert_ids.shape, jnp.int32),
                pltpu.VMEM(gate_numer.shape, jnp.int32),
                pltpu.SemaphoreType.DMA((3,)),
            ],
            compiler_params=small,
            name="with_routing",
        )(*own)
        hops = []
        for axis, size in axes:
            by = size // 2
            while by:
                hops.append((axis, size, by))
                by //= 2
        slots = min(SLOTS, units // step_units)
        ring_shapes = [
            pltpu.VMEM((n, step_units, depth), jnp.bfloat16) for n in (slots, slots, slots + 1)
        ]
        ring = []
        early = 0
        for number, hop in enumerate(hops):
            theirs = swap(rows, *hop)
            steps = EARLY[number] if number < len(EARLY) and units >= 8 * step_units else 0
            ends = []
            if steps:
                *ring, end = pl.pallas_call(
                    functools.partial(bring, early, steps),
                    out_shape=ring_shapes + [jax.ShapeDtypeStruct((8, 128), jnp.float32)],
                    in_specs=[HBM] * 3 + [pl.BlockSpec(memory_space=pl.ANY)] + [VMEM] * len(ring),
                    out_specs=[VMEM] * 4,
                    scratch_shapes=[pltpu.SemaphoreType.DMA((3, steps, 2))],
                    input_output_aliases={4 + i: i for i in range(len(ring))},
                    compiler_params=small,
                    cost_estimate=pl.CostEstimate(
                        flops=0,
                        bytes_accessed=6 * steps * step_units * depth,
                        transcendentals=0,
                    ),
                    name="bring_weights",
                )(*weights, rows, *ring)
                early += steps
                ends = [end]
            if hop is hops[-1]:
                break
            count = rows.shape[0]
            if count <= 64:
                rows = pl.pallas_call(
                    join,
                    out_shape=jax.ShapeDtypeStruct((2 * count, depth + SIDE), jnp.bfloat16),
                    in_specs=[VMEM] * 2 + [pl.BlockSpec(memory_space=pl.ANY)] * len(ends),
                    out_specs=VMEM,
                    compiler_params=small,
                    name="join",
                )(rows, theirs, *ends)
            else:
                rows = jnp.concatenate([rows, theirs], axis=0)
        half = rows.shape[0]
        count = 2 * half
        row_block = min(count, 64)
        keep, send, *_ = pl.pallas_call(
            functools.partial(layer, top, ff_dev, row_block, step_units, early),
            out_shape=[
                jax.ShapeDtypeStruct((half, depth), jnp.float32),
                jax.ShapeDtypeStruct((half, depth), jnp.bfloat16),
            ]
            + (ring_shapes if early else []),
            in_specs=[VMEM] * 2 + [HBM] * 3 + [VMEM] * len(ring),
            out_specs=[VMEM] * (5 if early else 2),
            scratch_shapes=([] if early else ring_shapes)
            + [
                pltpu.VMEM((count, depth + SIDE), jnp.bfloat16),
                pltpu.VMEM((count, depth), jnp.float32),
                pltpu.VMEM((count, SIDE), jnp.bfloat16),
                pltpu.VMEM((2, count, step_units), jnp.bfloat16),
                pltpu.SemaphoreType.DMA((3, slots + 1)),
            ],
            input_output_aliases={5 + i: 2 + i for i in range(len(ring))},
            compiler_params=pltpu.CompilerParams(
                vmem_limit_bytes=GRANT if early else 60 << 20
            ),
            cost_estimate=pl.CostEstimate(
                flops=6 * count * units * depth,
                bytes_accessed=6 * (units - early * step_units) * depth,
                transcendentals=count * units,
            ),
            name="expert_layer",
        )(rows, theirs, *weights, *ring)
        total = keep + swap(send, *hops[-1]).astype(jnp.float32)
        for hop in reversed(hops[:-1]):
            half = total.shape[0] // 2
            theirs = swap(total[half:].astype(jnp.bfloat16), *hop)
            total = total[:half] + theirs.astype(jnp.float32)
        return total.astype(jnp.bfloat16)

    return local


def solution(mesh):
    rows = P(("grp", "wide", "sec", "sub"), None)
    weights = P("wide", ("sec", "sub"), None)
    axes = [(name, mesh.shape[name]) for name in ("wide", "sec", "sub")]
    return jax.shard_map(
        build(axes),
        mesh=mesh,
        in_specs=(rows, rows, rows, weights, weights, weights),
        out_specs=rows,
        check_vma=False,
    )
```

time: 64.3 us -> 56.7 us (0.88)
  Pallas kernels: 37 us -> 27.5 us
  starting transfers between devices: 10.1 us -> 13.6 us
  waiting for transfers between devices: 16.1 us -> 14.6 us
    pallas_call x4 -> x3, Pallas kernels: 36.1 us -> 26.5 us  [the longest x1 20.8 us: local(): pl.pallas_call(functools.partial(layer, top, ff_dev, row_block, step_unit...]
    ppermute x8, starting transfers between devices: 10.1 us -> 13.6 us  [swap(): return lax.ppermute(x, axis, [(i, i ^ by) for i in range(size)])]
    ppermute x8, waiting for transfers between devices: 16.1 us -> 14.6 us  [swap(): return lax.ppermute(x, axis, [(i, i ^ by) for i in range(size)])]
  transfers between devices with their start and end apart: 8 -> 8, of which waited for: 6 -> 7; matrix products, arithmetic and copies ran while one was open for 0% -> 0% of each run, Pallas kernels for 19% -> 10%
where the time goes in v7:
time: 56.7 us; the launch traced here: 56.5 us
  Pallas kernels  27.5 us (49%)
  waiting for transfers between devices  14.6 us (26%)
  starting transfers between devices  13.6 us (24%)
  other arithmetic  0.73 us (1%)
    pallas_call x1, Pallas kernels, local(): pl.pallas_call(functools.partial(layer, top, ff_dev, row_block, step_unit...  20.8 us
    ppermute x8, waiting for transfers between devices, swap(): return lax.ppermute(x, axis, [(i, i ^ by) for i in range(size)])  14.6 us
    ppermute x8, starting transfers between devices, swap(): return lax.ppermute(x, axis, [(i, i ^ by) for i in range(size)])  13.6 us
    pallas_call x2, Pallas kernels, local(): pl.pallas_call(functools.partial(bring, early, steps), out_shape=ring_sha...  5.71 us
  transfers between devices with their start and end apart: 8, of which 7 were waited for; matrix products, arithmetic and copies ran while one was open for 0% of the time, Pallas kernels for 10%

profile of v7, /device:TPU:0, one launch (start us, length us, event | category | flops | bytes accessed | tf_op | source)
XLA Modules:
  0.0 56.5 jit_solution(5247585031192653682)
XLA Ops:
  0.0 0.9 %with_routing.1.mine_ref = bf16[4,4224]{1,0:T(4,128)(2,1)S(1)} custom-call(bf16[4,4096]{1,0:T(4,128)(2,1)} %tokens_ref.1, s32[4,8]{1,0:T(4,128)} %ids_ref.1, s32[4,8]{1,0:T(4,128)} %numer_ref.1), custom_call_target="tpu_custom_call" | custom-call | tf_op jit(solution)/shard_map/with_routing/pallas_call | solution.py:196
  0.9 4.1 %collective-permute-start = (bf16[4,4224]{1,0:T(4,128)(2,1)S(1)}, bf16[4,4224]{1,0:T(4,128)(2,1)S(1)}, u32[]{:S(2)}, u32[]{:S(2)}) collective-permute-start(bf16[4,4224]{1,0:T(4,128)(2,1)S(1)} %with_routing.1.mine_ref), channel_id=1, source_target_pairs={{0,8},{4,12},{8,0},{12,4},{1,9},{5,13},{9,1},{13,5},{2,10},{6,14},... | collective-permute-start | bytes 101384 | tf_op jit(solution)/shard_map/ppermute | solution.py:22
  5.0 2.3 %collective-permute-done.theirs_ref = bf16[4,4224]{1,0:T(4,128)(2,1)S(1)} collective-permute-done((bf16[4,4224]{1,0:T(4,128)(2,1)S(1)}, bf16[4,4224]{1,0:T(4,128)(2,1)S(1)}, u32[]{:S(2)}, u32[]{:S(2)}) %collective-permute-start) | collective-permute-done | bytes 33824 | tf_op jit(solution)/shard_map/ppermute | solution.py:22
  7.3 1.6 %collective-permute-start.1 = (bf16[8,4224]{1,0:T(8,128)(2,1)S(1)}, bf16[8,4224]{1,0:T(8,128)(2,1)S(1)}, u32[]{:S(2)}, u32[]{:S(2)}) collective-permute-start(bf16[8,4224]{1,0:T(8,128)(2,1)S(1)} %join.3.after_ref.mine_ref), channel_id=1, source_target_pairs={{0,4},{4,0},{8,12},{12,8},{1,5},{5,1},{9,13},{13,9},{2,6},{6,2},{1... | collective-permute-start | bytes 202760 | tf_op jit(solution)/shard_map/ppermute | solution.py:22
  8.9 2.9 %bring_weights.2 = (bf16[3,256,4096]{2,1,0:T(8,128)(2,1)S(1)}, bf16[3,256,4096]{2,1,0:T(8,128)(2,1)S(1)}, bf16[4,256,4096]{2,1,0:T(8,128)(2,1)S(1)}, f32[8,128]{1,0:T(8,128)S(1)}) custom-call(bf16[3072,4096]{1,0:T(8,128)(2,1)} %bitcast.3, bf16[3072,4096]{1,0:T(8,128)(2,1)} %bitcast.6, bf16[3072,4096]{1,0:T(8,128)(2,1)} %bitcast.9, ...), custom_call_target="tpu_custom_call" | custom-call | bytes 6291456 | tf_op jit(solution)/shard_map/bring_weights/pallas_call | solution.py:226
  11.7 0.0 collective-permute-done.1.theirs_ref
  11.8 1.6 %collective-permute-start.2 = (bf16[16,4224]{1,0:T(8,128)(2,1)S(1)}, bf16[16,4224]{1,0:T(8,128)(2,1)S(1)}, u32[]{:S(2)}, u32[]{:S(2)}) collective-permute-start(bf16[16,4224]{1,0:T(8,128)(2,1)S(1)} %join.4.after_ref.mine_ref), channel_id=1, source_target_pairs={{0,2},{2,0},{1,3},{3,1},{4,6},{6,4},{5,7},{7,5},{8,10},{10,8},{9,1... | collective-permute-start | bytes 405512 | tf_op jit(solution)/shard_map/ppermute | solution.py:22
  13.4 2.9 %bring_weights.3 = (bf16[3,256,4096]{2,1,0:T(8,128)(2,1)S(1)}, bf16[3,256,4096]{2,1,0:T(8,128)(2,1)S(1)}, bf16[4,256,4096]{2,1,0:T(8,128)(2,1)S(1)}, f32[8,128]{1,0:T(8,128)S(1)}) custom-call(bf16[3072,4096]{1,0:T(8,128)(2,1)} %bitcast.4, bf16[3072,4096]{1,0:T(8,128)(2,1)} %bitcast.7, ...), custom_call_target="tpu_custom_call", output_to_operand_aliasing={{0}: (4, {}), {1}: (5, {}), {2}: (6, {})} | custom-call | bytes 6291456 | tf_op jit(solution)/shard_map/bring_weights/pallas_call | solution.py:226
  16.3 0.6 %collective-permute-done.2.theirs_ref = bf16[16,4224]{1,0:T(8,128)(2,1)S(1)} collective-permute-done((bf16[16,4224]{1,0:T(8,128)(2,1)S(1)}, bf16[16,4224]{1,0:T(8,128)(2,1)S(1)}, u32[]{:S(2)}, u32[]{:S(2)}) %collective-permute-start.2) | collective-permute-done | bytes 135200 | tf_op jit(solution)/shard_map/ppermute | solution.py:22
  16.9 0.1 collective-permute-start.3
  16.9 1.5 %collective-permute-done.3.theirs_ref = bf16[32,4224]{1,0:T(8,128)(2,1)S(1)} collective-permute-done((bf16[32,4224]{1,0:T(8,128)(2,1)S(1)}, bf16[32,4224]{1,0:T(8,128)(2,1)S(1)}, u32[]{:S(2)}, u32[]{:S(2)}) %collective-permute-start.3) | collective-permute-done | bytes 270368 | tf_op jit(solution)/shard_map/ppermute | solution.py:22
  18.5 20.8 %expert_layer.1 = (f32[32,4096]{1,0:T(8,128)S(1)}, bf16[32,4096]{1,0:T(8,128)(2,1)S(1)}, bf16[3,256,4096]{2,1,0:T(8,128)(2,1)S(1)}, bf16[3,256,4096]{2,1,0:T(8,128)(2,1)S(1)}, bf16[4,256,4096]{2,1,0:T(8,128)(2,1)S(1)}) custom-call(bf16[32,4224]{1,0:T(8,128)(2,1)S(1)} %join.5.mine_ref, ...), custom_call_target="tpu_custom_call", output_to_operand_aliasing={{2}: (5, {}), {3}: (6, {}), {4}: (7, {})} | custom-call | flops 4831838208 | bytes 62914560 | tf_op jit(solution)/shard_map/expert_layer/pallas_call | solution.py:260
  39.3 0.2 collective-permute-start.4
  39.5 1.4 %collective-permute-done.4 = bf16[32,4096]{1,0:T(8,128)(2,1)S(1)} collective-permute-done((bf16[32,4096]{1,0:T(8,128)(2,1)S(1)}, bf16[32,4096]{1,0:T(8,128)(2,1)S(1)}, u32[]{:S(2)}, u32[]{:S(2)}) %collective-permute-start.4) | collective-permute-done | bytes 262176 | tf_op jit(solution)/shard_map/ppermute | solution.py:22
  40.9 0.1 convert_add_fusion
  41.0 1.6 %collective-permute-start.5 = (bf16[16,4096]{1,0:T(8,128)(2,1)S(1)}, bf16[16,4096]{1,0:T(8,128)(2,1)S(1)}, u32[]{:S(2)}, u32[]{:S(2)}) collective-permute-start(bf16[16,4096]{1,0:T(8,128)(2,1)S(1)} %slice.41), channel_id=1, source_target_pairs={{0,2},{2,0},{1,3},{3,1},{4,6},{6,4},{5,7},{7,5},{8,10},{10,8},{9,1... | collective-permute-start | bytes 393224 | tf_op jit(solution)/shard_map/ppermute | solution.py:22
  42.6 4.0 %collective-permute-done.5 = bf16[16,4096]{1,0:T(8,128)(2,1)S(1)} collective-permute-done((bf16[16,4096]{1,0:T(8,128)(2,1)S(1)}, bf16[16,4096]{1,0:T(8,128)(2,1)S(1)}, u32[]{:S(2)}, u32[]{:S(2)}) %collective-permute-start.5) | collective-permute-done | bytes 131104 | tf_op jit(solution)/shard_map/ppermute | solution.py:22
  46.7 1.5 %collective-permute-start.6 = (bf16[8,4096]{1,0:T(8,128)(2,1)S(1)}, bf16[8,4096]{1,0:T(8,128)(2,1)S(1)}, u32[]{:S(2)}, u32[]{:S(2)}) collective-permute-start(bf16[8,4096]{1,0:T(8,128)(2,1)S(1)} %slice.42), channel_id=1, source_target_pairs={{0,4},{4,0},{8,12},{12,8},{1,5},{5,1},{9,13},{13,9},{2,6},{6,2},{1... | collective-permute-start | bytes 196616 | tf_op jit(solution)/shard_map/ppermute | solution.py:22
  48.1 2.9 %collective-permute-done.6 = bf16[8,4096]{1,0:T(8,128)(2,1)S(1)} collective-permute-done((bf16[8,4096]{1,0:T(8,128)(2,1)S(1)}, bf16[8,4096]{1,0:T(8,128)(2,1)S(1)}, u32[]{:S(2)}, u32[]{:S(2)}) %collective-permute-start.6) | collective-permute-done | bytes 65568 | tf_op jit(solution)/shard_map/ppermute | solution.py:22
  51.0 2.9 %collective-permute-start.7 = (bf16[4,4096]{1,0:T(4,128)(2,1)S(1)}, bf16[4,4096]{1,0:T(4,128)(2,1)S(1)}, u32[]{:S(2)}, u32[]{:S(2)}) collective-permute-start(bf16[4,4096]{1,0:T(4,128)(2,1)S(1)} %slice.43), channel_id=1, source_target_pairs={{0,8},{4,12},{8,0},{12,4},{1,9},{5,13},{9,1},{13,5},{2,10},{6,14},... | collective-permute-start | bytes 98312 | tf_op jit(solution)/shard_map/ppermute | solution.py:22
  53.9 2.0 %collective-permute-done.7 = bf16[4,4096]{1,0:T(4,128)(2,1)S(1)} collective-permute-done((bf16[4,4096]{1,0:T(4,128)(2,1)S(1)}, bf16[4,4096]{1,0:T(4,128)(2,1)S(1)}, u32[]{:S(2)}, u32[]{:S(2)}) %collective-permute-start.7) | collective-permute-done | bytes 32800 | tf_op jit(solution)/shard_map/ppermute | solution.py:22
  55.9 0.6 %fusion = bf16[4,4096]{1,0:T(4,128)(2,1)} fusion(f32[8,4096]{1,0:T(8,128)S(1)} %slice_add_fusion.1, bf16[4,4096]{1,0:T(4,128)(2,1)S(1)} %collective-permute-done.7), kind=kLoop, calls=%fused_computation.7 | loop fusion | flops 49152 | bytes 131072 | tf_op jit(solution)/shard_map/convert_element_type | solution.py:293
  (8 shorter events, 0.1 us)
Async XLA Ops:
  0.9 6.4 %collective-permute-start = (bf16[4,4224]{1,0:T(4,128)(2,1)S(1)}, bf16[4,4224]{1,0:T(4,128)(2,1)S(1)}, u32[]{:S(2)}, u32[]{:S(2)}) collective-permute-start(bf16[4,4224]{1,0:T(4,128)(2,1)S(1)} %with_routing.1.mine_ref), channel_id=1, source_target_pairs={{0,8},{4,12},{8,0},{12,4},{1,9},{5,13},{9,1},{13,5},{2,10},{6,14},... | collective-permute-start | bytes 101384 | tf_op jit(solution)/shard_map/ppermute | solution.py:22
  7.3 4.5 %collective-permute-start.1 = (bf16[8,4224]{1,0:T(8,128)(2,1)S(1)}, bf16[8,4224]{1,0:T(8,128)(2,1)S(1)}, u32[]{:S(2)}, u32[]{:S(2)}) collective-permute-start(bf16[8,4224]{1,0:T(8,128)(2,1)S(1)} %join.3.after_ref.mine_ref), channel_id=1, source_target_pairs={{0,4},{4,0},{8,12},{12,8},{1,5},{5,1},{9,13},{13,9},{2,6},{6,2},{1... | collective-permute-start | bytes 202760 | tf_op jit(solution)/shard_map/ppermute | solution.py:22
  11.8 5.1 %collective-permute-start.2 = (bf16[16,4224]{1,0:T(8,128)(2,1)S(1)}, bf16[16,4224]{1,0:T(8,128)(2,1)S(1)}, u32[]{:S(2)}, u32[]{:S(2)}) collective-permute-start(bf16[16,4224]{1,0:T(8,128)(2,1)S(1)} %join.4.after_ref.mine_ref), channel_id=1, source_target_pairs={{0,2},{2,0},{1,3},{3,1},{4,6},{6,4},{5,7},{7,5},{8,10},{10,8},{9,1... | collective-permute-start | bytes 405512 | tf_op jit(solution)/shard_map/ppermute | solution.py:22
  16.9 1.6 %collective-permute-start.3 = (bf16[32,4224]{1,0:T(8,128)(2,1)S(1)}, bf16[32,4224]{1,0:T(8,128)(2,1)S(1)}, u32[]{:S(2)}, u32[]{:S(2)}) collective-permute-start(bf16[32,4224]{1,0:T(8,128)(2,1)S(1)} %join.5.mine_ref), channel_id=1, source_target_pairs={{0,1},{1,0},{2,3},{3,2},{4,5},{5,4},{6,7},{7,6},{8,9},{9,8},{10,11... | collective-permute-start | bytes 811016 | tf_op jit(solution)/shard_map/ppermute | solution.py:22
  39.3 1.6 %collective-permute-start.4 = (bf16[32,4096]{1,0:T(8,128)(2,1)S(1)}, bf16[32,4096]{1,0:T(8,128)(2,1)S(1)}, u32[]{:S(2)}, u32[]{:S(2)}) collective-permute-start(bf16[32,4096]{1,0:T(8,128)(2,1)S(1)} %get-tuple-element.24), channel_id=1, source_target_pairs={{0,1},{1,0},{2,3},{3,2},{4,5},{5,4},{6,7},{7,6},{8,9},{9,8},{10,11... | collective-permute-start | bytes 786440 | tf_op jit(solution)/shard_map/ppermute | solution.py:22
  41.0 5.6 %collective-permute-start.5 = (bf16[16,4096]{1,0:T(8,128)(2,1)S(1)}, bf16[16,4096]{1,0:T(8,128)(2,1)S(1)}, u32[]{:S(2)}, u32[]{:S(2)}) collective-permute-start(bf16[16,4096]{1,0:T(8,128)(2,1)S(1)} %slice.41), channel_id=1, source_target_pairs={{0,2},{2,0},{1,3},{3,1},{4,6},{6,4},{5,7},{7,5},{8,10},{10,8},{9,1... | collective-permute-start | bytes 393224 | tf_op jit(solution)/shard_map/ppermute | solution.py:22
  46.7 4.3 %collective-permute-start.6 = (bf16[8,4096]{1,0:T(8,128)(2,1)S(1)}, bf16[8,4096]{1,0:T(8,128)(2,1)S(1)}, u32[]{:S(2)}, u32[]{:S(2)}) collective-permute-start(bf16[8,4096]{1,0:T(8,128)(2,1)S(1)} %slice.42), channel_id=1, source_target_pairs={{0,4},{4,0},{8,12},{12,8},{1,5},{5,1},{9,13},{13,9},{2,6},{6,2},{1... | collective-permute-start | bytes 196616 | tf_op jit(solution)/shard_map/ppermute | solution.py:22
  51.0 4.9 %collective-permute-start.7 = (bf16[4,4096]{1,0:T(4,128)(2,1)S(1)}, bf16[4,4096]{1,0:T(4,128)(2,1)S(1)}, u32[]{:S(2)}, u32[]{:S(2)}) collective-permute-start(bf16[4,4096]{1,0:T(4,128)(2,1)S(1)} %slice.43), channel_id=1, source_target_pairs={{0,8},{4,12},{8,0},{12,4},{1,9},{5,13},{9,1},{13,5},{2,10},{6,14},... | collective-permute-start | bytes 98312 | tf_op jit(solution)/shard_map/ppermute | solution.py:22

commit v8 on v7

--- a/solution.py
+++ b/solution.py
@@ -9,8 +9,8 @@
 
 EXPERTS = 32
 SIDE = 128
-SLOTS = 3
-EARLY = (0, 1, 1)
+SLOTS = 4
+EARLY = (1, 1, 2)
 GRANT = 8 << 20
 
 VMEM = pl.BlockSpec(memory_space=pltpu.VMEM)

time: 56.7 us -> 57.8 us (1.019)
  Pallas kernels: 27.5 us -> 31.4 us
  starting transfers between devices: 13.6 us -> 11.9 us
  waiting for transfers between devices: 14.6 us -> 13.4 us
    pallas_call x2 -> x3, Pallas kernels: 5.71 us -> 10.4 us  [local(): pl.pallas_call(functools.partial(bring, early, steps), out_shape=ring_sha...]
    ppermute x8, starting transfers between devices: 13.6 us -> 11.9 us  [swap(): return lax.ppermute(x, axis, [(i, i ^ by) for i in range(size)])]
    ppermute x8, waiting for transfers between devices: 14.6 us -> 13.4 us  [swap(): return lax.ppermute(x, axis, [(i, i ^ by) for i in range(size)])]
    pallas_call x1, Pallas kernels: 20.8 us -> 20.1 us  [local(): pl.pallas_call(functools.partial(layer, top, ff_dev, row_block, step_unit...]
  transfers between devices with their start and end apart: 8 -> 8, of which waited for: 7 -> 5; matrix products, arithmetic and copies ran while one was open for 0% -> 0% of each run, Pallas kernels for 10% -> 18%
where the time goes in v8:
time: 57.8 us; the launch traced here: 57.6 us
  Pallas kernels  31.4 us (54%)
  waiting for transfers between devices  13.4 us (23%)
  starting transfers between devices  11.9 us (21%)
  other arithmetic  0.73 us (1%)
    pallas_call x1, Pallas kernels, local(): pl.pallas_call(functools.partial(layer, top, ff_dev, row_block, step_unit...  20.1 us
    ppermute x8, waiting for transfers between devices, swap(): return lax.ppermute(x, axis, [(i, i ^ by) for i in range(size)])  13.4 us
    ppermute x8, starting transfers between devices, swap(): return lax.ppermute(x, axis, [(i, i ^ by) for i in range(size)])  11.9 us
    pallas_call x3, Pallas kernels, local(): pl.pallas_call(functools.partial(bring, early, steps), out_shape=ring_sha...  10.4 us
  transfers between devices with their start and end apart: 8, of which 5 were waited for; matrix products, arithmetic and copies ran while one was open for 0% of the time, Pallas kernels for 18%

profile of v8, /device:TPU:0, one launch (start us, length us, event | category | flops | bytes accessed | tf_op | source)
XLA Modules:
  0.0 57.6 jit_solution(15906487136594213195)
XLA Ops:
  0.0 0.9 %with_routing.1.after_ref.mine_ref = bf16[4,4224]{1,0:T(4,128)(2,1)S(1)} custom-call(bf16[4,4096]{1,0:T(4,128)(2,1)} %tokens_ref.1, s32[4,8]{1,0:T(4,128)} %ids_ref.1, s32[4,8]{1,0:T(4,128)} %numer_ref.1), custom_call_target="tpu_custom_call" | custom-call | tf_op jit(solution)/shard_map/with_routing/pallas_call | solution.py:196
  0.9 4.1 %collective-permute-start = (bf16[4,4224]{1,0:T(4,128)(2,1)S(1)}, bf16[4,4224]{1,0:T(4,128)(2,1)S(1)}, u32[]{:S(2)}, u32[]{:S(2)}) collective-permute-start(bf16[4,4224]{1,0:T(4,128)(2,1)S(1)} %with_routing.1.after_ref.mine_ref), channel_id=1, source_target_pairs={{0,8},{4,12},{8,0},{12,4},{1,9},{5,13},{9,1},{13,5},{2,10},{6,14},... | collective-permute-start | bytes 101384 | tf_op jit(solution)/shard_map/ppermute | solution.py:22
  5.0 2.9 %bring_weights.3 = (bf16[4,256,4096]{2,1,0:T(8,128)(2,1)S(1)}, bf16[4,256,4096]{2,1,0:T(8,128)(2,1)S(1)}, bf16[5,256,4096]{2,1,0:T(8,128)(2,1)S(1)}, f32[8,128]{1,0:T(8,128)S(1)}) custom-call(bf16[3072,4096]{1,0:T(8,128)(2,1)} %bitcast.3, bf16[3072,4096]{1,0:T(8,128)(2,1)} %bitcast.7, bf16[3072,4096]{1,0:T(8,128)(2,1)} %bitcast.11, ...), custom_call_target="tpu_custom_call" | custom-call | bytes 6291456 | tf_op jit(solution)/shard_map/bring_weights/pallas_call | solution.py:226
  7.8 0.0 collective-permute-done.theirs_ref
  7.9 1.6 %collective-permute-start.1 = (bf16[8,4224]{1,0:T(8,128)(2,1)S(1)}, bf16[8,4224]{1,0:T(8,128)(2,1)S(1)}, u32[]{:S(2)}, u32[]{:S(2)}) collective-permute-start(bf16[8,4224]{1,0:T(8,128)(2,1)S(1)} %join.3.after_ref.mine_ref), channel_id=1, source_target_pairs={{0,4},{4,0},{8,12},{12,8},{1,5},{5,1},{9,13},{13,9},{2,6},{6,2},{1... | collective-permute-start | bytes 202760 | tf_op jit(solution)/shard_map/ppermute | solution.py:22
  9.5 2.9 %bring_weights.4 = (bf16[4,256,4096]{2,1,0:T(8,128)(2,1)S(1)}, bf16[4,256,4096]{2,1,0:T(8,128)(2,1)S(1)}, bf16[5,256,4096]{2,1,0:T(8,128)(2,1)S(1)}, f32[8,128]{1,0:T(8,128)S(1)}) custom-call(bf16[3072,4096]{1,0:T(8,128)(2,1)} %bitcast.4, bf16[3072,4096]{1,0:T(8,128)(2,1)} %bitcast.8, ...), custom_call_target="tpu_custom_call", output_to_operand_aliasing={{0}: (4, {}), {1}: (5, {}), {2}: (6, {})} | custom-call | bytes 6291456 | tf_op jit(solution)/shard_map/bring_weights/pallas_call | solution.py:226
  12.4 0.0 collective-permute-done.1.theirs_ref
  12.4 1.6 %collective-permute-start.2 = (bf16[16,4224]{1,0:T(8,128)(2,1)S(1)}, bf16[16,4224]{1,0:T(8,128)(2,1)S(1)}, u32[]{:S(2)}, u32[]{:S(2)}) collective-permute-start(bf16[16,4224]{1,0:T(8,128)(2,1)S(1)} %join.4.after_ref.mine_ref), channel_id=1, source_target_pairs={{0,2},{2,0},{1,3},{3,1},{4,6},{6,4},{5,7},{7,5},{8,10},{10,8},{9,1... | collective-permute-start | bytes 405512 | tf_op jit(solution)/shard_map/ppermute | solution.py:22
  14.0 4.7 %bring_weights.5 = (bf16[4,256,4096]{2,1,0:T(8,128)(2,1)S(1)}, bf16[4,256,4096]{2,1,0:T(8,128)(2,1)S(1)}, bf16[5,256,4096]{2,1,0:T(8,128)(2,1)S(1)}, f32[8,128]{1,0:T(8,128)S(1)}) custom-call(bf16[3072,4096]{1,0:T(8,128)(2,1)} %bitcast.5, bf16[3072,4096]{1,0:T(8,128)(2,1)} %bitcast.9, ...), custom_call_target="tpu_custom_call", output_to_operand_aliasing={{0}: (4, {}), {1}: (5, {}), {2}: (6, {})} | custom-call | bytes 12582912 | tf_op jit(solution)/shard_map/bring_weights/pallas_call | solution.py:226
  18.7 0.0 collective-permute-done.2.theirs_ref
  18.7 0.1 collective-permute-start.3
  18.8 1.5 %collective-permute-done.3.theirs_ref = bf16[32,4224]{1,0:T(8,128)(2,1)S(1)} collective-permute-done((bf16[32,4224]{1,0:T(8,128)(2,1)S(1)}, bf16[32,4224]{1,0:T(8,128)(2,1)S(1)}, u32[]{:S(2)}, u32[]{:S(2)}) %collective-permute-start.3) | collective-permute-done | bytes 270368 | tf_op jit(solution)/shard_map/ppermute | solution.py:22
  20.3 20.1 %expert_layer.1 = (f32[32,4096]{1,0:T(8,128)S(1)}, bf16[32,4096]{1,0:T(8,128)(2,1)S(1)}, bf16[4,256,4096]{2,1,0:T(8,128)(2,1)S(1)}, bf16[4,256,4096]{2,1,0:T(8,128)(2,1)S(1)}, bf16[5,256,4096]{2,1,0:T(8,128)(2,1)S(1)}) custom-call(bf16[32,4224]{1,0:T(8,128)(2,1)S(1)} %join.5.mine_ref, ...), custom_call_target="tpu_custom_call", output_to_operand_aliasing={{2}: (5, {}), {3}: (6, {}), {4}: (7, {})} | custom-call | flops 4831838208 | bytes 50331648 | tf_op jit(solution)/shard_map/expert_layer/pallas_call | solution.py:260
  40.4 0.2 collective-permute-start.4
  40.6 1.4 %collective-permute-done.4 = bf16[32,4096]{1,0:T(8,128)(2,1)S(1)} collective-permute-done((bf16[32,4096]{1,0:T(8,128)(2,1)S(1)}, bf16[32,4096]{1,0:T(8,128)(2,1)S(1)}, u32[]{:S(2)}, u32[]{:S(2)}) %collective-permute-start.4) | collective-permute-done | bytes 262176 | tf_op jit(solution)/shard_map/ppermute | solution.py:22
  42.0 0.1 convert_add_fusion
  42.1 0.6 %collective-permute-start.5 = (bf16[16,4096]{1,0:T(8,128)(2,1)S(1)}, bf16[16,4096]{1,0:T(8,128)(2,1)S(1)}, u32[]{:S(2)}, u32[]{:S(2)}) collective-permute-start(bf16[16,4096]{1,0:T(8,128)(2,1)S(1)} %slice.41), channel_id=1, source_target_pairs={{0,2},{2,0},{1,3},{3,1},{4,6},{6,4},{5,7},{7,5},{8,10},{10,8},{9,1... | collective-permute-start | bytes 393224 | tf_op jit(solution)/shard_map/ppermute | solution.py:22
  42.7 5.0 %collective-permute-done.5 = bf16[16,4096]{1,0:T(8,128)(2,1)S(1)} collective-permute-done((bf16[16,4096]{1,0:T(8,128)(2,1)S(1)}, bf16[16,4096]{1,0:T(8,128)(2,1)S(1)}, u32[]{:S(2)}, u32[]{:S(2)}) %collective-permute-start.5) | collective-permute-done | bytes 131104 | tf_op jit(solution)/shard_map/ppermute | solution.py:22
  47.8 1.5 %collective-permute-start.6 = (bf16[8,4096]{1,0:T(8,128)(2,1)S(1)}, bf16[8,4096]{1,0:T(8,128)(2,1)S(1)}, u32[]{:S(2)}, u32[]{:S(2)}) collective-permute-start(bf16[8,4096]{1,0:T(8,128)(2,1)S(1)} %slice.42), channel_id=1, source_target_pairs={{0,4},{4,0},{8,12},{12,8},{1,5},{5,1},{9,13},{13,9},{2,6},{6,2},{1... | collective-permute-start | bytes 196616 | tf_op jit(solution)/shard_map/ppermute | solution.py:22
  49.2 2.9 %collective-permute-done.6 = bf16[8,4096]{1,0:T(8,128)(2,1)S(1)} collective-permute-done((bf16[8,4096]{1,0:T(8,128)(2,1)S(1)}, bf16[8,4096]{1,0:T(8,128)(2,1)S(1)}, u32[]{:S(2)}, u32[]{:S(2)}) %collective-permute-start.6) | collective-permute-done | bytes 65568 | tf_op jit(solution)/shard_map/ppermute | solution.py:22
  52.1 2.3 %collective-permute-start.7 = (bf16[4,4096]{1,0:T(4,128)(2,1)S(1)}, bf16[4,4096]{1,0:T(4,128)(2,1)S(1)}, u32[]{:S(2)}, u32[]{:S(2)}) collective-permute-start(bf16[4,4096]{1,0:T(4,128)(2,1)S(1)} %slice.43), channel_id=1, source_target_pairs={{0,8},{4,12},{8,0},{12,4},{1,9},{5,13},{9,1},{13,5},{2,10},{6,14},... | collective-permute-start | bytes 98312 | tf_op jit(solution)/shard_map/ppermute | solution.py:22
  54.4 2.6 %collective-permute-done.7 = bf16[4,4096]{1,0:T(4,128)(2,1)S(1)} collective-permute-done((bf16[4,4096]{1,0:T(4,128)(2,1)S(1)}, bf16[4,4096]{1,0:T(4,128)(2,1)S(1)}, u32[]{:S(2)}, u32[]{:S(2)}) %collective-permute-start.7) | collective-permute-done | bytes 32800 | tf_op jit(solution)/shard_map/ppermute | solution.py:22
  57.0 0.6 %fusion = bf16[4,4096]{1,0:T(4,128)(2,1)} fusion(f32[8,4096]{1,0:T(8,128)S(1)} %slice_add_fusion.1, bf16[4,4096]{1,0:T(4,128)(2,1)S(1)} %collective-permute-done.7), kind=kLoop, calls=%fused_computation.7 | loop fusion | flops 49152 | bytes 131072 | tf_op jit(solution)/shard_map/convert_element_type | solution.py:293
  (8 shorter events, 0.1 us)
Async XLA Ops:
  0.9 7.0 %collective-permute-start = (bf16[4,4224]{1,0:T(4,128)(2,1)S(1)}, bf16[4,4224]{1,0:T(4,128)(2,1)S(1)}, u32[]{:S(2)}, u32[]{:S(2)}) collective-permute-start(bf16[4,4224]{1,0:T(4,128)(2,1)S(1)} %with_routing.1.after_ref.mine_ref), channel_id=1, source_target_pairs={{0,8},{4,12},{8,0},{12,4},{1,9},{5,13},{9,1},{13,5},{2,10},{6,14},... | collective-permute-start | bytes 101384 | tf_op jit(solution)/shard_map/ppermute | solution.py:22
  7.9 4.5 %collective-permute-start.1 = (bf16[8,4224]{1,0:T(8,128)(2,1)S(1)}, bf16[8,4224]{1,0:T(8,128)(2,1)S(1)}, u32[]{:S(2)}, u32[]{:S(2)}) collective-permute-start(bf16[8,4224]{1,0:T(8,128)(2,1)S(1)} %join.3.after_ref.mine_ref), channel_id=1, source_target_pairs={{0,4},{4,0},{8,12},{12,8},{1,5},{5,1},{9,13},{13,9},{2,6},{6,2},{1... | collective-permute-start | bytes 202760 | tf_op jit(solution)/shard_map/ppermute | solution.py:22
  12.4 6.3 %collective-permute-start.2 = (bf16[16,4224]{1,0:T(8,128)(2,1)S(1)}, bf16[16,4224]{1,0:T(8,128)(2,1)S(1)}, u32[]{:S(2)}, u32[]{:S(2)}) collective-permute-start(bf16[16,4224]{1,0:T(8,128)(2,1)S(1)} %join.4.after_ref.mine_ref), channel_id=1, source_target_pairs={{0,2},{2,0},{1,3},{3,1},{4,6},{6,4},{5,7},{7,5},{8,10},{10,8},{9,1... | collective-permute-start | bytes 405512 | tf_op jit(solution)/shard_map/ppermute | solution.py:22
  18.7 1.6 %collective-permute-start.3 = (bf16[32,4224]{1,0:T(8,128)(2,1)S(1)}, bf16[32,4224]{1,0:T(8,128)(2,1)S(1)}, u32[]{:S(2)}, u32[]{:S(2)}) collective-permute-start(bf16[32,4224]{1,0:T(8,128)(2,1)S(1)} %join.5.mine_ref), channel_id=1, source_target_pairs={{0,1},{1,0},{2,3},{3,2},{4,5},{5,4},{6,7},{7,6},{8,9},{9,8},{10,11... | collective-permute-start | bytes 811016 | tf_op jit(solution)/shard_map/ppermute | solution.py:22
  40.4 1.6 %collective-permute-start.4 = (bf16[32,4096]{1,0:T(8,128)(2,1)S(1)}, bf16[32,4096]{1,0:T(8,128)(2,1)S(1)}, u32[]{:S(2)}, u32[]{:S(2)}) collective-permute-start(bf16[32,4096]{1,0:T(8,128)(2,1)S(1)} %get-tuple-element.32), channel_id=1, source_target_pairs={{0,1},{1,0},{2,3},{3,2},{4,5},{5,4},{6,7},{7,6},{8,9},{9,8},{10,11... | collective-permute-start | bytes 786440 | tf_op jit(solution)/shard_map/ppermute | solution.py:22
  42.1 5.6 %collective-permute-start.5 = (bf16[16,4096]{1,0:T(8,128)(2,1)S(1)}, bf16[16,4096]{1,0:T(8,128)(2,1)S(1)}, u32[]{:S(2)}, u32[]{:S(2)}) collective-permute-start(bf16[16,4096]{1,0:T(8,128)(2,1)S(1)} %slice.41), channel_id=1, source_target_pairs={{0,2},{2,0},{1,3},{3,1},{4,6},{6,4},{5,7},{7,5},{8,10},{10,8},{9,1... | collective-permute-start | bytes 393224 | tf_op jit(solution)/shard_map/ppermute | solution.py:22
  47.8 4.3 %collective-permute-start.6 = (bf16[8,4096]{1,0:T(8,128)(2,1)S(1)}, bf16[8,4096]{1,0:T(8,128)(2,1)S(1)}, u32[]{:S(2)}, u32[]{:S(2)}) collective-permute-start(bf16[8,4096]{1,0:T(8,128)(2,1)S(1)} %slice.42), channel_id=1, source_target_pairs={{0,4},{4,0},{8,12},{12,8},{1,5},{5,1},{9,13},{13,9},{2,6},{6,2},{1... | collective-permute-start | bytes 196616 | tf_op jit(solution)/shard_map/ppermute | solution.py:22
  52.1 4.9 %collective-permute-start.7 = (bf16[4,4096]{1,0:T(4,128)(2,1)S(1)}, bf16[4,4096]{1,0:T(4,128)(2,1)S(1)}, u32[]{:S(2)}, u32[]{:S(2)}) collective-permute-start(bf16[4,4096]{1,0:T(4,128)(2,1)S(1)} %slice.43), channel_id=1, source_target_pairs={{0,8},{4,12},{8,0},{12,4},{1,9},{5,13},{9,1},{13,5},{2,10},{6,14},... | collective-permute-start | bytes 98312 | tf_op jit(solution)/shard_map/ppermute | solution.py:22

commit v9 on v7

--- a/solution.py
+++ b/solution.py
@@ -19,7 +19,16 @@
 
 
 def swap(x, axis, size, by):
-    return lax.ppermute(x, axis, [(i, i ^ by) for i in range(size)])
+    if axis == "sub":
+        return [lax.ppermute(x, axis, [(i, i ^ by) for i in range(size)])]
+    return [
+        lax.ppermute(x, axis, [(i, i ^ by) for i in range(size) if i & by == way])
+        for way in (0, by)
+    ]
+
+
+def received(theirs):
+    return sum(t.astype(jnp.float32) for t in theirs)
 
 
 def with_routing(tokens_ref, ids_ref, numer_ref, out_ref, ids, numer, sem):
@@ -36,11 +45,11 @@
     out_ref[:, depth:] = side.astype(jnp.float32).astype(jnp.bfloat16)
 
 
-def join(mine_ref, theirs_ref, *refs):
+def join(mine_ref, up_ref, down_ref, *refs):
     out_ref = refs[-1]
     count = mine_ref.shape[0]
     out_ref[:count, :] = mine_ref[...]
-    out_ref[count:, :] = theirs_ref[...]
+    out_ref[count:, :] = up_ref[...] + down_ref[...]
 
 
 def bring(first, count, gate_ref, up_ref, down_ref, after_ref, *refs):
@@ -247,13 +256,13 @@
                 rows = pl.pallas_call(
                     join,
                     out_shape=jax.ShapeDtypeStruct((2 * count, depth + SIDE), jnp.bfloat16),
-                    in_specs=[VMEM] * 2 + [pl.BlockSpec(memory_space=pl.ANY)] * len(ends),
+                    in_specs=[VMEM] * 3 + [pl.BlockSpec(memory_space=pl.ANY)] * len(ends),
                     out_specs=VMEM,
                     compiler_params=small,
                     name="join",
-                )(rows, theirs, *ends)
+                )(rows, *theirs, *ends)
             else:
-                rows = jnp.concatenate([rows, theirs], axis=0)
+                rows = jnp.concatenate([rows, sum(theirs)], axis=0)
         half = rows.shape[0]
         count = 2 * half
         row_block = min(count, 64)
@@ -284,12 +293,12 @@
                 transcendentals=count * units,
             ),
             name="expert_layer",
-        )(rows, theirs, *weights, *ring)
-        total = keep + swap(send, *hops[-1]).astype(jnp.float32)
+        )(rows, *theirs, *weights, *ring)
+        total = keep + received(swap(send, *hops[-1]))
         for hop in reversed(hops[:-1]):
             half = total.shape[0] // 2
             theirs = swap(total[half:].astype(jnp.bfloat16), *hop)
-            total = total[:half] + theirs.astype(jnp.float32)
+            total = total[:half] + received(theirs)
         return total.astype(jnp.bfloat16)
 
     return local

time: 56.7 us -> 85 us (1.50)
  starting transfers between devices: 13.6 us -> 35.5 us
  waiting for transfers between devices: 14.6 us -> 20.6 us
    ppermute x8 -> x14, starting transfers between devices: 13.6 us -> 35.5 us  [the longest x12 35.2 us: swap(): lax.ppermute(x, axis, [(i, i ^ by) for i in range(size) if i & by == way])]
    ppermute x8 -> x14, waiting for transfers between devices: 14.6 us -> 20.6 us  [the longest x12 17.7 us: swap(): lax.ppermute(x, axis, [(i, i ^ by) for i in range(size) if i & by == way])]
  transfers between devices with their start and end apart: 8 -> 14, of which waited for: 7 -> 9; matrix products, arithmetic and copies ran while one was open for 0% -> 0% of each run, Pallas kernels for 10% -> 7%
where the time goes in v9:
time: 85 us; the launch traced here: 84.6 us
  starting transfers between devices  35.5 us (42%)
  Pallas kernels  27.5 us (32%)
  waiting for transfers between devices  20.6 us (24%)
    ppermute x12, starting transfers between devices, swap(): lax.ppermute(x, axis, [(i, i ^ by) for i in range(size) if i & by == way])  35.2 us
    pallas_call x1, Pallas kernels, local(): pl.pallas_call(functools.partial(layer, top, ff_dev, row_block, step_unit...  20.8 us
    ppermute x12, waiting for transfers between devices, swap(): lax.ppermute(x, axis, [(i, i ^ by) for i in range(size) if i & by == way])  17.7 us
    pallas_call x2, Pallas kernels, local(): pl.pallas_call(functools.partial(bring, early, steps), out_shape=ring_sha...  5.72 us
    ppermute x2, waiting for transfers between devices, swap(): return [lax.ppermute(x, axis, [(i, i ^ by) for i in range(size)])]  2.93 us
  transfers between devices with their start and end apart: 14, of which 9 were waited for; matrix products, arithmetic and copies ran while one was open for 0% of the time, Pallas kernels for 7%

profile of v9, /device:TPU:0, one launch (start us, length us, event | category | flops | bytes accessed | tf_op | source)
XLA Modules:
  0.0 84.6 jit_solution(6698771226241428756)
XLA Ops:
  0.0 0.9 %with_routing.1.mine_ref = bf16[4,4224]{1,0:T(4,128)(2,1)S(1)} custom-call(bf16[4,4096]{1,0:T(4,128)(2,1)} %tokens_ref.1, s32[4,8]{1,0:T(4,128)} %ids_ref.1, s32[4,8]{1,0:T(4,128)} %numer_ref.1), custom_call_target="tpu_custom_call" | custom-call | tf_op jit(solution)/shard_map/with_routing/pallas_call | solution.py:205
  0.9 1.3 %collective-permute-start.1 = (bf16[4,4224]{1,0:T(4,128)(2,1)S(1)}, bf16[4,4224]{1,0:T(4,128)(2,1)S(1)}, u32[]{:S(2)}, u32[]{:S(2)}) collective-permute-start(bf16[4,4224]{1,0:T(4,128)(2,1)S(1)} %with_routing.1.mine_ref), channel_id=1, source_target_pairs={{8,0},{12,4},{9,1},{13,5},{10,2},{14,6},{11,3},{15,7},{24,16},{28,... | collective-permute-start | bytes 101384 | tf_op jit(solution)/shard_map/ppermute | solution.py:25
  2.2 5.9 %collective-permute-start = (bf16[4,4224]{1,0:T(4,128)(2,1)S(1)}, bf16[4,4224]{1,0:T(4,128)(2,1)S(1)}, u32[]{:S(2)}, u32[]{:S(2)}) collective-permute-start(bf16[4,4224]{1,0:T(4,128)(2,1)S(1)} %with_routing.1.mine_ref), channel_id=1, source_target_pairs={{0,8},{4,12},{1,9},{5,13},{2,10},{6,14},{3,11},{7,15},{16,24},{20,... | collective-permute-start | bytes 101384 | tf_op jit(solution)/shard_map/ppermute | solution.py:25
  8.1 0.0 collective-permute-done.1.down_ref
  8.1 1.6 %collective-permute-done.up_ref = bf16[4,4224]{1,0:T(4,128)(2,1)S(1)} collective-permute-done((bf16[4,4224]{1,0:T(4,128)(2,1)S(1)}, bf16[4,4224]{1,0:T(4,128)(2,1)S(1)}, u32[]{:S(2)}, u32[]{:S(2)}) %collective-permute-start) | collective-permute-done | bytes 33824 | tf_op jit(solution)/shard_map/ppermute | solution.py:25
  9.7 1.3 %collective-permute-start.3 = (bf16[8,4224]{1,0:T(8,128)(2,1)S(1)}, bf16[8,4224]{1,0:T(8,128)(2,1)S(1)}, u32[]{:S(2)}, u32[]{:S(2)}) collective-permute-start(bf16[8,4224]{1,0:T(8,128)(2,1)S(1)} %join.3.after_ref.mine_ref), channel_id=1, source_target_pairs={{4,0},{12,8},{5,1},{13,9},{6,2},{14,10},{7,3},{15,11},{20,16},{28,... | collective-permute-start | bytes 202760 | tf_op jit(solution)/shard_map/ppermute | solution.py:25
  11.0 4.5 %collective-permute-start.2 = (bf16[8,4224]{1,0:T(8,128)(2,1)S(1)}, bf16[8,4224]{1,0:T(8,128)(2,1)S(1)}, u32[]{:S(2)}, u32[]{:S(2)}) collective-permute-start(bf16[8,4224]{1,0:T(8,128)(2,1)S(1)} %join.3.after_ref.mine_ref), channel_id=1, source_target_pairs={{0,4},{8,12},{1,5},{9,13},{2,6},{10,14},{3,7},{11,15},{16,20},{24,... | collective-permute-start | bytes 202760 | tf_op jit(solution)/shard_map/ppermute | solution.py:25
  15.6 2.9 %bring_weights.2 = (bf16[3,256,4096]{2,1,0:T(8,128)(2,1)S(1)}, bf16[3,256,4096]{2,1,0:T(8,128)(2,1)S(1)}, bf16[4,256,4096]{2,1,0:T(8,128)(2,1)S(1)}, f32[8,128]{1,0:T(8,128)S(1)}) custom-call(bf16[3072,4096]{1,0:T(8,128)(2,1)} %bitcast.3, bf16[3072,4096]{1,0:T(8,128)(2,1)} %bitcast.6, bf16[3072,4096]{1,0:T(8,128)(2,1)} %bitcast.9, ...), custom_call_target="tpu_custom_call" | custom-call | bytes 6291456 | tf_op jit(solution)/shard_map/bring_weights/pallas_call | solution.py:235
  18.5 0.0 collective-permute-done.3.down_ref
  18.5 0.0 collective-permute-done.2.up_ref
  18.5 1.3 %collective-permute-start.5 = (bf16[16,4224]{1,0:T(8,128)(2,1)S(1)}, bf16[16,4224]{1,0:T(8,128)(2,1)S(1)}, u32[]{:S(2)}, u32[]{:S(2)}) collective-permute-start(bf16[16,4224]{1,0:T(8,128)(2,1)S(1)} %join.4.after_ref.mine_ref), channel_id=1, source_target_pairs={{2,0},{3,1},{6,4},{7,5},{10,8},{11,9},{14,12},{15,13},{18,16},{19,... | collective-permute-start | bytes 405512 | tf_op jit(solution)/shard_map/ppermute | solution.py:25
  19.8 4.6 %collective-permute-start.4 = (bf16[16,4224]{1,0:T(8,128)(2,1)S(1)}, bf16[16,4224]{1,0:T(8,128)(2,1)S(1)}, u32[]{:S(2)}, u32[]{:S(2)}) collective-permute-start(bf16[16,4224]{1,0:T(8,128)(2,1)S(1)} %join.4.after_ref.mine_ref), channel_id=1, source_target_pairs={{0,2},{1,3},{4,6},{5,7},{8,10},{9,11},{12,14},{13,15},{16,18},{17,... | collective-permute-start | bytes 405512 | tf_op jit(solution)/shard_map/ppermute | solution.py:25
  24.4 2.9 %bring_weights.3 = (bf16[3,256,4096]{2,1,0:T(8,128)(2,1)S(1)}, bf16[3,256,4096]{2,1,0:T(8,128)(2,1)S(1)}, bf16[4,256,4096]{2,1,0:T(8,128)(2,1)S(1)}, f32[8,128]{1,0:T(8,128)S(1)}) custom-call(bf16[3072,4096]{1,0:T(8,128)(2,1)} %bitcast.4, bf16[3072,4096]{1,0:T(8,128)(2,1)} %bitcast.7, ...), custom_call_target="tpu_custom_call", output_to_operand_aliasing={{0}: (4, {}), {1}: (5, {}), {2}: (6, {})} | custom-call | bytes 6291456 | tf_op jit(solution)/shard_map/bring_weights/pallas_call | solution.py:235
  27.2 0.0 collective-permute-done.5.down_ref
  27.2 0.0 collective-permute-done.4.up_ref
  27.3 0.1 collective-permute-start.6
  27.4 1.5 %collective-permute-done.6.theirs_ref = bf16[32,4224]{1,0:T(8,128)(2,1)S(1)} collective-permute-done((bf16[32,4224]{1,0:T(8,128)(2,1)S(1)}, bf16[32,4224]{1,0:T(8,128)(2,1)S(1)}, u32[]{:S(2)}, u32[]{:S(2)}) %collective-permute-start.6) | collective-permute-done | bytes 270368 | tf_op jit(solution)/shard_map/ppermute | solution.py:23
  28.9 20.8 %expert_layer.1 = (f32[32,4096]{1,0:T(8,128)S(1)}, bf16[32,4096]{1,0:T(8,128)(2,1)S(1)}, bf16[3,256,4096]{2,1,0:T(8,128)(2,1)S(1)}, bf16[3,256,4096]{2,1,0:T(8,128)(2,1)S(1)}, bf16[4,256,4096]{2,1,0:T(8,128)(2,1)S(1)}) custom-call(bf16[32,4224]{1,0:T(8,128)(2,1)S(1)} %join.5.mine_ref, ...), custom_call_target="tpu_custom_call", output_to_operand_aliasing={{2}: (5, {}), {3}: (6, {}), {4}: (7, {})} | custom-call | flops 4831838208 | bytes 62914560 | tf_op jit(solution)/shard_map/expert_layer/pallas_call | solution.py:269
  49.7 0.2 collective-permute-start.7
  50.0 1.4 %collective-permute-done.7 = bf16[32,4096]{1,0:T(8,128)(2,1)S(1)} collective-permute-done((bf16[32,4096]{1,0:T(8,128)(2,1)S(1)}, bf16[32,4096]{1,0:T(8,128)(2,1)S(1)}, u32[]{:S(2)}, u32[]{:S(2)}) %collective-permute-start.7) | collective-permute-done | bytes 262176 | tf_op jit(solution)/shard_map/ppermute | solution.py:23
  51.4 0.1 convert_add_fusion
  51.4 4.0 %collective-permute-start.8 = (bf16[16,4096]{1,0:T(8,128)(2,1)S(1)}, bf16[16,4096]{1,0:T(8,128)(2,1)S(1)}, u32[]{:S(2)}, u32[]{:S(2)}) collective-permute-start(bf16[16,4096]{1,0:T(8,128)(2,1)S(1)} %slice.41), channel_id=1, source_target_pairs={{0,2},{1,3},{4,6},{5,7},{8,10},{9,11},{12,14},{13,15},{16,18},{17,... | collective-permute-start | bytes 393224 | tf_op jit(solution)/shard_map/ppermute | solution.py:25
  55.5 1.3 %collective-permute-start.9 = (bf16[16,4096]{1,0:T(8,128)(2,1)S(1)}, bf16[16,4096]{1,0:T(8,128)(2,1)S(1)}, u32[]{:S(2)}, u32[]{:S(2)}) collective-permute-start(bf16[16,4096]{1,0:T(8,128)(2,1)S(1)} %slice.41), channel_id=1, source_target_pairs={{2,0},{3,1},{6,4},{7,5},{10,8},{11,9},{14,12},{15,13},{18,16},{19,... | collective-permute-start | bytes 393224 | tf_op jit(solution)/shard_map/ppermute | solution.py:25
  56.8 1.7 %collective-permute-done.8 = bf16[16,4096]{1,0:T(8,128)(2,1)S(1)} collective-permute-done((bf16[16,4096]{1,0:T(8,128)(2,1)S(1)}, bf16[16,4096]{1,0:T(8,128)(2,1)S(1)}, u32[]{:S(2)}, u32[]{:S(2)}) %collective-permute-start.8) | collective-permute-done | bytes 131104 | tf_op jit(solution)/shard_map/ppermute | solution.py:25
  58.5 4.1 %collective-permute-done.9 = bf16[16,4096]{1,0:T(8,128)(2,1)S(1)} collective-permute-done((bf16[16,4096]{1,0:T(8,128)(2,1)S(1)}, bf16[16,4096]{1,0:T(8,128)(2,1)S(1)}, u32[]{:S(2)}, u32[]{:S(2)}) %collective-permute-start.9) | collective-permute-done | bytes 131104 | tf_op jit(solution)/shard_map/ppermute | solution.py:25
  62.7 3.3 %collective-permute-start.10 = (bf16[8,4096]{1,0:T(8,128)(2,1)S(1)}, bf16[8,4096]{1,0:T(8,128)(2,1)S(1)}, u32[]{:S(2)}, u32[]{:S(2)}) collective-permute-start(bf16[8,4096]{1,0:T(8,128)(2,1)S(1)} %slice.42), channel_id=1, source_target_pairs={{0,4},{8,12},{1,5},{9,13},{2,6},{10,14},{3,7},{11,15},{16,20},{24,... | collective-permute-start | bytes 196616 | tf_op jit(solution)/shard_map/ppermute | solution.py:25
  65.9 1.3 %collective-permute-start.11 = (bf16[8,4096]{1,0:T(8,128)(2,1)S(1)}, bf16[8,4096]{1,0:T(8,128)(2,1)S(1)}, u32[]{:S(2)}, u32[]{:S(2)}) collective-permute-start(bf16[8,4096]{1,0:T(8,128)(2,1)S(1)} %slice.42), channel_id=1, source_target_pairs={{4,0},{12,8},{5,1},{13,9},{6,2},{14,10},{7,3},{15,11},{20,16},{28,... | collective-permute-start | bytes 196616 | tf_op jit(solution)/shard_map/ppermute | solution.py:25
  67.2 0.6 collective-permute-done.10
  67.8 4.3 %collective-permute-done.11 = bf16[8,4096]{1,0:T(8,128)(2,1)S(1)} collective-permute-done((bf16[8,4096]{1,0:T(8,128)(2,1)S(1)}, bf16[8,4096]{1,0:T(8,128)(2,1)S(1)}, u32[]{:S(2)}, u32[]{:S(2)}) %collective-permute-start.11) | collective-permute-done | bytes 65568 | tf_op jit(solution)/shard_map/ppermute | solution.py:25
  72.2 5.1 %collective-permute-start.12 = (bf16[4,4096]{1,0:T(4,128)(2,1)S(1)}, bf16[4,4096]{1,0:T(4,128)(2,1)S(1)}, u32[]{:S(2)}, u32[]{:S(2)}) collective-permute-start(bf16[4,4096]{1,0:T(4,128)(2,1)S(1)} %slice.43), channel_id=1, source_target_pairs={{0,8},{4,12},{1,9},{5,13},{2,10},{6,14},{3,11},{7,15},{16,24},{20,... | collective-permute-start | bytes 98312 | tf_op jit(solution)/shard_map/ppermute | solution.py:25
  77.3 1.3 %collective-permute-start.13 = (bf16[4,4096]{1,0:T(4,128)(2,1)S(1)}, bf16[4,4096]{1,0:T(4,128)(2,1)S(1)}, u32[]{:S(2)}, u32[]{:S(2)}) collective-permute-start(bf16[4,4096]{1,0:T(4,128)(2,1)S(1)} %slice.43), channel_id=1, source_target_pairs={{8,0},{12,4},{9,1},{13,5},{10,2},{14,6},{11,3},{15,7},{24,16},{28,... | collective-permute-start | bytes 98312 | tf_op jit(solution)/shard_map/ppermute | solution.py:25
  78.6 0.3 collective-permute-done.12
  78.9 5.1 %collective-permute-done.13 = bf16[4,4096]{1,0:T(4,128)(2,1)S(1)} collective-permute-done((bf16[4,4096]{1,0:T(4,128)(2,1)S(1)}, bf16[4,4096]{1,0:T(4,128)(2,1)S(1)}, u32[]{:S(2)}, u32[]{:S(2)}) %collective-permute-start.13) | collective-permute-done | bytes 32800 | tf_op jit(solution)/shard_map/ppermute | solution.py:25
  84.0 0.6 fusion
  (8 shorter events, 0.2 us)
Async XLA Ops:
  0.9 7.3 %collective-permute-start.1 = (bf16[4,4224]{1,0:T(4,128)(2,1)S(1)}, bf16[4,4224]{1,0:T(4,128)(2,1)S(1)}, u32[]{:S(2)}, u32[]{:S(2)}) collective-permute-start(bf16[4,4224]{1,0:T(4,128)(2,1)S(1)} %with_routing.1.mine_ref), channel_id=1, source_target_pairs={{8,0},{12,4},{9,1},{13,5},{10,2},{14,6},{11,3},{15,7},{24,16},{28,... | collective-permute-start | bytes 101384 | tf_op jit(solution)/shard_map/ppermute | solution.py:25
  2.2 7.5 %collective-permute-start = (bf16[4,4224]{1,0:T(4,128)(2,1)S(1)}, bf16[4,4224]{1,0:T(4,128)(2,1)S(1)}, u32[]{:S(2)}, u32[]{:S(2)}) collective-permute-start(bf16[4,4224]{1,0:T(4,128)(2,1)S(1)} %with_routing.1.mine_ref), channel_id=1, source_target_pairs={{0,8},{4,12},{1,9},{5,13},{2,10},{6,14},{3,11},{7,15},{16,24},{20,... | collective-permute-start | bytes 101384 | tf_op jit(solution)/shard_map/ppermute | solution.py:25
  9.7 8.7 %collective-permute-start.3 = (bf16[8,4224]{1,0:T(8,128)(2,1)S(1)}, bf16[8,4224]{1,0:T(8,128)(2,1)S(1)}, u32[]{:S(2)}, u32[]{:S(2)}) collective-permute-start(bf16[8,4224]{1,0:T(8,128)(2,1)S(1)} %join.3.after_ref.mine_ref), channel_id=1, source_target_pairs={{4,0},{12,8},{5,1},{13,9},{6,2},{14,10},{7,3},{15,11},{20,16},{28,... | collective-permute-start | bytes 202760 | tf_op jit(solution)/shard_map/ppermute | solution.py:25
  11.0 7.4 %collective-permute-start.2 = (bf16[8,4224]{1,0:T(8,128)(2,1)S(1)}, bf16[8,4224]{1,0:T(8,128)(2,1)S(1)}, u32[]{:S(2)}, u32[]{:S(2)}) collective-permute-start(bf16[8,4224]{1,0:T(8,128)(2,1)S(1)} %join.3.after_ref.mine_ref), channel_id=1, source_target_pairs={{0,4},{8,12},{1,5},{9,13},{2,6},{10,14},{3,7},{11,15},{16,20},{24,... | collective-permute-start | bytes 202760 | tf_op jit(solution)/shard_map/ppermute | solution.py:25
  18.5 8.7 %collective-permute-start.5 = (bf16[16,4224]{1,0:T(8,128)(2,1)S(1)}, bf16[16,4224]{1,0:T(8,128)(2,1)S(1)}, u32[]{:S(2)}, u32[]{:S(2)}) collective-permute-start(bf16[16,4224]{1,0:T(8,128)(2,1)S(1)} %join.4.after_ref.mine_ref), channel_id=1, source_target_pairs={{2,0},{3,1},{6,4},{7,5},{10,8},{11,9},{14,12},{15,13},{18,16},{19,... | collective-permute-start | bytes 405512 | tf_op jit(solution)/shard_map/ppermute | solution.py:25
  19.8 7.4 %collective-permute-start.4 = (bf16[16,4224]{1,0:T(8,128)(2,1)S(1)}, bf16[16,4224]{1,0:T(8,128)(2,1)S(1)}, u32[]{:S(2)}, u32[]{:S(2)}) collective-permute-start(bf16[16,4224]{1,0:T(8,128)(2,1)S(1)} %join.4.after_ref.mine_ref), channel_id=1, source_target_pairs={{0,2},{1,3},{4,6},{5,7},{8,10},{9,11},{12,14},{13,15},{16,18},{17,... | collective-permute-start | bytes 405512 | tf_op jit(solution)/shard_map/ppermute | solution.py:25
  27.3 1.6 %collective-permute-start.6 = (bf16[32,4224]{1,0:T(8,128)(2,1)S(1)}, bf16[32,4224]{1,0:T(8,128)(2,1)S(1)}, u32[]{:S(2)}, u32[]{:S(2)}) collective-permute-start(bf16[32,4224]{1,0:T(8,128)(2,1)S(1)} %join.5.mine_ref), channel_id=1, source_target_pairs={{0,1},{1,0},{2,3},{3,2},{4,5},{5,4},{6,7},{7,6},{8,9},{9,8},{10,11... | collective-permute-start | bytes 811016 | tf_op jit(solution)/shard_map/ppermute | solution.py:23
  49.7 1.6 %collective-permute-start.7 = (bf16[32,4096]{1,0:T(8,128)(2,1)S(1)}, bf16[32,4096]{1,0:T(8,128)(2,1)S(1)}, u32[]{:S(2)}, u32[]{:S(2)}) collective-permute-start(bf16[32,4096]{1,0:T(8,128)(2,1)S(1)} %get-tuple-element.24), channel_id=1, source_target_pairs={{0,1},{1,0},{2,3},{3,2},{4,5},{5,4},{6,7},{7,6},{8,9},{9,8},{10,11... | collective-permute-start | bytes 786440 | tf_op jit(solution)/shard_map/ppermute | solution.py:23
  51.4 7.0 %collective-permute-start.8 = (bf16[16,4096]{1,0:T(8,128)(2,1)S(1)}, bf16[16,4096]{1,0:T(8,128)(2,1)S(1)}, u32[]{:S(2)}, u32[]{:S(2)}) collective-permute-start(bf16[16,4096]{1,0:T(8,128)(2,1)S(1)} %slice.41), channel_id=1, source_target_pairs={{0,2},{1,3},{4,6},{5,7},{8,10},{9,11},{12,14},{13,15},{16,18},{17,... | collective-permute-start | bytes 393224 | tf_op jit(solution)/shard_map/ppermute | solution.py:25
  55.5 7.2 %collective-permute-start.9 = (bf16[16,4096]{1,0:T(8,128)(2,1)S(1)}, bf16[16,4096]{1,0:T(8,128)(2,1)S(1)}, u32[]{:S(2)}, u32[]{:S(2)}) collective-permute-start(bf16[16,4096]{1,0:T(8,128)(2,1)S(1)} %slice.41), channel_id=1, source_target_pairs={{2,0},{3,1},{6,4},{7,5},{10,8},{11,9},{14,12},{15,13},{18,16},{19,... | collective-permute-start | bytes 393224 | tf_op jit(solution)/shard_map/ppermute | solution.py:25
  62.7 5.2 %collective-permute-start.10 = (bf16[8,4096]{1,0:T(8,128)(2,1)S(1)}, bf16[8,4096]{1,0:T(8,128)(2,1)S(1)}, u32[]{:S(2)}, u32[]{:S(2)}) collective-permute-start(bf16[8,4096]{1,0:T(8,128)(2,1)S(1)} %slice.42), channel_id=1, source_target_pairs={{0,4},{8,12},{1,5},{9,13},{2,6},{10,14},{3,7},{11,15},{16,20},{24,... | collective-permute-start | bytes 196616 | tf_op jit(solution)/shard_map/ppermute | solution.py:25
  65.9 6.2 %collective-permute-start.11 = (bf16[8,4096]{1,0:T(8,128)(2,1)S(1)}, bf16[8,4096]{1,0:T(8,128)(2,1)S(1)}, u32[]{:S(2)}, u32[]{:S(2)}) collective-permute-start(bf16[8,4096]{1,0:T(8,128)(2,1)S(1)} %slice.42), channel_id=1, source_target_pairs={{4,0},{12,8},{5,1},{13,9},{6,2},{14,10},{7,3},{15,11},{20,16},{28,... | collective-permute-start | bytes 196616 | tf_op jit(solution)/shard_map/ppermute | solution.py:25
  72.2 6.7 %collective-permute-start.12 = (bf16[4,4096]{1,0:T(4,128)(2,1)S(1)}, bf16[4,4096]{1,0:T(4,128)(2,1)S(1)}, u32[]{:S(2)}, u32[]{:S(2)}) collective-permute-start(bf16[4,4096]{1,0:T(4,128)(2,1)S(1)} %slice.43), channel_id=1, source_target_pairs={{0,8},{4,12},{1,9},{5,13},{2,10},{6,14},{3,11},{7,15},{16,24},{20,... | collective-permute-start | bytes 98312 | tf_op jit(solution)/shard_map/ppermute | solution.py:25
  77.3 6.7 %collective-permute-start.13 = (bf16[4,4096]{1,0:T(4,128)(2,1)S(1)}, bf16[4,4096]{1,0:T(4,128)(2,1)S(1)}, u32[]{:S(2)}, u32[]{:S(2)}) collective-permute-start(bf16[4,4096]{1,0:T(4,128)(2,1)S(1)} %slice.43), channel_id=1, source_target_pairs={{8,0},{12,4},{9,1},{13,5},{10,2},{14,6},{11,3},{15,7},{24,16},{28,... | collective-permute-start | bytes 98312 | tf_op jit(solution)/shard_map/ppermute | solution.py:25

commit v10 on v7

--- a/solution.py
+++ b/solution.py
@@ -78,7 +78,7 @@
     return jnp.where(lane < EXPERTS, high, full - high).astype(jnp.bfloat16)
 
 
-def layer(top, ff_dev, row_block, step_units, early, mine_ref, theirs_ref, gate_ref, up_ref,
+def layer(top, ff_dev, row_block, step_units, early, places, mine_ref, theirs_ref, gate_ref, up_ref,
           down_ref, *refs):
     if early:
         refs = refs[3:]
@@ -178,8 +178,14 @@
 
     wait(2, steps - 1)
     each_block(lambda block: down_product(jnp.int32(steps - 1), block))
-    keep_ref[...] = total[:half, :]
-    send_ref[...] = total[half:, :].astype(jnp.bfloat16)
+    tok = half // len(places)
+    me = [lax.axis_index(name) for name in ("wide", "sec")]
+    sections = lax.axis_size("sec")
+    for block, (wide, sec) in enumerate(places):
+        place = (me[0] ^ wide) * sections + (me[1] ^ sec)
+        low = block * tok
+        keep_ref[place] = total[low:low + tok, :]
+        send_ref[place] = total[half + low:half + low + tok, :].astype(jnp.bfloat16)
 
 
 def build(axes):
@@ -256,12 +262,17 @@
                 rows = jnp.concatenate([rows, theirs], axis=0)
         half = rows.shape[0]
         count = 2 * half
+        tok = tokens.shape[0]
+        places = [(0, 0)]
+        for axis, _, by in hops[:-1]:
+            places += [(w ^ by, c) if axis == "wide" else (w, c ^ by) for w, c in places]
+        blocks = (len(places), tok, depth)
         row_block = min(count, 64)
         keep, send, *_ = pl.pallas_call(
-            functools.partial(layer, top, ff_dev, row_block, step_units, early),
+            functools.partial(layer, top, ff_dev, row_block, step_units, early, places),
             out_shape=[
-                jax.ShapeDtypeStruct((half, depth), jnp.float32),
-                jax.ShapeDtypeStruct((half, depth), jnp.bfloat16),
+                jax.ShapeDtypeStruct(blocks, jnp.float32),
+                jax.ShapeDtypeStruct(blocks, jnp.bfloat16),
             ]
             + (ring_shapes if early else []),
             in_specs=[VMEM] * 2 + [HBM] * 3 + [VMEM] * len(ring),
@@ -286,11 +297,10 @@
             name="expert_layer",
         )(rows, theirs, *weights, *ring)
         total = keep + swap(send, *hops[-1]).astype(jnp.float32)
-        for hop in reversed(hops[:-1]):
-            half = total.shape[0] // 2
-            theirs = swap(total[half:].astype(jnp.bfloat16), *hop)
-            total = total[:half] + theirs.astype(jnp.float32)
-        return total.astype(jnp.bfloat16)
+        arrived = lax.all_to_all(
+            total.astype(jnp.bfloat16), ("wide", "sec"), split_axis=0, concat_axis=0, tiled=True
+        )
+        return jnp.sum(arrived.astype(jnp.float32), axis=0).astype(jnp.bfloat16)
 
     return local
 

time: 56.7 us -> 57 us (level)
  blocking collectives: 0 us -> 14.9 us
  waiting for transfers between devices: 14.6 us -> 5.78 us
  starting transfers between devices: 13.6 us -> 7.62 us
    all_to_all x0 -> x1, blocking collectives: none -> 14.9 us  [local(): lax.all_to_all(total.astype(jnp.bfloat16), ('wide', 'sec'), split_axis=0,...]
    ppermute x8 -> x5, waiting for transfers between devices: 14.6 us -> 5.78 us  [swap(): return lax.ppermute(x, axis, [(i, i ^ by) for i in range(size)])]
    ppermute x8 -> x5, starting transfers between devices: 13.6 us -> 7.62 us  [swap(): return lax.ppermute(x, axis, [(i, i ^ by) for i in range(size)])]
    reduce_sum x0 -> x1, other arithmetic: none -> 0.73 us  [local(): return jnp.sum(arrived.astype(jnp.float32), axis=0).astype(jnp.bfloat16)]
  transfers between devices with their start and end apart: 8 -> 5, of which waited for: 7 -> 4; matrix products, arithmetic and copies ran while one was open for 0% -> 0% of each run, Pallas kernels for 10% -> 10%
where the time goes in v10:
time: 57 us; the launch traced here: 56.8 us
  Pallas kernels  27.6 us (48%)
  blocking collectives  14.9 us (26%)
  starting transfers between devices  7.62 us (13%)
  waiting for transfers between devices  5.78 us (10%)
  other arithmetic  0.89 us (2%)
    pallas_call x1, Pallas kernels, local(): pl.pallas_call(functools.partial(layer, top, ff_dev, row_block, step_unit...  20.9 us
    all_to_all x1, blocking collectives, local(): lax.all_to_all(total.astype(jnp.bfloat16), ('wide', 'sec'), split_axis=0,...  14.9 us
    ppermute x5, starting transfers between devices, swap(): return lax.ppermute(x, axis, [(i, i ^ by) for i in range(size)])  7.62 us
    ppermute x5, waiting for transfers between devices, swap(): return lax.ppermute(x, axis, [(i, i ^ by) for i in range(size)])  5.78 us
    pallas_call x2, Pallas kernels, local(): pl.pallas_call(functools.partial(bring, early, steps), out_shape=ring_sha...  5.71 us
  transfers between devices with their start and end apart: 5, of which 4 were waited for; matrix products, arithmetic and copies ran while one was open for 0% of the time, Pallas kernels for 10%

profile of v10, /device:TPU:0, one launch (start us, length us, event | category | flops | bytes accessed | tf_op | source)
XLA Modules:
  0.0 56.8 jit_solution(7791384606373932561)
XLA Ops:
  0.0 0.9 %with_routing.1.mine_ref = bf16[4,4224]{1,0:T(4,128)(2,1)S(1)} custom-call(bf16[4,4096]{1,0:T(4,128)(2,1)} %tokens_ref.1, s32[4,8]{1,0:T(4,128)} %ids_ref.1, s32[4,8]{1,0:T(4,128)} %numer_ref.1), custom_call_target="tpu_custom_call" | custom-call | tf_op jit(solution)/shard_map/with_routing/pallas_call | solution.py:202
  0.9 4.1 %collective-permute-start = (bf16[4,4224]{1,0:T(4,128)(2,1)S(1)}, bf16[4,4224]{1,0:T(4,128)(2,1)S(1)}, u32[]{:S(2)}, u32[]{:S(2)}) collective-permute-start(bf16[4,4224]{1,0:T(4,128)(2,1)S(1)} %with_routing.1.mine_ref), channel_id=1, source_target_pairs={{0,8},{4,12},{8,0},{12,4},{1,9},{5,13},{9,1},{13,5},{2,10},{6,14},... | collective-permute-start | bytes 101384 | tf_op jit(solution)/shard_map/ppermute | solution.py:22
  5.0 2.3 %collective-permute-done.theirs_ref = bf16[4,4224]{1,0:T(4,128)(2,1)S(1)} collective-permute-done((bf16[4,4224]{1,0:T(4,128)(2,1)S(1)}, bf16[4,4224]{1,0:T(4,128)(2,1)S(1)}, u32[]{:S(2)}, u32[]{:S(2)}) %collective-permute-start) | collective-permute-done | bytes 33824 | tf_op jit(solution)/shard_map/ppermute | solution.py:22
  7.3 1.6 %collective-permute-start.1 = (bf16[8,4224]{1,0:T(8,128)(2,1)S(1)}, bf16[8,4224]{1,0:T(8,128)(2,1)S(1)}, u32[]{:S(2)}, u32[]{:S(2)}) collective-permute-start(bf16[8,4224]{1,0:T(8,128)(2,1)S(1)} %join.3.after_ref.mine_ref), channel_id=1, source_target_pairs={{0,4},{4,0},{8,12},{12,8},{1,5},{5,1},{9,13},{13,9},{2,6},{6,2},{1... | collective-permute-start | bytes 202760 | tf_op jit(solution)/shard_map/ppermute | solution.py:22
  8.9 2.9 %bring_weights.2 = (bf16[3,256,4096]{2,1,0:T(8,128)(2,1)S(1)}, bf16[3,256,4096]{2,1,0:T(8,128)(2,1)S(1)}, bf16[4,256,4096]{2,1,0:T(8,128)(2,1)S(1)}, f32[8,128]{1,0:T(8,128)S(1)}) custom-call(bf16[3072,4096]{1,0:T(8,128)(2,1)} %bitcast.3, bf16[3072,4096]{1,0:T(8,128)(2,1)} %bitcast.6, bf16[3072,4096]{1,0:T(8,128)(2,1)} %bitcast.9, ...), custom_call_target="tpu_custom_call" | custom-call | bytes 6291456 | tf_op jit(solution)/shard_map/bring_weights/pallas_call | solution.py:232
  11.7 0.0 collective-permute-done.1.theirs_ref
  11.8 1.6 %collective-permute-start.2 = (bf16[16,4224]{1,0:T(8,128)(2,1)S(1)}, bf16[16,4224]{1,0:T(8,128)(2,1)S(1)}, u32[]{:S(2)}, u32[]{:S(2)}) collective-permute-start(bf16[16,4224]{1,0:T(8,128)(2,1)S(1)} %join.4.after_ref.mine_ref), channel_id=1, source_target_pairs={{0,2},{2,0},{1,3},{3,1},{4,6},{6,4},{5,7},{7,5},{8,10},{10,8},{9,1... | collective-permute-start | bytes 405512 | tf_op jit(solution)/shard_map/ppermute | solution.py:22
  13.4 2.9 %bring_weights.3 = (bf16[3,256,4096]{2,1,0:T(8,128)(2,1)S(1)}, bf16[3,256,4096]{2,1,0:T(8,128)(2,1)S(1)}, bf16[4,256,4096]{2,1,0:T(8,128)(2,1)S(1)}, f32[8,128]{1,0:T(8,128)S(1)}) custom-call(bf16[3072,4096]{1,0:T(8,128)(2,1)} %bitcast.4, bf16[3072,4096]{1,0:T(8,128)(2,1)} %bitcast.7, ...), custom_call_target="tpu_custom_call", output_to_operand_aliasing={{0}: (4, {}), {1}: (5, {}), {2}: (6, {})} | custom-call | bytes 6291456 | tf_op jit(solution)/shard_map/bring_weights/pallas_call | solution.py:232
  16.3 0.6 %collective-permute-done.2.theirs_ref = bf16[16,4224]{1,0:T(8,128)(2,1)S(1)} collective-permute-done((bf16[16,4224]{1,0:T(8,128)(2,1)S(1)}, bf16[16,4224]{1,0:T(8,128)(2,1)S(1)}, u32[]{:S(2)}, u32[]{:S(2)}) %collective-permute-start.2) | collective-permute-done | bytes 135200 | tf_op jit(solution)/shard_map/ppermute | solution.py:22
  16.9 0.1 collective-permute-start.3
  16.9 1.5 %collective-permute-done.3.theirs_ref = bf16[32,4224]{1,0:T(8,128)(2,1)S(1)} collective-permute-done((bf16[32,4224]{1,0:T(8,128)(2,1)S(1)}, bf16[32,4224]{1,0:T(8,128)(2,1)S(1)}, u32[]{:S(2)}, u32[]{:S(2)}) %collective-permute-start.3) | collective-permute-done | bytes 270368 | tf_op jit(solution)/shard_map/ppermute | solution.py:22
  18.5 20.9 %expert_layer.1 = (f32[8,4,4096]{2,1,0:T(4,128)S(1)}, bf16[8,4,4096]{2,1,0:T(4,128)(2,1)S(1)}, bf16[3,256,4096]{2,1,0:T(8,128)(2,1)S(1)}, bf16[3,256,4096]{2,1,0:T(8,128)(2,1)S(1)}, bf16[4,256,4096]{2,1,0:T(8,128)(2,1)S(1)}) custom-call(bf16[32,4224]{1,0:T(8,128)(2,1)S(1)} %join.5.mine_ref, ...), custom_call_target="tpu_custom_call", output_to_operand_aliasing={{2}: (5, {}), {3}: (6, {}), {4}: (7, {})} | custom-call | flops 4831838208 | bytes 62914560 | tf_op jit(solution)/shard_map/expert_layer/pallas_call | solution.py:271
  39.4 0.2 collective-permute-start.4
  39.6 1.4 %collective-permute-done.4 = bf16[8,4,4096]{2,1,0:T(4,128)(2,1)S(1)} collective-permute-done((bf16[8,4,4096]{2,1,0:T(4,128)(2,1)S(1)}, bf16[8,4,4096]{2,1,0:T(4,128)(2,1)S(1)}, u32[]{:S(2)}, u32[]{:S(2)}) %collective-permute-start.4) | collective-permute-done | bytes 262176 | tf_op jit(solution)/shard_map/ppermute | solution.py:22
  41.0 0.2 add_convert_fusion
  41.2 14.9 %all_to_all.5 = bf16[8,4,4096]{2,1,0:T(4,128)(2,1)S(1)} all-to-all(bf16[8,4,4096]{2,1,0:T(4,128)(2,1)S(1)} %add_convert_fusion), channel_id=1, replica_groups=mesh['grp'=2,'wide'=4,'sec'=2,'sub'=2] {'wide','sec'}, dimensions={0} | all-to-all | bytes 524288 | tf_op jit(solution)/shard_map/all_to_all | solution.py:300
  56.1 0.7 %reduce_sum.12 = bf16[4,4096]{1,0:T(4,128)(2,1)} reduce(bf16[8,4,4096]{2,1,0:T(4,128)(2,1)S(1)} %all_to_all.5, bf16[]{:T(256)} %constant.2.clone.1), dimensions={0}, to_apply=%region_0.0 | reduce | flops 114688 | bytes 294914 | tf_op jit(solution)/shard_map/reduce_sum | solution.py:303
  (3 shorter events, 0.0 us)
Async XLA Ops:
  0.9 6.4 %collective-permute-start = (bf16[4,4224]{1,0:T(4,128)(2,1)S(1)}, bf16[4,4224]{1,0:T(4,128)(2,1)S(1)}, u32[]{:S(2)}, u32[]{:S(2)}) collective-permute-start(bf16[4,4224]{1,0:T(4,128)(2,1)S(1)} %with_routing.1.mine_ref), channel_id=1, source_target_pairs={{0,8},{4,12},{8,0},{12,4},{1,9},{5,13},{9,1},{13,5},{2,10},{6,14},... | collective-permute-start | bytes 101384 | tf_op jit(solution)/shard_map/ppermute | solution.py:22
  7.3 4.5 %collective-permute-start.1 = (bf16[8,4224]{1,0:T(8,128)(2,1)S(1)}, bf16[8,4224]{1,0:T(8,128)(2,1)S(1)}, u32[]{:S(2)}, u32[]{:S(2)}) collective-permute-start(bf16[8,4224]{1,0:T(8,128)(2,1)S(1)} %join.3.after_ref.mine_ref), channel_id=1, source_target_pairs={{0,4},{4,0},{8,12},{12,8},{1,5},{5,1},{9,13},{13,9},{2,6},{6,2},{1... | collective-permute-start | bytes 202760 | tf_op jit(solution)/shard_map/ppermute | solution.py:22
  11.8 5.1 %collective-permute-start.2 = (bf16[16,4224]{1,0:T(8,128)(2,1)S(1)}, bf16[16,4224]{1,0:T(8,128)(2,1)S(1)}, u32[]{:S(2)}, u32[]{:S(2)}) collective-permute-start(bf16[16,4224]{1,0:T(8,128)(2,1)S(1)} %join.4.after_ref.mine_ref), channel_id=1, source_target_pairs={{0,2},{2,0},{1,3},{3,1},{4,6},{6,4},{5,7},{7,5},{8,10},{10,8},{9,1... | collective-permute-start | bytes 405512 | tf_op jit(solution)/shard_map/ppermute | solution.py:22
  16.9 1.6 %collective-permute-start.3 = (bf16[32,4224]{1,0:T(8,128)(2,1)S(1)}, bf16[32,4224]{1,0:T(8,128)(2,1)S(1)}, u32[]{:S(2)}, u32[]{:S(2)}) collective-permute-start(bf16[32,4224]{1,0:T(8,128)(2,1)S(1)} %join.5.mine_ref), channel_id=1, source_target_pairs={{0,1},{1,0},{2,3},{3,2},{4,5},{5,4},{6,7},{7,6},{8,9},{9,8},{10,11... | collective-permute-start | bytes 811016 | tf_op jit(solution)/shard_map/ppermute | solution.py:22
  39.4 1.6 %collective-permute-start.4 = (bf16[8,4,4096]{2,1,0:T(4,128)(2,1)S(1)}, bf16[8,4,4096]{2,1,0:T(4,128)(2,1)S(1)}, u32[]{:S(2)}, u32[]{:S(2)}) collective-permute-start(bf16[8,4,4096]{2,1,0:T(4,128)(2,1)S(1)} %get-tuple-element.24), channel_id=1, source_target_pairs={{0,1},{1,0},{2,3},{3,2},{4,5},{5,4},{6,7},{7,6},{8,9},{9,8},{10,11... | collective-permute-start | bytes 786440 | tf_op jit(solution)/shard_map/ppermute | solution.py:22

commit v11 on v10

--- a/solution.py
+++ b/solution.py
@@ -178,11 +178,10 @@
 
     wait(2, steps - 1)
     each_block(lambda block: down_product(jnp.int32(steps - 1), block))
-    tok = half // len(places)
-    me = [lax.axis_index(name) for name in ("wide", "sec")]
-    sections = lax.axis_size("sec")
-    for block, (wide, sec) in enumerate(places):
-        place = (me[0] ^ wide) * sections + (me[1] ^ sec)
+    tok = half // (keep_ref.shape[0] * len(places))
+    me = lax.axis_index("wide")
+    for block in range(half // tok):
+        place = (block // len(places), me ^ places[block % len(places)])
         low = block * tok
         keep_ref[place] = total[low:low + tok, :]
         send_ref[place] = total[half + low:half + low + tok, :].astype(jnp.bfloat16)
@@ -263,10 +262,11 @@
         half = rows.shape[0]
         count = 2 * half
         tok = tokens.shape[0]
-        places = [(0, 0)]
-        for axis, _, by in hops[:-1]:
-            places += [(w ^ by, c) if axis == "wide" else (w, c ^ by) for w, c in places]
-        blocks = (len(places), tok, depth)
+        places = [0]
+        for axis, _, by in hops:
+            if axis == "wide":
+                places += [w ^ by for w in places]
+        blocks = (half // (tok * len(places)), len(places), tok, depth)
         row_block = min(count, 64)
         keep, send, *_ = pl.pallas_call(
             functools.partial(layer, top, ff_dev, row_block, step_units, early, places),
@@ -297,8 +297,13 @@
             name="expert_layer",
         )(rows, theirs, *weights, *ring)
         total = keep + swap(send, *hops[-1]).astype(jnp.float32)
+        for hop in reversed(hops[:-1]):
+            if hop[0] != "wide":
+                left = total.shape[0] // 2
+                theirs = swap(total[left:].astype(jnp.bfloat16), *hop)
+                total = total[:left] + theirs.astype(jnp.float32)
         arrived = lax.all_to_all(
-            total.astype(jnp.bfloat16), ("wide", "sec"), split_axis=0, concat_axis=0, tiled=True
+            total[0].astype(jnp.bfloat16), "wide", split_axis=0, concat_axis=0, tiled=True
         )
         return jnp.sum(arrived.astype(jnp.float32), axis=0).astype(jnp.bfloat16)
 

time: 57 us -> 58.4 us (1.025)
  blocking collectives: 14.9 us -> 10.7 us
  waiting for transfers between devices: 5.78 us -> 9.76 us
  starting transfers between devices: 7.62 us -> 9.25 us
    all_to_all x1, blocking collectives: 14.9 us -> 10.7 us  [local(): lax.all_to_all(total[0].astype(jnp.bfloat16), 'wide', split_axis=0, conca...]
    ppermute x5 -> x6, waiting for transfers between devices: 5.78 us -> 9.76 us  [swap(): return lax.ppermute(x, axis, [(i, i ^ by) for i in range(size)])]
    ppermute x5 -> x6, starting transfers between devices: 7.62 us -> 9.25 us  [swap(): return lax.ppermute(x, axis, [(i, i ^ by) for i in range(size)])]
  transfers between devices with their start and end apart: 5 -> 6, of which waited for: 4 -> 5; matrix products, arithmetic and copies ran while one was open for 0% -> 0% of each run, Pallas kernels for 10% -> 10%
where the time goes in v11:
time: 58.4 us; the launch traced here: 58.2 us
  Pallas kernels  27.6 us (47%)
  blocking collectives  10.7 us (18%)
  waiting for transfers between devices  9.76 us (17%)
  starting transfers between devices  9.25 us (16%)
  other arithmetic  0.81 us (1%)
    pallas_call x1, Pallas kernels, local(): pl.pallas_call(functools.partial(layer, top, ff_dev, row_block, step_unit...  20.9 us
    all_to_all x1, blocking collectives, local(): lax.all_to_all(total[0].astype(jnp.bfloat16), 'wide', split_axis=0, conca...  10.7 us
    ppermute x6, waiting for transfers between devices, swap(): return lax.ppermute(x, axis, [(i, i ^ by) for i in range(size)])  9.76 us
    ppermute x6, starting transfers between devices, swap(): return lax.ppermute(x, axis, [(i, i ^ by) for i in range(size)])  9.25 us
    pallas_call x2, Pallas kernels, local(): pl.pallas_call(functools.partial(bring, early, steps), out_shape=ring_sha...  5.71 us
  transfers between devices with their start and end apart: 6, of which 5 were waited for; matrix products, arithmetic and copies ran while one was open for 0% of the time, Pallas kernels for 10%

profile of v11, /device:TPU:0, one launch (start us, length us, event | category | flops | bytes accessed | tf_op | source)
XLA Modules:
  0.0 58.2 jit_solution(9511671138984605039)
XLA Ops:
  0.0 0.9 %with_routing.1.mine_ref = bf16[4,4224]{1,0:T(4,128)(2,1)S(1)} custom-call(bf16[4,4096]{1,0:T(4,128)(2,1)} %tokens_ref.1, s32[4,8]{1,0:T(4,128)} %ids_ref.1, s32[4,8]{1,0:T(4,128)} %numer_ref.1), custom_call_target="tpu_custom_call" | custom-call | tf_op jit(solution)/shard_map/with_routing/pallas_call | solution.py:201
  0.9 4.1 %collective-permute-start = (bf16[4,4224]{1,0:T(4,128)(2,1)S(1)}, bf16[4,4224]{1,0:T(4,128)(2,1)S(1)}, u32[]{:S(2)}, u32[]{:S(2)}) collective-permute-start(bf16[4,4224]{1,0:T(4,128)(2,1)S(1)} %with_routing.1.mine_ref), channel_id=1, source_target_pairs={{0,8},{4,12},{8,0},{12,4},{1,9},{5,13},{9,1},{13,5},{2,10},{6,14},... | collective-permute-start | bytes 101384 | tf_op jit(solution)/shard_map/ppermute | solution.py:22
  5.0 2.3 %collective-permute-done.theirs_ref = bf16[4,4224]{1,0:T(4,128)(2,1)S(1)} collective-permute-done((bf16[4,4224]{1,0:T(4,128)(2,1)S(1)}, bf16[4,4224]{1,0:T(4,128)(2,1)S(1)}, u32[]{:S(2)}, u32[]{:S(2)}) %collective-permute-start) | collective-permute-done | bytes 33824 | tf_op jit(solution)/shard_map/ppermute | solution.py:22
  7.3 1.6 %collective-permute-start.1 = (bf16[8,4224]{1,0:T(8,128)(2,1)S(1)}, bf16[8,4224]{1,0:T(8,128)(2,1)S(1)}, u32[]{:S(2)}, u32[]{:S(2)}) collective-permute-start(bf16[8,4224]{1,0:T(8,128)(2,1)S(1)} %join.3.after_ref.mine_ref), channel_id=1, source_target_pairs={{0,4},{4,0},{8,12},{12,8},{1,5},{5,1},{9,13},{13,9},{2,6},{6,2},{1... | collective-permute-start | bytes 202760 | tf_op jit(solution)/shard_map/ppermute | solution.py:22
  8.9 2.9 %bring_weights.2 = (bf16[3,256,4096]{2,1,0:T(8,128)(2,1)S(1)}, bf16[3,256,4096]{2,1,0:T(8,128)(2,1)S(1)}, bf16[4,256,4096]{2,1,0:T(8,128)(2,1)S(1)}, f32[8,128]{1,0:T(8,128)S(1)}) custom-call(bf16[3072,4096]{1,0:T(8,128)(2,1)} %bitcast.9, bf16[3072,4096]{1,0:T(8,128)(2,1)} %bitcast.12, bf16[3072,4096]{1,0:T(8,128)(2,1)} %bitcast.15, ...), custom_call_target="tpu_custom_call" | custom-call | bytes 6291456 | tf_op jit(solution)/shard_map/bring_weights/pallas_call | solution.py:231
  11.7 0.0 collective-permute-done.1.theirs_ref
  11.8 1.6 %collective-permute-start.2 = (bf16[16,4224]{1,0:T(8,128)(2,1)S(1)}, bf16[16,4224]{1,0:T(8,128)(2,1)S(1)}, u32[]{:S(2)}, u32[]{:S(2)}) collective-permute-start(bf16[16,4224]{1,0:T(8,128)(2,1)S(1)} %join.4.after_ref.mine_ref), channel_id=1, source_target_pairs={{0,2},{2,0},{1,3},{3,1},{4,6},{6,4},{5,7},{7,5},{8,10},{10,8},{9,1... | collective-permute-start | bytes 405512 | tf_op jit(solution)/shard_map/ppermute | solution.py:22
  13.4 2.9 %bring_weights.3 = (bf16[3,256,4096]{2,1,0:T(8,128)(2,1)S(1)}, bf16[3,256,4096]{2,1,0:T(8,128)(2,1)S(1)}, bf16[4,256,4096]{2,1,0:T(8,128)(2,1)S(1)}, f32[8,128]{1,0:T(8,128)S(1)}) custom-call(bf16[3072,4096]{1,0:T(8,128)(2,1)} %bitcast.10, bf16[3072,4096]{1,0:T(8,128)(2,1)} %bitcast.13, ...), custom_call_target="tpu_custom_call", output_to_operand_aliasing={{0}: (4, {}), {1}: (5, {}), {2}: (6, {})} | custom-call | bytes 6291456 | tf_op jit(solution)/shard_map/bring_weights/pallas_call | solution.py:231
  16.3 0.6 %collective-permute-done.2.theirs_ref = bf16[16,4224]{1,0:T(8,128)(2,1)S(1)} collective-permute-done((bf16[16,4224]{1,0:T(8,128)(2,1)S(1)}, bf16[16,4224]{1,0:T(8,128)(2,1)S(1)}, u32[]{:S(2)}, u32[]{:S(2)}) %collective-permute-start.2) | collective-permute-done | bytes 135200 | tf_op jit(solution)/shard_map/ppermute | solution.py:22
  16.9 0.1 collective-permute-start.3
  16.9 1.5 %collective-permute-done.3.theirs_ref = bf16[32,4224]{1,0:T(8,128)(2,1)S(1)} collective-permute-done((bf16[32,4224]{1,0:T(8,128)(2,1)S(1)}, bf16[32,4224]{1,0:T(8,128)(2,1)S(1)}, u32[]{:S(2)}, u32[]{:S(2)}) %collective-permute-start.3) | collective-permute-done | bytes 270368 | tf_op jit(solution)/shard_map/ppermute | solution.py:22
  18.5 20.9 %expert_layer.1 = (f32[2,4,4,4096]{3,2,1,0:T(4,128)S(1)}, bf16[2,4,4,4096]{3,2,1,0:T(4,128)(2,1)S(1)}, bf16[3,256,4096]{2,1,0:T(8,128)(2,1)S(1)}, bf16[3,256,409...) custom-call(bf16[32,4224]{1,0:T(8,128)(2,1)S(1)} %join.5.mine_ref, ...), custom_call_target="tpu_custom_call", output_to_operand_aliasing={{2}: (5, {}), {3}: (6, {}), {4}: (7, {})} | custom-call | flops 4831838208 | bytes 62914560 | tf_op jit(solution)/shard_map/expert_layer/pallas_call | solution.py:271
  39.4 0.2 collective-permute-start.4
  39.6 1.4 %collective-permute-done.4 = bf16[2,4,4,4096]{3,2,1,0:T(4,128)(2,1)S(1)} collective-permute-done((bf16[2,4,4,4096]{3,2,1,0:T(4,128)(2,1)S(1)}, bf16[2,4,4,4096]{3,2,1,0:T(4,128)(2,1)S(1)}, u32[]{:S(2)}, u32[]{:S(2)}) %collective-permute-start.4) | collective-permute-done | bytes 262176 | tf_op jit(solution)/shard_map/ppermute | solution.py:22
  41.0 0.1 convert_add_fusion
  41.1 1.6 %collective-permute-start.5 = (bf16[1,4,4,4096]{3,2,1,0:T(4,128)(2,1)S(1)}, bf16[1,4,4,4096]{3,2,1,0:T(4,128)(2,1)S(1)}, u32[]{:S(2)}, u32[]{:S(2)}) collective-permute-start(bf16[1,4,4,4096]{3,2,1,0:T(4,128)(2,1)S(1)} %slice.17), channel_id=1, source_target_pairs={{0,2},{2,0},{1,3},{3,1},{4,6},{6,4},{5,7},{7,5},{8,10},{10,8},{9,1... | collective-permute-start | bytes 393224 | tf_op jit(solution)/shard_map/ppermute | solution.py:22
  42.8 4.0 %collective-permute-done.5 = bf16[1,4,4,4096]{3,2,1,0:T(4,128)(2,1)S(1)} collective-permute-done((bf16[1,4,4,4096]{3,2,1,0:T(4,128)(2,1)S(1)}, bf16[1,4,4,4096]{3,2,1,0:T(4,128)(2,1)S(1)}, u32[]{:S(2)}, u32[]{:S(2)}) %collective-permute-start.5) | collective-permute-done | bytes 131104 | tf_op jit(solution)/shard_map/ppermute | solution.py:22
  46.7 0.1 fusion.1
  46.8 10.7 %all_to_all.5 = bf16[4,4,4096]{2,1,0:T(4,128)(2,1)S(1)} all-to-all(bf16[4,4,4096]{2,1,0:T(4,128)(2,1)S(1)} %fusion.1), channel_id=1, replica_groups=mesh['grp'=2,'wide'=4,'sec'=2,'sub'=2] {'wide'}, dimensions={0} | all-to-all | bytes 262144 | tf_op jit(solution)/shard_map/all_to_all | solution.py:305
  57.5 0.7 %reduce_sum.12 = bf16[4,4096]{1,0:T(4,128)(2,1)} reduce(bf16[4,4,4096]{2,1,0:T(4,128)(2,1)S(1)} %all_to_all.5, bf16[]{:T(256)} %constant.2.clone.1), dimensions={0}, to_apply=%region_0.0 | reduce | flops 49152 | bytes 163842 | tf_op jit(solution)/shard_map/reduce_sum | solution.py:308
  (4 shorter events, 0.1 us)
Async XLA Ops:
  0.9 6.4 %collective-permute-start = (bf16[4,4224]{1,0:T(4,128)(2,1)S(1)}, bf16[4,4224]{1,0:T(4,128)(2,1)S(1)}, u32[]{:S(2)}, u32[]{:S(2)}) collective-permute-start(bf16[4,4224]{1,0:T(4,128)(2,1)S(1)} %with_routing.1.mine_ref), channel_id=1, source_target_pairs={{0,8},{4,12},{8,0},{12,4},{1,9},{5,13},{9,1},{13,5},{2,10},{6,14},... | collective-permute-start | bytes 101384 | tf_op jit(solution)/shard_map/ppermute | solution.py:22
  7.3 4.5 %collective-permute-start.1 = (bf16[8,4224]{1,0:T(8,128)(2,1)S(1)}, bf16[8,4224]{1,0:T(8,128)(2,1)S(1)}, u32[]{:S(2)}, u32[]{:S(2)}) collective-permute-start(bf16[8,4224]{1,0:T(8,128)(2,1)S(1)} %join.3.after_ref.mine_ref), channel_id=1, source_target_pairs={{0,4},{4,0},{8,12},{12,8},{1,5},{5,1},{9,13},{13,9},{2,6},{6,2},{1... | collective-permute-start | bytes 202760 | tf_op jit(solution)/shard_map/ppermute | solution.py:22
  11.8 5.1 %collective-permute-start.2 = (bf16[16,4224]{1,0:T(8,128)(2,1)S(1)}, bf16[16,4224]{1,0:T(8,128)(2,1)S(1)}, u32[]{:S(2)}, u32[]{:S(2)}) collective-permute-start(bf16[16,4224]{1,0:T(8,128)(2,1)S(1)} %join.4.after_ref.mine_ref), channel_id=1, source_target_pairs={{0,2},{2,0},{1,3},{3,1},{4,6},{6,4},{5,7},{7,5},{8,10},{10,8},{9,1... | collective-permute-start | bytes 405512 | tf_op jit(solution)/shard_map/ppermute | solution.py:22
  16.9 1.6 %collective-permute-start.3 = (bf16[32,4224]{1,0:T(8,128)(2,1)S(1)}, bf16[32,4224]{1,0:T(8,128)(2,1)S(1)}, u32[]{:S(2)}, u32[]{:S(2)}) collective-permute-start(bf16[32,4224]{1,0:T(8,128)(2,1)S(1)} %join.5.mine_ref), channel_id=1, source_target_pairs={{0,1},{1,0},{2,3},{3,2},{4,5},{5,4},{6,7},{7,6},{8,9},{9,8},{10,11... | collective-permute-start | bytes 811016 | tf_op jit(solution)/shard_map/ppermute | solution.py:22
  39.4 1.6 %collective-permute-start.4 = (bf16[2,4,4,4096]{3,2,1,0:T(4,128)(2,1)S(1)}, bf16[2,4,4,4096]{3,2,1,0:T(4,128)(2,1)S(1)}, u32[]{:S(2)}, u32[]{:S(2)}) collective-permute-start(bf16[2,4,4,4096]{3,2,1,0:T(4,128)(2,1)S(1)} %get-tuple-element.24), channel_id=1, source_target_pairs={{0,1},{1,0},{2,3},{3,2},{4,5},{5,4},{6,7},{7,6},{8,9},{9,8},{10,11... | collective-permute-start | bytes 786440 | tf_op jit(solution)/shard_map/ppermute | solution.py:22
  41.1 5.6 %collective-permute-start.5 = (bf16[1,4,4,4096]{3,2,1,0:T(4,128)(2,1)S(1)}, bf16[1,4,4,4096]{3,2,1,0:T(4,128)(2,1)S(1)}, u32[]{:S(2)}, u32[]{:S(2)}) collective-permute-start(bf16[1,4,4,4096]{3,2,1,0:T(4,128)(2,1)S(1)} %slice.17), channel_id=1, source_target_pairs={{0,2},{2,0},{1,3},{3,1},{4,6},{6,4},{5,7},{7,5},{8,10},{10,8},{9,1... | collective-permute-start | bytes 393224 | tf_op jit(solution)/shard_map/ppermute | solution.py:22

commit v12 on v7

--- a/solution.py
+++ b/solution.py
@@ -10,7 +10,7 @@
 EXPERTS = 32
 SIDE = 128
 SLOTS = 3
-EARLY = (0, 1, 1)
+EARLY = (1, 1)
 GRANT = 8 << 20
 
 VMEM = pl.BlockSpec(memory_space=pltpu.VMEM)
@@ -20,6 +20,10 @@
 
 def swap(x, axis, size, by):
     return lax.ppermute(x, axis, [(i, i ^ by) for i in range(size)])
+
+
+def shift(x, axis, size, by):
+    return lax.ppermute(x, axis, [(i, (i + by) % size) for i in range(size)])
 
 
 def with_routing(tokens_ref, ids_ref, numer_ref, out_ref, ids, numer, sem):
@@ -36,11 +40,11 @@
     out_ref[:, depth:] = side.astype(jnp.float32).astype(jnp.bfloat16)
 
 
-def join(mine_ref, theirs_ref, *refs):
+def join(parts, *refs):
     out_ref = refs[-1]
-    count = mine_ref.shape[0]
-    out_ref[:count, :] = mine_ref[...]
-    out_ref[count:, :] = theirs_ref[...]
+    count = refs[0].shape[0]
+    for part in range(parts):
+        out_ref[part * count:(part + 1) * count, :] = refs[part][...]
 
 
 def bring(first, count, gate_ref, up_ref, down_ref, after_ref, *refs):
@@ -206,12 +210,13 @@
             compiler_params=small,
             name="with_routing",
         )(*own)
-        hops = []
+        hops = [None]
         for axis, size in axes:
             by = size // 2
             while by:
                 hops.append((axis, size, by))
                 by //= 2
+        span = lax.axis_size("wide")
         slots = min(SLOTS, units // step_units)
         ring_shapes = [
             pltpu.VMEM((n, step_units, depth), jnp.bfloat16) for n in (slots, slots, slots + 1)
@@ -219,7 +224,10 @@
         ring = []
         early = 0
         for number, hop in enumerate(hops):
-            theirs = swap(rows, *hop)
+            if hop is None:
+                theirs = [shift(rows, "wide", span, -by) for by in range(1, span)]
+            else:
+                theirs = [swap(rows, *hop)]
             steps = EARLY[number] if number < len(EARLY) and units >= 8 * step_units else 0
             ends = []
             if steps:
@@ -242,18 +250,20 @@
                 ends = [end]
             if hop is hops[-1]:
                 break
-            count = rows.shape[0]
+            all_rows = [rows] + theirs
+            count = sum(part.shape[0] for part in all_rows)
             if count <= 64:
                 rows = pl.pallas_call(
-                    join,
-                    out_shape=jax.ShapeDtypeStruct((2 * count, depth + SIDE), jnp.bfloat16),
-                    in_specs=[VMEM] * 2 + [pl.BlockSpec(memory_space=pl.ANY)] * len(ends),
+                    functools.partial(join, len(all_rows)),
+                    out_shape=jax.ShapeDtypeStruct((count, depth + SIDE), jnp.bfloat16),
+                    in_specs=[VMEM] * len(all_rows)
+                    + [pl.BlockSpec(memory_space=pl.ANY)] * len(ends),
                     out_specs=VMEM,
                     compiler_params=small,
                     name="join",
-                )(rows, theirs, *ends)
+                )(*all_rows, *ends)
             else:
-                rows = jnp.concatenate([rows, theirs], axis=0)
+                rows = jnp.concatenate(all_rows, axis=0)
         half = rows.shape[0]
         count = 2 * half
         row_block = min(count, 64)
@@ -284,12 +294,17 @@
                 transcendentals=count * units,
             ),
             name="expert_layer",
-        )(rows, theirs, *weights, *ring)
+        )(rows, *theirs, *weights, *ring)
         total = keep + swap(send, *hops[-1]).astype(jnp.float32)
-        for hop in reversed(hops[:-1]):
+        for hop in reversed(hops[1:-1]):
             half = total.shape[0] // 2
             theirs = swap(total[half:].astype(jnp.bfloat16), *hop)
             total = total[:half] + theirs.astype(jnp.float32)
+        blocks = total.reshape(span, tokens.shape[0], depth)
+        total = blocks[0]
+        for by in range(1, span):
+            theirs = shift(blocks[by].astype(jnp.bfloat16), "wide", span, by)
+            total = total + theirs.astype(jnp.float32)
         return total.astype(jnp.bfloat16)
 
     return local
@@ -298,7 +313,7 @@
 def solution(mesh):
     rows = P(("grp", "wide", "sec", "sub"), None)
     weights = P("wide", ("sec", "sub"), None)
-    axes = [(name, mesh.shape[name]) for name in ("wide", "sec", "sub")]
+    axes = [(name, mesh.shape[name]) for name in ("sec", "sub")]
     return jax.shard_map(
         build(axes),
         mesh=mesh,

time: 56.7 us -> 55.3 us (0.975)
  waiting for transfers between devices: 14.6 us -> 12.4 us
  starting transfers between devices: 13.6 us -> 14.3 us
    ppermute x0 -> x6, starting transfers between devices: none -> 10.9 us  [shift(): return lax.ppermute(x, axis, [(i, (i + by) % size) for i in range(size)])]
    ppermute x8 -> x4, starting transfers between devices: 13.6 us -> 3.39 us  [swap(): return lax.ppermute(x, axis, [(i, i ^ by) for i in range(size)])]
    ppermute x8 -> x4, waiting for transfers between devices: 14.6 us -> 7.63 us  [swap(): return lax.ppermute(x, axis, [(i, i ^ by) for i in range(size)])]
    ppermute x0 -> x6, waiting for transfers between devices: none -> 4.82 us  [shift(): return lax.ppermute(x, axis, [(i, (i + by) % size) for i in range(size)])]
  transfers between devices with their start and end apart: 8 -> 10, of which waited for: 7 -> 6; matrix products, arithmetic and copies ran while one was open for 0% -> 0% of each run, Pallas kernels for 10% -> 10%
where the time goes in v12:
time: 55.3 us; the launch traced here: 55.1 us
  Pallas kernels  27.5 us (50%)
  starting transfers between devices  14.3 us (26%)
  waiting for transfers between devices  12.4 us (22%)
  other arithmetic  0.74 us (1%)
    pallas_call x1, Pallas kernels, local(): pl.pallas_call(functools.partial(layer, top, ff_dev, row_block, step_unit...  20.8 us
    ppermute x6, starting transfers between devices, shift(): return lax.ppermute(x, axis, [(i, (i + by) % size) for i in range(size)])  10.9 us
    ppermute x4, waiting for transfers between devices, swap(): return lax.ppermute(x, axis, [(i, i ^ by) for i in range(size)])  7.63 us
    pallas_call x2, Pallas kernels, local(): pl.pallas_call(functools.partial(bring, early, steps), out_shape=ring_sha...  5.71 us
    ppermute x6, waiting for transfers between devices, shift(): return lax.ppermute(x, axis, [(i, (i + by) % size) for i in range(size)])  4.82 us
    ppermute x4, starting transfers between devices, swap(): return lax.ppermute(x, axis, [(i, i ^ by) for i in range(size)])  3.39 us
  transfers between devices with their start and end apart: 10, of which 6 were waited for; matrix products, arithmetic and copies ran while one was open for 0% of the time, Pallas kernels for 10%

profile of v12, /device:TPU:0, one launch (start us, length us, event | category | flops | bytes accessed | tf_op | source)
XLA Modules:
  0.0 55.1 jit_solution(13427917881219038105)
XLA Ops:
  0.0 0.9 %with_routing.1.after_ref.refs_0_ = bf16[4,4224]{1,0:T(4,128)(2,1)S(1)} custom-call(bf16[4,4096]{1,0:T(4,128)(2,1)} %tokens_ref.1, s32[4,8]{1,0:T(4,128)} %ids_ref.1, s32[4,8]{1,0:T(4,128)} %numer_ref.1), custom_call_target="tpu_custom_call" | custom-call | tf_op jit(solution)/shard_map/with_routing/pallas_call | solution.py:200
  0.9 3.1 %collective-permute-start.2 = (bf16[4,4224]{1,0:T(4,128)(2,1)S(1)}, bf16[4,4224]{1,0:T(4,128)(2,1)S(1)}, u32[]{:S(2)}, u32[]{:S(2)}) collective-permute-start(bf16[4,4224]{1,0:T(4,128)(2,1)S(1)} %with_routing.1.after_ref.refs_0_), channel_id=1, source_target_pairs={{0,4},{4,8},{8,12},{12,0},{1,5},{5,9},{9,13},{13,1},{2,6},{6,10},{... | collective-permute-start | bytes 101384 | tf_op jit(solution)/shard_map/ppermute | solution.py:26
  3.9 2.6 %collective-permute-start.1 = (bf16[4,4224]{1,0:T(4,128)(2,1)S(1)}, bf16[4,4224]{1,0:T(4,128)(2,1)S(1)}, u32[]{:S(2)}, u32[]{:S(2)}) collective-permute-start(bf16[4,4224]{1,0:T(4,128)(2,1)S(1)} %with_routing.1.after_ref.refs_0_), channel_id=1, source_target_pairs={{0,8},{4,12},{8,0},{12,4},{1,9},{5,13},{9,1},{13,5},{2,10},{6,14},... | collective-permute-start | bytes 101384 | tf_op jit(solution)/shard_map/ppermute | solution.py:26
  6.5 1.3 %collective-permute-start = (bf16[4,4224]{1,0:T(4,128)(2,1)S(1)}, bf16[4,4224]{1,0:T(4,128)(2,1)S(1)}, u32[]{:S(2)}, u32[]{:S(2)}) collective-permute-start(bf16[4,4224]{1,0:T(4,128)(2,1)S(1)} %with_routing.1.after_ref.refs_0_), channel_id=1, source_target_pairs={{0,12},{4,0},{8,4},{12,8},{1,13},{5,1},{9,5},{13,9},{2,14},{6,2},{... | collective-permute-start | bytes 101384 | tf_op jit(solution)/shard_map/ppermute | solution.py:26
  7.9 2.9 %bring_weights.2 = (bf16[3,256,4096]{2,1,0:T(8,128)(2,1)S(1)}, bf16[3,256,4096]{2,1,0:T(8,128)(2,1)S(1)}, bf16[4,256,4096]{2,1,0:T(8,128)(2,1)S(1)}, f32[8,128]{1,0:T(8,128)S(1)}) custom-call(bf16[3072,4096]{1,0:T(8,128)(2,1)} %bitcast.3, bf16[3072,4096]{1,0:T(8,128)(2,1)} %bitcast.6, bf16[3072,4096]{1,0:T(8,128)(2,1)} %bitcast.9, ...), custom_call_target="tpu_custom_call" | custom-call | bytes 6291456 | tf_op jit(solution)/shard_map/bring_weights/pallas_call | solution.py:234
  10.7 0.0 collective-permute-done.2.refs_3_
  10.8 0.0 collective-permute-done.1.refs_2_
  10.8 0.0 collective-permute-done.refs_1_
  10.8 1.6 %collective-permute-start.3 = (bf16[16,4224]{1,0:T(8,128)(2,1)S(1)}, bf16[16,4224]{1,0:T(8,128)(2,1)S(1)}, u32[]{:S(2)}, u32[]{:S(2)}) collective-permute-start(bf16[16,4224]{1,0:T(8,128)(2,1)S(1)} %join.2.after_ref.refs_0_), channel_id=1, source_target_pairs={{0,2},{2,0},{1,3},{3,1},{4,6},{6,4},{5,7},{7,5},{8,10},{10,8},{9,1... | collective-permute-start | bytes 405512 | tf_op jit(solution)/shard_map/ppermute | solution.py:22
  12.4 2.9 %bring_weights.3 = (bf16[3,256,4096]{2,1,0:T(8,128)(2,1)S(1)}, bf16[3,256,4096]{2,1,0:T(8,128)(2,1)S(1)}, bf16[4,256,4096]{2,1,0:T(8,128)(2,1)S(1)}, f32[8,128]{1,0:T(8,128)S(1)}) custom-call(bf16[3072,4096]{1,0:T(8,128)(2,1)} %bitcast.4, bf16[3072,4096]{1,0:T(8,128)(2,1)} %bitcast.7, ...), custom_call_target="tpu_custom_call", output_to_operand_aliasing={{0}: (4, {}), {1}: (5, {}), {2}: (6, {})} | custom-call | bytes 6291456 | tf_op jit(solution)/shard_map/bring_weights/pallas_call | solution.py:234
  15.2 0.7 %collective-permute-done.3.refs_1_ = bf16[16,4224]{1,0:T(8,128)(2,1)S(1)} collective-permute-done((bf16[16,4224]{1,0:T(8,128)(2,1)S(1)}, bf16[16,4224]{1,0:T(8,128)(2,1)S(1)}, u32[]{:S(2)}, u32[]{:S(2)}) %collective-permute-start.3) | collective-permute-done | bytes 135200 | tf_op jit(solution)/shard_map/ppermute | solution.py:22
  15.9 0.1 collective-permute-start.4
  16.0 1.5 %collective-permute-done.4.theirs_ref = bf16[32,4224]{1,0:T(8,128)(2,1)S(1)} collective-permute-done((bf16[32,4224]{1,0:T(8,128)(2,1)S(1)}, bf16[32,4224]{1,0:T(8,128)(2,1)S(1)}, u32[]{:S(2)}, u32[]{:S(2)}) %collective-permute-start.4) | collective-permute-done | bytes 270368 | tf_op jit(solution)/shard_map/ppermute | solution.py:22
  17.5 20.8 %expert_layer.1 = (f32[32,4096]{1,0:T(8,128)S(1)}, bf16[32,4096]{1,0:T(8,128)(2,1)S(1)}, bf16[3,256,4096]{2,1,0:T(8,128)(2,1)S(1)}, bf16[3,256,4096]{2,1,0:T(8,128)(2,1)S(1)}, bf16[4,256,4096]{2,1,0:T(8,128)(2,1)S(1)}) custom-call(bf16[32,4224]{1,0:T(8,128)(2,1)S(1)} %join.3.mine_ref, ...), custom_call_target="tpu_custom_call", output_to_operand_aliasing={{2}: (5, {}), {3}: (6, {}), {4}: (7, {})} | custom-call | flops 4831838208 | bytes 62914560 | tf_op jit(solution)/shard_map/expert_layer/pallas_call | solution.py:270
  38.4 0.2 collective-permute-start.5
  38.6 1.4 %collective-permute-done.5 = bf16[32,4096]{1,0:T(8,128)(2,1)S(1)} collective-permute-done((bf16[32,4096]{1,0:T(8,128)(2,1)S(1)}, bf16[32,4096]{1,0:T(8,128)(2,1)S(1)}, u32[]{:S(2)}, u32[]{:S(2)}) %collective-permute-start.5) | collective-permute-done | bytes 262176 | tf_op jit(solution)/shard_map/ppermute | solution.py:22
  40.0 0.1 convert_add_fusion
  40.1 1.6 %collective-permute-start.6 = (bf16[16,4096]{1,0:T(8,128)(2,1)S(1)}, bf16[16,4096]{1,0:T(8,128)(2,1)S(1)}, u32[]{:S(2)}, u32[]{:S(2)}) collective-permute-start(bf16[16,4096]{1,0:T(8,128)(2,1)S(1)} %slice.47), channel_id=1, source_target_pairs={{0,2},{2,0},{1,3},{3,1},{4,6},{6,4},{5,7},{7,5},{8,10},{10,8},{9,1... | collective-permute-start | bytes 393224 | tf_op jit(solution)/shard_map/ppermute | solution.py:22
  41.6 4.0 %collective-permute-done.6 = bf16[16,4096]{1,0:T(8,128)(2,1)S(1)} collective-permute-done((bf16[16,4096]{1,0:T(8,128)(2,1)S(1)}, bf16[16,4096]{1,0:T(8,128)(2,1)S(1)}, u32[]{:S(2)}, u32[]{:S(2)}) %collective-permute-start.6) | collective-permute-done | bytes 131104 | tf_op jit(solution)/shard_map/ppermute | solution.py:22
  45.8 0.7 %collective-permute-start.7 = (bf16[4,4096]{1,0:T(4,128)(2,1)S(1)}, bf16[4,4096]{1,0:T(4,128)(2,1)S(1)}, u32[]{:S(2)}, u32[]{:S(2)}) collective-permute-start(bf16[4,4096]{1,0:T(4,128)(2,1)S(1)} %get-tuple-element.27), channel_id=1, source_target_pairs={{0,4},{4,8},{8,12},{12,0},{1,5},{5,9},{9,13},{13,1},{2,6},{6,10},{... | collective-permute-start | bytes 98312 | tf_op jit(solution)/shard_map/ppermute | solution.py:26
  46.5 3.1 %collective-permute-start.9 = (bf16[4,4096]{1,0:T(4,128)(2,1)S(1)}, bf16[4,4096]{1,0:T(4,128)(2,1)S(1)}, u32[]{:S(2)}, u32[]{:S(2)}) collective-permute-start(bf16[4,4096]{1,0:T(4,128)(2,1)S(1)} %get-tuple-element.28), channel_id=1, source_target_pairs={{0,12},{4,0},{8,4},{12,8},{1,13},{5,1},{9,5},{13,9},{2,14},{6,2},{... | collective-permute-start | bytes 98312 | tf_op jit(solution)/shard_map/ppermute | solution.py:26
  49.6 0.0 collective-permute-start.8
  49.6 1.9 %collective-permute-done.7 = bf16[4,4096]{1,0:T(4,128)(2,1)S(1)} collective-permute-done((bf16[4,4096]{1,0:T(4,128)(2,1)S(1)}, bf16[4,4096]{1,0:T(4,128)(2,1)S(1)}, u32[]{:S(2)}, u32[]{:S(2)}) %collective-permute-start.7) | collective-permute-done | bytes 32800 | tf_op jit(solution)/shard_map/ppermute | solution.py:26
  51.6 0.0 collective-permute-done.9
  51.6 2.9 %collective-permute-done.8 = bf16[4,4096]{1,0:T(4,128)(2,1)S(1)} collective-permute-done((bf16[4,4096]{1,0:T(4,128)(2,1)S(1)}, bf16[4,4096]{1,0:T(4,128)(2,1)S(1)}, u32[]{:S(2)}, u32[]{:S(2)}) %collective-permute-start.8) | collective-permute-done | bytes 32800 | tf_op jit(solution)/shard_map/ppermute | solution.py:26
  54.4 0.6 %fusion.2 = bf16[4,4096]{1,0:T(4,128)(2,1)} fusion(f32[16,4096]{1,0:T(8,128)S(1)} %get-tuple-element.26, bf16[4,4096]{1,0:T(4,128)(2,1)S(1)} %collective-permute-done.9, bf16[4,4096]{1,0:T(4,128)(2,1)S(1)} %collective-permute-done.8, bf16[4,4096]{1,0:T(4,128)(2,1)S(1)} %collective-permute-done.7), kind=kLoop, calls=%fused_computation.6 | loop fusion | flops 114688 | bytes 196608 | tf_op jit(solution)/shard_map/convert_element_type | solution.py:308
  (5 shorter events, 0.1 us)
Async XLA Ops:
  0.9 9.9 %collective-permute-start.2 = (bf16[4,4224]{1,0:T(4,128)(2,1)S(1)}, bf16[4,4224]{1,0:T(4,128)(2,1)S(1)}, u32[]{:S(2)}, u32[]{:S(2)}) collective-permute-start(bf16[4,4224]{1,0:T(4,128)(2,1)S(1)} %with_routing.1.after_ref.refs_0_), channel_id=1, source_target_pairs={{0,4},{4,8},{8,12},{12,0},{1,5},{5,9},{9,13},{13,1},{2,6},{6,10},{... | collective-permute-start | bytes 101384 | tf_op jit(solution)/shard_map/ppermute | solution.py:26
  3.9 6.8 %collective-permute-start.1 = (bf16[4,4224]{1,0:T(4,128)(2,1)S(1)}, bf16[4,4224]{1,0:T(4,128)(2,1)S(1)}, u32[]{:S(2)}, u32[]{:S(2)}) collective-permute-start(bf16[4,4224]{1,0:T(4,128)(2,1)S(1)} %with_routing.1.after_ref.refs_0_), channel_id=1, source_target_pairs={{0,8},{4,12},{8,0},{12,4},{1,9},{5,13},{9,1},{13,5},{2,10},{6,14},... | collective-permute-start | bytes 101384 | tf_op jit(solution)/shard_map/ppermute | solution.py:26
  6.5 4.2 %collective-permute-start = (bf16[4,4224]{1,0:T(4,128)(2,1)S(1)}, bf16[4,4224]{1,0:T(4,128)(2,1)S(1)}, u32[]{:S(2)}, u32[]{:S(2)}) collective-permute-start(bf16[4,4224]{1,0:T(4,128)(2,1)S(1)} %with_routing.1.after_ref.refs_0_), channel_id=1, source_target_pairs={{0,12},{4,0},{8,4},{12,8},{1,13},{5,1},{9,5},{13,9},{2,14},{6,2},{... | collective-permute-start | bytes 101384 | tf_op jit(solution)/shard_map/ppermute | solution.py:26
  10.8 5.1 %collective-permute-start.3 = (bf16[16,4224]{1,0:T(8,128)(2,1)S(1)}, bf16[16,4224]{1,0:T(8,128)(2,1)S(1)}, u32[]{:S(2)}, u32[]{:S(2)}) collective-permute-start(bf16[16,4224]{1,0:T(8,128)(2,1)S(1)} %join.2.after_ref.refs_0_), channel_id=1, source_target_pairs={{0,2},{2,0},{1,3},{3,1},{4,6},{6,4},{5,7},{7,5},{8,10},{10,8},{9,1... | collective-permute-start | bytes 405512 | tf_op jit(solution)/shard_map/ppermute | solution.py:22
  15.9 1.6 %collective-permute-start.4 = (bf16[32,4224]{1,0:T(8,128)(2,1)S(1)}, bf16[32,4224]{1,0:T(8,128)(2,1)S(1)}, u32[]{:S(2)}, u32[]{:S(2)}) collective-permute-start(bf16[32,4224]{1,0:T(8,128)(2,1)S(1)} %join.3.mine_ref), channel_id=1, source_target_pairs={{0,1},{1,0},{2,3},{3,2},{4,5},{5,4},{6,7},{7,6},{8,9},{9,8},{10,11... | collective-permute-start | bytes 811016 | tf_op jit(solution)/shard_map/ppermute | solution.py:22
  38.4 1.6 %collective-permute-start.5 = (bf16[32,4096]{1,0:T(8,128)(2,1)S(1)}, bf16[32,4096]{1,0:T(8,128)(2,1)S(1)}, u32[]{:S(2)}, u32[]{:S(2)}) collective-permute-start(bf16[32,4096]{1,0:T(8,128)(2,1)S(1)} %get-tuple-element.24), channel_id=1, source_target_pairs={{0,1},{1,0},{2,3},{3,2},{4,5},{5,4},{6,7},{7,6},{8,9},{9,8},{10,11... | collective-permute-start | bytes 786440 | tf_op jit(solution)/shard_map/ppermute | solution.py:22
  40.1 5.6 %collective-permute-start.6 = (bf16[16,4096]{1,0:T(8,128)(2,1)S(1)}, bf16[16,4096]{1,0:T(8,128)(2,1)S(1)}, u32[]{:S(2)}, u32[]{:S(2)}) collective-permute-start(bf16[16,4096]{1,0:T(8,128)(2,1)S(1)} %slice.47), channel_id=1, source_target_pairs={{0,2},{2,0},{1,3},{3,1},{4,6},{6,4},{5,7},{7,5},{8,10},{10,8},{9,1... | collective-permute-start | bytes 393224 | tf_op jit(solution)/shard_map/ppermute | solution.py:22
  45.8 5.8 %collective-permute-start.7 = (bf16[4,4096]{1,0:T(4,128)(2,1)S(1)}, bf16[4,4096]{1,0:T(4,128)(2,1)S(1)}, u32[]{:S(2)}, u32[]{:S(2)}) collective-permute-start(bf16[4,4096]{1,0:T(4,128)(2,1)S(1)} %get-tuple-element.27), channel_id=1, source_target_pairs={{0,4},{4,8},{8,12},{12,0},{1,5},{5,9},{9,13},{13,1},{2,6},{6,10},{... | collective-permute-start | bytes 98312 | tf_op jit(solution)/shard_map/ppermute | solution.py:26
  46.5 5.1 %collective-permute-start.9 = (bf16[4,4096]{1,0:T(4,128)(2,1)S(1)}, bf16[4,4096]{1,0:T(4,128)(2,1)S(1)}, u32[]{:S(2)}, u32[]{:S(2)}) collective-permute-start(bf16[4,4096]{1,0:T(4,128)(2,1)S(1)} %get-tuple-element.28), channel_id=1, source_target_pairs={{0,12},{4,0},{8,4},{12,8},{1,13},{5,1},{9,5},{13,9},{2,14},{6,2},{... | collective-permute-start | bytes 98312 | tf_op jit(solution)/shard_map/ppermute | solution.py:26
  49.6 4.8 %collective-permute-start.8 = (bf16[4,4096]{1,0:T(4,128)(2,1)S(1)}, bf16[4,4096]{1,0:T(4,128)(2,1)S(1)}, u32[]{:S(2)}, u32[]{:S(2)}) collective-permute-start(bf16[4,4096]{1,0:T(4,128)(2,1)S(1)} %get-tuple-element.29), channel_id=1, source_target_pairs={{0,8},{4,12},{8,0},{12,4},{1,9},{5,13},{9,1},{13,5},{2,10},{6,14},... | collective-permute-start | bytes 98312 | tf_op jit(solution)/shard_map/ppermute | solution.py:26

commit v13 on v12

--- a/solution.py
+++ b/solution.py
@@ -9,8 +9,8 @@
 
 EXPERTS = 32
 SIDE = 128
-SLOTS = 3
-EARLY = (1, 1)
+SLOTS = 4
+EARLY = ((1, 1, 1), (2, 1, 1), (0, 1, 0))
 GRANT = 8 << 20
 
 VMEM = pl.BlockSpec(memory_space=pltpu.VMEM)
@@ -47,19 +47,19 @@
         out_ref[part * count:(part + 1) * count, :] = refs[part][...]
 
 
-def bring(first, count, gate_ref, up_ref, down_ref, after_ref, *refs):
+def bring(firsts, counts, gate_ref, up_ref, down_ref, after_ref, *refs):
     gates, ups, downs, end_ref, sem = refs[-5:]
     size = gates.shape[1]
+    half = size // 2
     started = []
-    for step in range(first, first + count):
-        for i, (ref, ring) in enumerate([(gate_ref, gates), (up_ref, ups), (down_ref, downs)]):
+    for i, (ref, ring) in enumerate([(gate_ref, gates), (up_ref, ups), (down_ref, downs)]):
+        for step in range(firsts[i], firsts[i] + counts[i]):
             for part in range(2):
-                half = size // 2
                 started.append(
                     pltpu.make_async_copy(
                         ref.at[pl.ds(step * size + part * half, half)],
                         ring.at[step, pl.ds(part * half, half)],
-                        sem.at[i, step - first, part],
+                        sem.at[i, step - firsts[i], part],
                     )
                 )
     for copy in started:
@@ -84,7 +84,7 @@
 
 def layer(top, ff_dev, row_block, step_units, early, mine_ref, theirs_ref, gate_ref, up_ref,
           down_ref, *refs):
-    if early:
+    if max(early):
         refs = refs[3:]
     keep_ref, send_ref, gates, ups, downs, rows_ref, total, weights, hidden, sem = refs
     units, depth = down_ref.shape
@@ -105,15 +105,17 @@
 
     def wait(i, step):
         if isinstance(step, int):
-            if step >= early:
+            if step >= early[i]:
                 copy_of(i, jnp.int32(step)).wait()
         else:
-            @pl.when(step >= early)
+            @pl.when(step >= early[i])
             def _():
                 copy_of(i, step).wait()
 
-    for step in range(early, min(slots, steps)):
-        start(jnp.int32(step))
+    for step in range(min(slots, steps)):
+        for i in range(3):
+            if step >= early[i]:
+                copy_of(i, jnp.int32(step)).start()
 
     first = lax.axis_index("wide") * (units // ff_dev)
 
@@ -222,31 +224,31 @@
             pltpu.VMEM((n, step_units, depth), jnp.bfloat16) for n in (slots, slots, slots + 1)
         ]
         ring = []
-        early = 0
+        early = (0, 0, 0)
         for number, hop in enumerate(hops):
             if hop is None:
                 theirs = [shift(rows, "wide", span, -by) for by in range(1, span)]
             else:
                 theirs = [swap(rows, *hop)]
-            steps = EARLY[number] if number < len(EARLY) and units >= 8 * step_units else 0
+            more = EARLY[number] if number < len(EARLY) and units >= 8 * step_units else (0, 0, 0)
             ends = []
-            if steps:
+            if max(more):
                 *ring, end = pl.pallas_call(
-                    functools.partial(bring, early, steps),
+                    functools.partial(bring, early, more),
                     out_shape=ring_shapes + [jax.ShapeDtypeStruct((8, 128), jnp.float32)],
                     in_specs=[HBM] * 3 + [pl.BlockSpec(memory_space=pl.ANY)] + [VMEM] * len(ring),
                     out_specs=[VMEM] * 4,
-                    scratch_shapes=[pltpu.SemaphoreType.DMA((3, steps, 2))],
+                    scratch_shapes=[pltpu.SemaphoreType.DMA((3, max(more), 2))],
                     input_output_aliases={4 + i: i for i in range(len(ring))},
                     compiler_params=small,
                     cost_estimate=pl.CostEstimate(
                         flops=0,
-                        bytes_accessed=6 * steps * step_units * depth,
+                        bytes_accessed=2 * sum(more) * step_units * depth,
                         transcendentals=0,
                     ),
                     name="bring_weights",
                 )(*weights, rows, *ring)
-                early += steps
+                early = tuple(a + b for a, b in zip(early, more))
                 ends = [end]
             if hop is hops[-1]:
                 break
@@ -273,10 +275,10 @@
                 jax.ShapeDtypeStruct((half, depth), jnp.float32),
                 jax.ShapeDtypeStruct((half, depth), jnp.bfloat16),
             ]
-            + (ring_shapes if early else []),
+            + (ring_shapes if ring else []),
             in_specs=[VMEM] * 2 + [HBM] * 3 + [VMEM] * len(ring),
-            out_specs=[VMEM] * (5 if early else 2),
-            scratch_shapes=([] if early else ring_shapes)
+            out_specs=[VMEM] * (5 if ring else 2),
+            scratch_shapes=([] if ring else ring_shapes)
             + [
                 pltpu.VMEM((count, depth + SIDE), jnp.bfloat16),
                 pltpu.VMEM((count, depth), jnp.float32),
@@ -286,11 +288,11 @@
             ],
             input_output_aliases={5 + i: 2 + i for i in range(len(ring))},
             compiler_params=pltpu.CompilerParams(
-                vmem_limit_bytes=GRANT if early else 60 << 20
+                vmem_limit_bytes=GRANT if ring else 60 << 20
             ),
             cost_estimate=pl.CostEstimate(
                 flops=6 * count * units * depth,
-                bytes_accessed=6 * (units - early * step_units) * depth,
+                bytes_accessed=2 * (3 * units - sum(early) * step_units) * depth,
                 transcendentals=count * units,
             ),
             name="expert_layer",

time: 55.3 us -> 55.6 us (level)
  Pallas kernels: 27.5 us -> 29.6 us
  waiting for transfers between devices: 12.4 us -> 10.3 us
    pallas_call x2 -> x3, Pallas kernels: 5.71 us -> 8.55 us  [local(): pl.pallas_call(functools.partial(bring, early, more), out_shape=ring_shap...]
    ppermute x4, waiting for transfers between devices: 7.63 us -> 5.45 us  [swap(): return lax.ppermute(x, axis, [(i, i ^ by) for i in range(size)])]
    pallas_call x1, Pallas kernels: 20.8 us -> 20.1 us  [local(): pl.pallas_call(functools.partial(layer, top, ff_dev, row_block, step_unit...]
  transfers between devices with their start and end apart: 10 -> 10, of which waited for: 6 -> 4; matrix products, arithmetic and copies ran while one was open for 0% -> 0% of each run, Pallas kernels for 10% -> 15%
where the time goes in v13:
time: 55.6 us; the launch traced here: 55.4 us
  Pallas kernels  29.6 us (53%)
  starting transfers between devices  14.6 us (26%)
  waiting for transfers between devices  10.3 us (19%)
  other arithmetic  0.74 us (1%)
    pallas_call x1, Pallas kernels, local(): pl.pallas_call(functools.partial(layer, top, ff_dev, row_block, step_unit...  20.1 us
    ppermute x6, starting transfers between devices, shift(): return lax.ppermute(x, axis, [(i, (i + by) % size) for i in range(size)])  10.9 us
    pallas_call x3, Pallas kernels, local(): pl.pallas_call(functools.partial(bring, early, more), out_shape=ring_shap...  8.55 us
    ppermute x4, waiting for transfers between devices, swap(): return lax.ppermute(x, axis, [(i, i ^ by) for i in range(size)])  5.45 us
    ppermute x6, waiting for transfers between devices, shift(): return lax.ppermute(x, axis, [(i, (i + by) % size) for i in range(size)])  4.82 us
    ppermute x4, starting transfers between devices, swap(): return lax.ppermute(x, axis, [(i, i ^ by) for i in range(size)])  3.73 us
  transfers between devices with their start and end apart: 10, of which 4 were waited for; matrix products, arithmetic and copies ran while one was open for 0% of the time, Pallas kernels for 15%

profile of v13, /device:TPU:0, one launch (start us, length us, event | category | flops | bytes accessed | tf_op | source)
XLA Modules:
  0.0 55.4 jit_solution(13518365923341869036)
XLA Ops:
  0.0 0.9 %with_routing.1.after_ref.refs_0_ = bf16[4,4224]{1,0:T(4,128)(2,1)S(1)} custom-call(bf16[4,4096]{1,0:T(4,128)(2,1)} %tokens_ref.1, s32[4,8]{1,0:T(4,128)} %ids_ref.1, s32[4,8]{1,0:T(4,128)} %numer_ref.1), custom_call_target="tpu_custom_call" | custom-call | tf_op jit(solution)/shard_map/with_routing/pallas_call | solution.py:202
  0.9 3.1 %collective-permute-start.2 = (bf16[4,4224]{1,0:T(4,128)(2,1)S(1)}, bf16[4,4224]{1,0:T(4,128)(2,1)S(1)}, u32[]{:S(2)}, u32[]{:S(2)}) collective-permute-start(bf16[4,4224]{1,0:T(4,128)(2,1)S(1)} %with_routing.1.after_ref.refs_0_), channel_id=1, source_target_pairs={{0,4},{4,8},{8,12},{12,0},{1,5},{5,9},{9,13},{13,1},{2,6},{6,10},{... | collective-permute-start | bytes 101384 | tf_op jit(solution)/shard_map/ppermute | solution.py:26
  3.9 2.6 %collective-permute-start.1 = (bf16[4,4224]{1,0:T(4,128)(2,1)S(1)}, bf16[4,4224]{1,0:T(4,128)(2,1)S(1)}, u32[]{:S(2)}, u32[]{:S(2)}) collective-permute-start(bf16[4,4224]{1,0:T(4,128)(2,1)S(1)} %with_routing.1.after_ref.refs_0_), channel_id=1, source_target_pairs={{0,8},{4,12},{8,0},{12,4},{1,9},{5,13},{9,1},{13,5},{2,10},{6,14},... | collective-permute-start | bytes 101384 | tf_op jit(solution)/shard_map/ppermute | solution.py:26
  6.5 1.3 %collective-permute-start = (bf16[4,4224]{1,0:T(4,128)(2,1)S(1)}, bf16[4,4224]{1,0:T(4,128)(2,1)S(1)}, u32[]{:S(2)}, u32[]{:S(2)}) collective-permute-start(bf16[4,4224]{1,0:T(4,128)(2,1)S(1)} %with_routing.1.after_ref.refs_0_), channel_id=1, source_target_pairs={{0,12},{4,0},{8,4},{12,8},{1,13},{5,1},{9,5},{13,9},{2,14},{6,2},{... | collective-permute-start | bytes 101384 | tf_op jit(solution)/shard_map/ppermute | solution.py:26
  7.9 2.9 %bring_weights.3 = (bf16[4,256,4096]{2,1,0:T(8,128)(2,1)S(1)}, bf16[4,256,4096]{2,1,0:T(8,128)(2,1)S(1)}, bf16[5,256,4096]{2,1,0:T(8,128)(2,1)S(1)}, f32[8,128]{1,0:T(8,128)S(1)}) custom-call(bf16[3072,4096]{1,0:T(8,128)(2,1)} %bitcast.3, bf16[3072,4096]{1,0:T(8,128)(2,1)} %bitcast.7, bf16[3072,4096]{1,0:T(8,128)(2,1)} %bitcast.11, ...), custom_call_target="tpu_custom_call" | custom-call | bytes 6291456 | tf_op jit(solution)/shard_map/bring_weights/pallas_call | solution.py:236
  10.7 0.0 collective-permute-done.2.refs_3_
  10.8 0.0 collective-permute-done.1.refs_2_
  10.8 0.0 collective-permute-done.refs_1_
  10.8 1.6 %collective-permute-start.3 = (bf16[16,4224]{1,0:T(8,128)(2,1)S(1)}, bf16[16,4224]{1,0:T(8,128)(2,1)S(1)}, u32[]{:S(2)}, u32[]{:S(2)}) collective-permute-start(bf16[16,4224]{1,0:T(8,128)(2,1)S(1)} %join.2.after_ref.refs_0_), channel_id=1, source_target_pairs={{0,2},{2,0},{1,3},{3,1},{4,6},{6,4},{5,7},{7,5},{8,10},{10,8},{9,1... | collective-permute-start | bytes 405512 | tf_op jit(solution)/shard_map/ppermute | solution.py:22
  12.4 3.5 %bring_weights.4 = (bf16[4,256,4096]{2,1,0:T(8,128)(2,1)S(1)}, bf16[4,256,4096]{2,1,0:T(8,128)(2,1)S(1)}, bf16[5,256,4096]{2,1,0:T(8,128)(2,1)S(1)}, f32[8,128]{1,0:T(8,128)S(1)}) custom-call(bf16[3072,4096]{1,0:T(8,128)(2,1)} %bitcast.4, bf16[3072,4096]{1,0:T(8,128)(2,1)} %bitcast.8, ...), custom_call_target="tpu_custom_call", output_to_operand_aliasing={{0}: (4, {}), {1}: (5, {}), {2}: (6, {})} | custom-call | bytes 8388608 | tf_op jit(solution)/shard_map/bring_weights/pallas_call | solution.py:236
  15.9 0.0 collective-permute-done.3.refs_1_
  15.9 0.1 collective-permute-start.4
  16.0 2.2 %bring_weights.5 = (bf16[4,256,4096]{2,1,0:T(8,128)(2,1)S(1)}, bf16[4,256,4096]{2,1,0:T(8,128)(2,1)S(1)}, bf16[5,256,4096]{2,1,0:T(8,128)(2,1)S(1)}, f32[8,128]{1,0:T(8,128)}) custom-call(bf16[3072,4096]{1,0:T(8,128)(2,1)} %bitcast.5, bf16[3072,4096]{1,0:T(8,128)(2,1)} %bitcast.9, ...), custom_call_target="tpu_custom_call", output_to_operand_aliasing={{0}: (4, {}), {1}: (5, {}), {2}: (6, {})} | custom-call | bytes 2097152 | tf_op jit(solution)/shard_map/bring_weights/pallas_call | solution.py:236
  18.2 0.0 collective-permute-done.4.theirs_ref
  18.2 20.1 %expert_layer.1 = (f32[32,4096]{1,0:T(8,128)S(1)}, bf16[32,4096]{1,0:T(8,128)(2,1)S(1)}, bf16[4,256,4096]{2,1,0:T(8,128)(2,1)S(1)}, bf16[4,256,4096]{2,1,0:T(8,128)(2,1)S(1)}, bf16[5,256,4096]{2,1,0:T(8,128)(2,1)S(1)}) custom-call(bf16[32,4224]{1,0:T(8,128)(2,1)S(1)} %join.3.after_ref.mine_ref, ...), custom_call_target="tpu_custom_call", output_to_operand_aliasing={{2}: (5, {}), {3}: (6, {}), {4}: (7, {})} | custom-call | flops 4831838208 | bytes 58720256 | tf_op jit(solution)/shard_map/expert_layer/pallas_call | solution.py:272
  38.3 0.5 collective-permute-start.5
  38.9 1.2 %collective-permute-done.5 = bf16[32,4096]{1,0:T(8,128)(2,1)S(1)} collective-permute-done((bf16[32,4096]{1,0:T(8,128)(2,1)S(1)}, bf16[32,4096]{1,0:T(8,128)(2,1)S(1)}, u32[]{:S(2)}, u32[]{:S(2)}) %collective-permute-start.5) | collective-permute-done | bytes 262176 | tf_op jit(solution)/shard_map/ppermute | solution.py:22
  40.0 0.1 convert_add_fusion
  40.1 1.6 %collective-permute-start.6 = (bf16[16,4096]{1,0:T(8,128)(2,1)S(1)}, bf16[16,4096]{1,0:T(8,128)(2,1)S(1)}, u32[]{:S(2)}, u32[]{:S(2)}) collective-permute-start(bf16[16,4096]{1,0:T(8,128)(2,1)S(1)} %slice.47), channel_id=1, source_target_pairs={{0,2},{2,0},{1,3},{3,1},{4,6},{6,4},{5,7},{7,5},{8,10},{10,8},{9,1... | collective-permute-start | bytes 393224 | tf_op jit(solution)/shard_map/ppermute | solution.py:22
  41.7 4.3 %collective-permute-done.6 = bf16[16,4096]{1,0:T(8,128)(2,1)S(1)} collective-permute-done((bf16[16,4096]{1,0:T(8,128)(2,1)S(1)}, bf16[16,4096]{1,0:T(8,128)(2,1)S(1)}, u32[]{:S(2)}, u32[]{:S(2)}) %collective-permute-start.6) | collective-permute-done | bytes 131104 | tf_op jit(solution)/shard_map/ppermute | solution.py:22
  46.1 0.7 %collective-permute-start.7 = (bf16[4,4096]{1,0:T(4,128)(2,1)S(1)}, bf16[4,4096]{1,0:T(4,128)(2,1)S(1)}, u32[]{:S(2)}, u32[]{:S(2)}) collective-permute-start(bf16[4,4096]{1,0:T(4,128)(2,1)S(1)} %get-tuple-element.33), channel_id=1, source_target_pairs={{0,4},{4,8},{8,12},{12,0},{1,5},{5,9},{9,13},{13,1},{2,6},{6,10},{... | collective-permute-start | bytes 98312 | tf_op jit(solution)/shard_map/ppermute | solution.py:26
  46.8 3.1 %collective-permute-start.9 = (bf16[4,4096]{1,0:T(4,128)(2,1)S(1)}, bf16[4,4096]{1,0:T(4,128)(2,1)S(1)}, u32[]{:S(2)}, u32[]{:S(2)}) collective-permute-start(bf16[4,4096]{1,0:T(4,128)(2,1)S(1)} %get-tuple-element.34), channel_id=1, source_target_pairs={{0,12},{4,0},{8,4},{12,8},{1,13},{5,1},{9,5},{13,9},{2,14},{6,2},{... | collective-permute-start | bytes 98312 | tf_op jit(solution)/shard_map/ppermute | solution.py:26
  49.9 0.0 collective-permute-start.8
  49.9 2.1 %collective-permute-done.7 = bf16[4,4096]{1,0:T(4,128)(2,1)S(1)} collective-permute-done((bf16[4,4096]{1,0:T(4,128)(2,1)S(1)}, bf16[4,4096]{1,0:T(4,128)(2,1)S(1)}, u32[]{:S(2)}, u32[]{:S(2)}) %collective-permute-start.7) | collective-permute-done | bytes 32800 | tf_op jit(solution)/shard_map/ppermute | solution.py:26
  52.0 0.0 collective-permute-done.9
  52.0 2.7 %collective-permute-done.8 = bf16[4,4096]{1,0:T(4,128)(2,1)S(1)} collective-permute-done((bf16[4,4096]{1,0:T(4,128)(2,1)S(1)}, bf16[4,4096]{1,0:T(4,128)(2,1)S(1)}, u32[]{:S(2)}, u32[]{:S(2)}) %collective-permute-start.8) | collective-permute-done | bytes 32800 | tf_op jit(solution)/shard_map/ppermute | solution.py:26
  54.7 0.6 %fusion.2 = bf16[4,4096]{1,0:T(4,128)(2,1)} fusion(f32[16,4096]{1,0:T(8,128)S(1)} %get-tuple-element.32, bf16[4,4096]{1,0:T(4,128)(2,1)S(1)} %collective-permute-done.9, bf16[4,4096]{1,0:T(4,128)(2,1)S(1)} %collective-permute-done.8, bf16[4,4096]{1,0:T(4,128)(2,1)S(1)} %collective-permute-done.7), kind=kLoop, calls=%fused_computation.6 | loop fusion | flops 114688 | bytes 196608 | tf_op jit(solution)/shard_map/convert_element_type | solution.py:310
  (5 shorter events, 0.1 us)
Async XLA Ops:
  0.9 9.9 %collective-permute-start.2 = (bf16[4,4224]{1,0:T(4,128)(2,1)S(1)}, bf16[4,4224]{1,0:T(4,128)(2,1)S(1)}, u32[]{:S(2)}, u32[]{:S(2)}) collective-permute-start(bf16[4,4224]{1,0:T(4,128)(2,1)S(1)} %with_routing.1.after_ref.refs_0_), channel_id=1, source_target_pairs={{0,4},{4,8},{8,12},{12,0},{1,5},{5,9},{9,13},{13,1},{2,6},{6,10},{... | collective-permute-start | bytes 101384 | tf_op jit(solution)/shard_map/ppermute | solution.py:26
  3.9 6.8 %collective-permute-start.1 = (bf16[4,4224]{1,0:T(4,128)(2,1)S(1)}, bf16[4,4224]{1,0:T(4,128)(2,1)S(1)}, u32[]{:S(2)}, u32[]{:S(2)}) collective-permute-start(bf16[4,4224]{1,0:T(4,128)(2,1)S(1)} %with_routing.1.after_ref.refs_0_), channel_id=1, source_target_pairs={{0,8},{4,12},{8,0},{12,4},{1,9},{5,13},{9,1},{13,5},{2,10},{6,14},... | collective-permute-start | bytes 101384 | tf_op jit(solution)/shard_map/ppermute | solution.py:26
  6.5 4.2 %collective-permute-start = (bf16[4,4224]{1,0:T(4,128)(2,1)S(1)}, bf16[4,4224]{1,0:T(4,128)(2,1)S(1)}, u32[]{:S(2)}, u32[]{:S(2)}) collective-permute-start(bf16[4,4224]{1,0:T(4,128)(2,1)S(1)} %with_routing.1.after_ref.refs_0_), channel_id=1, source_target_pairs={{0,12},{4,0},{8,4},{12,8},{1,13},{5,1},{9,5},{13,9},{2,14},{6,2},{... | collective-permute-start | bytes 101384 | tf_op jit(solution)/shard_map/ppermute | solution.py:26
  10.8 5.1 %collective-permute-start.3 = (bf16[16,4224]{1,0:T(8,128)(2,1)S(1)}, bf16[16,4224]{1,0:T(8,128)(2,1)S(1)}, u32[]{:S(2)}, u32[]{:S(2)}) collective-permute-start(bf16[16,4224]{1,0:T(8,128)(2,1)S(1)} %join.2.after_ref.refs_0_), channel_id=1, source_target_pairs={{0,2},{2,0},{1,3},{3,1},{4,6},{6,4},{5,7},{7,5},{8,10},{10,8},{9,1... | collective-permute-start | bytes 405512 | tf_op jit(solution)/shard_map/ppermute | solution.py:22
  15.9 2.3 %collective-permute-start.4 = (bf16[32,4224]{1,0:T(8,128)(2,1)S(1)}, bf16[32,4224]{1,0:T(8,128)(2,1)S(1)}, u32[]{:S(2)}, u32[]{:S(2)}) collective-permute-start(bf16[32,4224]{1,0:T(8,128)(2,1)S(1)} %join.3.after_ref.mine_ref), channel_id=1, source_target_pairs={{0,1},{1,0},{2,3},{3,2},{4,5},{5,4},{6,7},{7,6},{8,9},{9,8},{10,11... | collective-permute-start | bytes 811016 | tf_op jit(solution)/shard_map/ppermute | solution.py:22
  38.3 1.7 %collective-permute-start.5 = (bf16[32,4096]{1,0:T(8,128)(2,1)S(1)}, bf16[32,4096]{1,0:T(8,128)(2,1)S(1)}, u32[]{:S(2)}, u32[]{:S(2)}) collective-permute-start(bf16[32,4096]{1,0:T(8,128)(2,1)S(1)} %get-tuple-element.30), channel_id=1, source_target_pairs={{0,1},{1,0},{2,3},{3,2},{4,5},{5,4},{6,7},{7,6},{8,9},{9,8},{10,11... | collective-permute-start | bytes 786440 | tf_op jit(solution)/shard_map/ppermute | solution.py:22
  40.1 5.8 %collective-permute-start.6 = (bf16[16,4096]{1,0:T(8,128)(2,1)S(1)}, bf16[16,4096]{1,0:T(8,128)(2,1)S(1)}, u32[]{:S(2)}, u32[]{:S(2)}) collective-permute-start(bf16[16,4096]{1,0:T(8,128)(2,1)S(1)} %slice.47), channel_id=1, source_target_pairs={{0,2},{2,0},{1,3},{3,1},{4,6},{6,4},{5,7},{7,5},{8,10},{10,8},{9,1... | collective-permute-start | bytes 393224 | tf_op jit(solution)/shard_map/ppermute | solution.py:22
  46.1 5.9 %collective-permute-start.7 = (bf16[4,4096]{1,0:T(4,128)(2,1)S(1)}, bf16[4,4096]{1,0:T(4,128)(2,1)S(1)}, u32[]{:S(2)}, u32[]{:S(2)}) collective-permute-start(bf16[4,4096]{1,0:T(4,128)(2,1)S(1)} %get-tuple-element.33), channel_id=1, source_target_pairs={{0,4},{4,8},{8,12},{12,0},{1,5},{5,9},{9,13},{13,1},{2,6},{6,10},{... | collective-permute-start | bytes 98312 | tf_op jit(solution)/shard_map/ppermute | solution.py:26
  46.8 5.2 %collective-permute-start.9 = (bf16[4,4096]{1,0:T(4,128)(2,1)S(1)}, bf16[4,4096]{1,0:T(4,128)(2,1)S(1)}, u32[]{:S(2)}, u32[]{:S(2)}) collective-permute-start(bf16[4,4096]{1,0:T(4,128)(2,1)S(1)} %get-tuple-element.34), channel_id=1, source_target_pairs={{0,12},{4,0},{8,4},{12,8},{1,13},{5,1},{9,5},{13,9},{2,14},{6,2},{... | collective-permute-start | bytes 98312 | tf_op jit(solution)/shard_map/ppermute | solution.py:26
  49.9 4.8 %collective-permute-start.8 = (bf16[4,4096]{1,0:T(4,128)(2,1)S(1)}, bf16[4,4096]{1,0:T(4,128)(2,1)S(1)}, u32[]{:S(2)}, u32[]{:S(2)}) collective-permute-start(bf16[4,4096]{1,0:T(4,128)(2,1)S(1)} %get-tuple-element.35), channel_id=1, source_target_pairs={{0,8},{4,12},{8,0},{12,4},{1,9},{5,13},{9,1},{13,5},{2,10},{6,14},... | collective-permute-start | bytes 98312 | tf_op jit(solution)/shard_map/ppermute | solution.py:26

commit v14 on v13

--- a/solution.py
+++ b/solution.py
@@ -10,7 +10,7 @@
 EXPERTS = 32
 SIDE = 128
 SLOTS = 4
-EARLY = ((1, 1, 1), (2, 1, 1), (0, 1, 0))
+EARLY = ((1, 1, 1), (2, 1, 1))
 GRANT = 8 << 20
 
 VMEM = pl.BlockSpec(memory_space=pltpu.VMEM)
@@ -47,18 +47,26 @@
         out_ref[part * count:(part + 1) * count, :] = refs[part][...]
 
 
+def slot_of(i, step, pairs, downs):
+    if i == 2:
+        return downs.at[lax.rem(step, downs.shape[0])]
+    size = pairs.shape[1] // 2
+    return pairs.at[lax.rem(step, pairs.shape[0]), pl.ds(i * size, size)]
+
+
 def bring(firsts, counts, gate_ref, up_ref, down_ref, after_ref, *refs):
-    gates, ups, downs, end_ref, sem = refs[-5:]
-    size = gates.shape[1]
+    pairs, downs, end_ref, sem = refs[-4:]
+    size = downs.shape[1]
     half = size // 2
     started = []
-    for i, (ref, ring) in enumerate([(gate_ref, gates), (up_ref, ups), (down_ref, downs)]):
+    for i, ref in enumerate([gate_ref, up_ref, down_ref]):
         for step in range(firsts[i], firsts[i] + counts[i]):
+            slot = slot_of(i, jnp.int32(step), pairs, downs)
             for part in range(2):
                 started.append(
                     pltpu.make_async_copy(
                         ref.at[pl.ds(step * size + part * half, half)],
-                        ring.at[step, pl.ds(part * half, half)],
+                        slot.at[pl.ds(part * half, half)],
                         sem.at[i, step - firsts[i], part],
                     )
                 )
@@ -85,19 +93,22 @@
 def layer(top, ff_dev, row_block, step_units, early, mine_ref, theirs_ref, gate_ref, up_ref,
           down_ref, *refs):
     if max(early):
-        refs = refs[3:]
-    keep_ref, send_ref, gates, ups, downs, rows_ref, total, weights, hidden, sem = refs
+        refs = refs[2:]
+    keep_ref, send_ref, pairs, downs, rows_ref, total, weights, hidden, sem = refs
     units, depth = down_ref.shape
     steps = units // step_units
     count = rows_ref.shape[0]
     half = count // 2
-    slots = gates.shape[0]
+    slots = pairs.shape[0]
 
     def copy_of(i, step):
-        src, ring = [(gate_ref, gates), (up_ref, ups), (down_ref, downs)][i]
-        slot = lax.rem(step, ring.shape[0])
+        src = [gate_ref, up_ref, down_ref][i]
         span = pl.ds(pl.multiple_of(step * step_units, step_units), step_units)
-        return pltpu.make_async_copy(src.at[span], ring.at[slot], sem.at[i, slot])
+        return pltpu.make_async_copy(
+            src.at[span],
+            slot_of(i, step, pairs, downs),
+            sem.at[i, lax.rem(step, downs.shape[0] if i == 2 else slots)],
+        )
 
     def start(step):
         for i in range(3):
@@ -139,10 +150,9 @@
 
     def products(step, block):
         x = rows_ref[block, :depth]
-        gate, up = [ring.at[lax.rem(step, ring.shape[0])] for ring in (gates, ups)]
-        g = lax.dot_general(gate[...], x, LAST, preferred_element_type=jnp.float32)
-        u = lax.dot_general(up[...], x, LAST, preferred_element_type=jnp.float32)
-        return g, u
+        pair = pairs[lax.rem(step, slots)]
+        both = lax.dot_general(pair, x, LAST, preferred_element_type=jnp.float32)
+        return both[:step_units], both[step_units:]
 
     def activate(step, block, g, u):
         expert = lax.broadcasted_iota(jnp.int32, (step_units, SIDE), 1)
@@ -221,7 +231,8 @@
         span = lax.axis_size("wide")
         slots = min(SLOTS, units // step_units)
         ring_shapes = [
-            pltpu.VMEM((n, step_units, depth), jnp.bfloat16) for n in (slots, slots, slots + 1)
+            pltpu.VMEM((slots, 2 * step_units, depth), jnp.bfloat16),
+            pltpu.VMEM((slots + 1, step_units, depth), jnp.bfloat16),
         ]
         ring = []
         early = (0, 0, 0)
@@ -237,7 +248,7 @@
                     functools.partial(bring, early, more),
                     out_shape=ring_shapes + [jax.ShapeDtypeStruct((8, 128), jnp.float32)],
                     in_specs=[HBM] * 3 + [pl.BlockSpec(memory_space=pl.ANY)] + [VMEM] * len(ring),
-                    out_specs=[VMEM] * 4,
+                    out_specs=[VMEM] * 3,
                     scratch_shapes=[pltpu.SemaphoreType.DMA((3, max(more), 2))],
                     input_output_aliases={4 + i: i for i in range(len(ring))},
                     compiler_params=small,
@@ -277,7 +288,7 @@
             ]
             + (ring_shapes if ring else []),
             in_specs=[VMEM] * 2 + [HBM] * 3 + [VMEM] * len(ring),
-            out_specs=[VMEM] * (5 if ring else 2),
+            out_specs=[VMEM] * (4 if ring else 2),
             scratch_shapes=([] if ring else ring_shapes)
             + [
                 pltpu.VMEM((count, depth + SIDE), jnp.bfloat16),

time: 55.6 us -> 55.3 us (level)
  Pallas kernels: 29.6 us -> 28.1 us
  waiting for transfers between devices: 10.3 us -> 11.8 us
    pallas_call x3 -> x2, Pallas kernels: 8.55 us -> 6.36 us  [local(): pl.pallas_call(functools.partial(bring, early, more), out_shape=ring_shap...]
    ppermute x4, waiting for transfers between devices: 5.45 us -> 6.99 us  [swap(): return lax.ppermute(x, axis, [(i, i ^ by) for i in range(size)])]
    pallas_call x1, Pallas kernels: 20.1 us -> 20.9 us  [local(): pl.pallas_call(functools.partial(layer, top, ff_dev, row_block, step_unit...]
  transfers between devices with their start and end apart: 10 -> 10, of which waited for: 4 -> 5; matrix products, arithmetic and copies ran while one was open for 0% -> 0% of each run, Pallas kernels for 15% -> 12%
where the time goes in v14:
time: 55.3 us; the launch traced here: 55.1 us
  Pallas kernels  28.1 us (51%)
  starting transfers between devices  14.3 us (26%)
  waiting for transfers between devices  11.8 us (21%)
  other arithmetic  0.74 us (1%)
    pallas_call x1, Pallas kernels, local(): pl.pallas_call(functools.partial(layer, top, ff_dev, row_block, step_unit...  20.9 us
    ppermute x6, starting transfers between devices, shift(): return lax.ppermute(x, axis, [(i, (i + by) % size) for i in range(size)])  10.9 us
    ppermute x4, waiting for transfers between devices, swap(): return lax.ppermute(x, axis, [(i, i ^ by) for i in range(size)])  6.99 us
    pallas_call x2, Pallas kernels, local(): pl.pallas_call(functools.partial(bring, early, more), out_shape=ring_shap...  6.36 us
    ppermute x6, waiting for transfers between devices, shift(): return lax.ppermute(x, axis, [(i, (i + by) % size) for i in range(size)])  4.82 us
    ppermute x4, starting transfers between devices, swap(): return lax.ppermute(x, axis, [(i, i ^ by) for i in range(size)])  3.4 us
  transfers between devices with their start and end apart: 10, of which 5 were waited for; matrix products, arithmetic and copies ran while one was open for 0% of the time, Pallas kernels for 12%

profile of v14, /device:TPU:0, one launch (start us, length us, event | category | flops | bytes accessed | tf_op | source)
XLA Modules:
  0.0 55.1 jit_solution(9258950184715585201)
XLA Ops:
  0.0 0.9 %with_routing.1.after_ref.refs_0_ = bf16[4,4224]{1,0:T(4,128)(2,1)S(1)} custom-call(bf16[4,4096]{1,0:T(4,128)(2,1)} %tokens_ref.1, s32[4,8]{1,0:T(4,128)} %ids_ref.1, s32[4,8]{1,0:T(4,128)} %numer_ref.1), custom_call_target="tpu_custom_call" | custom-call | tf_op jit(solution)/shard_map/with_routing/pallas_call | solution.py:212
  0.9 3.1 %collective-permute-start.2 = (bf16[4,4224]{1,0:T(4,128)(2,1)S(1)}, bf16[4,4224]{1,0:T(4,128)(2,1)S(1)}, u32[]{:S(2)}, u32[]{:S(2)}) collective-permute-start(bf16[4,4224]{1,0:T(4,128)(2,1)S(1)} %with_routing.1.after_ref.refs_0_), channel_id=1, source_target_pairs={{0,4},{4,8},{8,12},{12,0},{1,5},{5,9},{9,13},{13,1},{2,6},{6,10},{... | collective-permute-start | bytes 101384 | tf_op jit(solution)/shard_map/ppermute | solution.py:26
  3.9 2.6 %collective-permute-start.1 = (bf16[4,4224]{1,0:T(4,128)(2,1)S(1)}, bf16[4,4224]{1,0:T(4,128)(2,1)S(1)}, u32[]{:S(2)}, u32[]{:S(2)}) collective-permute-start(bf16[4,4224]{1,0:T(4,128)(2,1)S(1)} %with_routing.1.after_ref.refs_0_), channel_id=1, source_target_pairs={{0,8},{4,12},{8,0},{12,4},{1,9},{5,13},{9,1},{13,5},{2,10},{6,14},... | collective-permute-start | bytes 101384 | tf_op jit(solution)/shard_map/ppermute | solution.py:26
  6.5 1.3 %collective-permute-start = (bf16[4,4224]{1,0:T(4,128)(2,1)S(1)}, bf16[4,4224]{1,0:T(4,128)(2,1)S(1)}, u32[]{:S(2)}, u32[]{:S(2)}) collective-permute-start(bf16[4,4224]{1,0:T(4,128)(2,1)S(1)} %with_routing.1.after_ref.refs_0_), channel_id=1, source_target_pairs={{0,12},{4,0},{8,4},{12,8},{1,13},{5,1},{9,5},{13,9},{2,14},{6,2},{... | collective-permute-start | bytes 101384 | tf_op jit(solution)/shard_map/ppermute | solution.py:26
  7.9 2.9 %bring_weights.2 = (bf16[4,512,4096]{2,1,0:T(8,128)(2,1)S(1)}, bf16[5,256,4096]{2,1,0:T(8,128)(2,1)S(1)}, f32[8,128]{1,0:T(8,128)S(1)}) custom-call(bf16[3072,4096]{1,0:T(8,128)(2,1)} %bitcast.3, bf16[3072,4096]{1,0:T(8,128)(2,1)} %bitcast.6, bf16[3072,4096]{1,0:T(8,128)(2,1)} %bitcast.9, bf16[4,4224]{1,0:T(4,128)(2,1)S(1)} %with_routing.1.after_ref.refs_0_), custom_call_target="tpu_custom_call" | custom-call | bytes 6291456 | tf_op jit(solution)/shard_map/bring_weights/pallas_call | solution.py:247
  10.7 0.0 collective-permute-done.2.refs_3_
  10.8 0.0 collective-permute-done.1.refs_2_
  10.8 0.0 collective-permute-done.refs_1_
  10.8 1.6 %collective-permute-start.3 = (bf16[16,4224]{1,0:T(8,128)(2,1)S(1)}, bf16[16,4224]{1,0:T(8,128)(2,1)S(1)}, u32[]{:S(2)}, u32[]{:S(2)}) collective-permute-start(bf16[16,4224]{1,0:T(8,128)(2,1)S(1)} %join.2.after_ref.refs_0_), channel_id=1, source_target_pairs={{0,2},{2,0},{1,3},{3,1},{4,6},{6,4},{5,7},{7,5},{8,10},{10,8},{9,1... | collective-permute-start | bytes 405512 | tf_op jit(solution)/shard_map/ppermute | solution.py:22
  12.4 3.5 %bring_weights.3 = (bf16[4,512,4096]{2,1,0:T(8,128)(2,1)S(1)}, bf16[5,256,4096]{2,1,0:T(8,128)(2,1)S(1)}, f32[8,128]{1,0:T(8,128)S(1)}) custom-call(bf16[3072,4096]{1,0:T(8,128)(2,1)} %bitcast.4, bf16[3072,4096]{1,0:T(8,128)(2,1)} %bitcast.7, bf16[3072,4096]{1,0:T(8,128)(2,1)} %bitcast.10, ...), custom_call_target="tpu_custom_call", output_to_operand_aliasing={{0}: (4, {}), {1}: (5, {})} | custom-call | bytes 8388608 | tf_op jit(solution)/shard_map/bring_weights/pallas_call | solution.py:247
  15.9 0.0 collective-permute-done.3.refs_1_
  15.9 0.1 collective-permute-start.4
  16.0 1.5 %collective-permute-done.4.theirs_ref = bf16[32,4224]{1,0:T(8,128)(2,1)S(1)} collective-permute-done((bf16[32,4224]{1,0:T(8,128)(2,1)S(1)}, bf16[32,4224]{1,0:T(8,128)(2,1)S(1)}, u32[]{:S(2)}, u32[]{:S(2)}) %collective-permute-start.4) | collective-permute-done | bytes 270368 | tf_op jit(solution)/shard_map/ppermute | solution.py:22
  17.5 20.9 %expert_layer.1 = (f32[32,4096]{1,0:T(8,128)S(1)}, bf16[32,4096]{1,0:T(8,128)(2,1)S(1)}, bf16[4,512,4096]{2,1,0:T(8,128)(2,1)S(1)}, bf16[5,256,4096]{2,1,0:T(8,128)(2,1)S(1)}) custom-call(bf16[32,4224]{1,0:T(8,128)(2,1)S(1)} %join.3.mine_ref, bf16[32,4224]{1,0:T(8,128)(2,1)S(1)} %collective-permute-done.4.theirs_ref, ...), custom_call_target="tpu_custom_call", output_to_operand_aliasing={{2}: (5, {}), {3}: (6, {})} | custom-call | flops 4831838208 | bytes 60817408 | tf_op jit(solution)/shard_map/expert_layer/pallas_call | solution.py:283
  38.4 0.2 collective-permute-start.5
  38.6 1.4 %collective-permute-done.5 = bf16[32,4096]{1,0:T(8,128)(2,1)S(1)} collective-permute-done((bf16[32,4096]{1,0:T(8,128)(2,1)S(1)}, bf16[32,4096]{1,0:T(8,128)(2,1)S(1)}, u32[]{:S(2)}, u32[]{:S(2)}) %collective-permute-start.5) | collective-permute-done | bytes 262176 | tf_op jit(solution)/shard_map/ppermute | solution.py:22
  40.0 0.1 convert_add_fusion
  40.1 1.5 %collective-permute-start.6 = (bf16[16,4096]{1,0:T(8,128)(2,1)S(1)}, bf16[16,4096]{1,0:T(8,128)(2,1)S(1)}, u32[]{:S(2)}, u32[]{:S(2)}) collective-permute-start(bf16[16,4096]{1,0:T(8,128)(2,1)S(1)} %slice.47), channel_id=1, source_target_pairs={{0,2},{2,0},{1,3},{3,1},{4,6},{6,4},{5,7},{7,5},{8,10},{10,8},{9,1... | collective-permute-start | bytes 393224 | tf_op jit(solution)/shard_map/ppermute | solution.py:22
  41.6 4.1 %collective-permute-done.6 = bf16[16,4096]{1,0:T(8,128)(2,1)S(1)} collective-permute-done((bf16[16,4096]{1,0:T(8,128)(2,1)S(1)}, bf16[16,4096]{1,0:T(8,128)(2,1)S(1)}, u32[]{:S(2)}, u32[]{:S(2)}) %collective-permute-start.6) | collective-permute-done | bytes 131104 | tf_op jit(solution)/shard_map/ppermute | solution.py:22
  45.8 0.7 %collective-permute-start.7 = (bf16[4,4096]{1,0:T(4,128)(2,1)S(1)}, bf16[4,4096]{1,0:T(4,128)(2,1)S(1)}, u32[]{:S(2)}, u32[]{:S(2)}) collective-permute-start(bf16[4,4096]{1,0:T(4,128)(2,1)S(1)} %get-tuple-element.23), channel_id=1, source_target_pairs={{0,4},{4,8},{8,12},{12,0},{1,5},{5,9},{9,13},{13,1},{2,6},{6,10},{... | collective-permute-start | bytes 98312 | tf_op jit(solution)/shard_map/ppermute | solution.py:26
  46.5 3.1 %collective-permute-start.9 = (bf16[4,4096]{1,0:T(4,128)(2,1)S(1)}, bf16[4,4096]{1,0:T(4,128)(2,1)S(1)}, u32[]{:S(2)}, u32[]{:S(2)}) collective-permute-start(bf16[4,4096]{1,0:T(4,128)(2,1)S(1)} %get-tuple-element.24), channel_id=1, source_target_pairs={{0,12},{4,0},{8,4},{12,8},{1,13},{5,1},{9,5},{13,9},{2,14},{6,2},{... | collective-permute-start | bytes 98312 | tf_op jit(solution)/shard_map/ppermute | solution.py:26
  49.7 0.0 collective-permute-start.8
  49.7 1.9 %collective-permute-done.7 = bf16[4,4096]{1,0:T(4,128)(2,1)S(1)} collective-permute-done((bf16[4,4096]{1,0:T(4,128)(2,1)S(1)}, bf16[4,4096]{1,0:T(4,128)(2,1)S(1)}, u32[]{:S(2)}, u32[]{:S(2)}) %collective-permute-start.7) | collective-permute-done | bytes 32800 | tf_op jit(solution)/shard_map/ppermute | solution.py:26
  51.6 0.0 collective-permute-done.9
  51.6 2.9 %collective-permute-done.8 = bf16[4,4096]{1,0:T(4,128)(2,1)S(1)} collective-permute-done((bf16[4,4096]{1,0:T(4,128)(2,1)S(1)}, bf16[4,4096]{1,0:T(4,128)(2,1)S(1)}, u32[]{:S(2)}, u32[]{:S(2)}) %collective-permute-start.8) | collective-permute-done | bytes 32800 | tf_op jit(solution)/shard_map/ppermute | solution.py:26
  54.5 0.6 %fusion.2 = bf16[4,4096]{1,0:T(4,128)(2,1)} fusion(f32[16,4096]{1,0:T(8,128)S(1)} %get-tuple-element.22, bf16[4,4096]{1,0:T(4,128)(2,1)S(1)} %collective-permute-done.9, bf16[4,4096]{1,0:T(4,128)(2,1)S(1)} %collective-permute-done.8, bf16[4,4096]{1,0:T(4,128)(2,1)S(1)} %collective-permute-done.7), kind=kLoop, calls=%fused_computation.6 | loop fusion | flops 114688 | bytes 196608 | tf_op jit(solution)/shard_map/convert_element_type | solution.py:321
  (5 shorter events, 0.1 us)
Async XLA Ops:
  0.9 9.9 %collective-permute-start.2 = (bf16[4,4224]{1,0:T(4,128)(2,1)S(1)}, bf16[4,4224]{1,0:T(4,128)(2,1)S(1)}, u32[]{:S(2)}, u32[]{:S(2)}) collective-permute-start(bf16[4,4224]{1,0:T(4,128)(2,1)S(1)} %with_routing.1.after_ref.refs_0_), channel_id=1, source_target_pairs={{0,4},{4,8},{8,12},{12,0},{1,5},{5,9},{9,13},{13,1},{2,6},{6,10},{... | collective-permute-start | bytes 101384 | tf_op jit(solution)/shard_map/ppermute | solution.py:26
  3.9 6.8 %collective-permute-start.1 = (bf16[4,4224]{1,0:T(4,128)(2,1)S(1)}, bf16[4,4224]{1,0:T(4,128)(2,1)S(1)}, u32[]{:S(2)}, u32[]{:S(2)}) collective-permute-start(bf16[4,4224]{1,0:T(4,128)(2,1)S(1)} %with_routing.1.after_ref.refs_0_), channel_id=1, source_target_pairs={{0,8},{4,12},{8,0},{12,4},{1,9},{5,13},{9,1},{13,5},{2,10},{6,14},... | collective-permute-start | bytes 101384 | tf_op jit(solution)/shard_map/ppermute | solution.py:26
  6.5 4.2 %collective-permute-start = (bf16[4,4224]{1,0:T(4,128)(2,1)S(1)}, bf16[4,4224]{1,0:T(4,128)(2,1)S(1)}, u32[]{:S(2)}, u32[]{:S(2)}) collective-permute-start(bf16[4,4224]{1,0:T(4,128)(2,1)S(1)} %with_routing.1.after_ref.refs_0_), channel_id=1, source_target_pairs={{0,12},{4,0},{8,4},{12,8},{1,13},{5,1},{9,5},{13,9},{2,14},{6,2},{... | collective-permute-start | bytes 101384 | tf_op jit(solution)/shard_map/ppermute | solution.py:26
  10.8 5.1 %collective-permute-start.3 = (bf16[16,4224]{1,0:T(8,128)(2,1)S(1)}, bf16[16,4224]{1,0:T(8,128)(2,1)S(1)}, u32[]{:S(2)}, u32[]{:S(2)}) collective-permute-start(bf16[16,4224]{1,0:T(8,128)(2,1)S(1)} %join.2.after_ref.refs_0_), channel_id=1, source_target_pairs={{0,2},{2,0},{1,3},{3,1},{4,6},{6,4},{5,7},{7,5},{8,10},{10,8},{9,1... | collective-permute-start | bytes 405512 | tf_op jit(solution)/shard_map/ppermute | solution.py:22
  15.9 1.6 %collective-permute-start.4 = (bf16[32,4224]{1,0:T(8,128)(2,1)S(1)}, bf16[32,4224]{1,0:T(8,128)(2,1)S(1)}, u32[]{:S(2)}, u32[]{:S(2)}) collective-permute-start(bf16[32,4224]{1,0:T(8,128)(2,1)S(1)} %join.3.mine_ref), channel_id=1, source_target_pairs={{0,1},{1,0},{2,3},{3,2},{4,5},{5,4},{6,7},{7,6},{8,9},{9,8},{10,11... | collective-permute-start | bytes 811016 | tf_op jit(solution)/shard_map/ppermute | solution.py:22
  38.4 1.6 %collective-permute-start.5 = (bf16[32,4096]{1,0:T(8,128)(2,1)S(1)}, bf16[32,4096]{1,0:T(8,128)(2,1)S(1)}, u32[]{:S(2)}, u32[]{:S(2)}) collective-permute-start(bf16[32,4096]{1,0:T(8,128)(2,1)S(1)} %get-tuple-element.20), channel_id=1, source_target_pairs={{0,1},{1,0},{2,3},{3,2},{4,5},{5,4},{6,7},{7,6},{8,9},{9,8},{10,11... | collective-permute-start | bytes 786440 | tf_op jit(solution)/shard_map/ppermute | solution.py:22
  40.1 5.6 %collective-permute-start.6 = (bf16[16,4096]{1,0:T(8,128)(2,1)S(1)}, bf16[16,4096]{1,0:T(8,128)(2,1)S(1)}, u32[]{:S(2)}, u32[]{:S(2)}) collective-permute-start(bf16[16,4096]{1,0:T(8,128)(2,1)S(1)} %slice.47), channel_id=1, source_target_pairs={{0,2},{2,0},{1,3},{3,1},{4,6},{6,4},{5,7},{7,5},{8,10},{10,8},{9,1... | collective-permute-start | bytes 393224 | tf_op jit(solution)/shard_map/ppermute | solution.py:22
  45.8 5.8 %collective-permute-start.7 = (bf16[4,4096]{1,0:T(4,128)(2,1)S(1)}, bf16[4,4096]{1,0:T(4,128)(2,1)S(1)}, u32[]{:S(2)}, u32[]{:S(2)}) collective-permute-start(bf16[4,4096]{1,0:T(4,128)(2,1)S(1)} %get-tuple-element.23), channel_id=1, source_target_pairs={{0,4},{4,8},{8,12},{12,0},{1,5},{5,9},{9,13},{13,1},{2,6},{6,10},{... | collective-permute-start | bytes 98312 | tf_op jit(solution)/shard_map/ppermute | solution.py:26
  46.5 5.1 %collective-permute-start.9 = (bf16[4,4096]{1,0:T(4,128)(2,1)S(1)}, bf16[4,4096]{1,0:T(4,128)(2,1)S(1)}, u32[]{:S(2)}, u32[]{:S(2)}) collective-permute-start(bf16[4,4096]{1,0:T(4,128)(2,1)S(1)} %get-tuple-element.24), channel_id=1, source_target_pairs={{0,12},{4,0},{8,4},{12,8},{1,13},{5,1},{9,5},{13,9},{2,14},{6,2},{... | collective-permute-start | bytes 98312 | tf_op jit(solution)/shard_map/ppermute | solution.py:26
  49.7 4.8 %collective-permute-start.8 = (bf16[4,4096]{1,0:T(4,128)(2,1)S(1)}, bf16[4,4096]{1,0:T(4,128)(2,1)S(1)}, u32[]{:S(2)}, u32[]{:S(2)}) collective-permute-start(bf16[4,4096]{1,0:T(4,128)(2,1)S(1)} %get-tuple-element.25), channel_id=1, source_target_pairs={{0,8},{4,12},{8,0},{12,4},{1,9},{5,13},{9,1},{13,5},{2,10},{6,14},... | collective-permute-start | bytes 98312 | tf_op jit(solution)/shard_map/ppermute | solution.py:26

commit v15 on v13

--- a/solution.py
+++ b/solution.py
@@ -10,7 +10,7 @@
 EXPERTS = 32
 SIDE = 128
 SLOTS = 4
-EARLY = ((1, 1, 1), (2, 1, 1), (0, 1, 0))
+EARLY = ((1, 1, 1), (2, 1, 1))
 GRANT = 8 << 20
 
 VMEM = pl.BlockSpec(memory_space=pltpu.VMEM)

time: 55.6 us -> 54.7 us (0.984)
  Pallas kernels: 29.6 us -> 27.6 us
  waiting for transfers between devices: 10.3 us -> 11.8 us
    pallas_call x3 -> x2, Pallas kernels: 8.55 us -> 6.36 us  [local(): pl.pallas_call(functools.partial(bring, early, more), out_shape=ring_shap...]
    ppermute x4, waiting for transfers between devices: 5.45 us -> 6.99 us  [swap(): return lax.ppermute(x, axis, [(i, i ^ by) for i in range(size)])]
  transfers between devices with their start and end apart: 10 -> 10, of which waited for: 4 -> 5; matrix products, arithmetic and copies ran while one was open for 0% -> 0% of each run, Pallas kernels for 15% -> 12%
where the time goes in v15:
time: 54.7 us; the launch traced here: 54.5 us
  Pallas kernels  27.6 us (50%)
  starting transfers between devices  14.3 us (26%)
  waiting for transfers between devices  11.8 us (22%)
  other arithmetic  0.74 us (1%)
    pallas_call x1, Pallas kernels, local(): pl.pallas_call(functools.partial(layer, top, ff_dev, row_block, step_unit...  20.3 us
    ppermute x6, starting transfers between devices, shift(): return lax.ppermute(x, axis, [(i, (i + by) % size) for i in range(size)])  10.9 us
    ppermute x4, waiting for transfers between devices, swap(): return lax.ppermute(x, axis, [(i, i ^ by) for i in range(size)])  6.99 us
    pallas_call x2, Pallas kernels, local(): pl.pallas_call(functools.partial(bring, early, more), out_shape=ring_shap...  6.36 us
    ppermute x6, waiting for transfers between devices, shift(): return lax.ppermute(x, axis, [(i, (i + by) % size) for i in range(size)])  4.82 us
    ppermute x4, starting transfers between devices, swap(): return lax.ppermute(x, axis, [(i, i ^ by) for i in range(size)])  3.38 us
  transfers between devices with their start and end apart: 10, of which 5 were waited for; matrix products, arithmetic and copies ran while one was open for 0% of the time, Pallas kernels for 12%

profile of v15, /device:TPU:0, one launch (start us, length us, event | category | flops | bytes accessed | tf_op | source)
XLA Modules:
  0.0 54.5 jit_solution(9785237963716796906)
XLA Ops:
  0.0 0.9 %with_routing.1.after_ref.refs_0_ = bf16[4,4224]{1,0:T(4,128)(2,1)S(1)} custom-call(bf16[4,4096]{1,0:T(4,128)(2,1)} %tokens_ref.1, s32[4,8]{1,0:T(4,128)} %ids_ref.1, s32[4,8]{1,0:T(4,128)} %numer_ref.1), custom_call_target="tpu_custom_call" | custom-call | tf_op jit(solution)/shard_map/with_routing/pallas_call | solution.py:202
  0.9 3.1 %collective-permute-start.2 = (bf16[4,4224]{1,0:T(4,128)(2,1)S(1)}, bf16[4,4224]{1,0:T(4,128)(2,1)S(1)}, u32[]{:S(2)}, u32[]{:S(2)}) collective-permute-start(bf16[4,4224]{1,0:T(4,128)(2,1)S(1)} %with_routing.1.after_ref.refs_0_), channel_id=1, source_target_pairs={{0,4},{4,8},{8,12},{12,0},{1,5},{5,9},{9,13},{13,1},{2,6},{6,10},{... | collective-permute-start | bytes 101384 | tf_op jit(solution)/shard_map/ppermute | solution.py:26
  3.9 2.6 %collective-permute-start.1 = (bf16[4,4224]{1,0:T(4,128)(2,1)S(1)}, bf16[4,4224]{1,0:T(4,128)(2,1)S(1)}, u32[]{:S(2)}, u32[]{:S(2)}) collective-permute-start(bf16[4,4224]{1,0:T(4,128)(2,1)S(1)} %with_routing.1.after_ref.refs_0_), channel_id=1, source_target_pairs={{0,8},{4,12},{8,0},{12,4},{1,9},{5,13},{9,1},{13,5},{2,10},{6,14},... | collective-permute-start | bytes 101384 | tf_op jit(solution)/shard_map/ppermute | solution.py:26
  6.5 1.3 %collective-permute-start = (bf16[4,4224]{1,0:T(4,128)(2,1)S(1)}, bf16[4,4224]{1,0:T(4,128)(2,1)S(1)}, u32[]{:S(2)}, u32[]{:S(2)}) collective-permute-start(bf16[4,4224]{1,0:T(4,128)(2,1)S(1)} %with_routing.1.after_ref.refs_0_), channel_id=1, source_target_pairs={{0,12},{4,0},{8,4},{12,8},{1,13},{5,1},{9,5},{13,9},{2,14},{6,2},{... | collective-permute-start | bytes 101384 | tf_op jit(solution)/shard_map/ppermute | solution.py:26
  7.9 2.9 %bring_weights.2 = (bf16[4,256,4096]{2,1,0:T(8,128)(2,1)S(1)}, bf16[4,256,4096]{2,1,0:T(8,128)(2,1)S(1)}, bf16[5,256,4096]{2,1,0:T(8,128)(2,1)S(1)}, f32[8,128]{1,0:T(8,128)S(1)}) custom-call(bf16[3072,4096]{1,0:T(8,128)(2,1)} %bitcast.3, bf16[3072,4096]{1,0:T(8,128)(2,1)} %bitcast.6, bf16[3072,4096]{1,0:T(8,128)(2,1)} %bitcast.9, ...), custom_call_target="tpu_custom_call" | custom-call | bytes 6291456 | tf_op jit(solution)/shard_map/bring_weights/pallas_call | solution.py:236
  10.7 0.0 collective-permute-done.2.refs_3_
  10.8 0.0 collective-permute-done.1.refs_2_
  10.8 0.0 collective-permute-done.refs_1_
  10.8 1.6 %collective-permute-start.3 = (bf16[16,4224]{1,0:T(8,128)(2,1)S(1)}, bf16[16,4224]{1,0:T(8,128)(2,1)S(1)}, u32[]{:S(2)}, u32[]{:S(2)}) collective-permute-start(bf16[16,4224]{1,0:T(8,128)(2,1)S(1)} %join.2.after_ref.refs_0_), channel_id=1, source_target_pairs={{0,2},{2,0},{1,3},{3,1},{4,6},{6,4},{5,7},{7,5},{8,10},{10,8},{9,1... | collective-permute-start | bytes 405512 | tf_op jit(solution)/shard_map/ppermute | solution.py:22
  12.4 3.5 %bring_weights.3 = (bf16[4,256,4096]{2,1,0:T(8,128)(2,1)S(1)}, bf16[4,256,4096]{2,1,0:T(8,128)(2,1)S(1)}, bf16[5,256,4096]{2,1,0:T(8,128)(2,1)S(1)}, f32[8,128]{1,0:T(8,128)S(1)}) custom-call(bf16[3072,4096]{1,0:T(8,128)(2,1)} %bitcast.4, bf16[3072,4096]{1,0:T(8,128)(2,1)} %bitcast.7, ...), custom_call_target="tpu_custom_call", output_to_operand_aliasing={{0}: (4, {}), {1}: (5, {}), {2}: (6, {})} | custom-call | bytes 8388608 | tf_op jit(solution)/shard_map/bring_weights/pallas_call | solution.py:236
  15.9 0.0 collective-permute-done.3.refs_1_
  15.9 0.1 collective-permute-start.4
  16.0 1.5 %collective-permute-done.4.theirs_ref = bf16[32,4224]{1,0:T(8,128)(2,1)S(1)} collective-permute-done((bf16[32,4224]{1,0:T(8,128)(2,1)S(1)}, bf16[32,4224]{1,0:T(8,128)(2,1)S(1)}, u32[]{:S(2)}, u32[]{:S(2)}) %collective-permute-start.4) | collective-permute-done | bytes 270368 | tf_op jit(solution)/shard_map/ppermute | solution.py:22
  17.5 20.3 %expert_layer.1 = (f32[32,4096]{1,0:T(8,128)S(1)}, bf16[32,4096]{1,0:T(8,128)(2,1)S(1)}, bf16[4,256,4096]{2,1,0:T(8,128)(2,1)S(1)}, bf16[4,256,4096]{2,1,0:T(8,128)(2,1)S(1)}, bf16[5,256,4096]{2,1,0:T(8,128)(2,1)S(1)}) custom-call(bf16[32,4224]{1,0:T(8,128)(2,1)S(1)} %join.3.mine_ref, ...), custom_call_target="tpu_custom_call", output_to_operand_aliasing={{2}: (5, {}), {3}: (6, {}), {4}: (7, {})} | custom-call | flops 4831838208 | bytes 60817408 | tf_op jit(solution)/shard_map/expert_layer/pallas_call | solution.py:272
  37.8 0.2 collective-permute-start.5
  38.0 1.4 %collective-permute-done.5 = bf16[32,4096]{1,0:T(8,128)(2,1)S(1)} collective-permute-done((bf16[32,4096]{1,0:T(8,128)(2,1)S(1)}, bf16[32,4096]{1,0:T(8,128)(2,1)S(1)}, u32[]{:S(2)}, u32[]{:S(2)}) %collective-permute-start.5) | collective-permute-done | bytes 262176 | tf_op jit(solution)/shard_map/ppermute | solution.py:22
  39.4 0.1 convert_add_fusion
  39.5 1.5 %collective-permute-start.6 = (bf16[16,4096]{1,0:T(8,128)(2,1)S(1)}, bf16[16,4096]{1,0:T(8,128)(2,1)S(1)}, u32[]{:S(2)}, u32[]{:S(2)}) collective-permute-start(bf16[16,4096]{1,0:T(8,128)(2,1)S(1)} %slice.47), channel_id=1, source_target_pairs={{0,2},{2,0},{1,3},{3,1},{4,6},{6,4},{5,7},{7,5},{8,10},{10,8},{9,1... | collective-permute-start | bytes 393224 | tf_op jit(solution)/shard_map/ppermute | solution.py:22
  41.1 4.1 %collective-permute-done.6 = bf16[16,4096]{1,0:T(8,128)(2,1)S(1)} collective-permute-done((bf16[16,4096]{1,0:T(8,128)(2,1)S(1)}, bf16[16,4096]{1,0:T(8,128)(2,1)S(1)}, u32[]{:S(2)}, u32[]{:S(2)}) %collective-permute-start.6) | collective-permute-done | bytes 131104 | tf_op jit(solution)/shard_map/ppermute | solution.py:22
  45.2 0.7 %collective-permute-start.7 = (bf16[4,4096]{1,0:T(4,128)(2,1)S(1)}, bf16[4,4096]{1,0:T(4,128)(2,1)S(1)}, u32[]{:S(2)}, u32[]{:S(2)}) collective-permute-start(bf16[4,4096]{1,0:T(4,128)(2,1)S(1)} %get-tuple-element.27), channel_id=1, source_target_pairs={{0,4},{4,8},{8,12},{12,0},{1,5},{5,9},{9,13},{13,1},{2,6},{6,10},{... | collective-permute-start | bytes 98312 | tf_op jit(solution)/shard_map/ppermute | solution.py:26
  45.9 3.1 %collective-permute-start.9 = (bf16[4,4096]{1,0:T(4,128)(2,1)S(1)}, bf16[4,4096]{1,0:T(4,128)(2,1)S(1)}, u32[]{:S(2)}, u32[]{:S(2)}) collective-permute-start(bf16[4,4096]{1,0:T(4,128)(2,1)S(1)} %get-tuple-element.28), channel_id=1, source_target_pairs={{0,12},{4,0},{8,4},{12,8},{1,13},{5,1},{9,5},{13,9},{2,14},{6,2},{... | collective-permute-start | bytes 98312 | tf_op jit(solution)/shard_map/ppermute | solution.py:26
  49.1 0.0 collective-permute-start.8
  49.1 1.9 %collective-permute-done.7 = bf16[4,4096]{1,0:T(4,128)(2,1)S(1)} collective-permute-done((bf16[4,4096]{1,0:T(4,128)(2,1)S(1)}, bf16[4,4096]{1,0:T(4,128)(2,1)S(1)}, u32[]{:S(2)}, u32[]{:S(2)}) %collective-permute-start.7) | collective-permute-done | bytes 32800 | tf_op jit(solution)/shard_map/ppermute | solution.py:26
  51.0 0.0 collective-permute-done.9
  51.0 2.9 %collective-permute-done.8 = bf16[4,4096]{1,0:T(4,128)(2,1)S(1)} collective-permute-done((bf16[4,4096]{1,0:T(4,128)(2,1)S(1)}, bf16[4,4096]{1,0:T(4,128)(2,1)S(1)}, u32[]{:S(2)}, u32[]{:S(2)}) %collective-permute-start.8) | collective-permute-done | bytes 32800 | tf_op jit(solution)/shard_map/ppermute | solution.py:26
  53.9 0.6 %fusion.2 = bf16[4,4096]{1,0:T(4,128)(2,1)} fusion(f32[16,4096]{1,0:T(8,128)S(1)} %get-tuple-element.26, bf16[4,4096]{1,0:T(4,128)(2,1)S(1)} %collective-permute-done.9, bf16[4,4096]{1,0:T(4,128)(2,1)S(1)} %collective-permute-done.8, bf16[4,4096]{1,0:T(4,128)(2,1)S(1)} %collective-permute-done.7), kind=kLoop, calls=%fused_computation.6 | loop fusion | flops 114688 | bytes 196608 | tf_op jit(solution)/shard_map/convert_element_type | solution.py:310
  (5 shorter events, 0.1 us)
Async XLA Ops:
  0.9 9.9 %collective-permute-start.2 = (bf16[4,4224]{1,0:T(4,128)(2,1)S(1)}, bf16[4,4224]{1,0:T(4,128)(2,1)S(1)}, u32[]{:S(2)}, u32[]{:S(2)}) collective-permute-start(bf16[4,4224]{1,0:T(4,128)(2,1)S(1)} %with_routing.1.after_ref.refs_0_), channel_id=1, source_target_pairs={{0,4},{4,8},{8,12},{12,0},{1,5},{5,9},{9,13},{13,1},{2,6},{6,10},{... | collective-permute-start | bytes 101384 | tf_op jit(solution)/shard_map/ppermute | solution.py:26
  3.9 6.8 %collective-permute-start.1 = (bf16[4,4224]{1,0:T(4,128)(2,1)S(1)}, bf16[4,4224]{1,0:T(4,128)(2,1)S(1)}, u32[]{:S(2)}, u32[]{:S(2)}) collective-permute-start(bf16[4,4224]{1,0:T(4,128)(2,1)S(1)} %with_routing.1.after_ref.refs_0_), channel_id=1, source_target_pairs={{0,8},{4,12},{8,0},{12,4},{1,9},{5,13},{9,1},{13,5},{2,10},{6,14},... | collective-permute-start | bytes 101384 | tf_op jit(solution)/shard_map/ppermute | solution.py:26
  6.5 4.2 %collective-permute-start = (bf16[4,4224]{1,0:T(4,128)(2,1)S(1)}, bf16[4,4224]{1,0:T(4,128)(2,1)S(1)}, u32[]{:S(2)}, u32[]{:S(2)}) collective-permute-start(bf16[4,4224]{1,0:T(4,128)(2,1)S(1)} %with_routing.1.after_ref.refs_0_), channel_id=1, source_target_pairs={{0,12},{4,0},{8,4},{12,8},{1,13},{5,1},{9,5},{13,9},{2,14},{6,2},{... | collective-permute-start | bytes 101384 | tf_op jit(solution)/shard_map/ppermute | solution.py:26
  10.8 5.1 %collective-permute-start.3 = (bf16[16,4224]{1,0:T(8,128)(2,1)S(1)}, bf16[16,4224]{1,0:T(8,128)(2,1)S(1)}, u32[]{:S(2)}, u32[]{:S(2)}) collective-permute-start(bf16[16,4224]{1,0:T(8,128)(2,1)S(1)} %join.2.after_ref.refs_0_), channel_id=1, source_target_pairs={{0,2},{2,0},{1,3},{3,1},{4,6},{6,4},{5,7},{7,5},{8,10},{10,8},{9,1... | collective-permute-start | bytes 405512 | tf_op jit(solution)/shard_map/ppermute | solution.py:22
  15.9 1.6 %collective-permute-start.4 = (bf16[32,4224]{1,0:T(8,128)(2,1)S(1)}, bf16[32,4224]{1,0:T(8,128)(2,1)S(1)}, u32[]{:S(2)}, u32[]{:S(2)}) collective-permute-start(bf16[32,4224]{1,0:T(8,128)(2,1)S(1)} %join.3.mine_ref), channel_id=1, source_target_pairs={{0,1},{1,0},{2,3},{3,2},{4,5},{5,4},{6,7},{7,6},{8,9},{9,8},{10,11... | collective-permute-start | bytes 811016 | tf_op jit(solution)/shard_map/ppermute | solution.py:22
  37.8 1.6 %collective-permute-start.5 = (bf16[32,4096]{1,0:T(8,128)(2,1)S(1)}, bf16[32,4096]{1,0:T(8,128)(2,1)S(1)}, u32[]{:S(2)}, u32[]{:S(2)}) collective-permute-start(bf16[32,4096]{1,0:T(8,128)(2,1)S(1)} %get-tuple-element.24), channel_id=1, source_target_pairs={{0,1},{1,0},{2,3},{3,2},{4,5},{5,4},{6,7},{7,6},{8,9},{9,8},{10,11... | collective-permute-start | bytes 786440 | tf_op jit(solution)/shard_map/ppermute | solution.py:22
  39.5 5.6 %collective-permute-start.6 = (bf16[16,4096]{1,0:T(8,128)(2,1)S(1)}, bf16[16,4096]{1,0:T(8,128)(2,1)S(1)}, u32[]{:S(2)}, u32[]{:S(2)}) collective-permute-start(bf16[16,4096]{1,0:T(8,128)(2,1)S(1)} %slice.47), channel_id=1, source_target_pairs={{0,2},{2,0},{1,3},{3,1},{4,6},{6,4},{5,7},{7,5},{8,10},{10,8},{9,1... | collective-permute-start | bytes 393224 | tf_op jit(solution)/shard_map/ppermute | solution.py:22
  45.2 5.8 %collective-permute-start.7 = (bf16[4,4096]{1,0:T(4,128)(2,1)S(1)}, bf16[4,4096]{1,0:T(4,128)(2,1)S(1)}, u32[]{:S(2)}, u32[]{:S(2)}) collective-permute-start(bf16[4,4096]{1,0:T(4,128)(2,1)S(1)} %get-tuple-element.27), channel_id=1, source_target_pairs={{0,4},{4,8},{8,12},{12,0},{1,5},{5,9},{9,13},{13,1},{2,6},{6,10},{... | collective-permute-start | bytes 98312 | tf_op jit(solution)/shard_map/ppermute | solution.py:26
  45.9 5.1 %collective-permute-start.9 = (bf16[4,4096]{1,0:T(4,128)(2,1)S(1)}, bf16[4,4096]{1,0:T(4,128)(2,1)S(1)}, u32[]{:S(2)}, u32[]{:S(2)}) collective-permute-start(bf16[4,4096]{1,0:T(4,128)(2,1)S(1)} %get-tuple-element.28), channel_id=1, source_target_pairs={{0,12},{4,0},{8,4},{12,8},{1,13},{5,1},{9,5},{13,9},{2,14},{6,2},{... | collective-permute-start | bytes 98312 | tf_op jit(solution)/shard_map/ppermute | solution.py:26
  49.1 4.8 %collective-permute-start.8 = (bf16[4,4096]{1,0:T(4,128)(2,1)S(1)}, bf16[4,4096]{1,0:T(4,128)(2,1)S(1)}, u32[]{:S(2)}, u32[]{:S(2)}) collective-permute-start(bf16[4,4096]{1,0:T(4,128)(2,1)S(1)} %get-tuple-element.29), channel_id=1, source_target_pairs={{0,8},{4,12},{8,0},{12,4},{1,9},{5,13},{9,1},{13,5},{2,10},{6,14},... | collective-permute-start | bytes 98312 | tf_op jit(solution)/shard_map/ppermute | solution.py:26

commit v16 on v15

--- a/solution.py
+++ b/solution.py
@@ -1,4 +1,5 @@
 import functools
+import math
 
 import jax
 import jax.numpy as jnp
@@ -73,13 +74,11 @@
     ids = side[:, :top]
     numer = side[:, top:2 * top] * 32.0 + side[:, 2 * top:3 * top]
     weight = numer / jnp.sum(numer, axis=-1, keepdims=True)
-    lane = lax.broadcasted_iota(jnp.int32, (side.shape[0], SIDE), 1)
-    expert = jnp.where(lane < EXPERTS, lane, lane - EXPERTS).astype(jnp.float32)
+    expert = lax.broadcasted_iota(jnp.int32, (side.shape[0], SIDE), 1).astype(jnp.float32)
     full = jnp.zeros((side.shape[0], SIDE), jnp.float32)
     for k in range(top):
         full = full + jnp.where(expert == ids[:, k:k + 1], weight[:, k:k + 1], 0.0)
-    high = full.astype(jnp.bfloat16).astype(jnp.float32)
-    return jnp.where(lane < EXPERTS, high, full - high).astype(jnp.bfloat16)
+    return jnp.transpose(full)
 
 
 def layer(top, ff_dev, row_block, step_units, early, mine_ref, theirs_ref, gate_ref, up_ref,
@@ -121,18 +120,18 @@
 
     def each_block(body):
         if count == row_block:
-            body(pl.ds(0, row_block))
+            body(0, pl.ds(0, row_block))
         else:
             @pl.loop(0, count // row_block)
             def _(b):
-                body(pl.ds(pl.multiple_of(b * row_block, row_block), row_block))
+                body(b, pl.ds(pl.multiple_of(b * row_block, row_block), row_block))
 
     rows_ref[:half, :] = mine_ref[...]
     rows_ref[half:, :] = theirs_ref[...]
 
-    def prepare(block):
+    def prepare(b, block):
         side = rows_ref[block, depth:depth + SIDE].astype(jnp.float32)
-        weights[block, :] = dense_weights(side, top)
+        weights[b] = dense_weights(side, top)
         total[block, :] = jnp.zeros((row_block, depth), jnp.float32)
 
     each_block(prepare)
@@ -144,15 +143,14 @@
         u = lax.dot_general(up[...], x, LAST, preferred_element_type=jnp.float32)
         return g, u
 
-    def activate(step, block, g, u):
-        expert = lax.broadcasted_iota(jnp.int32, (step_units, SIDE), 1)
-        place = jnp.where(expert < EXPERTS, expert, expert - EXPERTS) - first
-        unit = step * step_units + lax.broadcasted_iota(jnp.int32, (step_units, SIDE), 0)
-        low = place * ff_dev
-        pick = (unit >= low) & (unit < low + ff_dev) & (expert < 2 * EXPERTS)
-        pick = jnp.where(pick, 1.0, 0.0).astype(jnp.bfloat16)
-        scale = lax.dot_general(pick, weights[block, :], LAST, preferred_element_type=jnp.float32)
-        h = g / (1.0 + jnp.exp(-g)) * u * scale
+    def activate(step, b, block, g, u):
+        run = math.gcd(step_units, ff_dev)
+        h = g / (1.0 + jnp.exp(-g)) * u
+        scaled = []
+        for low in range(0, step_units, run):
+            expert = first + lax.div(step * step_units + low, jnp.int32(ff_dev))
+            scaled.append(h[low:low + run, :] * weights[b, pl.ds(expert, 1), :])
+        h = jnp.concatenate(scaled, axis=0)
         hidden[lax.rem(step, 2), block, :] = jnp.transpose(h).astype(jnp.bfloat16)
 
     def down_product(step, block):
@@ -163,7 +161,7 @@
 
     wait(0, 0)
     wait(1, 0)
-    each_block(lambda block: activate(0, block, *products(jnp.int32(0), block)))
+    each_block(lambda b, block: activate(jnp.int32(0), b, block, *products(jnp.int32(0), block)))
 
     @pl.loop(1, steps)
     def _(step):
@@ -175,15 +173,15 @@
         wait(1, step)
         wait(2, step - 1)
 
-        def both(block):
+        def both(b, block):
             g, u = products(step, block)
             down_product(step - 1, block)
-            activate(step, block, g, u)
+            activate(step, b, block, g, u)
 
         each_block(both)
 
     wait(2, steps - 1)
-    each_block(lambda block: down_product(jnp.int32(steps - 1), block))
+    each_block(lambda b, block: down_product(jnp.int32(steps - 1), block))
     keep_ref[...] = total[:half, :]
     send_ref[...] = total[half:, :].astype(jnp.bfloat16)
 
@@ -282,7 +280,7 @@
             + [
                 pltpu.VMEM((count, depth + SIDE), jnp.bfloat16),
                 pltpu.VMEM((count, depth), jnp.float32),
-                pltpu.VMEM((count, SIDE), jnp.bfloat16),
+                pltpu.VMEM((count // row_block, SIDE, row_block), jnp.float32),
                 pltpu.VMEM((2, count, step_units), jnp.bfloat16),
                 pltpu.SemaphoreType.DMA((3, slots + 1)),
             ],

time: 54.7 us -> 54.6 us (level)
  no operation moved by 1% of the time
where the time goes in v16:
time: 54.6 us; the launch traced here: 54.5 us
  Pallas kernels  27.5 us (50%)
  starting transfers between devices  14.3 us (26%)
  waiting for transfers between devices  11.8 us (22%)
  other arithmetic  0.74 us (1%)
    pallas_call x1, Pallas kernels, local(): pl.pallas_call(functools.partial(layer, top, ff_dev, row_block, step_unit...  20.2 us
    ppermute x6, starting transfers between devices, shift(): return lax.ppermute(x, axis, [(i, (i + by) % size) for i in range(size)])  10.9 us
    ppermute x4, waiting for transfers between devices, swap(): return lax.ppermute(x, axis, [(i, i ^ by) for i in range(size)])  7 us
    pallas_call x2, Pallas kernels, local(): pl.pallas_call(functools.partial(bring, early, more), out_shape=ring_shap...  6.36 us
    ppermute x6, waiting for transfers between devices, shift(): return lax.ppermute(x, axis, [(i, (i + by) % size) for i in range(size)])  4.82 us
    ppermute x4, starting transfers between devices, swap(): return lax.ppermute(x, axis, [(i, i ^ by) for i in range(size)])  3.37 us
  transfers between devices with their start and end apart: 10, of which 5 were waited for; matrix products, arithmetic and copies ran while one was open for 0% of the time, Pallas kernels for 12%

profile of v16, /device:TPU:0, one launch (start us, length us, event | category | flops | bytes accessed | tf_op | source)
XLA Modules:
  0.0 54.5 jit_solution(14303016125232983253)
XLA Ops:
  0.0 0.9 %with_routing.1.after_ref.refs_0_ = bf16[4,4224]{1,0:T(4,128)(2,1)S(1)} custom-call(bf16[4,4096]{1,0:T(4,128)(2,1)} %tokens_ref.1, s32[4,8]{1,0:T(4,128)} %ids_ref.1, s32[4,8]{1,0:T(4,128)} %numer_ref.1), custom_call_target="tpu_custom_call" | custom-call | tf_op jit(solution)/shard_map/with_routing/pallas_call | solution.py:200
  0.9 3.1 %collective-permute-start.2 = (bf16[4,4224]{1,0:T(4,128)(2,1)S(1)}, bf16[4,4224]{1,0:T(4,128)(2,1)S(1)}, u32[]{:S(2)}, u32[]{:S(2)}) collective-permute-start(bf16[4,4224]{1,0:T(4,128)(2,1)S(1)} %with_routing.1.after_ref.refs_0_), channel_id=1, source_target_pairs={{0,4},{4,8},{8,12},{12,0},{1,5},{5,9},{9,13},{13,1},{2,6},{6,10},{... | collective-permute-start | bytes 101384 | tf_op jit(solution)/shard_map/ppermute | solution.py:27
  3.9 2.6 %collective-permute-start.1 = (bf16[4,4224]{1,0:T(4,128)(2,1)S(1)}, bf16[4,4224]{1,0:T(4,128)(2,1)S(1)}, u32[]{:S(2)}, u32[]{:S(2)}) collective-permute-start(bf16[4,4224]{1,0:T(4,128)(2,1)S(1)} %with_routing.1.after_ref.refs_0_), channel_id=1, source_target_pairs={{0,8},{4,12},{8,0},{12,4},{1,9},{5,13},{9,1},{13,5},{2,10},{6,14},... | collective-permute-start | bytes 101384 | tf_op jit(solution)/shard_map/ppermute | solution.py:27
  6.5 1.3 %collective-permute-start = (bf16[4,4224]{1,0:T(4,128)(2,1)S(1)}, bf16[4,4224]{1,0:T(4,128)(2,1)S(1)}, u32[]{:S(2)}, u32[]{:S(2)}) collective-permute-start(bf16[4,4224]{1,0:T(4,128)(2,1)S(1)} %with_routing.1.after_ref.refs_0_), channel_id=1, source_target_pairs={{0,12},{4,0},{8,4},{12,8},{1,13},{5,1},{9,5},{13,9},{2,14},{6,2},{... | collective-permute-start | bytes 101384 | tf_op jit(solution)/shard_map/ppermute | solution.py:27
  7.9 2.9 %bring_weights.2 = (bf16[4,256,4096]{2,1,0:T(8,128)(2,1)S(1)}, bf16[4,256,4096]{2,1,0:T(8,128)(2,1)S(1)}, bf16[5,256,4096]{2,1,0:T(8,128)(2,1)S(1)}, f32[8,128]{1,0:T(8,128)S(1)}) custom-call(bf16[3072,4096]{1,0:T(8,128)(2,1)} %bitcast.3, bf16[3072,4096]{1,0:T(8,128)(2,1)} %bitcast.6, bf16[3072,4096]{1,0:T(8,128)(2,1)} %bitcast.9, ...), custom_call_target="tpu_custom_call" | custom-call | bytes 6291456 | tf_op jit(solution)/shard_map/bring_weights/pallas_call | solution.py:234
  10.7 0.0 collective-permute-done.2.refs_3_
  10.8 0.0 collective-permute-done.1.refs_2_
  10.8 0.0 collective-permute-done.refs_1_
  10.8 1.6 %collective-permute-start.3 = (bf16[16,4224]{1,0:T(8,128)(2,1)S(1)}, bf16[16,4224]{1,0:T(8,128)(2,1)S(1)}, u32[]{:S(2)}, u32[]{:S(2)}) collective-permute-start(bf16[16,4224]{1,0:T(8,128)(2,1)S(1)} %join.2.after_ref.refs_0_), channel_id=1, source_target_pairs={{0,2},{2,0},{1,3},{3,1},{4,6},{6,4},{5,7},{7,5},{8,10},{10,8},{9,1... | collective-permute-start | bytes 405512 | tf_op jit(solution)/shard_map/ppermute | solution.py:23
  12.4 3.5 %bring_weights.3 = (bf16[4,256,4096]{2,1,0:T(8,128)(2,1)S(1)}, bf16[4,256,4096]{2,1,0:T(8,128)(2,1)S(1)}, bf16[5,256,4096]{2,1,0:T(8,128)(2,1)S(1)}, f32[8,128]{1,0:T(8,128)S(1)}) custom-call(bf16[3072,4096]{1,0:T(8,128)(2,1)} %bitcast.4, bf16[3072,4096]{1,0:T(8,128)(2,1)} %bitcast.7, ...), custom_call_target="tpu_custom_call", output_to_operand_aliasing={{0}: (4, {}), {1}: (5, {}), {2}: (6, {})} | custom-call | bytes 8388608 | tf_op jit(solution)/shard_map/bring_weights/pallas_call | solution.py:234
  15.9 0.0 collective-permute-done.3.refs_1_
  15.9 0.1 collective-permute-start.4
  16.0 1.5 %collective-permute-done.4.theirs_ref = bf16[32,4224]{1,0:T(8,128)(2,1)S(1)} collective-permute-done((bf16[32,4224]{1,0:T(8,128)(2,1)S(1)}, bf16[32,4224]{1,0:T(8,128)(2,1)S(1)}, u32[]{:S(2)}, u32[]{:S(2)}) %collective-permute-start.4) | collective-permute-done | bytes 270368 | tf_op jit(solution)/shard_map/ppermute | solution.py:23
  17.5 20.2 %expert_layer.1 = (f32[32,4096]{1,0:T(8,128)S(1)}, bf16[32,4096]{1,0:T(8,128)(2,1)S(1)}, bf16[4,256,4096]{2,1,0:T(8,128)(2,1)S(1)}, bf16[4,256,4096]{2,1,0:T(8,128)(2,1)S(1)}, bf16[5,256,4096]{2,1,0:T(8,128)(2,1)S(1)}) custom-call(bf16[32,4224]{1,0:T(8,128)(2,1)S(1)} %join.3.mine_ref, ...), custom_call_target="tpu_custom_call", output_to_operand_aliasing={{2}: (5, {}), {3}: (6, {}), {4}: (7, {})} | custom-call | flops 4831838208 | bytes 60817408 | tf_op jit(solution)/shard_map/expert_layer/pallas_call | solution.py:270
  37.7 0.2 collective-permute-start.5
  37.9 1.4 %collective-permute-done.5 = bf16[32,4096]{1,0:T(8,128)(2,1)S(1)} collective-permute-done((bf16[32,4096]{1,0:T(8,128)(2,1)S(1)}, bf16[32,4096]{1,0:T(8,128)(2,1)S(1)}, u32[]{:S(2)}, u32[]{:S(2)}) %collective-permute-start.5) | collective-permute-done | bytes 262176 | tf_op jit(solution)/shard_map/ppermute | solution.py:23
  39.3 0.1 convert_add_fusion
  39.4 1.5 %collective-permute-start.6 = (bf16[16,4096]{1,0:T(8,128)(2,1)S(1)}, bf16[16,4096]{1,0:T(8,128)(2,1)S(1)}, u32[]{:S(2)}, u32[]{:S(2)}) collective-permute-start(bf16[16,4096]{1,0:T(8,128)(2,1)S(1)} %slice.47), channel_id=1, source_target_pairs={{0,2},{2,0},{1,3},{3,1},{4,6},{6,4},{5,7},{7,5},{8,10},{10,8},{9,1... | collective-permute-start | bytes 393224 | tf_op jit(solution)/shard_map/ppermute | solution.py:23
  41.0 4.1 %collective-permute-done.6 = bf16[16,4096]{1,0:T(8,128)(2,1)S(1)} collective-permute-done((bf16[16,4096]{1,0:T(8,128)(2,1)S(1)}, bf16[16,4096]{1,0:T(8,128)(2,1)S(1)}, u32[]{:S(2)}, u32[]{:S(2)}) %collective-permute-start.6) | collective-permute-done | bytes 131104 | tf_op jit(solution)/shard_map/ppermute | solution.py:23
  45.1 0.7 %collective-permute-start.7 = (bf16[4,4096]{1,0:T(4,128)(2,1)S(1)}, bf16[4,4096]{1,0:T(4,128)(2,1)S(1)}, u32[]{:S(2)}, u32[]{:S(2)}) collective-permute-start(bf16[4,4096]{1,0:T(4,128)(2,1)S(1)} %get-tuple-element.27), channel_id=1, source_target_pairs={{0,4},{4,8},{8,12},{12,0},{1,5},{5,9},{9,13},{13,1},{2,6},{6,10},{... | collective-permute-start | bytes 98312 | tf_op jit(solution)/shard_map/ppermute | solution.py:27
  45.9 3.1 %collective-permute-start.9 = (bf16[4,4096]{1,0:T(4,128)(2,1)S(1)}, bf16[4,4096]{1,0:T(4,128)(2,1)S(1)}, u32[]{:S(2)}, u32[]{:S(2)}) collective-permute-start(bf16[4,4096]{1,0:T(4,128)(2,1)S(1)} %get-tuple-element.28), channel_id=1, source_target_pairs={{0,12},{4,0},{8,4},{12,8},{1,13},{5,1},{9,5},{13,9},{2,14},{6,2},{... | collective-permute-start | bytes 98312 | tf_op jit(solution)/shard_map/ppermute | solution.py:27
  49.0 0.0 collective-permute-start.8
  49.0 1.9 %collective-permute-done.7 = bf16[4,4096]{1,0:T(4,128)(2,1)S(1)} collective-permute-done((bf16[4,4096]{1,0:T(4,128)(2,1)S(1)}, bf16[4,4096]{1,0:T(4,128)(2,1)S(1)}, u32[]{:S(2)}, u32[]{:S(2)}) %collective-permute-start.7) | collective-permute-done | bytes 32800 | tf_op jit(solution)/shard_map/ppermute | solution.py:27
  50.9 0.0 collective-permute-done.9
  50.9 2.9 %collective-permute-done.8 = bf16[4,4096]{1,0:T(4,128)(2,1)S(1)} collective-permute-done((bf16[4,4096]{1,0:T(4,128)(2,1)S(1)}, bf16[4,4096]{1,0:T(4,128)(2,1)S(1)}, u32[]{:S(2)}, u32[]{:S(2)}) %collective-permute-start.8) | collective-permute-done | bytes 32800 | tf_op jit(solution)/shard_map/ppermute | solution.py:27
  53.8 0.6 %fusion.2 = bf16[4,4096]{1,0:T(4,128)(2,1)} fusion(f32[16,4096]{1,0:T(8,128)S(1)} %get-tuple-element.26, bf16[4,4096]{1,0:T(4,128)(2,1)S(1)} %collective-permute-done.9, bf16[4,4096]{1,0:T(4,128)(2,1)S(1)} %collective-permute-done.8, bf16[4,4096]{1,0:T(4,128)(2,1)S(1)} %collective-permute-done.7), kind=kLoop, calls=%fused_computation.6 | loop fusion | flops 114688 | bytes 196608 | tf_op jit(solution)/shard_map/convert_element_type | solution.py:308
  (5 shorter events, 0.1 us)
Async XLA Ops:
  0.9 9.9 %collective-permute-start.2 = (bf16[4,4224]{1,0:T(4,128)(2,1)S(1)}, bf16[4,4224]{1,0:T(4,128)(2,1)S(1)}, u32[]{:S(2)}, u32[]{:S(2)}) collective-permute-start(bf16[4,4224]{1,0:T(4,128)(2,1)S(1)} %with_routing.1.after_ref.refs_0_), channel_id=1, source_target_pairs={{0,4},{4,8},{8,12},{12,0},{1,5},{5,9},{9,13},{13,1},{2,6},{6,10},{... | collective-permute-start | bytes 101384 | tf_op jit(solution)/shard_map/ppermute | solution.py:27
  3.9 6.8 %collective-permute-start.1 = (bf16[4,4224]{1,0:T(4,128)(2,1)S(1)}, bf16[4,4224]{1,0:T(4,128)(2,1)S(1)}, u32[]{:S(2)}, u32[]{:S(2)}) collective-permute-start(bf16[4,4224]{1,0:T(4,128)(2,1)S(1)} %with_routing.1.after_ref.refs_0_), channel_id=1, source_target_pairs={{0,8},{4,12},{8,0},{12,4},{1,9},{5,13},{9,1},{13,5},{2,10},{6,14},... | collective-permute-start | bytes 101384 | tf_op jit(solution)/shard_map/ppermute | solution.py:27
  6.5 4.2 %collective-permute-start = (bf16[4,4224]{1,0:T(4,128)(2,1)S(1)}, bf16[4,4224]{1,0:T(4,128)(2,1)S(1)}, u32[]{:S(2)}, u32[]{:S(2)}) collective-permute-start(bf16[4,4224]{1,0:T(4,128)(2,1)S(1)} %with_routing.1.after_ref.refs_0_), channel_id=1, source_target_pairs={{0,12},{4,0},{8,4},{12,8},{1,13},{5,1},{9,5},{13,9},{2,14},{6,2},{... | collective-permute-start | bytes 101384 | tf_op jit(solution)/shard_map/ppermute | solution.py:27
  10.8 5.1 %collective-permute-start.3 = (bf16[16,4224]{1,0:T(8,128)(2,1)S(1)}, bf16[16,4224]{1,0:T(8,128)(2,1)S(1)}, u32[]{:S(2)}, u32[]{:S(2)}) collective-permute-start(bf16[16,4224]{1,0:T(8,128)(2,1)S(1)} %join.2.after_ref.refs_0_), channel_id=1, source_target_pairs={{0,2},{2,0},{1,3},{3,1},{4,6},{6,4},{5,7},{7,5},{8,10},{10,8},{9,1... | collective-permute-start | bytes 405512 | tf_op jit(solution)/shard_map/ppermute | solution.py:23
  15.9 1.6 %collective-permute-start.4 = (bf16[32,4224]{1,0:T(8,128)(2,1)S(1)}, bf16[32,4224]{1,0:T(8,128)(2,1)S(1)}, u32[]{:S(2)}, u32[]{:S(2)}) collective-permute-start(bf16[32,4224]{1,0:T(8,128)(2,1)S(1)} %join.3.mine_ref), channel_id=1, source_target_pairs={{0,1},{1,0},{2,3},{3,2},{4,5},{5,4},{6,7},{7,6},{8,9},{9,8},{10,11... | collective-permute-start | bytes 811016 | tf_op jit(solution)/shard_map/ppermute | solution.py:23
  37.7 1.6 %collective-permute-start.5 = (bf16[32,4096]{1,0:T(8,128)(2,1)S(1)}, bf16[32,4096]{1,0:T(8,128)(2,1)S(1)}, u32[]{:S(2)}, u32[]{:S(2)}) collective-permute-start(bf16[32,4096]{1,0:T(8,128)(2,1)S(1)} %get-tuple-element.24), channel_id=1, source_target_pairs={{0,1},{1,0},{2,3},{3,2},{4,5},{5,4},{6,7},{7,6},{8,9},{9,8},{10,11... | collective-permute-start | bytes 786440 | tf_op jit(solution)/shard_map/ppermute | solution.py:23
  39.4 5.6 %collective-permute-start.6 = (bf16[16,4096]{1,0:T(8,128)(2,1)S(1)}, bf16[16,4096]{1,0:T(8,128)(2,1)S(1)}, u32[]{:S(2)}, u32[]{:S(2)}) collective-permute-start(bf16[16,4096]{1,0:T(8,128)(2,1)S(1)} %slice.47), channel_id=1, source_target_pairs={{0,2},{2,0},{1,3},{3,1},{4,6},{6,4},{5,7},{7,5},{8,10},{10,8},{9,1... | collective-permute-start | bytes 393224 | tf_op jit(solution)/shard_map/ppermute | solution.py:23
  45.1 5.8 %collective-permute-start.7 = (bf16[4,4096]{1,0:T(4,128)(2,1)S(1)}, bf16[4,4096]{1,0:T(4,128)(2,1)S(1)}, u32[]{:S(2)}, u32[]{:S(2)}) collective-permute-start(bf16[4,4096]{1,0:T(4,128)(2,1)S(1)} %get-tuple-element.27), channel_id=1, source_target_pairs={{0,4},{4,8},{8,12},{12,0},{1,5},{5,9},{9,13},{13,1},{2,6},{6,10},{... | collective-permute-start | bytes 98312 | tf_op jit(solution)/shard_map/ppermute | solution.py:27
  45.9 5.1 %collective-permute-start.9 = (bf16[4,4096]{1,0:T(4,128)(2,1)S(1)}, bf16[4,4096]{1,0:T(4,128)(2,1)S(1)}, u32[]{:S(2)}, u32[]{:S(2)}) collective-permute-start(bf16[4,4096]{1,0:T(4,128)(2,1)S(1)} %get-tuple-element.28), channel_id=1, source_target_pairs={{0,12},{4,0},{8,4},{12,8},{1,13},{5,1},{9,5},{13,9},{2,14},{6,2},{... | collective-permute-start | bytes 98312 | tf_op jit(solution)/shard_map/ppermute | solution.py:27
  49.0 4.8 %collective-permute-start.8 = (bf16[4,4096]{1,0:T(4,128)(2,1)S(1)}, bf16[4,4096]{1,0:T(4,128)(2,1)S(1)}, u32[]{:S(2)}, u32[]{:S(2)}) collective-permute-start(bf16[4,4096]{1,0:T(4,128)(2,1)S(1)} %get-tuple-element.29), channel_id=1, source_target_pairs={{0,8},{4,12},{8,0},{12,4},{1,9},{5,13},{9,1},{13,5},{2,10},{6,14},... | collective-permute-start | bytes 98312 | tf_op jit(solution)/shard_map/ppermute | solution.py:27

commit v17 on v16

--- a/solution.py
+++ b/solution.py
@@ -98,9 +98,7 @@
         span = pl.ds(pl.multiple_of(step * step_units, step_units), step_units)
         return pltpu.make_async_copy(src.at[span], ring.at[slot], sem.at[i, slot])
 
-    def start(step):
-        for i in range(3):
-            copy_of(i, step).start()
+    ahead = (slots, slots, max(1, slots - 2))
 
     def wait(i, step):
         if isinstance(step, int):
@@ -113,7 +111,7 @@
 
     for step in range(min(slots, steps)):
         for i in range(3):
-            if step >= early[i]:
+            if early[i] <= step < ahead[i]:
                 copy_of(i, jnp.int32(step)).start()
 
     first = lax.axis_index("wide") * (units // ff_dev)
@@ -165,9 +163,14 @@
 
     @pl.loop(1, steps)
     def _(step):
-        @pl.when(step - 1 + slots < steps)
+        @pl.when(step - 1 + ahead[0] < steps)
         def _():
-            start(step - 1 + slots)
+            copy_of(0, step - 1 + ahead[0]).start()
+            copy_of(1, step - 1 + ahead[1]).start()
+
+        @pl.when(step - 1 + ahead[2] < steps)
+        def _():
+            copy_of(2, step - 1 + ahead[2]).start()
 
         wait(0, step)
         wait(1, step)

time: 54.6 us -> 55.6 us (1.018)
  Pallas kernels: 27.5 us -> 28.4 us
    pallas_call x1, Pallas kernels: 20.2 us -> 21.2 us  [local(): pl.pallas_call(functools.partial(layer, top, ff_dev, row_block, step_unit...]
  transfers between devices with their start and end apart: 10 -> 10, of which waited for: 5 -> 5; matrix products, arithmetic and copies ran while one was open for 0% -> 0% of each run, Pallas kernels for 12% -> 11%
where the time goes in v17:
time: 55.6 us; the launch traced here: 55.4 us
  Pallas kernels  28.4 us (51%)
  starting transfers between devices  14.3 us (26%)
  waiting for transfers between devices  11.8 us (21%)
  other arithmetic  0.74 us (1%)
    pallas_call x1, Pallas kernels, local(): pl.pallas_call(functools.partial(layer, top, ff_dev, row_block, step_unit...  21.2 us
    ppermute x6, starting transfers between devices, shift(): return lax.ppermute(x, axis, [(i, (i + by) % size) for i in range(size)])  10.9 us
    ppermute x4, waiting for transfers between devices, swap(): return lax.ppermute(x, axis, [(i, i ^ by) for i in range(size)])  6.99 us
    pallas_call x2, Pallas kernels, local(): pl.pallas_call(functools.partial(bring, early, more), out_shape=ring_shap...  6.36 us
    ppermute x6, waiting for transfers between devices, shift(): return lax.ppermute(x, axis, [(i, (i + by) % size) for i in range(size)])  4.82 us
    ppermute x4, starting transfers between devices, swap(): return lax.ppermute(x, axis, [(i, i ^ by) for i in range(size)])  3.39 us
  transfers between devices with their start and end apart: 10, of which 5 were waited for; matrix products, arithmetic and copies ran while one was open for 0% of the time, Pallas kernels for 11%

profile of v17, /device:TPU:0, one launch (start us, length us, event | category | flops | bytes accessed | tf_op | source)
XLA Modules:
  0.0 55.4 jit_solution(1606462199437641888)
XLA Ops:
  0.0 0.9 %with_routing.1.after_ref.refs_0_ = bf16[4,4224]{1,0:T(4,128)(2,1)S(1)} custom-call(bf16[4,4096]{1,0:T(4,128)(2,1)} %tokens_ref.1, s32[4,8]{1,0:T(4,128)} %ids_ref.1, s32[4,8]{1,0:T(4,128)} %numer_ref.1), custom_call_target="tpu_custom_call" | custom-call | tf_op jit(solution)/shard_map/with_routing/pallas_call | solution.py:203
  0.9 3.1 %collective-permute-start.2 = (bf16[4,4224]{1,0:T(4,128)(2,1)S(1)}, bf16[4,4224]{1,0:T(4,128)(2,1)S(1)}, u32[]{:S(2)}, u32[]{:S(2)}) collective-permute-start(bf16[4,4224]{1,0:T(4,128)(2,1)S(1)} %with_routing.1.after_ref.refs_0_), channel_id=1, source_target_pairs={{0,4},{4,8},{8,12},{12,0},{1,5},{5,9},{9,13},{13,1},{2,6},{6,10},{... | collective-permute-start | bytes 101384 | tf_op jit(solution)/shard_map/ppermute | solution.py:27
  3.9 2.6 %collective-permute-start.1 = (bf16[4,4224]{1,0:T(4,128)(2,1)S(1)}, bf16[4,4224]{1,0:T(4,128)(2,1)S(1)}, u32[]{:S(2)}, u32[]{:S(2)}) collective-permute-start(bf16[4,4224]{1,0:T(4,128)(2,1)S(1)} %with_routing.1.after_ref.refs_0_), channel_id=1, source_target_pairs={{0,8},{4,12},{8,0},{12,4},{1,9},{5,13},{9,1},{13,5},{2,10},{6,14},... | collective-permute-start | bytes 101384 | tf_op jit(solution)/shard_map/ppermute | solution.py:27
  6.5 1.3 %collective-permute-start = (bf16[4,4224]{1,0:T(4,128)(2,1)S(1)}, bf16[4,4224]{1,0:T(4,128)(2,1)S(1)}, u32[]{:S(2)}, u32[]{:S(2)}) collective-permute-start(bf16[4,4224]{1,0:T(4,128)(2,1)S(1)} %with_routing.1.after_ref.refs_0_), channel_id=1, source_target_pairs={{0,12},{4,0},{8,4},{12,8},{1,13},{5,1},{9,5},{13,9},{2,14},{6,2},{... | collective-permute-start | bytes 101384 | tf_op jit(solution)/shard_map/ppermute | solution.py:27
  7.9 2.9 %bring_weights.2 = (bf16[4,256,4096]{2,1,0:T(8,128)(2,1)S(1)}, bf16[4,256,4096]{2,1,0:T(8,128)(2,1)S(1)}, bf16[5,256,4096]{2,1,0:T(8,128)(2,1)S(1)}, f32[8,128]{1,0:T(8,128)S(1)}) custom-call(bf16[3072,4096]{1,0:T(8,128)(2,1)} %bitcast.3, bf16[3072,4096]{1,0:T(8,128)(2,1)} %bitcast.6, bf16[3072,4096]{1,0:T(8,128)(2,1)} %bitcast.9, ...), custom_call_target="tpu_custom_call" | custom-call | bytes 6291456 | tf_op jit(solution)/shard_map/bring_weights/pallas_call | solution.py:237
  10.7 0.0 collective-permute-done.2.refs_3_
  10.8 0.0 collective-permute-done.1.refs_2_
  10.8 0.0 collective-permute-done.refs_1_
  10.8 1.6 %collective-permute-start.3 = (bf16[16,4224]{1,0:T(8,128)(2,1)S(1)}, bf16[16,4224]{1,0:T(8,128)(2,1)S(1)}, u32[]{:S(2)}, u32[]{:S(2)}) collective-permute-start(bf16[16,4224]{1,0:T(8,128)(2,1)S(1)} %join.2.after_ref.refs_0_), channel_id=1, source_target_pairs={{0,2},{2,0},{1,3},{3,1},{4,6},{6,4},{5,7},{7,5},{8,10},{10,8},{9,1... | collective-permute-start | bytes 405512 | tf_op jit(solution)/shard_map/ppermute | solution.py:23
  12.4 3.5 %bring_weights.3 = (bf16[4,256,4096]{2,1,0:T(8,128)(2,1)S(1)}, bf16[4,256,4096]{2,1,0:T(8,128)(2,1)S(1)}, bf16[5,256,4096]{2,1,0:T(8,128)(2,1)S(1)}, f32[8,128]{1,0:T(8,128)S(1)}) custom-call(bf16[3072,4096]{1,0:T(8,128)(2,1)} %bitcast.4, bf16[3072,4096]{1,0:T(8,128)(2,1)} %bitcast.7, ...), custom_call_target="tpu_custom_call", output_to_operand_aliasing={{0}: (4, {}), {1}: (5, {}), {2}: (6, {})} | custom-call | bytes 8388608 | tf_op jit(solution)/shard_map/bring_weights/pallas_call | solution.py:237
  15.9 0.0 collective-permute-done.3.refs_1_
  15.9 0.1 collective-permute-start.4
  16.0 1.5 %collective-permute-done.4.theirs_ref = bf16[32,4224]{1,0:T(8,128)(2,1)S(1)} collective-permute-done((bf16[32,4224]{1,0:T(8,128)(2,1)S(1)}, bf16[32,4224]{1,0:T(8,128)(2,1)S(1)}, u32[]{:S(2)}, u32[]{:S(2)}) %collective-permute-start.4) | collective-permute-done | bytes 270368 | tf_op jit(solution)/shard_map/ppermute | solution.py:23
  17.5 21.2 %expert_layer.1 = (f32[32,4096]{1,0:T(8,128)S(1)}, bf16[32,4096]{1,0:T(8,128)(2,1)S(1)}, bf16[4,256,4096]{2,1,0:T(8,128)(2,1)S(1)}, bf16[4,256,4096]{2,1,0:T(8,128)(2,1)S(1)}, bf16[5,256,4096]{2,1,0:T(8,128)(2,1)S(1)}) custom-call(bf16[32,4224]{1,0:T(8,128)(2,1)S(1)} %join.3.mine_ref, ...), custom_call_target="tpu_custom_call", output_to_operand_aliasing={{2}: (5, {}), {3}: (6, {}), {4}: (7, {})} | custom-call | flops 4831838208 | bytes 60817408 | tf_op jit(solution)/shard_map/expert_layer/pallas_call | solution.py:273
  38.7 0.2 collective-permute-start.5
  38.9 1.4 %collective-permute-done.5 = bf16[32,4096]{1,0:T(8,128)(2,1)S(1)} collective-permute-done((bf16[32,4096]{1,0:T(8,128)(2,1)S(1)}, bf16[32,4096]{1,0:T(8,128)(2,1)S(1)}, u32[]{:S(2)}, u32[]{:S(2)}) %collective-permute-start.5) | collective-permute-done | bytes 262176 | tf_op jit(solution)/shard_map/ppermute | solution.py:23
  40.3 0.1 convert_add_fusion
  40.4 1.6 %collective-permute-start.6 = (bf16[16,4096]{1,0:T(8,128)(2,1)S(1)}, bf16[16,4096]{1,0:T(8,128)(2,1)S(1)}, u32[]{:S(2)}, u32[]{:S(2)}) collective-permute-start(bf16[16,4096]{1,0:T(8,128)(2,1)S(1)} %slice.47), channel_id=1, source_target_pairs={{0,2},{2,0},{1,3},{3,1},{4,6},{6,4},{5,7},{7,5},{8,10},{10,8},{9,1... | collective-permute-start | bytes 393224 | tf_op jit(solution)/shard_map/ppermute | solution.py:23
  42.0 4.1 %collective-permute-done.6 = bf16[16,4096]{1,0:T(8,128)(2,1)S(1)} collective-permute-done((bf16[16,4096]{1,0:T(8,128)(2,1)S(1)}, bf16[16,4096]{1,0:T(8,128)(2,1)S(1)}, u32[]{:S(2)}, u32[]{:S(2)}) %collective-permute-start.6) | collective-permute-done | bytes 131104 | tf_op jit(solution)/shard_map/ppermute | solution.py:23
  46.1 0.7 %collective-permute-start.7 = (bf16[4,4096]{1,0:T(4,128)(2,1)S(1)}, bf16[4,4096]{1,0:T(4,128)(2,1)S(1)}, u32[]{:S(2)}, u32[]{:S(2)}) collective-permute-start(bf16[4,4096]{1,0:T(4,128)(2,1)S(1)} %get-tuple-element.27), channel_id=1, source_target_pairs={{0,4},{4,8},{8,12},{12,0},{1,5},{5,9},{9,13},{13,1},{2,6},{6,10},{... | collective-permute-start | bytes 98312 | tf_op jit(solution)/shard_map/ppermute | solution.py:27
  46.8 3.1 %collective-permute-start.9 = (bf16[4,4096]{1,0:T(4,128)(2,1)S(1)}, bf16[4,4096]{1,0:T(4,128)(2,1)S(1)}, u32[]{:S(2)}, u32[]{:S(2)}) collective-permute-start(bf16[4,4096]{1,0:T(4,128)(2,1)S(1)} %get-tuple-element.28), channel_id=1, source_target_pairs={{0,12},{4,0},{8,4},{12,8},{1,13},{5,1},{9,5},{13,9},{2,14},{6,2},{... | collective-permute-start | bytes 98312 | tf_op jit(solution)/shard_map/ppermute | solution.py:27
  50.0 0.0 collective-permute-start.8
  50.0 1.9 %collective-permute-done.7 = bf16[4,4096]{1,0:T(4,128)(2,1)S(1)} collective-permute-done((bf16[4,4096]{1,0:T(4,128)(2,1)S(1)}, bf16[4,4096]{1,0:T(4,128)(2,1)S(1)}, u32[]{:S(2)}, u32[]{:S(2)}) %collective-permute-start.7) | collective-permute-done | bytes 32800 | tf_op jit(solution)/shard_map/ppermute | solution.py:27
  51.9 0.0 collective-permute-done.9
  51.9 2.9 %collective-permute-done.8 = bf16[4,4096]{1,0:T(4,128)(2,1)S(1)} collective-permute-done((bf16[4,4096]{1,0:T(4,128)(2,1)S(1)}, bf16[4,4096]{1,0:T(4,128)(2,1)S(1)}, u32[]{:S(2)}, u32[]{:S(2)}) %collective-permute-start.8) | collective-permute-done | bytes 32800 | tf_op jit(solution)/shard_map/ppermute | solution.py:27
  54.8 0.6 %fusion.2 = bf16[4,4096]{1,0:T(4,128)(2,1)} fusion(f32[16,4096]{1,0:T(8,128)S(1)} %get-tuple-element.26, bf16[4,4096]{1,0:T(4,128)(2,1)S(1)} %collective-permute-done.9, bf16[4,4096]{1,0:T(4,128)(2,1)S(1)} %collective-permute-done.8, bf16[4,4096]{1,0:T(4,128)(2,1)S(1)} %collective-permute-done.7), kind=kLoop, calls=%fused_computation.6 | loop fusion | flops 114688 | bytes 196608 | tf_op jit(solution)/shard_map/convert_element_type | solution.py:311
  (5 shorter events, 0.1 us)
Async XLA Ops:
  0.9 9.9 %collective-permute-start.2 = (bf16[4,4224]{1,0:T(4,128)(2,1)S(1)}, bf16[4,4224]{1,0:T(4,128)(2,1)S(1)}, u32[]{:S(2)}, u32[]{:S(2)}) collective-permute-start(bf16[4,4224]{1,0:T(4,128)(2,1)S(1)} %with_routing.1.after_ref.refs_0_), channel_id=1, source_target_pairs={{0,4},{4,8},{8,12},{12,0},{1,5},{5,9},{9,13},{13,1},{2,6},{6,10},{... | collective-permute-start | bytes 101384 | tf_op jit(solution)/shard_map/ppermute | solution.py:27
  3.9 6.8 %collective-permute-start.1 = (bf16[4,4224]{1,0:T(4,128)(2,1)S(1)}, bf16[4,4224]{1,0:T(4,128)(2,1)S(1)}, u32[]{:S(2)}, u32[]{:S(2)}) collective-permute-start(bf16[4,4224]{1,0:T(4,128)(2,1)S(1)} %with_routing.1.after_ref.refs_0_), channel_id=1, source_target_pairs={{0,8},{4,12},{8,0},{12,4},{1,9},{5,13},{9,1},{13,5},{2,10},{6,14},... | collective-permute-start | bytes 101384 | tf_op jit(solution)/shard_map/ppermute | solution.py:27
  6.5 4.2 %collective-permute-start = (bf16[4,4224]{1,0:T(4,128)(2,1)S(1)}, bf16[4,4224]{1,0:T(4,128)(2,1)S(1)}, u32[]{:S(2)}, u32[]{:S(2)}) collective-permute-start(bf16[4,4224]{1,0:T(4,128)(2,1)S(1)} %with_routing.1.after_ref.refs_0_), channel_id=1, source_target_pairs={{0,12},{4,0},{8,4},{12,8},{1,13},{5,1},{9,5},{13,9},{2,14},{6,2},{... | collective-permute-start | bytes 101384 | tf_op jit(solution)/shard_map/ppermute | solution.py:27
  10.8 5.1 %collective-permute-start.3 = (bf16[16,4224]{1,0:T(8,128)(2,1)S(1)}, bf16[16,4224]{1,0:T(8,128)(2,1)S(1)}, u32[]{:S(2)}, u32[]{:S(2)}) collective-permute-start(bf16[16,4224]{1,0:T(8,128)(2,1)S(1)} %join.2.after_ref.refs_0_), channel_id=1, source_target_pairs={{0,2},{2,0},{1,3},{3,1},{4,6},{6,4},{5,7},{7,5},{8,10},{10,8},{9,1... | collective-permute-start | bytes 405512 | tf_op jit(solution)/shard_map/ppermute | solution.py:23
  15.9 1.6 %collective-permute-start.4 = (bf16[32,4224]{1,0:T(8,128)(2,1)S(1)}, bf16[32,4224]{1,0:T(8,128)(2,1)S(1)}, u32[]{:S(2)}, u32[]{:S(2)}) collective-permute-start(bf16[32,4224]{1,0:T(8,128)(2,1)S(1)} %join.3.mine_ref), channel_id=1, source_target_pairs={{0,1},{1,0},{2,3},{3,2},{4,5},{5,4},{6,7},{7,6},{8,9},{9,8},{10,11... | collective-permute-start | bytes 811016 | tf_op jit(solution)/shard_map/ppermute | solution.py:23
  38.7 1.6 %collective-permute-start.5 = (bf16[32,4096]{1,0:T(8,128)(2,1)S(1)}, bf16[32,4096]{1,0:T(8,128)(2,1)S(1)}, u32[]{:S(2)}, u32[]{:S(2)}) collective-permute-start(bf16[32,4096]{1,0:T(8,128)(2,1)S(1)} %get-tuple-element.24), channel_id=1, source_target_pairs={{0,1},{1,0},{2,3},{3,2},{4,5},{5,4},{6,7},{7,6},{8,9},{9,8},{10,11... | collective-permute-start | bytes 786440 | tf_op jit(solution)/shard_map/ppermute | solution.py:23
  40.4 5.6 %collective-permute-start.6 = (bf16[16,4096]{1,0:T(8,128)(2,1)S(1)}, bf16[16,4096]{1,0:T(8,128)(2,1)S(1)}, u32[]{:S(2)}, u32[]{:S(2)}) collective-permute-start(bf16[16,4096]{1,0:T(8,128)(2,1)S(1)} %slice.47), channel_id=1, source_target_pairs={{0,2},{2,0},{1,3},{3,1},{4,6},{6,4},{5,7},{7,5},{8,10},{10,8},{9,1... | collective-permute-start | bytes 393224 | tf_op jit(solution)/shard_map/ppermute | solution.py:23
  46.1 5.8 %collective-permute-start.7 = (bf16[4,4096]{1,0:T(4,128)(2,1)S(1)}, bf16[4,4096]{1,0:T(4,128)(2,1)S(1)}, u32[]{:S(2)}, u32[]{:S(2)}) collective-permute-start(bf16[4,4096]{1,0:T(4,128)(2,1)S(1)} %get-tuple-element.27), channel_id=1, source_target_pairs={{0,4},{4,8},{8,12},{12,0},{1,5},{5,9},{9,13},{13,1},{2,6},{6,10},{... | collective-permute-start | bytes 98312 | tf_op jit(solution)/shard_map/ppermute | solution.py:27
  46.8 5.1 %collective-permute-start.9 = (bf16[4,4096]{1,0:T(4,128)(2,1)S(1)}, bf16[4,4096]{1,0:T(4,128)(2,1)S(1)}, u32[]{:S(2)}, u32[]{:S(2)}) collective-permute-start(bf16[4,4096]{1,0:T(4,128)(2,1)S(1)} %get-tuple-element.28), channel_id=1, source_target_pairs={{0,12},{4,0},{8,4},{12,8},{1,13},{5,1},{9,5},{13,9},{2,14},{6,2},{... | collective-permute-start | bytes 98312 | tf_op jit(solution)/shard_map/ppermute | solution.py:27
  50.0 4.8 %collective-permute-start.8 = (bf16[4,4096]{1,0:T(4,128)(2,1)S(1)}, bf16[4,4096]{1,0:T(4,128)(2,1)S(1)}, u32[]{:S(2)}, u32[]{:S(2)}) collective-permute-start(bf16[4,4096]{1,0:T(4,128)(2,1)S(1)} %get-tuple-element.29), channel_id=1, source_target_pairs={{0,8},{4,12},{8,0},{12,4},{1,9},{5,13},{9,1},{13,5},{2,10},{6,14},... | collective-permute-start | bytes 98312 | tf_op jit(solution)/shard_map/ppermute | solution.py:27

commit v18 on v16

--- a/solution.py
+++ b/solution.py
@@ -10,7 +10,7 @@
 
 EXPERTS = 32
 SIDE = 128
-SLOTS = 4
+SLOTS = 6
 EARLY = ((1, 1, 1), (2, 1, 1))
 GRANT = 8 << 20
 

time: 54.6 us -> 72.9 us (1.34)
  local copies, waits for them, and re-layouts: 0.06 us -> 18.2 us
  starting transfers between devices: 14.3 us -> 13.3 us
  waiting for transfers between devices: 11.8 us -> 12.8 us
    unnamed x0 -> x8, local copies, waits for them, and re-layouts: none -> 18.2 us
    ppermute x4, waiting for transfers between devices: 7 us -> 7.94 us  [swap(): return lax.ppermute(x, axis, [(i, i ^ by) for i in range(size)])]
    ppermute x4, starting transfers between devices: 3.37 us -> 2.43 us  [swap(): return lax.ppermute(x, axis, [(i, i ^ by) for i in range(size)])]
  transfers between devices with their start and end apart: 10 -> 10, of which waited for: 5 -> 5; matrix products, arithmetic and copies ran while one was open for 0% -> 0% of each run, Pallas kernels for 12% -> 9%
where the time goes in v18:
time: 72.9 us; the launch traced here: 72.7 us
  Pallas kernels  27.5 us (38%)
  local copies, waits for them, and re-layouts  18.2 us (25%)
  starting transfers between devices  13.3 us (18%)
  waiting for transfers between devices  12.8 us (18%)
  other arithmetic  0.74 us (1%)
    pallas_call x1, Pallas kernels, local(): pl.pallas_call(functools.partial(layer, top, ff_dev, row_block, step_unit...  20.2 us
    unnamed x8, local copies, waits for them, and re-layouts  18.2 us
    ppermute x6, starting transfers between devices, shift(): return lax.ppermute(x, axis, [(i, (i + by) % size) for i in range(size)])  10.9 us
    ppermute x4, waiting for transfers between devices, swap(): return lax.ppermute(x, axis, [(i, i ^ by) for i in range(size)])  7.94 us
    pallas_call x2, Pallas kernels, local(): pl.pallas_call(functools.partial(bring, early, more), out_shape=ring_shap...  6.36 us
    ppermute x6, waiting for transfers between devices, shift(): return lax.ppermute(x, axis, [(i, (i + by) % size) for i in range(size)])  4.82 us
    ppermute x4, starting transfers between devices, swap(): return lax.ppermute(x, axis, [(i, i ^ by) for i in range(size)])  2.43 us
  transfers between devices with their start and end apart: 10, of which 5 were waited for; matrix products, arithmetic and copies ran while one was open for 0% of the time, Pallas kernels for 9%

profile of v18, /device:TPU:0, one launch (start us, length us, event | category | flops | bytes accessed | tf_op | source)
XLA Modules:
  0.0 72.7 jit_solution(16104363690034775652)
XLA Ops:
  0.0 0.9 %with_routing.1.after_ref.refs_0_ = bf16[4,4224]{1,0:T(4,128)(2,1)S(1)} custom-call(bf16[4,4096]{1,0:T(4,128)(2,1)} %tokens_ref.1, s32[4,8]{1,0:T(4,128)} %ids_ref.1, s32[4,8]{1,0:T(4,128)} %numer_ref.1), custom_call_target="tpu_custom_call" | custom-call | tf_op jit(solution)/shard_map/with_routing/pallas_call | solution.py:200
  0.9 3.1 %collective-permute-start.2 = (bf16[4,4224]{1,0:T(4,128)(2,1)S(1)}, bf16[4,4224]{1,0:T(4,128)(2,1)S(1)}, u32[]{:S(2)}, u32[]{:S(2)}) collective-permute-start(bf16[4,4224]{1,0:T(4,128)(2,1)S(1)} %with_routing.1.after_ref.refs_0_), channel_id=1, source_target_pairs={{0,4},{4,8},{8,12},{12,0},{1,5},{5,9},{9,13},{13,1},{2,6},{6,10},{... | collective-permute-start | bytes 101384 | tf_op jit(solution)/shard_map/ppermute | solution.py:27
  3.9 2.6 %collective-permute-start.1 = (bf16[4,4224]{1,0:T(4,128)(2,1)S(1)}, bf16[4,4224]{1,0:T(4,128)(2,1)S(1)}, u32[]{:S(2)}, u32[]{:S(2)}) collective-permute-start(bf16[4,4224]{1,0:T(4,128)(2,1)S(1)} %with_routing.1.after_ref.refs_0_), channel_id=1, source_target_pairs={{0,8},{4,12},{8,0},{12,4},{1,9},{5,13},{9,1},{13,5},{2,10},{6,14},... | collective-permute-start | bytes 101384 | tf_op jit(solution)/shard_map/ppermute | solution.py:27
  6.5 1.3 %collective-permute-start = (bf16[4,4224]{1,0:T(4,128)(2,1)S(1)}, bf16[4,4224]{1,0:T(4,128)(2,1)S(1)}, u32[]{:S(2)}, u32[]{:S(2)}) collective-permute-start(bf16[4,4224]{1,0:T(4,128)(2,1)S(1)} %with_routing.1.after_ref.refs_0_), channel_id=1, source_target_pairs={{0,12},{4,0},{8,4},{12,8},{1,13},{5,1},{9,5},{13,9},{2,14},{6,2},{... | collective-permute-start | bytes 101384 | tf_op jit(solution)/shard_map/ppermute | solution.py:27
  7.9 2.9 %bring_weights.2 = (bf16[6,256,4096]{2,1,0:T(8,128)(2,1)S(1)}, bf16[6,256,4096]{2,1,0:T(8,128)(2,1)S(1)}, bf16[7,256,4096]{2,1,0:T(8,128)(2,1)S(1)}, f32[8,128]{1,0:T(8,128)S(1)}) custom-call(bf16[3072,4096]{1,0:T(8,128)(2,1)} %bitcast.3, bf16[3072,4096]{1,0:T(8,128)(2,1)} %bitcast.6, bf16[3072,4096]{1,0:T(8,128)(2,1)} %bitcast.9, ...), custom_call_target="tpu_custom_call" | custom-call | bytes 6291456 | tf_op jit(solution)/shard_map/bring_weights/pallas_call | solution.py:234
  10.7 0.0 collective-permute-done.2.refs_3_
  10.8 0.0 collective-permute-done.1.refs_2_
  10.8 0.0 collective-permute-done.refs_1_
  10.8 1.6 %collective-permute-start.3 = (bf16[16,4224]{1,0:T(8,128)(2,1)S(1)}, bf16[16,4224]{1,0:T(8,128)(2,1)S(1)}, u32[]{:S(2)}, u32[]{:S(2)}) collective-permute-start(bf16[16,4224]{1,0:T(8,128)(2,1)S(1)} %join.2.after_ref.refs_0_), channel_id=1, source_target_pairs={{0,2},{2,0},{1,3},{3,1},{4,6},{6,4},{5,7},{7,5},{8,10},{10,8},{9,1... | collective-permute-start | bytes 405512 | tf_op jit(solution)/shard_map/ppermute | solution.py:23
  12.4 3.5 %bring_weights.3 = (bf16[6,256,4096]{2,1,0:T(8,128)(2,1)S(1)}, bf16[6,256,4096]{2,1,0:T(8,128)(2,1)S(1)}, bf16[7,256,4096]{2,1,0:T(8,128)(2,1)S(1)}, f32[8,128]{1,0:T(8,128)S(1)}) custom-call(bf16[3072,4096]{1,0:T(8,128)(2,1)} %bitcast.4, bf16[3072,4096]{1,0:T(8,128)(2,1)} %bitcast.7, ...), custom_call_target="tpu_custom_call", output_to_operand_aliasing={{0}: (4, {}), {1}: (5, {}), {2}: (6, {})} | custom-call | bytes 8388608 | tf_op jit(solution)/shard_map/bring_weights/pallas_call | solution.py:234
  15.9 0.0 copy-start
  15.9 4.5 %copy-done = bf16[6,256,4096]{2,1,0:T(8,128)(2,1)} copy-done((bf16[6,256,4096]{2,1,0:T(8,128)(2,1)}, bf16[6,256,4096]{2,1,0:T(8,128)(2,1)S(1)}, u32[]{:S(2)}) %copy-start) | copy-done | bytes 12582936
  20.4 0.0 copy-start.2
  20.4 4.5 %copy-done.2 = bf16[6,256,4096]{2,1,0:T(8,128)(2,1)} copy-done((bf16[6,256,4096]{2,1,0:T(8,128)(2,1)}, bf16[6,256,4096]{2,1,0:T(8,128)(2,1)S(1)}, u32[]{:S(2)}) %copy-start.2) | copy-done | bytes 12582936
  24.9 0.0 collective-permute-done.3.refs_1_
  24.9 0.1 collective-permute-start.4
  25.0 1.5 %collective-permute-done.4.theirs_ref = bf16[32,4224]{1,0:T(8,128)(2,1)S(1)} collective-permute-done((bf16[32,4224]{1,0:T(8,128)(2,1)S(1)}, bf16[32,4224]{1,0:T(8,128)(2,1)S(1)}, u32[]{:S(2)}, u32[]{:S(2)}) %collective-permute-start.4) | collective-permute-done | bytes 270368 | tf_op jit(solution)/shard_map/ppermute | solution.py:23
  26.6 0.0 copy-start.1
  26.6 4.6 %copy-done.1 = bf16[6,256,4096]{2,1,0:T(8,128)(2,1)S(1)} copy-done((bf16[6,256,4096]{2,1,0:T(8,128)(2,1)S(1)}, bf16[6,256,4096]{2,1,0:T(8,128)(2,1)}, u32[]{:S(2)}) %copy-start.1) | copy-done | bytes 12582936
  31.1 0.0 copy-start.3
  31.1 4.6 %copy-done.3 = bf16[6,256,4096]{2,1,0:T(8,128)(2,1)S(1)} copy-done((bf16[6,256,4096]{2,1,0:T(8,128)(2,1)S(1)}, bf16[6,256,4096]{2,1,0:T(8,128)(2,1)}, u32[]{:S(2)}) %copy-start.3) | copy-done | bytes 12582936
  35.7 20.2 %expert_layer.1 = (f32[32,4096]{1,0:T(8,128)S(1)}, bf16[32,4096]{1,0:T(8,128)(2,1)S(1)}, bf16[6,256,4096]{2,1,0:T(8,128)(2,1)S(1)}, bf16[6,256,4096]{2,1,0:T(8,128)(2,1)S(1)}, bf16[7,256,4096]{2,1,0:T(8,128)(2,1)S(1)}) custom-call(bf16[32,4224]{1,0:T(8,128)(2,1)S(1)} %join.3.mine_ref, ...), custom_call_target="tpu_custom_call", output_to_operand_aliasing={{2}: (5, {}), {3}: (6, {}), {4}: (7, {})} | custom-call | flops 4831838208 | bytes 60817408 | tf_op jit(solution)/shard_map/expert_layer/pallas_call | solution.py:270
  56.0 0.2 collective-permute-start.5
  56.2 1.4 %collective-permute-done.5 = bf16[32,4096]{1,0:T(8,128)(2,1)S(1)} collective-permute-done((bf16[32,4096]{1,0:T(8,128)(2,1)S(1)}, bf16[32,4096]{1,0:T(8,128)(2,1)S(1)}, u32[]{:S(2)}, u32[]{:S(2)}) %collective-permute-start.5) | collective-permute-done | bytes 262176 | tf_op jit(solution)/shard_map/ppermute | solution.py:23
  57.6 0.1 convert_add_fusion
  57.6 0.6 collective-permute-start.6
  58.2 5.0 %collective-permute-done.6 = bf16[16,4096]{1,0:T(8,128)(2,1)S(1)} collective-permute-done((bf16[16,4096]{1,0:T(8,128)(2,1)S(1)}, bf16[16,4096]{1,0:T(8,128)(2,1)S(1)}, u32[]{:S(2)}, u32[]{:S(2)}) %collective-permute-start.6) | collective-permute-done | bytes 131104 | tf_op jit(solution)/shard_map/ppermute | solution.py:23
  63.3 0.7 %collective-permute-start.7 = (bf16[4,4096]{1,0:T(4,128)(2,1)S(1)}, bf16[4,4096]{1,0:T(4,128)(2,1)S(1)}, u32[]{:S(2)}, u32[]{:S(2)}) collective-permute-start(bf16[4,4096]{1,0:T(4,128)(2,1)S(1)} %get-tuple-element.27), channel_id=1, source_target_pairs={{0,4},{4,8},{8,12},{12,0},{1,5},{5,9},{9,13},{13,1},{2,6},{6,10},{... | collective-permute-start | bytes 98312 | tf_op jit(solution)/shard_map/ppermute | solution.py:27
  64.1 3.1 %collective-permute-start.9 = (bf16[4,4096]{1,0:T(4,128)(2,1)S(1)}, bf16[4,4096]{1,0:T(4,128)(2,1)S(1)}, u32[]{:S(2)}, u32[]{:S(2)}) collective-permute-start(bf16[4,4096]{1,0:T(4,128)(2,1)S(1)} %get-tuple-element.28), channel_id=1, source_target_pairs={{0,12},{4,0},{8,4},{12,8},{1,13},{5,1},{9,5},{13,9},{2,14},{6,2},{... | collective-permute-start | bytes 98312 | tf_op jit(solution)/shard_map/ppermute | solution.py:27
  67.2 0.0 collective-permute-start.8
  67.2 1.9 %collective-permute-done.7 = bf16[4,4096]{1,0:T(4,128)(2,1)S(1)} collective-permute-done((bf16[4,4096]{1,0:T(4,128)(2,1)S(1)}, bf16[4,4096]{1,0:T(4,128)(2,1)S(1)}, u32[]{:S(2)}, u32[]{:S(2)}) %collective-permute-start.7) | collective-permute-done | bytes 32800 | tf_op jit(solution)/shard_map/ppermute | solution.py:27
  69.1 0.0 collective-permute-done.9
  69.1 2.9 %collective-permute-done.8 = bf16[4,4096]{1,0:T(4,128)(2,1)S(1)} collective-permute-done((bf16[4,4096]{1,0:T(4,128)(2,1)S(1)}, bf16[4,4096]{1,0:T(4,128)(2,1)S(1)}, u32[]{:S(2)}, u32[]{:S(2)}) %collective-permute-start.8) | collective-permute-done | bytes 32800 | tf_op jit(solution)/shard_map/ppermute | solution.py:27
  72.0 0.6 fusion.2
  (5 shorter events, 0.1 us)
Async XLA Ops:
  0.9 9.9 %collective-permute-start.2 = (bf16[4,4224]{1,0:T(4,128)(2,1)S(1)}, bf16[4,4224]{1,0:T(4,128)(2,1)S(1)}, u32[]{:S(2)}, u32[]{:S(2)}) collective-permute-start(bf16[4,4224]{1,0:T(4,128)(2,1)S(1)} %with_routing.1.after_ref.refs_0_), channel_id=1, source_target_pairs={{0,4},{4,8},{8,12},{12,0},{1,5},{5,9},{9,13},{13,1},{2,6},{6,10},{... | collective-permute-start | bytes 101384 | tf_op jit(solution)/shard_map/ppermute | solution.py:27
  3.9 6.8 %collective-permute-start.1 = (bf16[4,4224]{1,0:T(4,128)(2,1)S(1)}, bf16[4,4224]{1,0:T(4,128)(2,1)S(1)}, u32[]{:S(2)}, u32[]{:S(2)}) collective-permute-start(bf16[4,4224]{1,0:T(4,128)(2,1)S(1)} %with_routing.1.after_ref.refs_0_), channel_id=1, source_target_pairs={{0,8},{4,12},{8,0},{12,4},{1,9},{5,13},{9,1},{13,5},{2,10},{6,14},... | collective-permute-start | bytes 101384 | tf_op jit(solution)/shard_map/ppermute | solution.py:27
  6.5 4.2 %collective-permute-start = (bf16[4,4224]{1,0:T(4,128)(2,1)S(1)}, bf16[4,4224]{1,0:T(4,128)(2,1)S(1)}, u32[]{:S(2)}, u32[]{:S(2)}) collective-permute-start(bf16[4,4224]{1,0:T(4,128)(2,1)S(1)} %with_routing.1.after_ref.refs_0_), channel_id=1, source_target_pairs={{0,12},{4,0},{8,4},{12,8},{1,13},{5,1},{9,5},{13,9},{2,14},{6,2},{... | collective-permute-start | bytes 101384 | tf_op jit(solution)/shard_map/ppermute | solution.py:27
  10.8 14.1 %collective-permute-start.3 = (bf16[16,4224]{1,0:T(8,128)(2,1)S(1)}, bf16[16,4224]{1,0:T(8,128)(2,1)S(1)}, u32[]{:S(2)}, u32[]{:S(2)}) collective-permute-start(bf16[16,4224]{1,0:T(8,128)(2,1)S(1)} %join.2.after_ref.refs_0_), channel_id=1, source_target_pairs={{0,2},{2,0},{1,3},{3,1},{4,6},{6,4},{5,7},{7,5},{8,10},{10,8},{9,1... | collective-permute-start | bytes 405512 | tf_op jit(solution)/shard_map/ppermute | solution.py:23
  15.9 4.5 %copy-start = (bf16[6,256,4096]{2,1,0:T(8,128)(2,1)}, bf16[6,256,4096]{2,1,0:T(8,128)(2,1)S(1)}, u32[]{:S(2)}) copy-start(bf16[6,256,4096]{2,1,0:T(8,128)(2,1)S(1)} %get-tuple-element.20.refs_0_) | copy-start | bytes 37748740
  20.4 4.5 %copy-start.2 = (bf16[6,256,4096]{2,1,0:T(8,128)(2,1)}, bf16[6,256,4096]{2,1,0:T(8,128)(2,1)S(1)}, u32[]{:S(2)}) copy-start(bf16[6,256,4096]{2,1,0:T(8,128)(2,1)S(1)} %get-tuple-element.21.refs_1_) | copy-start | bytes 37748740
  24.9 1.6 %collective-permute-start.4 = (bf16[32,4224]{1,0:T(8,128)(2,1)S(1)}, bf16[32,4224]{1,0:T(8,128)(2,1)S(1)}, u32[]{:S(2)}, u32[]{:S(2)}) collective-permute-start(bf16[32,4224]{1,0:T(8,128)(2,1)S(1)} %join.3.mine_ref), channel_id=1, source_target_pairs={{0,1},{1,0},{2,3},{3,2},{4,5},{5,4},{6,7},{7,6},{8,9},{9,8},{10,11... | collective-permute-start | bytes 811016 | tf_op jit(solution)/shard_map/ppermute | solution.py:23
  26.6 4.6 %copy-start.1 = (bf16[6,256,4096]{2,1,0:T(8,128)(2,1)S(1)}, bf16[6,256,4096]{2,1,0:T(8,128)(2,1)}, u32[]{:S(2)}) copy-start(bf16[6,256,4096]{2,1,0:T(8,128)(2,1)} %copy-done) | copy-start | bytes 37748740
  31.1 4.6 %copy-start.3 = (bf16[6,256,4096]{2,1,0:T(8,128)(2,1)S(1)}, bf16[6,256,4096]{2,1,0:T(8,128)(2,1)}, u32[]{:S(2)}) copy-start(bf16[6,256,4096]{2,1,0:T(8,128)(2,1)} %copy-done.2) | copy-start | bytes 37748740
  56.0 1.6 %collective-permute-start.5 = (bf16[32,4096]{1,0:T(8,128)(2,1)S(1)}, bf16[32,4096]{1,0:T(8,128)(2,1)S(1)}, u32[]{:S(2)}, u32[]{:S(2)}) collective-permute-start(bf16[32,4096]{1,0:T(8,128)(2,1)S(1)} %get-tuple-element.24), channel_id=1, source_target_pairs={{0,1},{1,0},{2,3},{3,2},{4,5},{5,4},{6,7},{7,6},{8,9},{9,8},{10,11... | collective-permute-start | bytes 786440 | tf_op jit(solution)/shard_map/ppermute | solution.py:23
  57.6 5.6 %collective-permute-start.6 = (bf16[16,4096]{1,0:T(8,128)(2,1)S(1)}, bf16[16,4096]{1,0:T(8,128)(2,1)S(1)}, u32[]{:S(2)}, u32[]{:S(2)}) collective-permute-start(bf16[16,4096]{1,0:T(8,128)(2,1)S(1)} %slice.47), channel_id=1, source_target_pairs={{0,2},{2,0},{1,3},{3,1},{4,6},{6,4},{5,7},{7,5},{8,10},{10,8},{9,1... | collective-permute-start | bytes 393224 | tf_op jit(solution)/shard_map/ppermute | solution.py:23
  63.3 5.8 %collective-permute-start.7 = (bf16[4,4096]{1,0:T(4,128)(2,1)S(1)}, bf16[4,4096]{1,0:T(4,128)(2,1)S(1)}, u32[]{:S(2)}, u32[]{:S(2)}) collective-permute-start(bf16[4,4096]{1,0:T(4,128)(2,1)S(1)} %get-tuple-element.27), channel_id=1, source_target_pairs={{0,4},{4,8},{8,12},{12,0},{1,5},{5,9},{9,13},{13,1},{2,6},{6,10},{... | collective-permute-start | bytes 98312 | tf_op jit(solution)/shard_map/ppermute | solution.py:27
  64.1 5.1 %collective-permute-start.9 = (bf16[4,4096]{1,0:T(4,128)(2,1)S(1)}, bf16[4,4096]{1,0:T(4,128)(2,1)S(1)}, u32[]{:S(2)}, u32[]{:S(2)}) collective-permute-start(bf16[4,4096]{1,0:T(4,128)(2,1)S(1)} %get-tuple-element.28), channel_id=1, source_target_pairs={{0,12},{4,0},{8,4},{12,8},{1,13},{5,1},{9,5},{13,9},{2,14},{6,2},{... | collective-permute-start | bytes 98312 | tf_op jit(solution)/shard_map/ppermute | solution.py:27
  67.2 4.8 %collective-permute-start.8 = (bf16[4,4096]{1,0:T(4,128)(2,1)S(1)}, bf16[4,4096]{1,0:T(4,128)(2,1)S(1)}, u32[]{:S(2)}, u32[]{:S(2)}) collective-permute-start(bf16[4,4096]{1,0:T(4,128)(2,1)S(1)} %get-tuple-element.29), channel_id=1, source_target_pairs={{0,8},{4,12},{8,0},{12,4},{1,9},{5,13},{9,1},{13,5},{2,10},{6,14},... | collective-permute-start | bytes 98312 | tf_op jit(solution)/shard_map/ppermute | solution.py:27

commit v19 on v16

--- a/solution.py
+++ b/solution.py
@@ -302,7 +302,7 @@
             total = total[:half] + theirs.astype(jnp.float32)
         blocks = total.reshape(span, tokens.shape[0], depth)
         total = blocks[0]
-        for by in range(1, span):
+        for by in reversed(range(1, span)):
             theirs = shift(blocks[by].astype(jnp.bfloat16), "wide", span, by)
             total = total + theirs.astype(jnp.float32)
         return total.astype(jnp.bfloat16)

time: 54.6 us -> 54.5 us (level)
  no operation moved by 1% of the time
where the time goes in v19:
time: 54.5 us; the launch traced here: 54.4 us
  Pallas kernels  27.5 us (50%)
  starting transfers between devices  13.9 us (26%)
  waiting for transfers between devices  12.1 us (22%)
  other arithmetic  0.74 us (1%)
    pallas_call x1, Pallas kernels, local(): pl.pallas_call(functools.partial(layer, top, ff_dev, row_block, step_unit...  20.2 us
    ppermute x6, starting transfers between devices, shift(): return lax.ppermute(x, axis, [(i, (i + by) % size) for i in range(size)])  10.5 us
    ppermute x4, waiting for transfers between devices, swap(): return lax.ppermute(x, axis, [(i, i ^ by) for i in range(size)])  7 us
    pallas_call x2, Pallas kernels, local(): pl.pallas_call(functools.partial(bring, early, more), out_shape=ring_shap...  6.36 us
    ppermute x6, waiting for transfers between devices, shift(): return lax.ppermute(x, axis, [(i, (i + by) % size) for i in range(size)])  5.09 us
    ppermute x4, starting transfers between devices, swap(): return lax.ppermute(x, axis, [(i, i ^ by) for i in range(size)])  3.37 us
  transfers between devices with their start and end apart: 10, of which 5 were waited for; matrix products, arithmetic and copies ran while one was open for 0% of the time, Pallas kernels for 12%

profile of v19, /device:TPU:0, one launch (start us, length us, event | category | flops | bytes accessed | tf_op | source)
XLA Modules:
  0.0 54.4 jit_solution(6986372142671283539)
XLA Ops:
  0.0 0.9 %with_routing.1.after_ref.refs_0_ = bf16[4,4224]{1,0:T(4,128)(2,1)S(1)} custom-call(bf16[4,4096]{1,0:T(4,128)(2,1)} %tokens_ref.1, s32[4,8]{1,0:T(4,128)} %ids_ref.1, s32[4,8]{1,0:T(4,128)} %numer_ref.1), custom_call_target="tpu_custom_call" | custom-call | tf_op jit(solution)/shard_map/with_routing/pallas_call | solution.py:200
  0.9 3.1 %collective-permute-start.2 = (bf16[4,4224]{1,0:T(4,128)(2,1)S(1)}, bf16[4,4224]{1,0:T(4,128)(2,1)S(1)}, u32[]{:S(2)}, u32[]{:S(2)}) collective-permute-start(bf16[4,4224]{1,0:T(4,128)(2,1)S(1)} %with_routing.1.after_ref.refs_0_), channel_id=1, source_target_pairs={{0,4},{4,8},{8,12},{12,0},{1,5},{5,9},{9,13},{13,1},{2,6},{6,10},{... | collective-permute-start | bytes 101384 | tf_op jit(solution)/shard_map/ppermute | solution.py:27
  3.9 2.6 %collective-permute-start.1 = (bf16[4,4224]{1,0:T(4,128)(2,1)S(1)}, bf16[4,4224]{1,0:T(4,128)(2,1)S(1)}, u32[]{:S(2)}, u32[]{:S(2)}) collective-permute-start(bf16[4,4224]{1,0:T(4,128)(2,1)S(1)} %with_routing.1.after_ref.refs_0_), channel_id=1, source_target_pairs={{0,8},{4,12},{8,0},{12,4},{1,9},{5,13},{9,1},{13,5},{2,10},{6,14},... | collective-permute-start | bytes 101384 | tf_op jit(solution)/shard_map/ppermute | solution.py:27
  6.5 1.3 %collective-permute-start = (bf16[4,4224]{1,0:T(4,128)(2,1)S(1)}, bf16[4,4224]{1,0:T(4,128)(2,1)S(1)}, u32[]{:S(2)}, u32[]{:S(2)}) collective-permute-start(bf16[4,4224]{1,0:T(4,128)(2,1)S(1)} %with_routing.1.after_ref.refs_0_), channel_id=1, source_target_pairs={{0,12},{4,0},{8,4},{12,8},{1,13},{5,1},{9,5},{13,9},{2,14},{6,2},{... | collective-permute-start | bytes 101384 | tf_op jit(solution)/shard_map/ppermute | solution.py:27
  7.9 2.9 %bring_weights.2 = (bf16[4,256,4096]{2,1,0:T(8,128)(2,1)S(1)}, bf16[4,256,4096]{2,1,0:T(8,128)(2,1)S(1)}, bf16[5,256,4096]{2,1,0:T(8,128)(2,1)S(1)}, f32[8,128]{1,0:T(8,128)S(1)}) custom-call(bf16[3072,4096]{1,0:T(8,128)(2,1)} %bitcast.3, bf16[3072,4096]{1,0:T(8,128)(2,1)} %bitcast.6, bf16[3072,4096]{1,0:T(8,128)(2,1)} %bitcast.9, ...), custom_call_target="tpu_custom_call" | custom-call | bytes 6291456 | tf_op jit(solution)/shard_map/bring_weights/pallas_call | solution.py:234
  10.7 0.0 collective-permute-done.2.refs_3_
  10.8 0.0 collective-permute-done.1.refs_2_
  10.8 0.0 collective-permute-done.refs_1_
  10.8 1.6 %collective-permute-start.3 = (bf16[16,4224]{1,0:T(8,128)(2,1)S(1)}, bf16[16,4224]{1,0:T(8,128)(2,1)S(1)}, u32[]{:S(2)}, u32[]{:S(2)}) collective-permute-start(bf16[16,4224]{1,0:T(8,128)(2,1)S(1)} %join.2.after_ref.refs_0_), channel_id=1, source_target_pairs={{0,2},{2,0},{1,3},{3,1},{4,6},{6,4},{5,7},{7,5},{8,10},{10,8},{9,1... | collective-permute-start | bytes 405512 | tf_op jit(solution)/shard_map/ppermute | solution.py:23
  12.4 3.5 %bring_weights.3 = (bf16[4,256,4096]{2,1,0:T(8,128)(2,1)S(1)}, bf16[4,256,4096]{2,1,0:T(8,128)(2,1)S(1)}, bf16[5,256,4096]{2,1,0:T(8,128)(2,1)S(1)}, f32[8,128]{1,0:T(8,128)S(1)}) custom-call(bf16[3072,4096]{1,0:T(8,128)(2,1)} %bitcast.4, bf16[3072,4096]{1,0:T(8,128)(2,1)} %bitcast.7, ...), custom_call_target="tpu_custom_call", output_to_operand_aliasing={{0}: (4, {}), {1}: (5, {}), {2}: (6, {})} | custom-call | bytes 8388608 | tf_op jit(solution)/shard_map/bring_weights/pallas_call | solution.py:234
  15.9 0.0 collective-permute-done.3.refs_1_
  15.9 0.1 collective-permute-start.4
  16.0 1.5 %collective-permute-done.4.theirs_ref = bf16[32,4224]{1,0:T(8,128)(2,1)S(1)} collective-permute-done((bf16[32,4224]{1,0:T(8,128)(2,1)S(1)}, bf16[32,4224]{1,0:T(8,128)(2,1)S(1)}, u32[]{:S(2)}, u32[]{:S(2)}) %collective-permute-start.4) | collective-permute-done | bytes 270368 | tf_op jit(solution)/shard_map/ppermute | solution.py:23
  17.5 20.2 %expert_layer.1 = (f32[32,4096]{1,0:T(8,128)S(1)}, bf16[32,4096]{1,0:T(8,128)(2,1)S(1)}, bf16[4,256,4096]{2,1,0:T(8,128)(2,1)S(1)}, bf16[4,256,4096]{2,1,0:T(8,128)(2,1)S(1)}, bf16[5,256,4096]{2,1,0:T(8,128)(2,1)S(1)}) custom-call(bf16[32,4224]{1,0:T(8,128)(2,1)S(1)} %join.3.mine_ref, ...), custom_call_target="tpu_custom_call", output_to_operand_aliasing={{2}: (5, {}), {3}: (6, {}), {4}: (7, {})} | custom-call | flops 4831838208 | bytes 60817408 | tf_op jit(solution)/shard_map/expert_layer/pallas_call | solution.py:270
  37.7 0.2 collective-permute-start.5
  37.9 1.4 %collective-permute-done.5 = bf16[32,4096]{1,0:T(8,128)(2,1)S(1)} collective-permute-done((bf16[32,4096]{1,0:T(8,128)(2,1)S(1)}, bf16[32,4096]{1,0:T(8,128)(2,1)S(1)}, u32[]{:S(2)}, u32[]{:S(2)}) %collective-permute-start.5) | collective-permute-done | bytes 262176 | tf_op jit(solution)/shard_map/ppermute | solution.py:23
  39.3 0.1 convert_add_fusion
  39.4 1.5 %collective-permute-start.6 = (bf16[16,4096]{1,0:T(8,128)(2,1)S(1)}, bf16[16,4096]{1,0:T(8,128)(2,1)S(1)}, u32[]{:S(2)}, u32[]{:S(2)}) collective-permute-start(bf16[16,4096]{1,0:T(8,128)(2,1)S(1)} %slice.47), channel_id=1, source_target_pairs={{0,2},{2,0},{1,3},{3,1},{4,6},{6,4},{5,7},{7,5},{8,10},{10,8},{9,1... | collective-permute-start | bytes 393224 | tf_op jit(solution)/shard_map/ppermute | solution.py:23
  41.0 4.1 %collective-permute-done.6 = bf16[16,4096]{1,0:T(8,128)(2,1)S(1)} collective-permute-done((bf16[16,4096]{1,0:T(8,128)(2,1)S(1)}, bf16[16,4096]{1,0:T(8,128)(2,1)S(1)}, u32[]{:S(2)}, u32[]{:S(2)}) %collective-permute-start.6) | collective-permute-done | bytes 131104 | tf_op jit(solution)/shard_map/ppermute | solution.py:23
  45.1 2.9 %collective-permute-start.7 = (bf16[4,4096]{1,0:T(4,128)(2,1)S(1)}, bf16[4,4096]{1,0:T(4,128)(2,1)S(1)}, u32[]{:S(2)}, u32[]{:S(2)}) collective-permute-start(bf16[4,4096]{1,0:T(4,128)(2,1)S(1)} %get-tuple-element.27), channel_id=1, source_target_pairs={{0,12},{4,0},{8,4},{12,8},{1,13},{5,1},{9,5},{13,9},{2,14},{6,2},{... | collective-permute-start | bytes 98312 | tf_op jit(solution)/shard_map/ppermute | solution.py:27
  48.0 0.0 collective-permute-start.9
  48.0 0.6 %collective-permute-start.8 = (bf16[4,4096]{1,0:T(4,128)(2,1)S(1)}, bf16[4,4096]{1,0:T(4,128)(2,1)S(1)}, u32[]{:S(2)}, u32[]{:S(2)}) collective-permute-start(bf16[4,4096]{1,0:T(4,128)(2,1)S(1)} %get-tuple-element.29), channel_id=1, source_target_pairs={{0,8},{4,12},{8,0},{12,4},{1,9},{5,13},{9,1},{13,5},{2,10},{6,14},... | collective-permute-start | bytes 98312 | tf_op jit(solution)/shard_map/ppermute | solution.py:27
  48.6 1.0 %collective-permute-done.7 = bf16[4,4096]{1,0:T(4,128)(2,1)S(1)} collective-permute-done((bf16[4,4096]{1,0:T(4,128)(2,1)S(1)}, bf16[4,4096]{1,0:T(4,128)(2,1)S(1)}, u32[]{:S(2)}, u32[]{:S(2)}) %collective-permute-start.7) | collective-permute-done | bytes 32800 | tf_op jit(solution)/shard_map/ppermute | solution.py:27
  49.6 4.1 %collective-permute-done.9 = bf16[4,4096]{1,0:T(4,128)(2,1)S(1)} collective-permute-done((bf16[4,4096]{1,0:T(4,128)(2,1)S(1)}, bf16[4,4096]{1,0:T(4,128)(2,1)S(1)}, u32[]{:S(2)}, u32[]{:S(2)}) %collective-permute-start.9) | collective-permute-done | bytes 32800 | tf_op jit(solution)/shard_map/ppermute | solution.py:27
  53.7 0.0 collective-permute-done.8
  53.7 0.7 %fusion.2 = bf16[4,4096]{1,0:T(4,128)(2,1)} fusion(f32[16,4096]{1,0:T(8,128)S(1)} %get-tuple-element.26, bf16[4,4096]{1,0:T(4,128)(2,1)S(1)} %collective-permute-done.9, bf16[4,4096]{1,0:T(4,128)(2,1)S(1)} %collective-permute-done.8, bf16[4,4096]{1,0:T(4,128)(2,1)S(1)} %collective-permute-done.7), kind=kLoop, calls=%fused_computation.6 | loop fusion | flops 114688 | bytes 196608 | tf_op jit(solution)/shard_map/convert_element_type | solution.py:308
  (5 shorter events, 0.1 us)
Async XLA Ops:
  0.9 9.9 %collective-permute-start.2 = (bf16[4,4224]{1,0:T(4,128)(2,1)S(1)}, bf16[4,4224]{1,0:T(4,128)(2,1)S(1)}, u32[]{:S(2)}, u32[]{:S(2)}) collective-permute-start(bf16[4,4224]{1,0:T(4,128)(2,1)S(1)} %with_routing.1.after_ref.refs_0_), channel_id=1, source_target_pairs={{0,4},{4,8},{8,12},{12,0},{1,5},{5,9},{9,13},{13,1},{2,6},{6,10},{... | collective-permute-start | bytes 101384 | tf_op jit(solution)/shard_map/ppermute | solution.py:27
  3.9 6.8 %collective-permute-start.1 = (bf16[4,4224]{1,0:T(4,128)(2,1)S(1)}, bf16[4,4224]{1,0:T(4,128)(2,1)S(1)}, u32[]{:S(2)}, u32[]{:S(2)}) collective-permute-start(bf16[4,4224]{1,0:T(4,128)(2,1)S(1)} %with_routing.1.after_ref.refs_0_), channel_id=1, source_target_pairs={{0,8},{4,12},{8,0},{12,4},{1,9},{5,13},{9,1},{13,5},{2,10},{6,14},... | collective-permute-start | bytes 101384 | tf_op jit(solution)/shard_map/ppermute | solution.py:27
  6.5 4.2 %collective-permute-start = (bf16[4,4224]{1,0:T(4,128)(2,1)S(1)}, bf16[4,4224]{1,0:T(4,128)(2,1)S(1)}, u32[]{:S(2)}, u32[]{:S(2)}) collective-permute-start(bf16[4,4224]{1,0:T(4,128)(2,1)S(1)} %with_routing.1.after_ref.refs_0_), channel_id=1, source_target_pairs={{0,12},{4,0},{8,4},{12,8},{1,13},{5,1},{9,5},{13,9},{2,14},{6,2},{... | collective-permute-start | bytes 101384 | tf_op jit(solution)/shard_map/ppermute | solution.py:27
  10.8 5.1 %collective-permute-start.3 = (bf16[16,4224]{1,0:T(8,128)(2,1)S(1)}, bf16[16,4224]{1,0:T(8,128)(2,1)S(1)}, u32[]{:S(2)}, u32[]{:S(2)}) collective-permute-start(bf16[16,4224]{1,0:T(8,128)(2,1)S(1)} %join.2.after_ref.refs_0_), channel_id=1, source_target_pairs={{0,2},{2,0},{1,3},{3,1},{4,6},{6,4},{5,7},{7,5},{8,10},{10,8},{9,1... | collective-permute-start | bytes 405512 | tf_op jit(solution)/shard_map/ppermute | solution.py:23
  15.9 1.6 %collective-permute-start.4 = (bf16[32,4224]{1,0:T(8,128)(2,1)S(1)}, bf16[32,4224]{1,0:T(8,128)(2,1)S(1)}, u32[]{:S(2)}, u32[]{:S(2)}) collective-permute-start(bf16[32,4224]{1,0:T(8,128)(2,1)S(1)} %join.3.mine_ref), channel_id=1, source_target_pairs={{0,1},{1,0},{2,3},{3,2},{4,5},{5,4},{6,7},{7,6},{8,9},{9,8},{10,11... | collective-permute-start | bytes 811016 | tf_op jit(solution)/shard_map/ppermute | solution.py:23
  37.7 1.6 %collective-permute-start.5 = (bf16[32,4096]{1,0:T(8,128)(2,1)S(1)}, bf16[32,4096]{1,0:T(8,128)(2,1)S(1)}, u32[]{:S(2)}, u32[]{:S(2)}) collective-permute-start(bf16[32,4096]{1,0:T(8,128)(2,1)S(1)} %get-tuple-element.24), channel_id=1, source_target_pairs={{0,1},{1,0},{2,3},{3,2},{4,5},{5,4},{6,7},{7,6},{8,9},{9,8},{10,11... | collective-permute-start | bytes 786440 | tf_op jit(solution)/shard_map/ppermute | solution.py:23
  39.4 5.6 %collective-permute-start.6 = (bf16[16,4096]{1,0:T(8,128)(2,1)S(1)}, bf16[16,4096]{1,0:T(8,128)(2,1)S(1)}, u32[]{:S(2)}, u32[]{:S(2)}) collective-permute-start(bf16[16,4096]{1,0:T(8,128)(2,1)S(1)} %slice.47), channel_id=1, source_target_pairs={{0,2},{2,0},{1,3},{3,1},{4,6},{6,4},{5,7},{7,5},{8,10},{10,8},{9,1... | collective-permute-start | bytes 393224 | tf_op jit(solution)/shard_map/ppermute | solution.py:23
  45.1 4.5 %collective-permute-start.7 = (bf16[4,4096]{1,0:T(4,128)(2,1)S(1)}, bf16[4,4096]{1,0:T(4,128)(2,1)S(1)}, u32[]{:S(2)}, u32[]{:S(2)}) collective-permute-start(bf16[4,4096]{1,0:T(4,128)(2,1)S(1)} %get-tuple-element.27), channel_id=1, source_target_pairs={{0,12},{4,0},{8,4},{12,8},{1,13},{5,1},{9,5},{13,9},{2,14},{6,2},{... | collective-permute-start | bytes 98312 | tf_op jit(solution)/shard_map/ppermute | solution.py:27
  48.0 5.7 %collective-permute-start.9 = (bf16[4,4096]{1,0:T(4,128)(2,1)S(1)}, bf16[4,4096]{1,0:T(4,128)(2,1)S(1)}, u32[]{:S(2)}, u32[]{:S(2)}) collective-permute-start(bf16[4,4096]{1,0:T(4,128)(2,1)S(1)} %get-tuple-element.28), channel_id=1, source_target_pairs={{0,4},{4,8},{8,12},{12,0},{1,5},{5,9},{9,13},{13,1},{2,6},{6,10},{... | collective-permute-start | bytes 98312 | tf_op jit(solution)/shard_map/ppermute | solution.py:27
  48.0 5.7 %collective-permute-start.8 = (bf16[4,4096]{1,0:T(4,128)(2,1)S(1)}, bf16[4,4096]{1,0:T(4,128)(2,1)S(1)}, u32[]{:S(2)}, u32[]{:S(2)}) collective-permute-start(bf16[4,4096]{1,0:T(4,128)(2,1)S(1)} %get-tuple-element.29), channel_id=1, source_target_pairs={{0,8},{4,12},{8,0},{12,4},{1,9},{5,13},{9,1},{13,5},{2,10},{6,14},... | collective-permute-start | bytes 98312 | tf_op jit(solution)/shard_map/ppermute | solution.py:27
